TPU v7x, 512 devices: a whole 4x4x16 slice. The times are simulated.
512 devices in a mesh: cut: 32 (over z, y_lo), depth: 16 (over x, y_hi, core).
Axes of the slice: x: 4, y: 4 (y_hi: 2, y_lo: 2; y = y_hi * 2 + y_lo), z: 16, core: 2. Of those that a mesh axis runs over, the one named last changes fastest.
Arguments:
- positions: float32 [2, 64, 128, 128], P(None, 'cut', 'depth'), may hold values from 0 to 128, as said below
- velocity: float32 [2, 64, 128, 128], P(None, 'cut', 'depth'), may hold values from -3 to 3
- density: float32 [64, 128, 128], P('cut', 'depth'), may hold values from 0.9 to 1.1
- counts: int32 [64, 128], P('cut', 'depth'), may hold values from 16 to 128, as said below
- contact_mask: int32 [64, 128], P('cut', 'depth'), may hold values 0 or 1
- destination: int32 [32], replicated, may hold values from 0 to 31, each once
- tool: float32 [2], replicated, may hold values from -0.5 to 0.5
Outputs:
- particles: float32 [5, 64, 128, 128], P(None, 'cut', 'depth')
- tool_state: float32 [2], replicated
Inputs may be any that keep to these rules, and one draw needn't show every extreme that they name: `counts`: cell (0, 0) holds 128 live particles. `positions`: each particle lies inside its own cell: coordinates of cell (i, j) lie in [i, i+1) x [j, j+1).
All inputs are finite; a program needn't handle non-finite values. No bound on the sum of `contact_mask` on one device may be relied on, other than what follows from the above.
Results may differ from a plain program's by a relative error of at most 0.0003.
Values sent between devices are 32-bit elements; how exact they have to be, the bound alone decides.
No kernel may reach another device: no remote copies, remote signals or barrier semaphores. Data moves between devices by JAX's collectives and lax.ppermute only.
A program may use at most 64 MiB of HBM per device.

v0:
```python
import jax
import jax.numpy as jnp
from jax import lax
from jax.sharding import PartitionSpec as P

STEPS = 4


MASS = 0.02
SOUND = 20.0
VISCOSITY = 2.0
STIFF = 50.0
DT = 0.05


def extended(value, sides, width):
    for axis, dim in sides:
        size, length = (lax.axis_size(axis), value.shape[dim])
        up = [(i, (i + 1) % size) for i in range(size - 1)]
        down = [(j, i) for i, j in up]
        last = lax.slice_in_dim(value, length - width, length, axis=dim)
        leading = lax.slice_in_dim(value, 0, width, axis=dim)
        before = lax.ppermute(last, axis, up)
        after = lax.ppermute(leading, axis, down)
        value = jnp.concatenate([before, value, after], axis=dim)
    return value


def cell_rates(ext):
    rows = ext.shape[1] - 2
    cols = ext.shape[2] - 2
    mid = ext[:, 1 : rows + 1, 1 : cols + 1]
    xi = mid[0][..., :, None]
    yi = mid[1][..., :, None]
    ui = mid[2][..., :, None]
    vi = mid[3][..., :, None]
    rho_i = jnp.where(mid[5] > 0, mid[4], 1.0)[..., :, None]
    press_i = SOUND * (rho_i - 1.0) / (rho_i * rho_i)
    acc_x = jnp.zeros(mid[0].shape, ext.dtype)
    acc_y = jnp.zeros(mid[0].shape, ext.dtype)
    drho = jnp.zeros(mid[0].shape, ext.dtype)
    for a in range(3):
        for b in range(3):
            nbr = ext[:, a : a + rows, b : b + cols]
            dx = xi - nbr[0][..., None, :]
            dy = yi - nbr[1][..., None, :]
            q = jnp.maximum(0.0, 1.0 - dx * dx - dy * dy)
            live_j = nbr[5][..., None, :]
            rho_j = jnp.where(nbr[5] > 0, nbr[4], 1.0)[..., None, :]
            press_j = SOUND * (rho_j - 1.0) / (rho_j * rho_j)
            grad = -6.0 * q * q * live_j
            coef = MASS * (press_i + press_j) * grad
            du = ui - nbr[2][..., None, :]
            dv = vi - nbr[3][..., None, :]
            visc = VISCOSITY * MASS * q * q * q * live_j / rho_j
            acc_x = acc_x + jnp.sum(-coef * dx - visc * du, -1)
            acc_y = acc_y + jnp.sum(-coef * dy - visc * dv, -1)
            drho = drho + jnp.sum(MASS * grad * (du * dx + dv * dy), -1)
    return jnp.stack([acc_x, acc_y, drho])


def column_rates(ext):
    columns = ext.shape[1] - 2

    def one_column(index):
        return cell_rates(lax.dynamic_slice_in_dim(ext, index, 3, 1))[:, 0]

    found = lax.map(one_column, jnp.arange(columns))
    return jnp.moveaxis(found, 0, 1)


def contact(region, offset, first_col):
    cells = first_col + jnp.arange(region.shape[1]).astype(region.dtype)
    local = region[0] - cells[:, None, None]
    return region[6] * region[5] * jnp.maximum(0.0, local + offset - 0.5)


def update(region, rates, pen):
    live = region[5]
    u = region[2] + DT * live * (rates[0] - STIFF * pen)
    v = region[3] + DT * live * rates[1]
    x = region[0] + DT * live * u
    y = region[1] + DT * live * v
    rho = region[4] + DT * live * rates[2]
    return jnp.stack([x, y, u, v, rho, live, region[6]])


def tool_step(tool, force, slots):
    speed = tool[1] + DT * (1.0 - force / slots)
    return jnp.stack([tool[0] + DT * speed, speed])


def total_force(pen):
    return lax.psum(jnp.sum(STIFF * pen), ("cut", "depth"))


def body(positions, velocity, density, counts, contact_mask, destination, tool):
    dtype = positions.dtype
    cols = positions.shape[1]
    rows = positions.shape[2]
    slot_count = positions.shape[3]
    ncut = lax.axis_size("cut")
    slots = ncut * cols * lax.axis_size("depth") * rows * slot_count * 1.0
    here = lax.axis_index("cut")
    first_col = (here * cols).astype(dtype)
    slot = jnp.arange(slot_count)
    live = (slot[None, None, :] < counts[:, :, None]).astype(dtype)
    touch = jnp.broadcast_to(contact_mask[:, :, None].astype(dtype), live.shape)
    state = jnp.concatenate([positions, velocity, density[None], live[None], touch[None]], 0)
    for step in range(STEPS):
        ext = extended(state, (("cut", 1), ("depth", 2)), 1)
        rates = column_rates(ext)
        pen = contact(state, tool[0], first_col)
        force = total_force(pen)
        state = update(state, rates, pen)
        tool = tool_step(tool, force, slots)
    core = state[:5]
    blocks = jnp.arange(ncut)
    within = jnp.arange(cols)
    piece = lax.all_gather(core, "cut", axis=1, tiled=True)
    width = piece.shape[1]
    column = jnp.arange(width)
    owner = column // cols
    target = jnp.sum(jnp.where(owner[:, None] == blocks[None, :], destination[None, :], 0), 1)
    keep = (target == here)[:, None] & ((column % cols)[:, None] == within[None, :])
    table = keep.astype(dtype)
    moved = jnp.einsum("cjyp,jk->ckyp", piece, table, precision=lax.Precision.HIGHEST)
    return (moved, tool)


def solution(mesh):
    return jax.shard_map(
        body,
        mesh=mesh,
        in_specs=(
            P(None, "cut", "depth", None),
            P(None, "cut", "depth", None),
            P("cut", "depth", None),
            P("cut", "depth"),
            P("cut", "depth"),
            P(),
            P(),
        ),
        out_specs=(P(None, "cut", "depth", None), P()),
        check_vma=False,
    )
```

profile of v0, /device:TPU:4, one launch (start us, length us, event | category | flops | bytes accessed | tf_op | source)
XLA Modules:
  0.0 649.8 jit_solution(5432018301401568447)
XLA Ops:
  10.9 3.5 collective-permute-start
  17.0 3.1 collective-permute-done.1
  22.0 6.0 collective-permute-start.3
  29.6 28.2 %while.52 = (s32[]{:T(128)}, f32[2,3,8,128]{3,2,0,1:T(8,128)S(1)}, s32[2]{0:T(128)S(1)}, f32[7,4,10,128]{3,2,1,0:T(8,128)S(1)}, s32[]{:T(128)}, /*index=5*/s32[]...) while((s32[]{:T(128)}, f32[2,3,8,128]{3,2,0,1:T(8,128)S(1)}, s32[2]{0:T(128)S(1)}, ...), condition=%wide.region_29.30_spmd, body=%wide.region_1.29_spmd.sunk | while | flops 41346060 | bytes 1077551 | solution.py:68
  34.0 2.4 fusion.897
  36.4 2.4 fusion.896
  38.8 2.4 fusion.895
  41.2 2.4 fusion.894
  48.1 2.4 fusion.897
  50.5 2.4 fusion.896
  52.9 2.4 fusion.895
  55.3 2.4 fusion.894
  58.9 4.6 collective-permute-start.4
  65.0 4.2 collective-permute-done.5
  71.5 5.7 collective-permute-start.7
  78.6 106.8 %psum.28 = f32[]{:T(128)} all-reduce(f32[]{:T(128)} %fusion.781), channel_id=1, replica_groups=mesh['cut'=32,'depth'=16] {'cut','depth'}, use_global_device_ids=true, to_apply=%region_60.61 | all-reduce | flops 1 | bytes 8 | tf_op jit(solution)/shard_map/psum | solution.py:94
  187.4 27.7 %while.53 = (s32[]{:T(128)}, f32[2,3,8,128]{3,2,0,1:T(8,128)S(1)}, s32[2]{0:T(128)S(1)}, f32[7,4,10,128]{3,2,1,0:T(8,128)S(1)}, s32[]{:T(128)}, /*index=5*/s32[]...) while((s32[]{:T(128)}, f32[2,3,8,128]{3,2,0,1:T(8,128)S(1)}, s32[2]{0:T(128)S(1)}, ...), condition=%wide.region_58.59_spmd, body=%wide.region_30.58_spmd.sunk | while | flops 41346060 | bytes 1077551 | solution.py:68
  191.5 2.4 fusion.903
  193.9 2.4 fusion.902
  196.3 2.4 fusion.901
  198.8 2.4 fusion.900
  205.4 2.4 fusion.903
  207.8 2.4 fusion.902
  210.2 2.4 fusion.901
  215.6 3.0 collective-permute-start.8
  220.1 4.2 collective-permute-done.9
  226.3 6.0 collective-permute-start.11
  233.7 100.8 %psum.29 = f32[]{:T(128)} all-reduce(f32[]{:T(128)} %get-tuple-element.624), channel_id=1, replica_groups=mesh['cut'=32,'depth'=16] {'cut','depth'}, use_global_device_ids=true, to_apply=%region_91.92 | all-reduce | flops 1 | bytes 8 | tf_op jit(solution)/shard_map/psum | solution.py:94
  335.2 27.8 %while.54 = (s32[]{:T(128)}, f32[2,3,8,128]{3,2,0,1:T(8,128)S(1)}, s32[2]{0:T(128)S(1)}, f32[7,4,10,128]{3,2,1,0:T(8,128)S(1)}, s32[]{:T(128)}, /*index=5*/s32[]...) while((s32[]{:T(128)}, f32[2,3,8,128]{3,2,0,1:T(8,128)S(1)}, s32[2]{0:T(128)S(1)}, ...), condition=%wide.region_89.90_spmd, body=%wide.region_61.89_spmd.sunk | while | flops 41346060 | bytes 1077551 | solution.py:68
  339.4 2.4 fusion.909
  341.8 2.4 fusion.908
  344.2 2.4 fusion.907
  353.3 2.4 fusion.909
  355.7 2.4 fusion.908
  358.1 2.4 fusion.907
  363.4 3.6 collective-permute-start.12
  368.5 4.2 collective-permute-done.13
  374.7 6.0 collective-permute-start.15
  381.4 100.3 %psum.30 = f32[]{:T(128)} all-reduce(f32[]{:T(128)} %fusion.774), channel_id=1, replica_groups=mesh['cut'=32,'depth'=16] {'cut','depth'}, use_global_device_ids=true, to_apply=%region_122.123 | all-reduce | flops 1 | bytes 8 | tf_op jit(solution)/shard_map/psum | solution.py:94
  482.5 27.7 %while.55 = (s32[]{:T(128)}, f32[2,3,8,128]{3,2,0,1:T(8,128)S(1)}, s32[2]{0:T(128)S(1)}, f32[7,4,10,128]{3,2,1,0:T(8,128)S(1)}, s32[]{:T(128)}, /*index=5*/s32[]...) while((s32[]{:T(128)}, f32[2,3,8,128]{3,2,0,1:T(8,128)S(1)}, s32[2]{0:T(128)S(1)}, ...), condition=%wide.region_120.121_spmd, body=%wide.region_92.120_spmd.sunk | while | flops 41346060 | bytes 1077551 | solution.py:68
  486.7 2.4 fusion.915
  489.1 2.4 fusion.914
  491.5 2.4 fusion.913
  500.6 2.4 fusion.915
  503.0 2.4 fusion.914
  505.4 2.4 fusion.913
  512.2 100.2 %psum.31 = f32[]{:T(128)} all-reduce(f32[]{:T(128)} %fusion.737), channel_id=1, replica_groups=mesh['cut'=32,'depth'=16] {'cut','depth'}, use_global_device_ids=true, to_apply=%region_124.125 | all-reduce | flops 1 | bytes 8 | tf_op jit(solution)/shard_map/psum | solution.py:94
  613.6 26.8 %all-gather.2.cloned.1.call-done = f32[5,64,8,128]{3,2,0,1:T(8,128)} async-done(((f32[5,2,8,128]{3,2,0,1:T(8,128)}), f32[5,64,8,128]{3,2,0,1:T(8,128)}) %all-gather.2.cloned.1.call-update) | async-done | bytes 1310736 | tf_op jit(solution)/shard_map/all_gather | solution.py:120
  (160 shorter events, 60.7 us)
Async XLA Ops:
  7.2 633.3 %all-gather.2.cloned.1.call-start = ((), (), s32[]{:S(2)}) async-start(), calls=%async_computation | async-start | bytes 1351680 | tf_op jit(solution)/shard_map/all_gather | solution.py:120
  10.9 6.1 collective-permute-start
  14.3 5.8 collective-permute-start.1
  20.1 8.0 %collective-permute-start.2 = (f32[7,4,1,128]{3,2,1,0:T(1,128)S(1)}, f32[7,4,1,128]{3,2,1,0:T(1,128)S(1)}, u32[]{:S(2)}, u32[]{:S(2)}) collective-permute-start(f32[7,4,1,128]{3,2,1,0:T(1,128)S(1)} %get-tuple-element.891), channel_id=1, source_target_pairs={{0,1},{1,2},{2,3},{3,4},{4,5},{5,6},{6,7},{7,8},{8,9},{9,10},{10,1... | collective-permute-start | bytes 43016 | tf_op jit(solution)/shard_map/ppermute | solution.py:23
  22.0 7.5 %collective-permute-start.3 = (f32[7,4,1,128]{3,2,1,0:T(1,128)S(1)}, f32[7,4,1,128]{3,2,1,0:T(1,128)S(1)}, u32[]{:S(2)}, u32[]{:S(2)}) collective-permute-start(f32[7,4,1,128]{3,2,1,0:T(1,128)S(1)} %get-tuple-element.892), channel_id=1, source_target_pairs={{1,0},{2,1},{3,2},{4,3},{5,4},{6,5},{7,6},{8,7},{9,8},{10,9},{11,1... | collective-permute-start | bytes 43016 | tf_op jit(solution)/shard_map/ppermute | solution.py:24
  29.6 28.2 %copy-start = (s32[2,8]{1,0:T(2,128)S(1)}, s32[2,8]{1,0:T(2,128)}, u32[]{:S(2)}) copy-start(s32[2,8]{1,0:T(2,128)} %param.18) | copy-start | bytes 196
  29.6 28.2 %copy-start.1 = (f32[2,2,8,128]{3,2,1,0:T(8,128)S(1)}, f32[2,2,8,128]{3,2,1,0:T(8,128)}, u32[]{:S(2)}) copy-start(f32[2,2,8,128]{3,2,1,0:T(8,128)} %param.15) | copy-start | bytes 49156
  29.6 28.2 %copy-start.2 = (f32[2,2,8,128]{3,2,1,0:T(8,128)S(1)}, f32[2,2,8,128]{3,2,1,0:T(8,128)}, u32[]{:S(2)}) copy-start(f32[2,2,8,128]{3,2,1,0:T(8,128)} %param.16) | copy-start | bytes 49156
  29.6 29.0 %copy-start.3 = (f32[2,8,128]{2,1,0:T(8,128)S(1)}, f32[2,8,128]{2,1,0:T(8,128)}, u32[]{:S(2)}) copy-start(f32[2,8,128]{2,1,0:T(8,128)} %param.17) | copy-start | bytes 24580
  58.9 6.2 collective-permute-start.4
  63.5 5.8 collective-permute-start.5
  69.3 118.0 %collective-permute-start.6 = (f32[7,4,1,128]{3,2,1,0:T(1,128)S(1)}, f32[7,4,1,128]{3,2,1,0:T(1,128)S(1)}, u32[]{:S(2)}, u32[]{:S(2)}) collective-permute-start(f32[7,4,1,128]{3,2,1,0:T(1,128)S(1)} %get-tuple-element.889), channel_id=1, source_target_pairs={{0,1},{1,2},{2,3},{3,4},{4,5},{5,6},{6,7},{7,8},{8,9},{9,10},{10,1... | collective-permute-start | bytes 43016 | tf_op jit(solution)/shard_map/ppermute | solution.py:23
  71.5 115.7 %collective-permute-start.7 = (f32[7,4,1,128]{3,2,1,0:T(1,128)S(1)}, f32[7,4,1,128]{3,2,1,0:T(1,128)S(1)}, u32[]{:S(2)}, u32[]{:S(2)}) collective-permute-start(f32[7,4,1,128]{3,2,1,0:T(1,128)S(1)} %get-tuple-element.890), channel_id=1, source_target_pairs={{1,0},{2,1},{3,2},{4,3},{5,4},{6,5},{7,6},{8,7},{9,8},{10,9},{11,1... | collective-permute-start | bytes 43016 | tf_op jit(solution)/shard_map/ppermute | solution.py:24
  215.6 4.5 collective-permute-start.8
  218.6 5.8 collective-permute-start.9
  224.3 110.8 %collective-permute-start.10 = (f32[7,4,1,128]{3,2,1,0:T(1,128)S(1)}, f32[7,4,1,128]{3,2,1,0:T(1,128)S(1)}, u32[]{:S(2)}, u32[]{:S(2)}) collective-permute-start(f32[7,4,1,128]{3,2,1,0:T(1,128)S(1)} %get-tuple-element.887), channel_id=1, source_target_pairs={{0,1},{1,2},{2,3},{3,4},{4,5},{5,6},{6,7},{7,8},{8,9},{9,10},{10,1... | collective-permute-start | bytes 43016 | tf_op jit(solution)/shard_map/ppermute | solution.py:23
  226.3 108.9 %collective-permute-start.11 = (f32[7,4,1,128]{3,2,1,0:T(1,128)S(1)}, f32[7,4,1,128]{3,2,1,0:T(1,128)S(1)}, u32[]{:S(2)}, u32[]{:S(2)}) collective-permute-start(f32[7,4,1,128]{3,2,1,0:T(1,128)S(1)} %get-tuple-element.888), channel_id=1, source_target_pairs={{1,0},{2,1},{3,2},{4,3},{5,4},{6,5},{7,6},{8,7},{9,8},{10,9},{11,1... | collective-permute-start | bytes 43016 | tf_op jit(solution)/shard_map/ppermute | solution.py:24
  363.4 5.1 collective-permute-start.12
  367.0 5.8 collective-permute-start.13
  372.8 109.7 %collective-permute-start.14 = (f32[7,4,1,128]{3,2,1,0:T(1,128)S(1)}, f32[7,4,1,128]{3,2,1,0:T(1,128)S(1)}, u32[]{:S(2)}, u32[]{:S(2)}) collective-permute-start(f32[7,4,1,128]{3,2,1,0:T(1,128)S(1)} %get-tuple-element.885), channel_id=1, source_target_pairs={{0,1},{1,2},{2,3},{3,4},{4,5},{5,6},{6,7},{7,8},{8,9},{9,10},{10,1... | collective-permute-start | bytes 43016 | tf_op jit(solution)/shard_map/ppermute | solution.py:23
  374.7 107.8 %collective-permute-start.15 = (f32[7,4,1,128]{3,2,1,0:T(1,128)S(1)}, f32[7,4,1,128]{3,2,1,0:T(1,128)S(1)}, u32[]{:S(2)}, u32[]{:S(2)}) collective-permute-start(f32[7,4,1,128]{3,2,1,0:T(1,128)S(1)} %get-tuple-element.886), channel_id=1, source_target_pairs={{1,0},{2,1},{3,2},{4,3},{5,4},{6,5},{7,6},{8,7},{9,8},{10,9},{11,1... | collective-permute-start | bytes 43016 | tf_op jit(solution)/shard_map/ppermute | solution.py:24
  482.5 28.8 %copy-start.5 = (s32[32]{0:T(128)S(1)}, s32[32]{0:T(128)}, u32[]{:S(2)}) copy-start(s32[32]{0:T(128)} %param.20) | copy-start | bytes 388
  510.7 0.6 copy-start.4
Sparse Core Ops, SparseCore 0:
  511.5 128.9 all-gather.1
where the time goes:
time: 652 us; the launch traced here: 650 us
  blocking collectives  408 us (63%)
  other arithmetic  97.6 us (15%)
  starting transfers between devices  51.7 us (8%)
  waiting for transfers between devices  44.8 us (7%)
  between operations  18.3 us (3%)
  loops' own time  16.5 us (3%)
  local copies, waits for them, and re-layouts  10.9 us (2%)
    psum x4, blocking collectives, total_force(): return lax.psum(jnp.sum(STIFF * pen), ('cut', 'depth'))  408 us
    reduce_sum x40, other arithmetic, cell_rates(): acc_x = acc_x + jnp.sum(-coef * dx - visc * du, -1)  88.1 us
    ppermute x8, starting transfers between devices, extended(): after = lax.ppermute(leading, axis, down)  29 us
    all_gather x1, waiting for transfers between devices, body(): piece = lax.all_gather(core, 'cut', axis=1, tiled=True)  26.8 us
    ppermute x8, starting transfers between devices, extended(): before = lax.ppermute(last, axis, up)  22.6 us
    ppermute x8, waiting for transfers between devices, extended(): after = lax.ppermute(leading, axis, down)  17.2 us
    another operation x4, loops' own time, column_rates(): found = lax.map(one_column, jnp.arange(columns))  16.5 us
  transfers between devices with their start and end apart: 17, of which 9 were waited for; matrix products, arithmetic and copies ran while one was open for 1% of the time, Pallas kernels for 0%

commit v1 on v0

v1 whole, which is shorter than its diff:
```python
import functools

import jax
import jax.numpy as jnp
from jax import lax
from jax.experimental import pallas as pl
from jax.experimental.pallas import tpu as pltpu
from jax.sharding import PartitionSpec as P

STEPS = 4
MASS = 0.02
SOUND = 20.0
VISCOSITY = 2.0
STIFF = 50.0
DT = 0.05

F32 = jnp.float32
BF16 = jnp.bfloat16
PARAMS = pltpu.CompilerParams(vmem_limit_bytes=40 * 1024 * 1024)
VMEM = pl.BlockSpec(memory_space=pltpu.VMEM)
SMEM = pl.BlockSpec(memory_space=pltpu.SMEM)


def shape(*dims):
    return jax.ShapeDtypeStruct(dims, F32)


def pressure(rho, live):
    s = jnp.where(live > 0, rho, 1.0)
    inv = 1.0 / s
    return SOUND * (s - 1.0) * inv * inv, inv


def rates_kernel(origin, own, left, right, top, bottom, out, ext, feat, xcol, ycol, acc):
    cols, rows, slots = own.shape[1:]
    wide, tall = cols + 2, rows + 2
    x0, y0 = origin[0], origin[1]
    for f in range(6):
        ext[f, 0, 1 : rows + 1] = left[f]
        ext[f, wide - 1, 1 : rows + 1] = right[f]
        for c in range(cols):
            ext[f, c + 1, 1 : rows + 1] = own[f, c]
        for c in range(wide):
            ext[f, c, 0:1] = top[f, c : c + 1]
            ext[f, c, tall - 1 : tall] = bottom[f, c : c + 1]
    for c in range(wide):
        x, y = ext[0, c] - x0, ext[1, c] - y0
        u, v, live = ext[2, c], ext[3, c], ext[5, c]
        press, inv = pressure(ext[4, c], live)
        lp, li = live * press, live * inv
        parts = [live, live * x, live * y, lp, lp * x, lp * y, live * u, live * v, live * (u * x + v * y), li, li * u, li * v]
        for k, part in enumerate(parts):
            high = part.astype(BF16).astype(F32)
            feat[c, :, k, :] = high
            feat[c, :, 16 + k, :] = part - high
        for k in (12, 13, 14, 15, 28, 29, 30, 31):
            feat[c, :, k, :] = jnp.zeros((tall, slots), F32)

    def spread(i, carry):
        c = lax.div(i, tall)
        r = i - c * tall
        xcol[c, r] = jnp.broadcast_to(ext[0, c, pl.ds(r, 1), :], (slots, slots)).T
        ycol[c, r] = jnp.broadcast_to(ext[1, c, pl.ds(r, 1), :], (slots, slots)).T
        return carry

    lax.fori_loop(0, wide * tall, spread, 0, unroll=4)

    def one_cell(i, carry):
        c = lax.div(i, rows)
        r = i - c * rows
        xi = jnp.broadcast_to(ext[0, c + 1, pl.ds(r + 1, 1), :], (slots, slots))
        yi = jnp.broadcast_to(ext[1, c + 1, pl.ds(r + 1, 1), :], (slots, slots))

        def weights(a, b):
            dx = xi - xcol[c + a, r + b]
            dy = yi - ycol[c + a, r + b]
            q = jnp.maximum(0.0, 1.0 - dx * dx - dy * dy)
            q2 = q * q
            return jnp.concatenate([q2, q2 * q], axis=1).astype(BF16)

        around = [(a, b) for a in range(3) for b in range(3)]
        total = None
        for n in range(0, 9, 2):
            pair = around[n : n + 2]
            w = jnp.concatenate([weights(a, b) for a, b in pair], axis=0)
            f = jnp.concatenate([feat[c + a, r + b] for a, b in pair], axis=1).astype(BF16)
            found = jnp.dot(f, w, preferred_element_type=F32)
            total = found if total is None else total + found
        acc[i] = total
        return carry

    lax.fori_loop(0, cols * rows, one_cell, 0, unroll=2)

    for c in range(cols):

        def summed(k):
            lanes = slice(0, slots) if k < 9 else slice(slots, 2 * slots)
            return acc[rows * c : rows * (c + 1), k, lanes] + acc[rows * c : rows * (c + 1), 16 + k, lanes]

        x, y = own[0, c] - x0, own[1, c] - y0
        u, v = own[2, c], own[3, c]
        press, _ = pressure(own[4, c], own[5, c])
        a0, ax, ay, ap, apx, apy, au, av, aw, b0, bu, bv = [summed(k) for k in range(12)]
        sx, sy = x * a0 - ax, y * a0 - ay
        out[0, c] = (6.0 * MASS) * (press * sx + x * ap - apx) - (VISCOSITY * MASS) * (u * b0 - bu)
        out[1, c] = (6.0 * MASS) * (press * sy + y * ap - apy) - (VISCOSITY * MASS) * (v * b0 - bv)
        out[2, c] = (-6.0 * MASS) * (u * sx + v * sy - x * au - y * av + aw)


def rates(origin, own, left, right, top, bottom):
    cols, rows, slots = own.shape[1:]
    wide, tall = cols + 2, rows + 2
    return pl.pallas_call(
        rates_kernel,
        out_shape=shape(3, cols, rows, slots),
        in_specs=[SMEM] + [VMEM] * 5,
        out_specs=VMEM,
        scratch_shapes=[
            pltpu.VMEM((6, wide, tall, slots), F32),
            pltpu.VMEM((wide, tall, 32, slots), F32),
            pltpu.VMEM((wide, tall, slots, slots), F32),
            pltpu.VMEM((wide, tall, slots, slots), F32),
            pltpu.VMEM((cols * rows, 32, 2 * slots), F32),
        ],
        compiler_params=PARAMS,
    )(origin, own, left, right, top, bottom)


def rims_kernel(before, own, after, first_rim, last_rim):
    cols, rows = own.shape[1:3]
    for f in range(6):
        for rim, r in ((first_rim, 0), (last_rim, rows - 1)):
            rim[f, 0:1] = before[f, r : r + 1]
            for c in range(cols):
                rim[f, c + 1 : c + 2] = own[f, c, r : r + 1]
            rim[f, cols + 1 : cols + 2] = after[f, r : r + 1]


def rims(before, own, after):
    cols, _, slots = own.shape[1:]
    return pl.pallas_call(
        rims_kernel,
        out_shape=[shape(6, cols + 2, slots)] * 2,
        in_specs=[VMEM] * 3,
        out_specs=[VMEM] * 2,
        compiler_params=PARAMS,
    )(before, own, after)


def penalties(x, touch, live, offset, first, c):
    return touch * live * jnp.maximum(0.0, x - (first + c) + offset - 0.5)


def send_force(x, touch, live, offset, first, force):
    cols = len(x)
    total = sum(STIFF * penalties(x[c], touch[c], live[c], offset, first, c) for c in range(cols))
    total = jnp.sum(jnp.sum(total, axis=0, keepdims=True), axis=1, keepdims=True)
    force[...] = jnp.broadcast_to(total[None], force.shape)


def start_kernel(origin, positions, velocity, density, marks, tool, own, left, right, force):
    cols = positions.shape[1]
    first = origin[2]
    fields = [positions[0], positions[1], velocity[0], velocity[1], density[...], marks[0]]
    for f, field in enumerate(fields):
        own[f] = field
        left[f] = field[0]
        right[f] = field[cols - 1]
    each = range(cols)
    send_force([positions[0, c] for c in each], [marks[1, c] for c in each], [marks[0, c] for c in each], tool[0:1], first, force)


def start(origin, positions, velocity, density, marks, tool, ncut):
    cols, rows, slots = density.shape
    return pl.pallas_call(
        start_kernel,
        out_shape=[shape(6, cols, rows, slots), shape(6, rows, slots), shape(6, rows, slots), shape(ncut, 1, slots)],
        in_specs=[SMEM] + [VMEM] * 5,
        out_specs=[VMEM] * 4,
        compiler_params=PARAMS,
    )(origin, positions, velocity, density, marks, tool)


def advance(total, tool, scale):
    force = jnp.sum(total[...], axis=0)
    speed = tool[1:2] + DT * (1.0 - force * scale)
    return tool[0:1] + DT * speed, speed


def moved_state(origin, own, found, marks, offset):
    cols = own.shape[1]
    first = origin[2]
    new = []
    for c in range(cols):
        live = own[5, c]
        pen = penalties(own[0, c], marks[1, c], live, offset, first, c)
        u = own[2, c] + DT * live * (found[0, c] - STIFF * pen)
        v = own[3, c] + DT * live * found[1, c]
        x = own[0, c] + DT * live * u
        y = own[1, c] + DT * live * v
        rho = own[4, c] + DT * live * found[2, c]
        new.append([x, y, u, v, rho, live])
    return new


def update_kernel(scale, origin, own, found, marks, total, tool, new_own, left, right, force, new_tool):
    cols = own.shape[1]
    new = moved_state(origin, own, found, marks, tool[0:1])
    for f in range(6):
        for c in range(cols):
            new_own[f, c] = new[c][f]
        left[f] = new[0][f]
        right[f] = new[cols - 1][f]
    offset, speed = advance(total, tool, scale)
    new_tool[0:1] = offset
    new_tool[1:2] = speed
    each = range(cols)
    send_force([new[c][0] for c in each], [marks[1, c] for c in each], [new[c][5] for c in each], offset, origin[2], force)


def update(origin, own, found, marks, total, tool, ncut, scale):
    cols, rows, slots = own.shape[1:]
    return pl.pallas_call(
        functools.partial(update_kernel, scale),
        out_shape=[
            shape(6, cols, rows, slots),
            shape(6, rows, slots),
            shape(6, rows, slots),
            shape(ncut, 1, slots),
            shape(2, slots),
        ],
        in_specs=[SMEM] + [VMEM] * 5,
        out_specs=[VMEM] * 5,
        compiler_params=PARAMS,
    )(origin, own, found, marks, total, tool)


def last_kernel(near, origin, place, own, found, marks, tool, sent):
    cols = own.shape[1]
    new = moved_state(origin, own, found, marks, tool[0:1])
    target = lax.rem(place[0], near)
    for k in range(near):
        for f in range(5):
            for c in range(cols):
                sent[k, f, c] = jnp.where(target == k, new[c][f], 0.0)


def last(origin, place, own, found, marks, tool, near):
    cols, rows, slots = own.shape[1:]
    return pl.pallas_call(
        functools.partial(last_kernel, near),
        out_shape=shape(near, 5, cols, rows, slots),
        in_specs=[SMEM, SMEM] + [VMEM] * 4,
        out_specs=VMEM,
        compiler_params=PARAMS,
    )(origin, place, own, found, marks, tool)


def sort_kernel(near, far, place, got, sent):
    sent[...] = jnp.zeros(sent.shape, F32)
    mine = place[1]
    for k in range(near):
        target = place[2 + k]
        wanted = lax.rem(target, near) == mine

        @pl.when(wanted)
        def _():
            sent[lax.div(target, near)] = got[k]


def sort(place, got, near, far):
    return pl.pallas_call(
        functools.partial(sort_kernel, near, far),
        out_shape=shape(far, *got.shape[1:]),
        in_specs=[SMEM, VMEM],
        out_specs=VMEM,
        compiler_params=PARAMS,
    )(place, got)


def take_kernel(place, got, out):
    out[...] = got[place[0]]


def take(place, got):
    return pl.pallas_call(
        take_kernel,
        out_shape=shape(*got.shape[1:]),
        in_specs=[SMEM, VMEM],
        out_specs=VMEM,
        compiler_params=PARAMS,
    )(place, got)


def exchange(up, down, axis):
    size = lax.axis_size(axis)
    forth = [(i, i + 1) for i in range(size - 1)]
    back = [(i + 1, i) for i in range(size - 1)]
    return lax.ppermute(up, axis, forth), lax.ppermute(down, axis, back)


def body(positions, velocity, density, counts, contact_mask, destination, tool):
    cols, rows, slots = density.shape
    ncut, ndepth = lax.axis_size("cut"), lax.axis_size("depth")
    here, depth = lax.axis_index("cut"), lax.axis_index("depth")
    scale = 1.0 / (ncut * cols * ndepth * rows * slots)
    first_col = (here * cols).astype(F32)
    first_row = (depth * rows).astype(F32)
    origin = jnp.stack([first_col + 0.5 * cols, first_row + 0.5 * rows, first_col])
    live = (jnp.arange(slots)[None, None, :] < counts[:, :, None]).astype(F32)
    touch = jnp.broadcast_to(contact_mask[:, :, None].astype(F32), live.shape)
    marks = jnp.stack([live, touch])
    tool = jnp.broadcast_to(tool[:, None], (2, slots))

    near = 8 if ncut % 8 == 0 else 1
    far = ncut // near
    group, digit = here // near, here % near
    from_group = lax.dynamic_slice_in_dim(destination, group * near, near)
    place = jnp.concatenate([destination[here][None], digit[None], from_group])
    source = jnp.sum(jnp.where(destination == here, jnp.arange(ncut), 0))
    source = (source // near)[None]

    own, left, right, force = start(origin, positions, velocity, density, marks, tool, ncut)
    for step in range(STEPS):
        before, after = exchange(right, left, "cut")
        got = lax.all_to_all(force, "cut", 0, 0, tiled=True)
        first_rim, last_rim = rims(before, own, after)
        top, bottom = exchange(last_rim, first_rim, "depth")
        got = jnp.broadcast_to(jnp.sum(got, axis=0, keepdims=True), (ndepth, 1, slots))
        total = lax.all_to_all(got, "depth", 0, 0, tiled=True)
        found = rates(origin, own, before, after, top, bottom)
        if step < STEPS - 1:
            own, left, right, force, tool = update(origin, own, found, marks, total, tool, ncut, scale)
        else:
            sent = last(origin, place, own, found, marks, tool, near)
            force = jnp.sum(total[:, 0, 0])
            speed = tool[1, 0] + DT * (1.0 - force * scale)
            tool = jnp.stack([tool[0, 0] + DT * speed, speed])
    close = [[g * near + k for k in range(near)] for g in range(far)]
    apart = [[g * near + k for g in range(far)] for k in range(near)]
    got = lax.all_to_all(sent, "cut", 0, 0, tiled=True, axis_index_groups=close)
    sent = sort(place, got, near, far)
    got = lax.all_to_all(sent, "cut", 0, 0, tiled=True, axis_index_groups=apart)
    return take(source, got), tool


def solution(mesh):
    return jax.shard_map(
        body,
        mesh=mesh,
        in_specs=(
            P(None, "cut", "depth", None),
            P(None, "cut", "depth", None),
            P("cut", "depth", None),
            P("cut", "depth"),
            P("cut", "depth"),
            P(),
            P(),
        ),
        out_specs=(P(None, "cut", "depth", None), P()),
        check_vma=False,
    )
```

time: 652 us -> 244 us (0.37)
  the two profiles are of different devices: /device:TPU:4 before, /device:TPU:8 now
where the time goes in v1:
time: 244 us; the launch traced here: 243 us
  starting transfers between devices  152 us (62%)
  waiting for transfers between devices  39.1 us (16%)
  Pallas kernels  37.2 us (15%)
  local copies, waits for them, and re-layouts  6.35 us (3%)
  between operations  5.64 us (2%)
  other arithmetic  2.93 us (1%)
    all_to_all x4, starting transfers between devices, body(): got = lax.all_to_all(force, 'cut', 0, 0, tiled=True)  57.8 us
    all_to_all x4, starting transfers between devices, body(): total = lax.all_to_all(got, 'depth', 0, 0, tiled=True)  44.9 us
    ppermute x16, starting transfers between devices, exchange(): return (lax.ppermute(up, axis, forth), lax.ppermute(down, axis, back))  33.7 us
    pallas_call x4, Pallas kernels, rates(): pl.pallas_call(rates_kernel, out_shape=shape(3, cols, rows, slots), in_sp...  28.9 us
    ppermute x16, waiting for transfers between devices, exchange(): return (lax.ppermute(up, axis, forth), lax.ppermute(down, axis, back))  16.7 us
    all_to_all x1, starting transfers between devices, body(): got = lax.all_to_all(sent, 'cut', 0, 0, tiled=True, axis_index_groups=apart)  9.38 us
    all_to_all x1, waiting for transfers between devices, body(): got = lax.all_to_all(sent, 'cut', 0, 0, tiled=True, axis_index_groups=apart)  8.74 us
    all_to_all x4, waiting for transfers between devices, body(): total = lax.all_to_all(got, 'depth', 0, 0, tiled=True)  6.9 us
  transfers between devices with their start and end apart: 26, of which 10 were waited for; matrix products, arithmetic and copies ran while one was open for 2% of the time, Pallas kernels for 13%

profile of v1, /device:TPU:8, one launch (start us, length us, event | category | flops | bytes accessed | tf_op | source)
XLA Modules:
  0.0 243.1 jit_solution(17337732213240484979)
XLA Ops:
  0.6 0.7 copy-done.4
  1.3 0.7 copy-done.3
  2.9 1.2 shard_map.86
  4.1 16.7 %all-to-all-start = ((f32[32,1,128]{2,1,0:T(1,128)}), f32[32,1,128]{2,1,0:T(1,128)S(1)}, u32[]{:S(2)}, u32[]{:S(2)}) async-start(f32[32,1,128]{2,1,0:T(1,128)} %get-tuple-element.34), calls=%async_computation | async-start | bytes 32768 | tf_op jit(solution)/shard_map/all_to_all | solution.py:326
  20.9 3.4 %collective-permute-start = (f32[6,8,128]{2,1,0:T(8,128)S(1)}, f32[6,8,128]{2,1,0:T(8,128)S(1)}, u32[]{:S(2)}, u32[]{:S(2)}) collective-permute-start(f32[6,8,128]{2,1,0:T(8,128)S(1)} %get-tuple-element.30), channel_id=1, source_target_pairs={{0,16},{16,32},{32,48},{48,64},{64,80},{80,96},{96,112},{112,128},... | collective-permute-start | bytes 73736 | tf_op jit(solution)/shard_map/ppermute | solution.py:299
  24.2 2.5 %collective-permute-start.1 = (f32[6,8,128]{2,1,0:T(8,128)S(1)}, f32[6,8,128]{2,1,0:T(8,128)S(1)}, u32[]{:S(2)}, u32[]{:S(2)}) collective-permute-start(f32[6,8,128]{2,1,0:T(8,128)S(1)} %get-tuple-element.31), channel_id=1, source_target_pairs={{16,0},{32,16},{48,32},{64,48},{80,64},{96,80},{112,96},{128,112},... | collective-permute-start | bytes 73736 | tf_op jit(solution)/shard_map/ppermute | solution.py:299
  26.7 4.1 %collective-permute-done.1.after.right = f32[6,8,128]{2,1,0:T(8,128)S(1)} collective-permute-done((f32[6,8,128]{2,1,0:T(8,128)S(1)}, f32[6,8,128]{2,1,0:T(8,128)S(1)}, u32[]{:S(2)}, u32[]{:S(2)}) %collective-permute-start.1) | collective-permute-done | bytes 24608 | tf_op jit(solution)/shard_map/ppermute | solution.py:299
  30.9 1.3 collective-permute-start.2
  32.2 1.3 collective-permute-start.3
  34.2 10.6 %all-to-all-start.1 = ((f32[16,1,128]{2,1,0:T(1,128)}), f32[16,1,128]{2,1,0:T(1,128)S(1)}, u32[]{:S(2)}, u32[]{:S(2)}) async-start(f32[16,1,128]{2,1,0:T(1,128)} %broadcast_in_dim.22), calls=%async_computation.1 | async-start | bytes 16384 | tf_op jit(solution)/shard_map/all_to_all | solution.py:330
  44.8 7.2 %shard_map.88.found = f32[3,2,8,128]{3,2,1,0:T(8,128)S(1)} custom-call(f32[3]{0:T(128)S(1)} %pad_maximum_fusion.1.origin, f32[6,2,8,128]{3,2,1,0:T(8,128)S(1)} %get-tuple-element.29.own, f32[6,8,128]{2,1,0:T(8,128)S(1)} %collective-permute-done.before.left, f32[6,8,128]{2,1,0:T(8,128)S(1)} %collective-permute-done.1.after.right, ...), custom_call_target="tpu_custom_call" | custom-call | tf_op jit(solution)/shard_map/pallas_call | solution.py:113
  52.3 1.3 shard_map.89
  53.5 13.4 %all-to-all-start.2 = ((f32[32,1,128]{2,1,0:T(1,128)}), f32[32,1,128]{2,1,0:T(1,128)S(1)}, u32[]{:S(2)}, u32[]{:S(2)}) async-start(f32[32,1,128]{2,1,0:T(1,128)} %get-tuple-element.40), calls=%async_computation.2 | async-start | bytes 32768 | tf_op jit(solution)/shard_map/all_to_all | solution.py:326
  66.9 3.4 %collective-permute-start.4 = (f32[6,8,128]{2,1,0:T(8,128)S(1)}, f32[6,8,128]{2,1,0:T(8,128)S(1)}, u32[]{:S(2)}, u32[]{:S(2)}) collective-permute-start(f32[6,8,128]{2,1,0:T(8,128)S(1)} %get-tuple-element.36), channel_id=1, source_target_pairs={{0,16},{16,32},{32,48},{48,64},{64,80},{80,96},{96,112},{112,128},... | collective-permute-start | bytes 73736 | tf_op jit(solution)/shard_map/ppermute | solution.py:299
  70.3 2.5 %collective-permute-start.5 = (f32[6,8,128]{2,1,0:T(8,128)S(1)}, f32[6,8,128]{2,1,0:T(8,128)S(1)}, u32[]{:S(2)}, u32[]{:S(2)}) collective-permute-start(f32[6,8,128]{2,1,0:T(8,128)S(1)} %get-tuple-element.37), channel_id=1, source_target_pairs={{16,0},{32,16},{48,32},{64,48},{80,64},{96,80},{112,96},{128,112},... | collective-permute-start | bytes 73736 | tf_op jit(solution)/shard_map/ppermute | solution.py:299
  72.8 4.1 %collective-permute-done.5.after.right = f32[6,8,128]{2,1,0:T(8,128)S(1)} collective-permute-done((f32[6,8,128]{2,1,0:T(8,128)S(1)}, f32[6,8,128]{2,1,0:T(8,128)S(1)}, u32[]{:S(2)}, u32[]{:S(2)}) %collective-permute-start.5) | collective-permute-done | bytes 24608 | tf_op jit(solution)/shard_map/ppermute | solution.py:299
  77.0 1.3 collective-permute-start.6
  78.3 1.3 collective-permute-start.7
  80.2 11.5 %all-to-all-start.3 = ((f32[16,1,128]{2,1,0:T(1,128)}), f32[16,1,128]{2,1,0:T(1,128)S(1)}, u32[]{:S(2)}, u32[]{:S(2)}) async-start(f32[16,1,128]{2,1,0:T(1,128)} %broadcast_in_dim.23), calls=%async_computation.3 | async-start | bytes 16384 | tf_op jit(solution)/shard_map/all_to_all | solution.py:330
  91.7 7.2 %shard_map.91.found = f32[3,2,8,128]{3,2,1,0:T(8,128)S(1)} custom-call(f32[3]{0:T(128)S(1)} %pad_maximum_fusion.1.origin, f32[6,2,8,128]{3,2,1,0:T(8,128)S(1)} %get-tuple-element.35.own, f32[6,8,128]{2,1,0:T(8,128)S(1)} %collective-permute-done.4.before.left, f32[6,8,128]{2,1,0:T(8,128)S(1)} %collective-permute-done.5.after.right, ...), custom_call_target="tpu_custom_call" | custom-call | tf_op jit(solution)/shard_map/pallas_call | solution.py:113
  99.2 1.3 shard_map.92
  100.5 13.4 %all-to-all-start.4 = ((f32[32,1,128]{2,1,0:T(1,128)}), f32[32,1,128]{2,1,0:T(1,128)S(1)}, u32[]{:S(2)}, u32[]{:S(2)}) async-start(f32[32,1,128]{2,1,0:T(1,128)} %get-tuple-element.47), calls=%async_computation.4 | async-start | bytes 32768 | tf_op jit(solution)/shard_map/all_to_all | solution.py:326
  113.8 3.4 %collective-permute-start.8 = (f32[6,8,128]{2,1,0:T(8,128)S(1)}, f32[6,8,128]{2,1,0:T(8,128)S(1)}, u32[]{:S(2)}, u32[]{:S(2)}) collective-permute-start(f32[6,8,128]{2,1,0:T(8,128)S(1)} %get-tuple-element.43), channel_id=1, source_target_pairs={{0,16},{16,32},{32,48},{48,64},{64,80},{80,96},{96,112},{112,128},... | collective-permute-start | bytes 73736 | tf_op jit(solution)/shard_map/ppermute | solution.py:299
  117.2 2.5 %collective-permute-start.9 = (f32[6,8,128]{2,1,0:T(8,128)S(1)}, f32[6,8,128]{2,1,0:T(8,128)S(1)}, u32[]{:S(2)}, u32[]{:S(2)}) collective-permute-start(f32[6,8,128]{2,1,0:T(8,128)S(1)} %get-tuple-element.44), channel_id=1, source_target_pairs={{16,0},{32,16},{48,32},{64,48},{80,64},{96,80},{112,96},{128,112},... | collective-permute-start | bytes 73736 | tf_op jit(solution)/shard_map/ppermute | solution.py:299
  119.7 4.1 %collective-permute-done.9.after.right = f32[6,8,128]{2,1,0:T(8,128)S(1)} collective-permute-done((f32[6,8,128]{2,1,0:T(8,128)S(1)}, f32[6,8,128]{2,1,0:T(8,128)S(1)}, u32[]{:S(2)}, u32[]{:S(2)}) %collective-permute-start.9) | collective-permute-done | bytes 24608 | tf_op jit(solution)/shard_map/ppermute | solution.py:299
  123.9 1.3 collective-permute-start.10
  125.2 1.3 collective-permute-start.11
  127.1 11.5 %all-to-all-start.5 = ((f32[16,1,128]{2,1,0:T(1,128)}), f32[16,1,128]{2,1,0:T(1,128)S(1)}, u32[]{:S(2)}, u32[]{:S(2)}) async-start(f32[16,1,128]{2,1,0:T(1,128)} %broadcast_in_dim.24), calls=%async_computation.5 | async-start | bytes 16384 | tf_op jit(solution)/shard_map/all_to_all | solution.py:330
  138.7 7.2 %shard_map.94.found = f32[3,2,8,128]{3,2,1,0:T(8,128)S(1)} custom-call(f32[3]{0:T(128)S(1)} %pad_maximum_fusion.1.origin, f32[6,2,8,128]{3,2,1,0:T(8,128)S(1)} %get-tuple-element.42.own, f32[6,8,128]{2,1,0:T(8,128)S(1)} %collective-permute-done.8.before.left, f32[6,8,128]{2,1,0:T(8,128)S(1)} %collective-permute-done.9.after.right, ...), custom_call_target="tpu_custom_call" | custom-call | tf_op jit(solution)/shard_map/pallas_call | solution.py:113
  146.1 1.3 shard_map.95
  147.4 3.1 %collective-permute-start.12 = (f32[6,8,128]{2,1,0:T(8,128)S(1)}, f32[6,8,128]{2,1,0:T(8,128)S(1)}, u32[]{:S(2)}, u32[]{:S(2)}) collective-permute-start(f32[6,8,128]{2,1,0:T(8,128)S(1)} %get-tuple-element.50), channel_id=1, source_target_pairs={{0,16},{16,32},{32,48},{48,64},{64,80},{80,96},{96,112},{112,128},... | collective-permute-start | bytes 73736 | tf_op jit(solution)/shard_map/ppermute | solution.py:299
  150.5 2.8 %collective-permute-start.13 = (f32[6,8,128]{2,1,0:T(8,128)S(1)}, f32[6,8,128]{2,1,0:T(8,128)S(1)}, u32[]{:S(2)}, u32[]{:S(2)}) collective-permute-start(f32[6,8,128]{2,1,0:T(8,128)S(1)} %get-tuple-element.51), channel_id=1, source_target_pairs={{16,0},{32,16},{48,32},{64,48},{80,64},{96,80},{112,96},{128,112},... | collective-permute-start | bytes 73736 | tf_op jit(solution)/shard_map/ppermute | solution.py:299
  153.3 0.6 copy-done.6
  154.6 14.3 %all-to-all-start.8 = ((f32[32,1,128]{2,1,0:T(1,128)}), f32[32,1,128]{2,1,0:T(1,128)S(1)}, u32[]{:S(2)}, u32[]{:S(2)}) async-start(f32[32,1,128]{2,1,0:T(1,128)} %get-tuple-element.55), calls=%async_computation.8 | async-start | bytes 32768 | tf_op jit(solution)/shard_map/all_to_all | solution.py:326
  169.0 1.3 collective-permute-start.14
  170.3 1.3 collective-permute-start.15
  171.6 0.7 pad_add_fusion.place
  172.3 4.2 %collective-permute-done.15.bottom = f32[6,4,128]{2,1,0:T(4,128)S(1)} collective-permute-done((f32[6,4,128]{2,1,0:T(4,128)S(1)}, f32[6,4,128]{2,1,0:T(4,128)S(1)}, u32[]{:S(2)}, u32[]{:S(2)}) %collective-permute-start.15) | collective-permute-done | bytes 12320 | tf_op jit(solution)/shard_map/ppermute | solution.py:299
  176.5 7.2 %shard_map.97.found = f32[3,2,8,128]{3,2,1,0:T(8,128)S(1)} custom-call(f32[3]{0:T(128)S(1)} %pad_maximum_fusion.1.origin, f32[6,2,8,128]{3,2,1,0:T(8,128)S(1)} %get-tuple-element.49.own, f32[6,8,128]{2,1,0:T(8,128)S(1)} %collective-permute-done.12.before.left, f32[6,8,128]{2,1,0:T(8,128)S(1)} %collective-permute-done.13.after.right, ...), custom_call_target="tpu_custom_call" | custom-call | tf_op jit(solution)/shard_map/pallas_call | solution.py:113
  183.7 1.3 shard_map.98
  185.0 6.0 %all-to-all-start.6 = ((f32[8,5,2,8,128]{4,3,2,1,0:T(8,128)}), f32[8,5,2,8,128]{4,3,2,1,0:T(8,128)S(1)}, u32[]{:S(2)}, u32[]{:S(2)}) async-start(f32[8,5,2,8,128]{4,3,2,1,0:T(8,128)} %shard_map.98), calls=%async_computation.6 | async-start | bytes 655360 | tf_op jit(solution)/shard_map/all_to_all | solution.py:341
  191.1 6.8 %all-to-all-done.6.got = f32[8,5,2,8,128]{4,3,2,1,0:T(8,128)S(1)} async-done(((f32[8,5,2,8,128]{4,3,2,1,0:T(8,128)}), f32[8,5,2,8,128]{4,3,2,1,0:T(8,128)S(1)}, u32[]{:S(2)}, u32[]{:S(2)}) %all-to-all-start.6) | async-done | bytes 327712 | tf_op jit(solution)/shard_map/all_to_all | solution.py:341
  198.5 11.4 %all-to-all-start.9 = ((f32[16,1,128]{2,1,0:T(1,128)}), f32[16,1,128]{2,1,0:T(1,128)S(1)}, u32[]{:S(2)}, u32[]{:S(2)}) async-start(f32[16,1,128]{2,1,0:T(1,128)} %broadcast_in_dim.25), calls=%async_computation.9 | async-start | bytes 16384 | tf_op jit(solution)/shard_map/all_to_all | solution.py:330
  209.9 1.3 shard_map.99
  211.1 6.2 %all-to-all-done.9 = f32[16,1,128]{2,1,0:T(1,128)S(1)} async-done(((f32[16,1,128]{2,1,0:T(1,128)}), f32[16,1,128]{2,1,0:T(1,128)S(1)}, u32[]{:S(2)}, u32[]{:S(2)}) %all-to-all-start.9) | async-done | bytes 8224 | tf_op jit(solution)/shard_map/all_to_all | solution.py:330
  217.3 9.4 %all-to-all-start.7 = ((f32[4,5,2,8,128]{4,3,2,1,0:T(8,128)}), f32[4,5,2,8,128]{4,3,2,1,0:T(8,128)S(1)}, u32[]{:S(2)}, u32[]{:S(2)}) async-start(f32[4,5,2,8,128]{4,3,2,1,0:T(8,128)} %shard_map.99), calls=%async_computation.7 | async-start | bytes 327680 | tf_op jit(solution)/shard_map/all_to_all | solution.py:343
  230.5 0.7 slice_reduce_fusion
  233.7 8.7 %all-to-all-done.7.got = f32[4,5,2,8,128]{4,3,2,1,0:T(8,128)S(1)} async-done(((f32[4,5,2,8,128]{4,3,2,1,0:T(8,128)}), f32[4,5,2,8,128]{4,3,2,1,0:T(8,128)S(1)}, u32[]{:S(2)}, u32[]{:S(2)}) %all-to-all-start.7) | async-done | bytes 163872 | tf_op jit(solution)/shard_map/all_to_all | solution.py:343
  (54 shorter events, 7.4 us)
Async XLA Ops:
  0.6 0.7 copy-start.4
  1.3 0.7 copy-start.3
  2.1 0.7 copy-start.5
  2.1 0.7 copy-start
  2.1 0.7 copy-start.1
  2.2 0.7 copy-start.2
  4.1 29.3 %all-to-all-start = ((f32[32,1,128]{2,1,0:T(1,128)}), f32[32,1,128]{2,1,0:T(1,128)S(1)}, u32[]{:S(2)}, u32[]{:S(2)}) async-start(f32[32,1,128]{2,1,0:T(1,128)} %get-tuple-element.34), calls=%async_computation | async-start | bytes 32768 | tf_op jit(solution)/shard_map/all_to_all | solution.py:326
  20.9 5.9 %collective-permute-start = (f32[6,8,128]{2,1,0:T(8,128)S(1)}, f32[6,8,128]{2,1,0:T(8,128)S(1)}, u32[]{:S(2)}, u32[]{:S(2)}) collective-permute-start(f32[6,8,128]{2,1,0:T(8,128)S(1)} %get-tuple-element.30), channel_id=1, source_target_pairs={{0,16},{16,32},{32,48},{48,64},{64,80},{80,96},{96,112},{112,128},... | collective-permute-start | bytes 73736 | tf_op jit(solution)/shard_map/ppermute | solution.py:299
  24.2 6.6 %collective-permute-start.1 = (f32[6,8,128]{2,1,0:T(8,128)S(1)}, f32[6,8,128]{2,1,0:T(8,128)S(1)}, u32[]{:S(2)}, u32[]{:S(2)}) collective-permute-start(f32[6,8,128]{2,1,0:T(8,128)S(1)} %get-tuple-element.31), channel_id=1, source_target_pairs={{16,0},{32,16},{48,32},{64,48},{80,64},{96,80},{112,96},{128,112},... | collective-permute-start | bytes 73736 | tf_op jit(solution)/shard_map/ppermute | solution.py:299
  30.9 13.9 %collective-permute-start.2 = (f32[6,4,128]{2,1,0:T(4,128)S(1)}, f32[6,4,128]{2,1,0:T(4,128)S(1)}, u32[]{:S(2)}, u32[]{:S(2)}) collective-permute-start(f32[6,4,128]{2,1,0:T(4,128)S(1)} %get-tuple-element.32), channel_id=1, source_target_pairs={{0,1},{1,2},{2,3},{3,4},{4,5},{5,6},{6,7},{7,8},{8,9},{9,10},{10,1... | collective-permute-start | bytes 36872 | tf_op jit(solution)/shard_map/ppermute | solution.py:299
  32.2 12.6 %collective-permute-start.3 = (f32[6,4,128]{2,1,0:T(4,128)S(1)}, f32[6,4,128]{2,1,0:T(4,128)S(1)}, u32[]{:S(2)}, u32[]{:S(2)}) collective-permute-start(f32[6,4,128]{2,1,0:T(4,128)S(1)} %get-tuple-element.33), channel_id=1, source_target_pairs={{1,0},{2,1},{3,2},{4,3},{5,4},{6,5},{7,6},{8,7},{9,8},{10,9},{11,1... | collective-permute-start | bytes 36872 | tf_op jit(solution)/shard_map/ppermute | solution.py:299
  34.2 18.1 %all-to-all-start.1 = ((f32[16,1,128]{2,1,0:T(1,128)}), f32[16,1,128]{2,1,0:T(1,128)S(1)}, u32[]{:S(2)}, u32[]{:S(2)}) async-start(f32[16,1,128]{2,1,0:T(1,128)} %broadcast_in_dim.22), calls=%async_computation.1 | async-start | bytes 16384 | tf_op jit(solution)/shard_map/all_to_all | solution.py:330
  53.5 26.0 %all-to-all-start.2 = ((f32[32,1,128]{2,1,0:T(1,128)}), f32[32,1,128]{2,1,0:T(1,128)S(1)}, u32[]{:S(2)}, u32[]{:S(2)}) async-start(f32[32,1,128]{2,1,0:T(1,128)} %get-tuple-element.40), calls=%async_computation.2 | async-start | bytes 32768 | tf_op jit(solution)/shard_map/all_to_all | solution.py:326
  66.9 5.9 %collective-permute-start.4 = (f32[6,8,128]{2,1,0:T(8,128)S(1)}, f32[6,8,128]{2,1,0:T(8,128)S(1)}, u32[]{:S(2)}, u32[]{:S(2)}) collective-permute-start(f32[6,8,128]{2,1,0:T(8,128)S(1)} %get-tuple-element.36), channel_id=1, source_target_pairs={{0,16},{16,32},{32,48},{48,64},{64,80},{80,96},{96,112},{112,128},... | collective-permute-start | bytes 73736 | tf_op jit(solution)/shard_map/ppermute | solution.py:299
  70.3 6.6 %collective-permute-start.5 = (f32[6,8,128]{2,1,0:T(8,128)S(1)}, f32[6,8,128]{2,1,0:T(8,128)S(1)}, u32[]{:S(2)}, u32[]{:S(2)}) collective-permute-start(f32[6,8,128]{2,1,0:T(8,128)S(1)} %get-tuple-element.37), channel_id=1, source_target_pairs={{16,0},{32,16},{48,32},{64,48},{80,64},{96,80},{112,96},{128,112},... | collective-permute-start | bytes 73736 | tf_op jit(solution)/shard_map/ppermute | solution.py:299
  77.0 14.8 %collective-permute-start.6 = (f32[6,4,128]{2,1,0:T(4,128)S(1)}, f32[6,4,128]{2,1,0:T(4,128)S(1)}, u32[]{:S(2)}, u32[]{:S(2)}) collective-permute-start(f32[6,4,128]{2,1,0:T(4,128)S(1)} %get-tuple-element.38), channel_id=1, source_target_pairs={{0,1},{1,2},{2,3},{3,4},{4,5},{5,6},{6,7},{7,8},{8,9},{9,10},{10,1... | collective-permute-start | bytes 36872 | tf_op jit(solution)/shard_map/ppermute | solution.py:299
  78.3 13.5 %collective-permute-start.7 = (f32[6,4,128]{2,1,0:T(4,128)S(1)}, f32[6,4,128]{2,1,0:T(4,128)S(1)}, u32[]{:S(2)}, u32[]{:S(2)}) collective-permute-start(f32[6,4,128]{2,1,0:T(4,128)S(1)} %get-tuple-element.39), channel_id=1, source_target_pairs={{1,0},{2,1},{3,2},{4,3},{5,4},{6,5},{7,6},{8,7},{9,8},{10,9},{11,1... | collective-permute-start | bytes 36872 | tf_op jit(solution)/shard_map/ppermute | solution.py:299
  80.2 19.0 %all-to-all-start.3 = ((f32[16,1,128]{2,1,0:T(1,128)}), f32[16,1,128]{2,1,0:T(1,128)S(1)}, u32[]{:S(2)}, u32[]{:S(2)}) async-start(f32[16,1,128]{2,1,0:T(1,128)} %broadcast_in_dim.23), calls=%async_computation.3 | async-start | bytes 16384 | tf_op jit(solution)/shard_map/all_to_all | solution.py:330
  100.5 26.0 %all-to-all-start.4 = ((f32[32,1,128]{2,1,0:T(1,128)}), f32[32,1,128]{2,1,0:T(1,128)S(1)}, u32[]{:S(2)}, u32[]{:S(2)}) async-start(f32[32,1,128]{2,1,0:T(1,128)} %get-tuple-element.47), calls=%async_computation.4 | async-start | bytes 32768 | tf_op jit(solution)/shard_map/all_to_all | solution.py:326
  113.8 5.9 %collective-permute-start.8 = (f32[6,8,128]{2,1,0:T(8,128)S(1)}, f32[6,8,128]{2,1,0:T(8,128)S(1)}, u32[]{:S(2)}, u32[]{:S(2)}) collective-permute-start(f32[6,8,128]{2,1,0:T(8,128)S(1)} %get-tuple-element.43), channel_id=1, source_target_pairs={{0,16},{16,32},{32,48},{48,64},{64,80},{80,96},{96,112},{112,128},... | collective-permute-start | bytes 73736 | tf_op jit(solution)/shard_map/ppermute | solution.py:299
  117.2 6.6 %collective-permute-start.9 = (f32[6,8,128]{2,1,0:T(8,128)S(1)}, f32[6,8,128]{2,1,0:T(8,128)S(1)}, u32[]{:S(2)}, u32[]{:S(2)}) collective-permute-start(f32[6,8,128]{2,1,0:T(8,128)S(1)} %get-tuple-element.44), channel_id=1, source_target_pairs={{16,0},{32,16},{48,32},{64,48},{80,64},{96,80},{112,96},{128,112},... | collective-permute-start | bytes 73736 | tf_op jit(solution)/shard_map/ppermute | solution.py:299
  123.9 14.8 %collective-permute-start.10 = (f32[6,4,128]{2,1,0:T(4,128)S(1)}, f32[6,4,128]{2,1,0:T(4,128)S(1)}, u32[]{:S(2)}, u32[]{:S(2)}) collective-permute-start(f32[6,4,128]{2,1,0:T(4,128)S(1)} %get-tuple-element.45), channel_id=1, source_target_pairs={{0,1},{1,2},{2,3},{3,4},{4,5},{5,6},{6,7},{7,8},{8,9},{9,10},{10,1... | collective-permute-start | bytes 36872 | tf_op jit(solution)/shard_map/ppermute | solution.py:299
  125.2 13.5 %collective-permute-start.11 = (f32[6,4,128]{2,1,0:T(4,128)S(1)}, f32[6,4,128]{2,1,0:T(4,128)S(1)}, u32[]{:S(2)}, u32[]{:S(2)}) collective-permute-start(f32[6,4,128]{2,1,0:T(4,128)S(1)} %get-tuple-element.46), channel_id=1, source_target_pairs={{1,0},{2,1},{3,2},{4,3},{5,4},{6,5},{7,6},{8,7},{9,8},{10,9},{11,1... | collective-permute-start | bytes 36872 | tf_op jit(solution)/shard_map/ppermute | solution.py:299
  127.1 19.0 %all-to-all-start.5 = ((f32[16,1,128]{2,1,0:T(1,128)}), f32[16,1,128]{2,1,0:T(1,128)S(1)}, u32[]{:S(2)}, u32[]{:S(2)}) async-start(f32[16,1,128]{2,1,0:T(1,128)} %broadcast_in_dim.24), calls=%async_computation.5 | async-start | bytes 16384 | tf_op jit(solution)/shard_map/all_to_all | solution.py:330
  147.4 21.6 %collective-permute-start.12 = (f32[6,8,128]{2,1,0:T(8,128)S(1)}, f32[6,8,128]{2,1,0:T(8,128)S(1)}, u32[]{:S(2)}, u32[]{:S(2)}) collective-permute-start(f32[6,8,128]{2,1,0:T(8,128)S(1)} %get-tuple-element.50), channel_id=1, source_target_pairs={{0,16},{16,32},{32,48},{48,64},{64,80},{80,96},{96,112},{112,128},... | collective-permute-start | bytes 73736 | tf_op jit(solution)/shard_map/ppermute | solution.py:299
  150.5 18.5 %collective-permute-start.13 = (f32[6,8,128]{2,1,0:T(8,128)S(1)}, f32[6,8,128]{2,1,0:T(8,128)S(1)}, u32[]{:S(2)}, u32[]{:S(2)}) collective-permute-start(f32[6,8,128]{2,1,0:T(8,128)S(1)} %get-tuple-element.51), channel_id=1, source_target_pairs={{16,0},{32,16},{48,32},{64,48},{80,64},{96,80},{112,96},{128,112},... | collective-permute-start | bytes 73736 | tf_op jit(solution)/shard_map/ppermute | solution.py:299
  153.2 0.7 copy-start.6
  154.6 30.4 %all-to-all-start.8 = ((f32[32,1,128]{2,1,0:T(1,128)}), f32[32,1,128]{2,1,0:T(1,128)S(1)}, u32[]{:S(2)}, u32[]{:S(2)}) async-start(f32[32,1,128]{2,1,0:T(1,128)} %get-tuple-element.55), calls=%async_computation.8 | async-start | bytes 32768 | tf_op jit(solution)/shard_map/all_to_all | solution.py:326
  169.0 3.3 %collective-permute-start.14 = (f32[6,4,128]{2,1,0:T(4,128)S(1)}, f32[6,4,128]{2,1,0:T(4,128)S(1)}, u32[]{:S(2)}, u32[]{:S(2)}) collective-permute-start(f32[6,4,128]{2,1,0:T(4,128)S(1)} %get-tuple-element.52), channel_id=1, source_target_pairs={{0,1},{1,2},{2,3},{3,4},{4,5},{5,6},{6,7},{7,8},{8,9},{9,10},{10,1... | collective-permute-start | bytes 36872 | tf_op jit(solution)/shard_map/ppermute | solution.py:299
  170.3 6.2 %collective-permute-start.15 = (f32[6,4,128]{2,1,0:T(4,128)S(1)}, f32[6,4,128]{2,1,0:T(4,128)S(1)}, u32[]{:S(2)}, u32[]{:S(2)}) collective-permute-start(f32[6,4,128]{2,1,0:T(4,128)S(1)} %get-tuple-element.53), channel_id=1, source_target_pairs={{1,0},{2,1},{3,2},{4,3},{5,4},{6,5},{7,6},{8,7},{9,8},{10,9},{11,1... | collective-permute-start | bytes 36872 | tf_op jit(solution)/shard_map/ppermute | solution.py:299
  185.0 12.8 %all-to-all-start.6 = ((f32[8,5,2,8,128]{4,3,2,1,0:T(8,128)}), f32[8,5,2,8,128]{4,3,2,1,0:T(8,128)S(1)}, u32[]{:S(2)}, u32[]{:S(2)}) async-start(f32[8,5,2,8,128]{4,3,2,1,0:T(8,128)} %shard_map.98), calls=%async_computation.6 | async-start | bytes 655360 | tf_op jit(solution)/shard_map/all_to_all | solution.py:341
  198.5 18.9 %all-to-all-start.9 = ((f32[16,1,128]{2,1,0:T(1,128)}), f32[16,1,128]{2,1,0:T(1,128)S(1)}, u32[]{:S(2)}, u32[]{:S(2)}) async-start(f32[16,1,128]{2,1,0:T(1,128)} %broadcast_in_dim.25), calls=%async_computation.9 | async-start | bytes 16384 | tf_op jit(solution)/shard_map/all_to_all | solution.py:330
  217.3 25.1 %all-to-all-start.7 = ((f32[4,5,2,8,128]{4,3,2,1,0:T(8,128)}), f32[4,5,2,8,128]{4,3,2,1,0:T(8,128)S(1)}, u32[]{:S(2)}, u32[]{:S(2)}) async-start(f32[4,5,2,8,128]{4,3,2,1,0:T(8,128)} %shard_map.99), calls=%async_computation.7 | async-start | bytes 327680 | tf_op jit(solution)/shard_map/all_to_all | solution.py:343

commit v2 on v0

v2 whole, which is shorter than its diff:
```python
import functools

import jax
import jax.numpy as jnp
from jax import lax
from jax.experimental import pallas as pl
from jax.experimental.pallas import tpu as pltpu
from jax.sharding import PartitionSpec as P

STEPS = 4
MASS = 0.02
SOUND = 20.0
VISCOSITY = 2.0
STIFF = 50.0
DT = 0.05

FAR = 1.0e6

F32 = jnp.float32
BF16 = jnp.bfloat16
PARAMS = pltpu.CompilerParams(vmem_limit_bytes=40 * 1024 * 1024)
VMEM = pl.BlockSpec(memory_space=pltpu.VMEM)
SMEM = pl.BlockSpec(memory_space=pltpu.SMEM)


def shape(*dims):
    return jax.ShapeDtypeStruct(dims, F32)


def call(kernel, outs, scalars, arrays, scratch=(), estimate=0):
    return pl.pallas_call(
        kernel,
        out_shape=outs,
        in_specs=[SMEM] * len(scalars) + [VMEM] * len(arrays),
        out_specs=[VMEM] * len(outs) if isinstance(outs, list) else VMEM,
        scratch_shapes=scratch,
        compiler_params=PARAMS,
        cost_estimate=pl.CostEstimate(flops=estimate, bytes_accessed=1 << 20, transcendentals=0) if estimate else None,
    )(*scalars, *arrays)


def pressure(s):
    inv = 1.0 / s
    return SOUND * (s - 1.0) * inv * inv, inv


def penalties(x, touch, live, offset, column):
    return touch * live * jnp.maximum(0.0, x - column + offset - 0.5)


def own_force(new, marks, offset, first):
    total = 0.0
    for c, fields in enumerate(new):
        total = total + STIFF * penalties(fields[0], marks[1, c], marks[0, c], offset, first + c)
    total = jnp.sum(total, axis=0, keepdims=True)
    return jnp.broadcast_to(jnp.sum(total, axis=1, keepdims=True), total.shape)


def visible(fields, live):
    alive = live > 0
    x, y, u, v, rho = fields
    return [jnp.where(alive, x, FAR), y, u, v, jnp.where(alive, rho, 1.0)]


def fill_depth(place, new, marks, force, sent):
    depth, ndepth = place[1], sent.shape[0]
    cols, rows = marks.shape[1:3]
    sent[...] = jnp.zeros(sent.shape, F32)
    sent[:, 5 * cols : 5 * cols + 1, :] = jnp.broadcast_to(force[None], (ndepth, 1, force.shape[1]))
    seen = [visible(new[c], marks[0, c]) for c in range(cols)]

    @pl.when(depth > 0)
    def _():
        for c in range(cols):
            for f in range(5):
                sent[depth - 1, f * cols + c : f * cols + c + 1] = seen[c][f][0:1]

    @pl.when(depth < ndepth - 1)
    def _():
        for c in range(cols):
            for f in range(5):
                sent[depth + 1, f * cols + c : f * cols + c + 1] = seen[c][f][rows - 1 : rows]


def start_kernel(place, origin, positions, velocity, density, marks, tool, sent):
    cols = positions.shape[1]
    new = [[positions[0, c], positions[1, c], velocity[0, c], velocity[1, c], density[c]] for c in range(cols)]
    fill_depth(place, new, marks, own_force(new, marks, tool[0:1], origin[2]), sent)


def extend_kernel(place, own, marks, got, left, right, force):
    depth, ndepth = place[1], got.shape[0]
    cols, rows = own.shape[1:3]
    above = got[jnp.maximum(depth - 1, 0)]
    below = got[jnp.minimum(depth + 1, ndepth - 1)]
    blank = [FAR, 0.0, 0.0, 0.0, 1.0]
    for c, column in ((0, left), (cols - 1, right)):
        seen = visible([own[f, c] for f in range(5)], marks[0, c])
        for f in range(5):
            k = f * cols + c
            column[f, 0:1] = jnp.where(depth > 0, above[k : k + 1], blank[f])
            column[f, 1 : rows + 1] = seen[f]
            column[f, rows + 1 : rows + 2] = jnp.where(depth < ndepth - 1, below[k : k + 1], blank[f])
    total = jnp.sum(got[:, 5 * cols : 5 * cols + 1, :], axis=0)
    force[...] = jnp.broadcast_to(total[None], force.shape)


def rates_kernel(place, origin, before, left, right, after, out, feat, acc2, acc3):
    ncut = place[2]
    tall, slots = left.shape[1:]
    rows = tall - 2
    x0, y0 = origin[0], origin[1]
    columns = []
    for c, ref in enumerate((before, left, right, after)):
        x, y, u, v, s = [ref[f] for f in range(5)]
        if c in (0, 3):
            outside = place[0] == (0 if c == 0 else ncut - 1)
            x = jnp.where(outside, FAR, x)
            s = jnp.where(outside, 1.0, s)
        columns.append((x, y))
        lx, ly = x - x0, y - y0
        press, inv = pressure(s)
        parts = [jnp.ones_like(x), lx, ly, press, press * lx, press * ly, u, v, u * lx + v * ly, inv, inv * u, inv * v]
        for k in range(16):
            high = parts[k].astype(BF16).astype(F32) if k < 12 else jnp.zeros_like(x)
            feat[pl.ds(c * tall * 32 + k, tall, stride=32), :] = high
            feat[pl.ds(c * tall * 32 + 16 + k, tall, stride=32), :] = parts[k] - high if k < 12 else high
    around = [(a, b) for a in range(3) for b in range(3)]
    for i in range(2 * rows):
        c, r = divmod(i, rows)
        xi, yi = [jnp.broadcast_to(f[r + 1 : r + 2], (slots, slots)).T for f in columns[c + 1]]

        def weights(a, b):
            dx = (xi - columns[c + a][0][r + b : r + b + 1]).astype(BF16)
            dy = (yi - columns[c + a][1][r + b : r + b + 1]).astype(BF16)
            q = jnp.maximum(BF16(0.0), BF16(1.0) - dx * dx - dy * dy)
            q2 = q * q
            return jnp.concatenate([q2, q2 * q], axis=0)

        total = None
        for n in range(0, 9, 2):
            pair = around[n : n + 2]
            w = jnp.concatenate([weights(a, b) for a, b in pair], axis=1)
            f = jnp.concatenate([feat[pl.ds(((c + a) * tall + r + b) * 32, 32), :] for a, b in pair], axis=1).astype(BF16)
            found = lax.dot_general(f, w, (((1,), (1,)), ((), ())), preferred_element_type=F32)
            total = found if total is None else total + found
        acc2[i * 32 : (i + 1) * 32] = total[:, :slots]
        acc3[i * 32 : (i + 1) * 32] = total[:, slots:]

    for c, ref in enumerate((left, right)):

        def summed(k):
            acc = acc2 if k < 9 else acc3
            return sum(acc[pl.ds(c * rows * 32 + k + low, rows, stride=32), :] for low in (0, 16))

        x, y, u, v, s = [ref[f, 1 : rows + 1] for f in range(5)]
        x, y = x - x0, y - y0
        press, _ = pressure(s)
        a0, ax, ay, ap, apx, apy, au, av, aw, b0, bu, bv = [summed(k) for k in range(12)]
        sx, sy = x * a0 - ax, y * a0 - ay
        out[0, c] = (6.0 * MASS) * (press * sx + x * ap - apx) - (VISCOSITY * MASS) * (u * b0 - bu)
        out[1, c] = (6.0 * MASS) * (press * sy + y * ap - apy) - (VISCOSITY * MASS) * (v * b0 - bv)
        out[2, c] = (-6.0 * MASS) * (u * sx + v * sy - x * au - y * av + aw)


def moved_state(own, found, marks, offset, first):
    new = []
    for c in range(own.shape[1]):
        live = marks[0, c]
        pen = penalties(own[0, c], marks[1, c], live, offset, first + c)
        u = own[2, c] + DT * live * (found[0, c] - STIFF * pen)
        v = own[3, c] + DT * live * found[1, c]
        x = own[0, c] + DT * live * u
        y = own[1, c] + DT * live * v
        rho = own[4, c] + DT * live * found[2, c]
        new.append([x, y, u, v, rho])
    return new


def tool_step(tool, force, scale):
    speed = tool[1:2] + DT * (1.0 - force * scale)
    return tool[0:1] + DT * speed, speed


def update_kernel(scale, place, origin, own, found, marks, total, tool, new_own, new_tool, sent):
    new = moved_state(own, found, marks, tool[0:1], origin[2])
    for c, fields in enumerate(new):
        for f in range(5):
            new_own[f, c] = fields[f]
    offset, speed = tool_step(tool, jnp.sum(total[...], axis=0), scale)
    new_tool[0:1] = offset
    new_tool[1:2] = speed
    fill_depth(place, new, marks, own_force(new, marks, offset, origin[2]), sent)


def last_kernel(near, place, destination, origin, own, found, marks, tool, force, sent):
    cols, rows, slots = own.shape[1:]
    size = 5 * cols * rows
    new = moved_state(own, found, marks, tool[0:1], origin[2])
    sent[...] = jnp.zeros(sent.shape, F32)
    sent[:, size:, :] = jnp.broadcast_to(force[0:1], (near, sent.shape[1] - size, slots))
    digit = lax.rem(destination[place[0]], near)
    for f in range(5):
        for c in range(cols):
            at = (f * cols + c) * rows
            sent[digit, at : at + rows] = new[c][f]


def sort_kernel(near, size, place, destination, got, sent):
    far, most, slots = sent.shape
    group, digit = lax.div(place[0], near), lax.rem(place[0], near)
    sent[...] = jnp.zeros(sent.shape, F32)
    total = jnp.sum(got[:, size : size + 1, :], axis=0, keepdims=True)
    sent[:, size:, :] = jnp.broadcast_to(total, (far, most - size, slots))
    for k in range(near):
        target = destination[group * near + k]

        @pl.when(lax.rem(target, near) == digit)
        def _():
            sent[lax.div(target, near), 0:size] = got[k, 0:size]


def take_kernel(near, scale, place, destination, got, tool, out, new_tool):
    cols, rows, slots = out.shape[1:]
    size = 5 * cols * rows
    source = 0
    for k in range(got.shape[0] * near):
        source = jnp.where(destination[k] == place[0], k // near, source)
    for f in range(5):
        for c in range(cols):
            at = (f * cols + c) * rows
            out[f, c] = got[source, at : at + rows]
    offset, speed = tool_step(tool, jnp.sum(got[:, size : size + 1, :], axis=0), scale)
    new_tool[0:1] = offset
    new_tool[1:2] = speed


def body(positions, velocity, density, counts, contact_mask, destination, tool):
    cols, rows, slots = density.shape
    ncut, ndepth = lax.axis_size("cut"), lax.axis_size("depth")
    here, depth = lax.axis_index("cut"), lax.axis_index("depth")
    scale = 1.0 / (ncut * cols * ndepth * rows * slots)
    place = jnp.stack([here, depth, jnp.int32(ncut)]).astype(jnp.int32)
    first_col = (here * cols).astype(F32)
    first_row = (depth * rows).astype(F32)
    origin = jnp.stack([first_col + 0.5 * cols, first_row + 0.5 * rows, first_col])
    live = (jnp.arange(slots)[None, None, :] < counts[:, :, None]).astype(F32)
    touch = jnp.broadcast_to(contact_mask[:, :, None].astype(F32), live.shape)
    marks = jnp.stack([live, touch])
    tool = jnp.broadcast_to(tool[:, None], (2, slots))
    own = jnp.concatenate([positions, velocity, density[None]], axis=0)
    near = 8 if ncut % 8 == 0 else 1
    far = ncut // near
    size = 5 * cols * rows
    tall = rows + 2
    message = shape(ndepth, 16, slots)
    forth = [(i, i + 1) for i in range(ncut - 1)]
    back = [(i + 1, i) for i in range(ncut - 1)]

    sent = call(start_kernel, message, (place, origin), (positions, velocity, density, marks, tool))
    for step in range(STEPS):
        got = lax.all_to_all(sent, "depth", 0, 0, tiled=True)
        outs = [shape(5, tall, slots), shape(5, tall, slots), shape(ncut, 1, slots)]
        left, right, force = call(extend_kernel, outs, (place,), (own, marks, got))
        before = lax.ppermute(right, "cut", forth)
        after = lax.ppermute(left, "cut", back)
        if step < STEPS - 1:
            total = lax.all_to_all(force, "cut", 0, 0, tiled=True)
        scratch = [pltpu.VMEM((4 * tall * 32, slots), F32)] + [pltpu.VMEM((cols * rows * 32, slots), F32)] * 2
        found = call(rates_kernel, shape(3, cols, rows, slots), (place, origin), (before, left, right, after), scratch, 1 << 27)
        if step < STEPS - 1:
            outs = [shape(5, cols, rows, slots), shape(2, slots), message]
            kernel = functools.partial(update_kernel, scale)
            own, tool, sent = call(kernel, outs, (place, origin), (own, found, marks, total, tool))
    kernel = functools.partial(last_kernel, near)
    sent = call(kernel, shape(near, size + 8, slots), (place, destination, origin), (own, found, marks, tool, force[:, 0]))
    close = [[g * near + k for k in range(near)] for g in range(far)]
    apart = [[g * near + k for g in range(far)] for k in range(near)]
    got = lax.all_to_all(sent, "cut", 0, 0, tiled=True, axis_index_groups=close)
    sent = call(functools.partial(sort_kernel, near, size), shape(far, size + 8, slots), (place, destination), (got,))
    got = lax.all_to_all(sent, "cut", 0, 0, tiled=True, axis_index_groups=apart)
    outs = [shape(5, cols, rows, slots), shape(2, slots)]
    moved, tool = call(functools.partial(take_kernel, near, scale), outs, (place, destination), (got, tool))
    return moved, tool[:, 0]


def solution(mesh):
    return jax.shard_map(
        body,
        mesh=mesh,
        in_specs=(
            P(None, "cut", "depth", None),
            P(None, "cut", "depth", None),
            P("cut", "depth", None),
            P("cut", "depth"),
            P("cut", "depth"),
            P(),
            P(),
        ),
        out_specs=(P(None, "cut", "depth", None), P()),
        check_vma=False,
    )
```

time: 652 us -> 199 us (0.31)
  the two profiles are of different devices: /device:TPU:4 before, /device:TPU:8 now
where the time goes in v2:
time: 199 us; the launch traced here: 198 us
  starting transfers between devices  73.1 us (37%)
  blocking collectives  71.5 us (36%)
  waiting for transfers between devices  24.6 us (12%)
  Pallas kernels  24.5 us (12%)
  local copies, waits for them, and re-layouts  3.35 us (2%)
    all_to_all x3, starting transfers between devices, body(): total = lax.all_to_all(force, 'cut', 0, 0, tiled=True)  43.5 us
    all_to_all x3, blocking collectives, body(): got = lax.all_to_all(sent, 'depth', 0, 0, tiled=True)  31.7 us
    pallas_call x15, Pallas kernels, call(): pl.pallas_call(kernel, out_shape=outs, in_specs=[SMEM] * len(scalars) + [...  24.5 us
    all_to_all x1, blocking collectives, body(): got = lax.all_to_all(sent, 'cut', 0, 0, tiled=True, axis_index_groups=apart)  21.9 us
    all_to_all x1, blocking collectives, body(): got = lax.all_to_all(sent, 'cut', 0, 0, tiled=True, axis_index_groups=close)  17.9 us
    ppermute x4, waiting for transfers between devices, body(): after = lax.ppermute(left, 'cut', back)  16.5 us
    ppermute x4, starting transfers between devices, body(): before = lax.ppermute(right, 'cut', forth)  13 us
    ppermute x4, starting transfers between devices, body(): after = lax.ppermute(left, 'cut', back)  10.5 us
  transfers between devices with their start and end apart: 12, of which 7 were waited for; matrix products, arithmetic and copies ran while one was open for 0% of the time, Pallas kernels for 6%

profile of v2, /device:TPU:8, one launch (start us, length us, event | category | flops | bytes accessed | tf_op | source)
XLA Modules:
  0.0 198.3 jit_solution(7533176206023905067)
XLA Ops:
  0.6 0.7 copy-done.5
  1.3 0.7 copy-done.4
  2.0 0.1 fusion
  2.1 0.1 stack_broadcast_in_dim.2
  2.2 0.1 pad_maximum_fusion.2.origin
  2.2 0.1 pad_add_fusion.place
  2.3 0.6 copy-done.6
  2.9 0.1 broadcast_in_dim.5.tool
  3.0 1.3 shard_map.86
  4.3 6.1 %all-to-all-start = ((f32[16,16,128]{2,1,0:T(8,128)}), f32[16,16,128]{2,1,0:T(8,128)S(1)}, u32[]{:S(2)}, u32[]{:S(2)}) async-start(f32[16,16,128]{2,1,0:T(8,128)} %shard_map.86), calls=%async_computation | async-start | bytes 262144 | tf_op jit(solution)/shard_map/all_to_all | solution.py:262
  10.4 8.0 %all-to-all-done.got = f32[16,16,128]{2,1,0:T(8,128)S(1)} async-done(((f32[16,16,128]{2,1,0:T(8,128)}), f32[16,16,128]{2,1,0:T(8,128)S(1)}, u32[]{:S(2)}, u32[]{:S(2)}) %all-to-all-start) | async-done | bytes 131104 | tf_op jit(solution)/shard_map/all_to_all | solution.py:262
  18.4 1.2 shard_map.87
  19.6 16.7 %all-to-all-start.1 = ((f32[32,1,128]{2,1,0:T(1,128)}), f32[32,1,128]{2,1,0:T(1,128)S(1)}, u32[]{:S(2)}, u32[]{:S(2)}) async-start(f32[32,1,128]{2,1,0:T(1,128)} %get-tuple-element.27), calls=%async_computation.1 | async-start | bytes 32768 | tf_op jit(solution)/shard_map/all_to_all | solution.py:268
  36.3 3.4 %collective-permute-start = (f32[5,10,128]{2,1,0:T(8,128)S(1)}, f32[5,10,128]{2,1,0:T(8,128)S(1)}, u32[]{:S(2)}, u32[]{:S(2)}) collective-permute-start(f32[5,10,128]{2,1,0:T(8,128)S(1)} %get-tuple-element.25.right), channel_id=1, source_target_pairs={{0,16},{16,32},{32,48},{48,64},{64,80},{80,96},{96,112},{112,128},... | collective-permute-start | bytes 76808 | tf_op jit(solution)/shard_map/ppermute | solution.py:265
  39.7 2.5 %collective-permute-start.1 = (f32[5,10,128]{2,1,0:T(8,128)S(1)}, f32[5,10,128]{2,1,0:T(8,128)S(1)}, u32[]{:S(2)}, u32[]{:S(2)}) collective-permute-start(f32[5,10,128]{2,1,0:T(8,128)S(1)} %get-tuple-element.26.left), channel_id=1, source_target_pairs={{16,0},{32,16},{48,32},{64,48},{80,64},{96,80},{112,96},{128,112},... | collective-permute-start | bytes 76808 | tf_op jit(solution)/shard_map/ppermute | solution.py:266
  42.1 0.1 collective-permute-done.before
  42.2 4.3 %collective-permute-done.1.after = f32[5,10,128]{2,1,0:T(8,128)S(1)} collective-permute-done((f32[5,10,128]{2,1,0:T(8,128)S(1)}, f32[5,10,128]{2,1,0:T(8,128)S(1)}, u32[]{:S(2)}, u32[]{:S(2)}) %collective-permute-start.1) | collective-permute-done | bytes 25632 | tf_op jit(solution)/shard_map/ppermute | solution.py:266
  46.5 3.7 %shard_map.88.found = f32[3,2,8,128]{3,2,1,0:T(8,128)S(1)} custom-call(s32[3]{0:T(128)S(1)} %pad_add_fusion.place, f32[3]{0:T(128)S(1)} %pad_maximum_fusion.2.origin, f32[5,10,128]{2,1,0:T(8,128)S(1)} %collective-permute-done.before, f32[5,10,128]{2,1,0:T(8,128)S(1)} %get-tuple-element.26.left, f32[5,10,128]{2,1,0:T(8,128)S(1)} %get-tuple-element.25.right, ...), custom_call_target="tpu_custom_call" | custom-call | flops 134217728 | bytes 1048576 | tf_op jit(solution)/shard_map/pallas_call | solution.py:31
  50.2 0.7 shard_map.89
  50.8 10.6 %all_to_all.45.got = f32[16,16,128]{2,1,0:T(8,128)S(1)} all-to-all(f32[16,16,128]{2,1,0:T(8,128)S(1)} %get-tuple-element.29), channel_id=1, replica_groups=mesh['cut'=32,'depth'=16] {'depth'}, dimensions={0} | all-to-all | bytes 262144 | tf_op jit(solution)/shard_map/all_to_all | solution.py:262
  61.4 1.2 shard_map.90
  62.6 13.4 %all-to-all-start.3 = ((f32[32,1,128]{2,1,0:T(1,128)}), f32[32,1,128]{2,1,0:T(1,128)S(1)}, u32[]{:S(2)}, u32[]{:S(2)}) async-start(f32[32,1,128]{2,1,0:T(1,128)} %get-tuple-element.32), calls=%async_computation.3 | async-start | bytes 32768 | tf_op jit(solution)/shard_map/all_to_all | solution.py:268
  76.0 3.4 %collective-permute-start.2 = (f32[5,10,128]{2,1,0:T(8,128)S(1)}, f32[5,10,128]{2,1,0:T(8,128)S(1)}, u32[]{:S(2)}, u32[]{:S(2)}) collective-permute-start(f32[5,10,128]{2,1,0:T(8,128)S(1)} %get-tuple-element.30.right), channel_id=1, source_target_pairs={{0,16},{16,32},{32,48},{48,64},{64,80},{80,96},{96,112},{112,128},... | collective-permute-start | bytes 76808 | tf_op jit(solution)/shard_map/ppermute | solution.py:265
  79.3 2.5 %collective-permute-start.3 = (f32[5,10,128]{2,1,0:T(8,128)S(1)}, f32[5,10,128]{2,1,0:T(8,128)S(1)}, u32[]{:S(2)}, u32[]{:S(2)}) collective-permute-start(f32[5,10,128]{2,1,0:T(8,128)S(1)} %get-tuple-element.31.left), channel_id=1, source_target_pairs={{16,0},{32,16},{48,32},{64,48},{80,64},{96,80},{112,96},{128,112},... | collective-permute-start | bytes 76808 | tf_op jit(solution)/shard_map/ppermute | solution.py:266
  81.9 4.3 %collective-permute-done.3.after = f32[5,10,128]{2,1,0:T(8,128)S(1)} collective-permute-done((f32[5,10,128]{2,1,0:T(8,128)S(1)}, f32[5,10,128]{2,1,0:T(8,128)S(1)}, u32[]{:S(2)}, u32[]{:S(2)}) %collective-permute-start.3) | collective-permute-done | bytes 25632 | tf_op jit(solution)/shard_map/ppermute | solution.py:266
  86.1 3.7 %shard_map.91.found = f32[3,2,8,128]{3,2,1,0:T(8,128)S(1)} custom-call(s32[3]{0:T(128)S(1)} %pad_add_fusion.place, f32[3]{0:T(128)S(1)} %pad_maximum_fusion.2.origin, f32[5,10,128]{2,1,0:T(8,128)S(1)} %collective-permute-done.2.before, f32[5,10,128]{2,1,0:T(8,128)S(1)} %get-tuple-element.31.left, f32[5,10,128]{2,1,0:T(8,128)S(1)} %get-tuple-element.30.right, ...), custom_call_target="tpu_custom_call" | custom-call | flops 134217728 | bytes 1048576 | tf_op jit(solution)/shard_map/pallas_call | solution.py:31
  89.8 0.7 shard_map.92
  90.5 10.6 %all_to_all.46.got = f32[16,16,128]{2,1,0:T(8,128)S(1)} all-to-all(f32[16,16,128]{2,1,0:T(8,128)S(1)} %get-tuple-element.35), channel_id=1, replica_groups=mesh['cut'=32,'depth'=16] {'depth'}, dimensions={0} | all-to-all | bytes 262144 | tf_op jit(solution)/shard_map/all_to_all | solution.py:262
  101.1 1.2 shard_map.93
  102.2 13.4 %all-to-all-start.5 = ((f32[32,1,128]{2,1,0:T(1,128)}), f32[32,1,128]{2,1,0:T(1,128)S(1)}, u32[]{:S(2)}, u32[]{:S(2)}) async-start(f32[32,1,128]{2,1,0:T(1,128)} %get-tuple-element.38), calls=%async_computation.5 | async-start | bytes 32768 | tf_op jit(solution)/shard_map/all_to_all | solution.py:268
  115.6 3.4 %collective-permute-start.4 = (f32[5,10,128]{2,1,0:T(8,128)S(1)}, f32[5,10,128]{2,1,0:T(8,128)S(1)}, u32[]{:S(2)}, u32[]{:S(2)}) collective-permute-start(f32[5,10,128]{2,1,0:T(8,128)S(1)} %get-tuple-element.36.right), channel_id=1, source_target_pairs={{0,16},{16,32},{32,48},{48,64},{64,80},{80,96},{96,112},{112,128},... | collective-permute-start | bytes 76808 | tf_op jit(solution)/shard_map/ppermute | solution.py:265
  119.0 2.6 %collective-permute-start.5 = (f32[5,10,128]{2,1,0:T(8,128)S(1)}, f32[5,10,128]{2,1,0:T(8,128)S(1)}, u32[]{:S(2)}, u32[]{:S(2)}) collective-permute-start(f32[5,10,128]{2,1,0:T(8,128)S(1)} %get-tuple-element.37.left), channel_id=1, source_target_pairs={{16,0},{32,16},{48,32},{64,48},{80,64},{96,80},{112,96},{128,112},... | collective-permute-start | bytes 76808 | tf_op jit(solution)/shard_map/ppermute | solution.py:266
  121.7 4.1 %collective-permute-done.5.after = f32[5,10,128]{2,1,0:T(8,128)S(1)} collective-permute-done((f32[5,10,128]{2,1,0:T(8,128)S(1)}, f32[5,10,128]{2,1,0:T(8,128)S(1)}, u32[]{:S(2)}, u32[]{:S(2)}) %collective-permute-start.5) | collective-permute-done | bytes 25632 | tf_op jit(solution)/shard_map/ppermute | solution.py:266
  125.8 3.7 %shard_map.94.found = f32[3,2,8,128]{3,2,1,0:T(8,128)S(1)} custom-call(s32[3]{0:T(128)S(1)} %pad_add_fusion.place, f32[3]{0:T(128)S(1)} %pad_maximum_fusion.2.origin, f32[5,10,128]{2,1,0:T(8,128)S(1)} %collective-permute-done.4.before, f32[5,10,128]{2,1,0:T(8,128)S(1)} %get-tuple-element.37.left, f32[5,10,128]{2,1,0:T(8,128)S(1)} %get-tuple-element.36.right, ...), custom_call_target="tpu_custom_call" | custom-call | flops 134217728 | bytes 1048576 | tf_op jit(solution)/shard_map/pallas_call | solution.py:31
  129.5 0.7 shard_map.95
  130.2 10.6 %all_to_all.47.got = f32[16,16,128]{2,1,0:T(8,128)S(1)} all-to-all(f32[16,16,128]{2,1,0:T(8,128)S(1)} %get-tuple-element.41), channel_id=1, replica_groups=mesh['cut'=32,'depth'=16] {'depth'}, dimensions={0} | all-to-all | bytes 262144 | tf_op jit(solution)/shard_map/all_to_all | solution.py:262
  140.8 0.6 shard_map.96
  141.3 2.9 %collective-permute-start.6 = (f32[5,10,128]{2,1,0:T(8,128)S(1)}, f32[5,10,128]{2,1,0:T(8,128)S(1)}, u32[]{:S(2)}, u32[]{:S(2)}) collective-permute-start(f32[5,10,128]{2,1,0:T(8,128)S(1)} %get-tuple-element.42.right), channel_id=1, source_target_pairs={{0,16},{16,32},{32,48},{48,64},{64,80},{80,96},{96,112},{112,128},... | collective-permute-start | bytes 76808 | tf_op jit(solution)/shard_map/ppermute | solution.py:265
  144.3 2.9 %collective-permute-start.7 = (f32[5,10,128]{2,1,0:T(8,128)S(1)}, f32[5,10,128]{2,1,0:T(8,128)S(1)}, u32[]{:S(2)}, u32[]{:S(2)}) collective-permute-start(f32[5,10,128]{2,1,0:T(8,128)S(1)} %get-tuple-element.43.left), channel_id=1, source_target_pairs={{16,0},{32,16},{48,32},{64,48},{80,64},{96,80},{112,96},{128,112},... | collective-permute-start | bytes 76808 | tf_op jit(solution)/shard_map/ppermute | solution.py:266
  147.2 3.8 %collective-permute-done.7.after = f32[5,10,128]{2,1,0:T(8,128)S(1)} collective-permute-done((f32[5,10,128]{2,1,0:T(8,128)S(1)}, f32[5,10,128]{2,1,0:T(8,128)S(1)}, u32[]{:S(2)}, u32[]{:S(2)}) %collective-permute-start.7) | collective-permute-done | bytes 25632 | tf_op jit(solution)/shard_map/ppermute | solution.py:266
  151.1 3.7 %shard_map.97.found = f32[3,2,8,128]{3,2,1,0:T(8,128)S(1)} custom-call(s32[3]{0:T(128)S(1)} %pad_add_fusion.place, f32[3]{0:T(128)S(1)} %pad_maximum_fusion.2.origin, f32[5,10,128]{2,1,0:T(8,128)S(1)} %collective-permute-done.6.before, f32[5,10,128]{2,1,0:T(8,128)S(1)} %get-tuple-element.43.left, f32[5,10,128]{2,1,0:T(8,128)S(1)} %get-tuple-element.42.right, ...), custom_call_target="tpu_custom_call" | custom-call | flops 134217728 | bytes 1048576 | tf_op jit(solution)/shard_map/pallas_call | solution.py:31
  154.7 0.6 copy-done.3
  155.4 0.6 shard_map.98
  156.0 17.9 %all_to_all.48.got = f32[8,88,128]{2,1,0:T(8,128)S(1)} all-to-all(f32[8,88,128]{2,1,0:T(8,128)S(1)} %shard_map.98), channel_id=1, replica_groups={{0,16,32,48,64,80,96,112},{128,144,160,176,192,208,224,240},{256,272,28..., dimensions={0} | all-to-all | bytes 720896 | tf_op jit(solution)/shard_map/all_to_all | solution.py:279
  173.9 0.6 shard_map.99
  174.5 21.9 %all_to_all.49.got = f32[4,88,128]{2,1,0:T(8,128)S(1)} all-to-all(f32[4,88,128]{2,1,0:T(8,128)S(1)} %shard_map.99), channel_id=1, replica_groups={{0,128,256,384},{16,144,272,400},{32,160,288,416},{48,176,304,432},{64,..., dimensions={0} | all-to-all | bytes 360448 | tf_op jit(solution)/shard_map/all_to_all | solution.py:281
  196.5 1.2 shard_map.100
  197.7 0.6 slice_reduce_fusion
  (19 shorter events, 0.1 us)
Async XLA Ops:
  0.6 0.7 copy-start.5
  1.3 0.7 copy-start.4
  2.1 0.8 copy-start
  2.1 0.8 copy-start.1
  2.1 0.8 copy-start.2
  2.2 0.7 copy-start.6
  4.3 14.1 %all-to-all-start = ((f32[16,16,128]{2,1,0:T(8,128)}), f32[16,16,128]{2,1,0:T(8,128)S(1)}, u32[]{:S(2)}, u32[]{:S(2)}) async-start(f32[16,16,128]{2,1,0:T(8,128)} %shard_map.86), calls=%async_computation | async-start | bytes 262144 | tf_op jit(solution)/shard_map/all_to_all | solution.py:262
  19.6 30.6 %all-to-all-start.1 = ((f32[32,1,128]{2,1,0:T(1,128)}), f32[32,1,128]{2,1,0:T(1,128)S(1)}, u32[]{:S(2)}, u32[]{:S(2)}) async-start(f32[32,1,128]{2,1,0:T(1,128)} %get-tuple-element.27), calls=%async_computation.1 | async-start | bytes 32768 | tf_op jit(solution)/shard_map/all_to_all | solution.py:268
  36.3 5.9 %collective-permute-start = (f32[5,10,128]{2,1,0:T(8,128)S(1)}, f32[5,10,128]{2,1,0:T(8,128)S(1)}, u32[]{:S(2)}, u32[]{:S(2)}) collective-permute-start(f32[5,10,128]{2,1,0:T(8,128)S(1)} %get-tuple-element.25.right), channel_id=1, source_target_pairs={{0,16},{16,32},{32,48},{48,64},{64,80},{80,96},{96,112},{112,128},... | collective-permute-start | bytes 76808 | tf_op jit(solution)/shard_map/ppermute | solution.py:265
  39.7 6.8 %collective-permute-start.1 = (f32[5,10,128]{2,1,0:T(8,128)S(1)}, f32[5,10,128]{2,1,0:T(8,128)S(1)}, u32[]{:S(2)}, u32[]{:S(2)}) collective-permute-start(f32[5,10,128]{2,1,0:T(8,128)S(1)} %get-tuple-element.26.left), channel_id=1, source_target_pairs={{16,0},{32,16},{48,32},{64,48},{80,64},{96,80},{112,96},{128,112},... | collective-permute-start | bytes 76808 | tf_op jit(solution)/shard_map/ppermute | solution.py:266
  62.6 27.2 %all-to-all-start.3 = ((f32[32,1,128]{2,1,0:T(1,128)}), f32[32,1,128]{2,1,0:T(1,128)S(1)}, u32[]{:S(2)}, u32[]{:S(2)}) async-start(f32[32,1,128]{2,1,0:T(1,128)} %get-tuple-element.32), calls=%async_computation.3 | async-start | bytes 32768 | tf_op jit(solution)/shard_map/all_to_all | solution.py:268
  76.0 5.9 %collective-permute-start.2 = (f32[5,10,128]{2,1,0:T(8,128)S(1)}, f32[5,10,128]{2,1,0:T(8,128)S(1)}, u32[]{:S(2)}, u32[]{:S(2)}) collective-permute-start(f32[5,10,128]{2,1,0:T(8,128)S(1)} %get-tuple-element.30.right), channel_id=1, source_target_pairs={{0,16},{16,32},{32,48},{48,64},{64,80},{80,96},{96,112},{112,128},... | collective-permute-start | bytes 76808 | tf_op jit(solution)/shard_map/ppermute | solution.py:265
  79.3 6.8 %collective-permute-start.3 = (f32[5,10,128]{2,1,0:T(8,128)S(1)}, f32[5,10,128]{2,1,0:T(8,128)S(1)}, u32[]{:S(2)}, u32[]{:S(2)}) collective-permute-start(f32[5,10,128]{2,1,0:T(8,128)S(1)} %get-tuple-element.31.left), channel_id=1, source_target_pairs={{16,0},{32,16},{48,32},{64,48},{80,64},{96,80},{112,96},{128,112},... | collective-permute-start | bytes 76808 | tf_op jit(solution)/shard_map/ppermute | solution.py:266
  102.2 27.2 %all-to-all-start.5 = ((f32[32,1,128]{2,1,0:T(1,128)}), f32[32,1,128]{2,1,0:T(1,128)S(1)}, u32[]{:S(2)}, u32[]{:S(2)}) async-start(f32[32,1,128]{2,1,0:T(1,128)} %get-tuple-element.38), calls=%async_computation.5 | async-start | bytes 32768 | tf_op jit(solution)/shard_map/all_to_all | solution.py:268
  115.6 6.0 %collective-permute-start.4 = (f32[5,10,128]{2,1,0:T(8,128)S(1)}, f32[5,10,128]{2,1,0:T(8,128)S(1)}, u32[]{:S(2)}, u32[]{:S(2)}) collective-permute-start(f32[5,10,128]{2,1,0:T(8,128)S(1)} %get-tuple-element.36.right), channel_id=1, source_target_pairs={{0,16},{16,32},{32,48},{48,64},{64,80},{80,96},{96,112},{112,128},... | collective-permute-start | bytes 76808 | tf_op jit(solution)/shard_map/ppermute | solution.py:265
  119.0 6.8 %collective-permute-start.5 = (f32[5,10,128]{2,1,0:T(8,128)S(1)}, f32[5,10,128]{2,1,0:T(8,128)S(1)}, u32[]{:S(2)}, u32[]{:S(2)}) collective-permute-start(f32[5,10,128]{2,1,0:T(8,128)S(1)} %get-tuple-element.37.left), channel_id=1, source_target_pairs={{16,0},{32,16},{48,32},{64,48},{80,64},{96,80},{112,96},{128,112},... | collective-permute-start | bytes 76808 | tf_op jit(solution)/shard_map/ppermute | solution.py:266
  141.3 5.9 %collective-permute-start.6 = (f32[5,10,128]{2,1,0:T(8,128)S(1)}, f32[5,10,128]{2,1,0:T(8,128)S(1)}, u32[]{:S(2)}, u32[]{:S(2)}) collective-permute-start(f32[5,10,128]{2,1,0:T(8,128)S(1)} %get-tuple-element.42.right), channel_id=1, source_target_pairs={{0,16},{16,32},{32,48},{48,64},{64,80},{80,96},{96,112},{112,128},... | collective-permute-start | bytes 76808 | tf_op jit(solution)/shard_map/ppermute | solution.py:265
  144.3 6.8 %collective-permute-start.7 = (f32[5,10,128]{2,1,0:T(8,128)S(1)}, f32[5,10,128]{2,1,0:T(8,128)S(1)}, u32[]{:S(2)}, u32[]{:S(2)}) collective-permute-start(f32[5,10,128]{2,1,0:T(8,128)S(1)} %get-tuple-element.43.left), channel_id=1, source_target_pairs={{16,0},{32,16},{48,32},{64,48},{80,64},{96,80},{112,96},{128,112},... | collective-permute-start | bytes 76808 | tf_op jit(solution)/shard_map/ppermute | solution.py:266
  154.7 0.7 copy-start.3

commit v3 on v2

v3 whole, which is shorter than its diff:
```python
import functools

import jax
import jax.numpy as jnp
from jax import lax
from jax.experimental import pallas as pl
from jax.experimental.pallas import tpu as pltpu
from jax.sharding import PartitionSpec as P

STEPS = 4
MASS = 0.02
SOUND = 20.0
VISCOSITY = 2.0
STIFF = 50.0
DT = 0.05

FAR = 1.0e6

COST = 20_000_000_000

F32 = jnp.float32
BF16 = jnp.bfloat16
PARAMS = pltpu.CompilerParams(vmem_limit_bytes=40 * 1024 * 1024)
VMEM = pl.BlockSpec(memory_space=pltpu.VMEM)
SMEM = pl.BlockSpec(memory_space=pltpu.SMEM)


def shape(*dims):
    return jax.ShapeDtypeStruct(dims, F32)


def call(kernel, outs, scalars, arrays, scratch=(), estimate=0):
    return pl.pallas_call(
        kernel,
        out_shape=outs,
        in_specs=[SMEM] * len(scalars) + [VMEM] * len(arrays),
        out_specs=[VMEM] * len(outs) if isinstance(outs, list) else VMEM,
        scratch_shapes=scratch,
        compiler_params=PARAMS,
        cost_estimate=pl.CostEstimate(flops=estimate, bytes_accessed=1 << 20, transcendentals=0) if estimate else None,
    )(*scalars, *arrays)


def pressure(s):
    inv = 1.0 / s
    return SOUND * (s - 1.0) * inv * inv, inv


def penalties(x, touch, live, offset, column):
    return touch * live * jnp.maximum(0.0, x - column + offset - 0.5)


def own_force(new, marks, offset, first):
    total = 0.0
    for c, fields in enumerate(new):
        total = total + STIFF * penalties(fields[0], marks[1, c], marks[0, c], offset, first + c)
    total = jnp.sum(total, axis=0, keepdims=True)
    return jnp.broadcast_to(jnp.sum(total, axis=1, keepdims=True), total.shape)


def visible(fields, live):
    alive = live > 0
    x, y, u, v, rho = fields
    return [jnp.where(alive, x, FAR), y, u, v, jnp.where(alive, rho, 1.0)]


def fill_depth(place, new, marks, force, sent):
    depth, ndepth = place[1], sent.shape[0]
    cols, rows = marks.shape[1:3]
    sent[...] = jnp.zeros(sent.shape, F32)
    sent[:, 5 * cols : 5 * cols + 1, :] = jnp.broadcast_to(force[None], (ndepth, 1, force.shape[1]))
    seen = [visible(new[c], marks[0, c]) for c in range(cols)]

    @pl.when(depth > 0)
    def _():
        for c in range(cols):
            for f in range(5):
                sent[depth - 1, f * cols + c : f * cols + c + 1] = seen[c][f][0:1]

    @pl.when(depth < ndepth - 1)
    def _():
        for c in range(cols):
            for f in range(5):
                sent[depth + 1, f * cols + c : f * cols + c + 1] = seen[c][f][rows - 1 : rows]


def origin(place, cols, rows):
    first = (place[0] * cols).astype(F32)
    return first + 0.5 * cols, (place[1] * rows).astype(F32) + 0.5 * rows, first


def start_kernel(place, counts, contact, first_tool, positions, velocity, density, own, marks, tool, sent):
    cols, rows, slots = density.shape
    row = lax.broadcasted_iota(jnp.int32, (rows, slots), 0)
    slot = lax.broadcasted_iota(jnp.int32, (rows, slots), 1)
    new = []
    for c in range(cols):
        filled = jnp.zeros((rows, slots), jnp.int32)
        touch = jnp.zeros((rows, slots), jnp.int32)
        for r in range(rows):
            filled = jnp.where(row == r, counts[c, r], filled)
            touch = jnp.where(row == r, contact[c, r], touch)
        marks[0, c] = jnp.where(slot < filled, 1.0, 0.0)
        marks[1, c] = touch.astype(F32)
        new.append([positions[0, c], positions[1, c], velocity[0, c], velocity[1, c], density[c]])
        for f in range(5):
            own[f, c] = new[c][f]
    offset = jnp.zeros((1, slots), F32) + first_tool[0]
    tool[0:1] = offset
    tool[1:2] = jnp.zeros((1, slots), F32) + first_tool[1]
    fill_depth(place, new, marks, own_force(new, marks, offset, origin(place, cols, rows)[2]), sent)


def extend_kernel(place, own, marks, got, *refs):
    left, right, force = refs[-3:]
    depth, ndepth = place[1], got.shape[0]
    cols, rows = own.shape[1:3]
    above = got[jnp.maximum(depth - 1, 0)]
    below = got[jnp.minimum(depth + 1, ndepth - 1)]
    blank = [FAR, 0.0, 0.0, 0.0, 1.0]
    for c, column in ((0, left), (cols - 1, right)):
        seen = visible([own[f, c] for f in range(5)], marks[0, c])
        for f in range(5):
            k = f * cols + c
            column[f, 0:1] = jnp.where(depth > 0, above[k : k + 1], blank[f])
            column[f, 1 : rows + 1] = seen[f]
            column[f, rows + 1 : rows + 2] = jnp.where(depth < ndepth - 1, below[k : k + 1], blank[f])
    total = jnp.sum(got[:, 5 * cols : 5 * cols + 1, :], axis=0)
    force[...] = jnp.broadcast_to(total[None], force.shape)


def pair_sums(columns, center, pairs, out, feat, acc2, acc3, earlier=None):
    x0, y0, _ = center
    tall, slots = columns[0][0].shape
    rows = len(pairs) // 2
    margin = (tall - rows) // 2
    for c, (x, y, u, v, s) in enumerate(columns):
        lx, ly = x - x0, y - y0
        press, inv = pressure(s)
        parts = [jnp.ones_like(x), lx, ly, press, press * lx, press * ly, u, v, u * lx + v * ly, inv, inv * u, inv * v]
        for k in range(16):
            high = parts[k].astype(BF16).astype(F32) if k < 12 else jnp.zeros_like(x)
            feat[pl.ds(c * tall * 32 + k, tall, stride=32), :] = high
            feat[pl.ds(c * tall * 32 + 16 + k, tall, stride=32), :] = parts[k] - high if k < 12 else high
    for i, ((c, r), around) in enumerate(pairs.items()):
        xi, yi = [jnp.broadcast_to(f[r : r + 1], (slots, slots)).T for f in columns[c][:2]]

        def weights(a, b):
            dx = (xi - columns[a][0][b : b + 1]).astype(BF16)
            dy = (yi - columns[a][1][b : b + 1]).astype(BF16)
            q = jnp.maximum(BF16(0.0), BF16(1.0) - dx * dx - dy * dy)
            q2 = q * q
            return jnp.concatenate([q2, q2 * q], axis=0)

        total = None
        for n in range(0, len(around), 2):
            pair = around[n : n + 2]
            w = jnp.concatenate([weights(a, b) for a, b in pair], axis=1)
            f = jnp.concatenate([feat[pl.ds((a * tall + b) * 32, 32), :] for a, b in pair], axis=1).astype(BF16)
            found = lax.dot_general(f, w, (((1,), (1,)), ((), ())), preferred_element_type=F32)
            total = found if total is None else total + found
        acc2[i * 32 : (i + 1) * 32] = total[:, :slots]
        acc3[i * 32 : (i + 1) * 32] = total[:, slots:]

    for n, c in enumerate(sorted({c for c, _ in pairs})):

        def summed(k):
            acc = acc2 if k < 9 else acc3
            return sum(acc[pl.ds(n * rows * 32 + k + low, rows, stride=32), :] for low in (0, 16))

        x, y, u, v, s = [f[margin : margin + rows] for f in columns[c]]
        x, y = x - x0, y - y0
        press, _ = pressure(s)
        a0, ax, ay, ap, apx, apy, au, av, aw, b0, bu, bv = [summed(k) for k in range(12)]
        sx, sy = x * a0 - ax, y * a0 - ay
        rates = [
            (6.0 * MASS) * (press * sx + x * ap - apx) - (VISCOSITY * MASS) * (u * b0 - bu),
            (6.0 * MASS) * (press * sy + y * ap - apy) - (VISCOSITY * MASS) * (v * b0 - bv),
            (-6.0 * MASS) * (u * sx + v * sy - x * au - y * av + aw),
        ]
        for f in range(3):
            out[f, n] = rates[f] if earlier is None else rates[f] + earlier[f, n]


def around_cell(c, r):
    return [(c + a, r + b) for a in (-1, 0, 1) for b in (-1, 0, 1)]


def inner_kernel(place, own, marks, out, feat, acc2, acc3):
    cols, rows = own.shape[1:3]
    columns = [visible([own[f, c] for f in range(5)], marks[0, c]) for c in range(cols)]
    cells = [(c, r) for c in range(cols) for r in range(rows)]
    pairs = {cell: [j for j in around_cell(*cell) if j in cells] for cell in cells}
    pair_sums(columns, origin(place, cols, rows), pairs, out, feat, acc2, acc3)


def outer_kernel(place, before, left, right, after, earlier, out, feat, acc2, acc3):
    cols, rows = earlier.shape[1:3]
    columns = []
    for c, ref in enumerate((before, left, right, after)):
        fields = [ref[f] for f in range(5)]
        if c in (0, 3):
            outside = place[0] == (0 if c == 0 else place[2] - 1)
            fields[0] = jnp.where(outside, FAR, fields[0])
            fields[4] = jnp.where(outside, 1.0, fields[4])
        columns.append(fields)
    cells = [(c + 1, r + 1) for c in range(cols) for r in range(rows)]
    pairs = {cell: [j for j in around_cell(*cell) if j not in cells] for cell in cells}
    pair_sums(columns, origin(place, cols, rows), pairs, out, feat, acc2, acc3, earlier)


def moved_state(own, found, marks, offset, first):
    new = []
    for c in range(own.shape[1]):
        live = marks[0, c]
        pen = penalties(own[0, c], marks[1, c], live, offset, first + c)
        u = own[2, c] + DT * live * (found[0, c] - STIFF * pen)
        v = own[3, c] + DT * live * found[1, c]
        x = own[0, c] + DT * live * u
        y = own[1, c] + DT * live * v
        rho = own[4, c] + DT * live * found[2, c]
        new.append([x, y, u, v, rho])
    return new


def tool_step(tool, force, scale):
    speed = tool[1:2] + DT * (1.0 - force * scale)
    return tool[0:1] + DT * speed, speed


def update_kernel(scale, place, own, found, marks, total, tool, new_own, new_tool, sent):
    first = origin(place, *own.shape[1:3])[2]
    new = moved_state(own, found, marks, tool[0:1], first)
    for c, fields in enumerate(new):
        for f in range(5):
            new_own[f, c] = fields[f]
    offset, speed = tool_step(tool, jnp.sum(total[...], axis=0), scale)
    new_tool[0:1] = offset
    new_tool[1:2] = speed
    fill_depth(place, new, marks, own_force(new, marks, offset, first), sent)


def last_kernel(near, place, own, found, marks, tool, force, sent):
    cols, rows, slots = own.shape[1:]
    size = 5 * cols * rows
    new = moved_state(own, found, marks, tool[0:1], origin(place, cols, rows)[2])
    sent[...] = jnp.zeros(sent.shape, F32)
    sent[:, size:, :] = jnp.broadcast_to(force[0:1], (near, sent.shape[1] - size, slots))
    digit = lax.rem(place[3 + place[0]], near)
    for f in range(5):
        for c in range(cols):
            at = (f * cols + c) * rows
            sent[digit, at : at + rows] = new[c][f]


def sort_kernel(near, size, place, got, sent):
    far, most, slots = sent.shape
    group, digit = lax.div(place[0], near), lax.rem(place[0], near)
    sent[...] = jnp.zeros(sent.shape, F32)
    total = jnp.sum(got[:, size : size + 1, :], axis=0, keepdims=True)
    sent[:, size:, :] = jnp.broadcast_to(total, (far, most - size, slots))
    for k in range(near):
        target = place[3 + group * near + k]

        @pl.when(lax.rem(target, near) == digit)
        def _():
            sent[lax.div(target, near), 0:size] = got[k, 0:size]


def take_kernel(near, scale, place, got, tool, out, new_tool):
    cols, rows, slots = out.shape[1:]
    size = 5 * cols * rows
    source = 0
    for k in range(got.shape[0] * near):
        source = jnp.where(place[3 + k] == place[0], k // near, source)
    for f in range(5):
        for c in range(cols):
            at = (f * cols + c) * rows
            out[f, c] = got[source, at : at + rows]
    offset, speed = tool_step(tool, jnp.sum(got[:, size : size + 1, :], axis=0), scale)
    new_tool[0] = offset[0, 0]
    new_tool[1] = speed[0, 0]


def body(positions, velocity, density, counts, contact_mask, destination, tool):
    cols, rows, slots = density.shape
    ncut, ndepth = lax.axis_size("cut"), lax.axis_size("depth")
    here, depth = lax.axis_index("cut"), lax.axis_index("depth")
    scale = 1.0 / (ncut * cols * ndepth * rows * slots)
    place = jnp.concatenate([jnp.stack([here, depth, jnp.int32(ncut)]).astype(jnp.int32), destination])
    near = 8 if ncut % 8 == 0 else 1
    far = ncut // near
    size = 5 * cols * rows
    tall = rows + 2
    state, block = shape(5, cols, rows, slots), shape(3, cols, rows, slots)
    message, vector = shape(ndepth, 16, slots), shape(2, slots)
    column = shape(5, tall, slots)
    sums = [pltpu.VMEM((cols * rows * 32, slots), F32)] * 2
    inner_scratch = [pltpu.VMEM((cols * rows * 32, slots), F32)] + sums
    outer_scratch = [pltpu.VMEM(((cols + 2) * tall * 32, slots), F32)] + sums
    forth = [(i, i + 1) for i in range(ncut - 1)]
    back = [(i + 1, i) for i in range(ncut - 1)]

    outs = [state, shape(2, cols, rows, slots), vector, message]
    own, marks, tool, sent = call(start_kernel, outs, (place, counts, contact_mask, tool), (positions, velocity, density))
    for step in range(STEPS):
        got = lax.all_to_all(sent, "depth", 0, 0, tiled=True)
        inner = call(inner_kernel, block, (place,), (own, marks), inner_scratch, COST)
        first = (inner,) if step < STEPS - 1 else ()
        left, right, force = call(extend_kernel, [column, column, shape(ncut, 1, slots)], (place,), (own, marks, got) + first)
        before = lax.ppermute(right, "cut", forth)
        after = lax.ppermute(left, "cut", back)
        if step < STEPS - 1:
            total = lax.all_to_all(force, "cut", 0, 0, tiled=True)
        found = call(outer_kernel, block, (place,), (before, left, right, after, inner), outer_scratch, COST)
        if step < STEPS - 1:
            kernel = functools.partial(update_kernel, scale)
            own, tool, sent = call(kernel, [state, vector, message], (place,), (own, found, marks, total, tool))
    kernel = functools.partial(last_kernel, near)
    sent = call(kernel, shape(near, size + 8, slots), (place,), (own, found, marks, tool, force[:, 0]))
    close = [[g * near + k for k in range(near)] for g in range(far)]
    apart = [[g * near + k for g in range(far)] for k in range(near)]
    got = lax.all_to_all(sent, "cut", 0, 0, tiled=True, axis_index_groups=close)
    sent = call(functools.partial(sort_kernel, near, size), shape(far, size + 8, slots), (place,), (got,))
    got = lax.all_to_all(sent, "cut", 0, 0, tiled=True, axis_index_groups=apart)
    return pl.pallas_call(
        functools.partial(take_kernel, near, scale),
        out_shape=[state, shape(2)],
        in_specs=[SMEM, VMEM, VMEM],
        out_specs=[VMEM, SMEM],
        compiler_params=PARAMS,
    )(place, got, tool)


def solution(mesh):
    return jax.shard_map(
        body,
        mesh=mesh,
        in_specs=(
            P(None, "cut", "depth", None),
            P(None, "cut", "depth", None),
            P("cut", "depth", None),
            P("cut", "depth"),
            P("cut", "depth"),
            P(),
            P(),
        ),
        out_specs=(P(None, "cut", "depth", None), P()),
        check_vma=False,
    )
```

time: 199 us -> 195 us (0.980)
  blocking collectives: 71.5 us -> 46.2 us
  waiting for transfers between devices: 24.6 us -> 47.8 us
  starting transfers between devices: 73.1 us -> 66.4 us
  Pallas kernels: 24.5 us -> 29.5 us
    all_to_all x3, waiting for transfers between devices: 0.01 us -> 29.8 us  [body(): total = lax.all_to_all(force, 'cut', 0, 0, tiled=True)]
    all_to_all x3 -> x1, blocking collectives: 31.7 us -> 10.6 us  [body(): got = lax.all_to_all(sent, 'depth', 0, 0, tiled=True)]
    ppermute x4, waiting for transfers between devices: 16.5 us -> 1.61 us  [body(): after = lax.ppermute(left, 'cut', back)]
    all_to_all x3, starting transfers between devices: 43.5 us -> 29.2 us  [body(): total = lax.all_to_all(force, 'cut', 0, 0, tiled=True)]
    all_to_all x1 -> x3, waiting for transfers between devices: 7.95 us -> 16.4 us  [body(): got = lax.all_to_all(sent, 'depth', 0, 0, tiled=True)]
    all_to_all x1 -> x3, starting transfers between devices: 6.14 us -> 13.2 us  [body(): got = lax.all_to_all(sent, 'depth', 0, 0, tiled=True)]
    all_to_all x1, blocking collectives: 17.9 us -> 13.6 us  [body(): got = lax.all_to_all(sent, 'cut', 0, 0, tiled=True, axis_index_groups=close)]
    pallas_call x15 -> x18, Pallas kernels: 24.5 us -> 28.3 us  [call(): pl.pallas_call(kernel, out_shape=outs, in_specs=[SMEM] * len(scalars) + [...]
  transfers between devices with their start and end apart: 12 -> 14, of which waited for: 7 -> 7; matrix products, arithmetic and copies ran while one was open for 0% -> 0% of each run, Pallas kernels for 6% -> 8%
where the time goes in v3:
time: 195 us; the launch traced here: 194 us
  starting transfers between devices  66.4 us (34%)
  waiting for transfers between devices  47.8 us (25%)
  blocking collectives  46.2 us (24%)
  Pallas kernels  29.5 us (15%)
  local copies, waits for them, and re-layouts  2.1 us (1%)
    all_to_all x3, waiting for transfers between devices, body(): total = lax.all_to_all(force, 'cut', 0, 0, tiled=True)  29.8 us
    all_to_all x3, starting transfers between devices, body(): total = lax.all_to_all(force, 'cut', 0, 0, tiled=True)  29.2 us
    pallas_call x18, Pallas kernels, call(): pl.pallas_call(kernel, out_shape=outs, in_specs=[SMEM] * len(scalars) + [...  28.3 us
    all_to_all x1, blocking collectives, body(): got = lax.all_to_all(sent, 'cut', 0, 0, tiled=True, axis_index_groups=apart)  21.9 us
    all_to_all x3, waiting for transfers between devices, body(): got = lax.all_to_all(sent, 'depth', 0, 0, tiled=True)  16.4 us
    ppermute x4, starting transfers between devices, body(): before = lax.ppermute(right, 'cut', forth)  14 us
    all_to_all x1, blocking collectives, body(): got = lax.all_to_all(sent, 'cut', 0, 0, tiled=True, axis_index_groups=close)  13.6 us
    all_to_all x3, starting transfers between devices, body(): got = lax.all_to_all(sent, 'depth', 0, 0, tiled=True)  13.2 us
  transfers between devices with their start and end apart: 14, of which 7 were waited for; matrix products, arithmetic and copies ran while one was open for 0% of the time, Pallas kernels for 8%

profile of v3, /device:TPU:8, one launch (start us, length us, event | category | flops | bytes accessed | tf_op | source)
XLA Modules:
  0.0 193.7 jit_solution(10901850669639161270)
XLA Ops:
  0.7 0.7 pad_add_fusion.place
  1.4 0.0 copy-start.1
  1.4 0.7 copy-done.1
  2.1 0.7 copy-done.2
  2.8 0.7 copy-done.4
  3.5 1.3 shard_map.86
  4.9 6.1 %all-to-all-start = ((f32[16,16,128]{2,1,0:T(8,128)}), f32[16,16,128]{2,1,0:T(8,128)S(1)}, u32[]{:S(2)}, u32[]{:S(2)}) async-start(f32[16,16,128]{2,1,0:T(8,128)} %get-tuple-element.29), calls=%async_computation | async-start | bytes 262144 | tf_op jit(solution)/shard_map/all_to_all | solution.py:307
  11.0 2.5 %shard_map.87.refs_0_.earlier = f32[3,2,8,128]{3,2,1,0:T(8,128)S(1)} custom-call(s32[35]{0:T(128)S(1)} %pad_add_fusion.place, f32[5,2,8,128]{3,2,1,0:T(8,128)S(1)} %get-tuple-element.27.own, f32[2,2,8,128]{3,2,1,0:T(8,128)S(1)} %get-tuple-element.28.marks), custom_call_target="tpu_custom_call" | custom-call | flops 20000000000 | bytes 1048576 | tf_op jit(solution)/shard_map/pallas_call | solution.py:33
  13.5 5.5 %all-to-all-done.got = f32[16,16,128]{2,1,0:T(8,128)S(1)} async-done(((f32[16,16,128]{2,1,0:T(8,128)}), f32[16,16,128]{2,1,0:T(8,128)S(1)}, u32[]{:S(2)}, u32[]{:S(2)}) %all-to-all-start) | async-done | bytes 131104 | tf_op jit(solution)/shard_map/all_to_all | solution.py:307
  19.0 1.2 shard_map.88
  20.1 4.6 %collective-permute-start = (f32[5,10,128]{2,1,0:T(8,128)S(1)}, f32[5,10,128]{2,1,0:T(8,128)S(1)}, u32[]{:S(2)}, u32[]{:S(2)}) collective-permute-start(f32[5,10,128]{2,1,0:T(8,128)S(1)} %get-tuple-element.30.right), channel_id=1, source_target_pairs={{0,16},{16,32},{32,48},{48,64},{64,80},{80,96},{96,112},{112,128},... | collective-permute-start | bytes 76808 | tf_op jit(solution)/shard_map/ppermute | solution.py:311
  24.7 1.9 collective-permute-start.1
  26.7 18.0 %all-to-all-start.1 = ((f32[32,1,128]{2,1,0:T(1,128)}), f32[32,1,128]{2,1,0:T(1,128)S(1)}, u32[]{:S(2)}, u32[]{:S(2)}) async-start(f32[32,1,128]{2,1,0:T(1,128)} %get-tuple-element.32), calls=%async_computation.1 | async-start | bytes 32768 | tf_op jit(solution)/shard_map/all_to_all | solution.py:314
  44.7 2.1 %shard_map.89.found = f32[3,2,8,128]{3,2,1,0:T(8,128)S(1)} custom-call(s32[35]{0:T(128)S(1)} %pad_add_fusion.place, f32[5,10,128]{2,1,0:T(8,128)S(1)} %collective-permute-done.before, f32[5,10,128]{2,1,0:T(8,128)S(1)} %get-tuple-element.31.left, f32[5,10,128]{2,1,0:T(8,128)S(1)} %get-tuple-element.30.right, f32[5,10,128]{2,1,0:T(8,128)S(1)} %collective-permute-done.1.after, ...), custom_call_target="tpu_custom_call" | custom-call | flops 20000000000 | bytes 1048576 | tf_op jit(solution)/shard_map/pallas_call | solution.py:33
  46.8 9.9 %all-to-all-done.1.total = f32[32,1,128]{2,1,0:T(1,128)S(1)} async-done(((f32[32,1,128]{2,1,0:T(1,128)}), f32[32,1,128]{2,1,0:T(1,128)S(1)}, u32[]{:S(2)}, u32[]{:S(2)}) %all-to-all-start.1) | async-done | bytes 16416 | tf_op jit(solution)/shard_map/all_to_all | solution.py:314
  56.8 1.3 shard_map.90
  58.1 3.5 %all-to-all-start.2 = ((f32[16,16,128]{2,1,0:T(8,128)}), f32[16,16,128]{2,1,0:T(8,128)S(1)}, u32[]{:S(2)}, u32[]{:S(2)}) async-start(f32[16,16,128]{2,1,0:T(8,128)} %get-tuple-element.35), calls=%async_computation.2 | async-start | bytes 262144 | tf_op jit(solution)/shard_map/all_to_all | solution.py:307
  61.6 2.5 %shard_map.91.refs_0_.earlier = f32[3,2,8,128]{3,2,1,0:T(8,128)S(1)} custom-call(s32[35]{0:T(128)S(1)} %pad_add_fusion.place, f32[5,2,8,128]{3,2,1,0:T(8,128)S(1)} %get-tuple-element.34.own, f32[2,2,8,128]{3,2,1,0:T(8,128)S(1)} %get-tuple-element.28.marks), custom_call_target="tpu_custom_call" | custom-call | flops 20000000000 | bytes 1048576 | tf_op jit(solution)/shard_map/pallas_call | solution.py:33
  64.1 5.5 %all-to-all-done.2.got = f32[16,16,128]{2,1,0:T(8,128)S(1)} async-done(((f32[16,16,128]{2,1,0:T(8,128)}), f32[16,16,128]{2,1,0:T(8,128)S(1)}, u32[]{:S(2)}, u32[]{:S(2)}) %all-to-all-start.2) | async-done | bytes 131104 | tf_op jit(solution)/shard_map/all_to_all | solution.py:307
  69.6 1.2 shard_map.92
  70.7 3.1 %collective-permute-start.2 = (f32[5,10,128]{2,1,0:T(8,128)S(1)}, f32[5,10,128]{2,1,0:T(8,128)S(1)}, u32[]{:S(2)}, u32[]{:S(2)}) collective-permute-start(f32[5,10,128]{2,1,0:T(8,128)S(1)} %get-tuple-element.36.right), channel_id=1, source_target_pairs={{0,16},{16,32},{32,48},{48,64},{64,80},{80,96},{96,112},{112,128},... | collective-permute-start | bytes 76808 | tf_op jit(solution)/shard_map/ppermute | solution.py:311
  73.9 2.7 %collective-permute-start.3 = (f32[5,10,128]{2,1,0:T(8,128)S(1)}, f32[5,10,128]{2,1,0:T(8,128)S(1)}, u32[]{:S(2)}, u32[]{:S(2)}) collective-permute-start(f32[5,10,128]{2,1,0:T(8,128)S(1)} %get-tuple-element.37.left), channel_id=1, source_target_pairs={{16,0},{32,16},{48,32},{64,48},{80,64},{96,80},{112,96},{128,112},... | collective-permute-start | bytes 76808 | tf_op jit(solution)/shard_map/ppermute | solution.py:312
  76.6 5.6 %all-to-all-start.3 = ((f32[32,1,128]{2,1,0:T(1,128)}), f32[32,1,128]{2,1,0:T(1,128)S(1)}, u32[]{:S(2)}, u32[]{:S(2)}) async-start(f32[32,1,128]{2,1,0:T(1,128)} %get-tuple-element.38), calls=%async_computation.3 | async-start | bytes 32768 | tf_op jit(solution)/shard_map/all_to_all | solution.py:314
  82.2 2.1 %shard_map.93.found = f32[3,2,8,128]{3,2,1,0:T(8,128)S(1)} custom-call(s32[35]{0:T(128)S(1)} %pad_add_fusion.place, f32[5,10,128]{2,1,0:T(8,128)S(1)} %collective-permute-done.2.before, f32[5,10,128]{2,1,0:T(8,128)S(1)} %get-tuple-element.37.left, f32[5,10,128]{2,1,0:T(8,128)S(1)} %get-tuple-element.36.right, ...), custom_call_target="tpu_custom_call" | custom-call | flops 20000000000 | bytes 1048576 | tf_op jit(solution)/shard_map/pallas_call | solution.py:33
  84.3 9.9 %all-to-all-done.3.total = f32[32,1,128]{2,1,0:T(1,128)S(1)} async-done(((f32[32,1,128]{2,1,0:T(1,128)}), f32[32,1,128]{2,1,0:T(1,128)S(1)}, u32[]{:S(2)}, u32[]{:S(2)}) %all-to-all-start.3) | async-done | bytes 16416 | tf_op jit(solution)/shard_map/all_to_all | solution.py:314
  94.2 1.3 shard_map.94
  95.6 3.5 %all-to-all-start.4 = ((f32[16,16,128]{2,1,0:T(8,128)}), f32[16,16,128]{2,1,0:T(8,128)S(1)}, u32[]{:S(2)}, u32[]{:S(2)}) async-start(f32[16,16,128]{2,1,0:T(8,128)} %get-tuple-element.41), calls=%async_computation.4 | async-start | bytes 262144 | tf_op jit(solution)/shard_map/all_to_all | solution.py:307
  99.1 2.5 %shard_map.95.refs_0_.earlier = f32[3,2,8,128]{3,2,1,0:T(8,128)S(1)} custom-call(s32[35]{0:T(128)S(1)} %pad_add_fusion.place, f32[5,2,8,128]{3,2,1,0:T(8,128)S(1)} %get-tuple-element.40.own, f32[2,2,8,128]{3,2,1,0:T(8,128)S(1)} %get-tuple-element.28.marks), custom_call_target="tpu_custom_call" | custom-call | flops 20000000000 | bytes 1048576 | tf_op jit(solution)/shard_map/pallas_call | solution.py:33
  101.6 5.5 %all-to-all-done.4.got = f32[16,16,128]{2,1,0:T(8,128)S(1)} async-done(((f32[16,16,128]{2,1,0:T(8,128)}), f32[16,16,128]{2,1,0:T(8,128)S(1)}, u32[]{:S(2)}, u32[]{:S(2)}) %all-to-all-start.4) | async-done | bytes 131104 | tf_op jit(solution)/shard_map/all_to_all | solution.py:307
  107.0 1.2 shard_map.96
  108.2 3.1 %collective-permute-start.4 = (f32[5,10,128]{2,1,0:T(8,128)S(1)}, f32[5,10,128]{2,1,0:T(8,128)S(1)}, u32[]{:S(2)}, u32[]{:S(2)}) collective-permute-start(f32[5,10,128]{2,1,0:T(8,128)S(1)} %get-tuple-element.42.right), channel_id=1, source_target_pairs={{0,16},{16,32},{32,48},{48,64},{64,80},{80,96},{96,112},{112,128},... | collective-permute-start | bytes 76808 | tf_op jit(solution)/shard_map/ppermute | solution.py:311
  111.4 2.7 %collective-permute-start.5 = (f32[5,10,128]{2,1,0:T(8,128)S(1)}, f32[5,10,128]{2,1,0:T(8,128)S(1)}, u32[]{:S(2)}, u32[]{:S(2)}) collective-permute-start(f32[5,10,128]{2,1,0:T(8,128)S(1)} %get-tuple-element.43.left), channel_id=1, source_target_pairs={{16,0},{32,16},{48,32},{64,48},{80,64},{96,80},{112,96},{128,112},... | collective-permute-start | bytes 76808 | tf_op jit(solution)/shard_map/ppermute | solution.py:312
  114.1 5.6 %all-to-all-start.5 = ((f32[32,1,128]{2,1,0:T(1,128)}), f32[32,1,128]{2,1,0:T(1,128)S(1)}, u32[]{:S(2)}, u32[]{:S(2)}) async-start(f32[32,1,128]{2,1,0:T(1,128)} %get-tuple-element.44), calls=%async_computation.5 | async-start | bytes 32768 | tf_op jit(solution)/shard_map/all_to_all | solution.py:314
  119.7 2.1 %shard_map.97.found = f32[3,2,8,128]{3,2,1,0:T(8,128)S(1)} custom-call(s32[35]{0:T(128)S(1)} %pad_add_fusion.place, f32[5,10,128]{2,1,0:T(8,128)S(1)} %collective-permute-done.4.before, f32[5,10,128]{2,1,0:T(8,128)S(1)} %get-tuple-element.43.left, f32[5,10,128]{2,1,0:T(8,128)S(1)} %get-tuple-element.42.right, ...), custom_call_target="tpu_custom_call" | custom-call | flops 20000000000 | bytes 1048576 | tf_op jit(solution)/shard_map/pallas_call | solution.py:33
  121.8 9.9 %all-to-all-done.5.total = f32[32,1,128]{2,1,0:T(1,128)S(1)} async-done(((f32[32,1,128]{2,1,0:T(1,128)}), f32[32,1,128]{2,1,0:T(1,128)S(1)}, u32[]{:S(2)}, u32[]{:S(2)}) %all-to-all-start.5) | async-done | bytes 16416 | tf_op jit(solution)/shard_map/all_to_all | solution.py:314
  131.7 0.7 shard_map.98
  132.4 10.6 %all_to_all.45.got = f32[16,16,128]{2,1,0:T(8,128)S(1)} all-to-all(f32[16,16,128]{2,1,0:T(8,128)S(1)} %get-tuple-element.47), channel_id=1, replica_groups=mesh['cut'=32,'depth'=16] {'depth'}, dimensions={0} | all-to-all | bytes 262144 | tf_op jit(solution)/shard_map/all_to_all | solution.py:307
  142.9 0.6 shard_map.99
  143.5 3.1 %collective-permute-start.6 = (f32[5,10,128]{2,1,0:T(8,128)S(1)}, f32[5,10,128]{2,1,0:T(8,128)S(1)}, u32[]{:S(2)}, u32[]{:S(2)}) collective-permute-start(f32[5,10,128]{2,1,0:T(8,128)S(1)} %get-tuple-element.48.right), channel_id=1, source_target_pairs={{0,16},{16,32},{32,48},{48,64},{64,80},{80,96},{96,112},{112,128},... | collective-permute-start | bytes 76808 | tf_op jit(solution)/shard_map/ppermute | solution.py:311
  146.7 2.7 %collective-permute-start.7 = (f32[5,10,128]{2,1,0:T(8,128)S(1)}, f32[5,10,128]{2,1,0:T(8,128)S(1)}, u32[]{:S(2)}, u32[]{:S(2)}) collective-permute-start(f32[5,10,128]{2,1,0:T(8,128)S(1)} %get-tuple-element.49.left), channel_id=1, source_target_pairs={{16,0},{32,16},{48,32},{64,48},{80,64},{96,80},{112,96},{128,112},... | collective-permute-start | bytes 76808 | tf_op jit(solution)/shard_map/ppermute | solution.py:312
  149.4 2.5 %shard_map.100.earlier = f32[3,2,8,128]{3,2,1,0:T(8,128)S(1)} custom-call(s32[35]{0:T(128)S(1)} %pad_add_fusion.place, f32[5,2,8,128]{3,2,1,0:T(8,128)S(1)} %get-tuple-element.46.own, f32[2,2,8,128]{3,2,1,0:T(8,128)S(1)} %get-tuple-element.28.marks), custom_call_target="tpu_custom_call" | custom-call | flops 20000000000 | bytes 1048576 | tf_op jit(solution)/shard_map/pallas_call | solution.py:33
  151.9 1.6 collective-permute-done.7.after
  153.5 2.1 %shard_map.101.found = f32[3,2,8,128]{3,2,1,0:T(8,128)S(1)} custom-call(s32[35]{0:T(128)S(1)} %pad_add_fusion.place, f32[5,10,128]{2,1,0:T(8,128)S(1)} %collective-permute-done.6.before, f32[5,10,128]{2,1,0:T(8,128)S(1)} %get-tuple-element.49.left, f32[5,10,128]{2,1,0:T(8,128)S(1)} %get-tuple-element.48.right, ...), custom_call_target="tpu_custom_call" | custom-call | flops 20000000000 | bytes 1048576 | tf_op jit(solution)/shard_map/pallas_call | solution.py:33
  155.6 0.6 shard_map.102
  156.2 13.6 %all_to_all.46.got = f32[8,88,128]{2,1,0:T(8,128)S(1)} all-to-all(f32[8,88,128]{2,1,0:T(8,128)S(1)} %shard_map.102), channel_id=1, replica_groups={{0,16,32,48,64,80,96,112},{128,144,160,176,192,208,224,240},{256,272,28..., dimensions={0} | all-to-all | bytes 720896 | tf_op jit(solution)/shard_map/all_to_all | solution.py:323
  169.8 0.6 shard_map.103
  170.4 21.9 %all_to_all.47.got = f32[4,88,128]{2,1,0:T(8,128)S(1)} all-to-all(f32[4,88,128]{2,1,0:T(8,128)S(1)} %shard_map.103), channel_id=1, replica_groups={{0,128,256,384},{16,144,272,400},{32,160,288,416},{48,176,304,432},{64,..., dimensions={0} | all-to-all | bytes 360448 | tf_op jit(solution)/shard_map/all_to_all | solution.py:325
  192.4 1.2 shard_map.104
  (15 shorter events, 0.0 us)
Async XLA Ops:
  0.6 0.8 copy-start
  0.6 0.8 copy-start.3
  0.7 0.8 copy-start.5
  1.4 0.7 copy-start.1
  2.1 0.7 copy-start.2
  2.8 0.7 copy-start.4
  4.9 14.1 %all-to-all-start = ((f32[16,16,128]{2,1,0:T(8,128)}), f32[16,16,128]{2,1,0:T(8,128)S(1)}, u32[]{:S(2)}, u32[]{:S(2)}) async-start(f32[16,16,128]{2,1,0:T(8,128)} %get-tuple-element.29), calls=%async_computation | async-start | bytes 262144 | tf_op jit(solution)/shard_map/all_to_all | solution.py:307
  20.1 24.6 %collective-permute-start = (f32[5,10,128]{2,1,0:T(8,128)S(1)}, f32[5,10,128]{2,1,0:T(8,128)S(1)}, u32[]{:S(2)}, u32[]{:S(2)}) collective-permute-start(f32[5,10,128]{2,1,0:T(8,128)S(1)} %get-tuple-element.30.right), channel_id=1, source_target_pairs={{0,16},{16,32},{32,48},{48,64},{64,80},{80,96},{96,112},{112,128},... | collective-permute-start | bytes 76808 | tf_op jit(solution)/shard_map/ppermute | solution.py:311
  24.7 20.0 %collective-permute-start.1 = (f32[5,10,128]{2,1,0:T(8,128)S(1)}, f32[5,10,128]{2,1,0:T(8,128)S(1)}, u32[]{:S(2)}, u32[]{:S(2)}) collective-permute-start(f32[5,10,128]{2,1,0:T(8,128)S(1)} %get-tuple-element.31.left), channel_id=1, source_target_pairs={{16,0},{32,16},{48,32},{64,48},{80,64},{96,80},{112,96},{128,112},... | collective-permute-start | bytes 76808 | tf_op jit(solution)/shard_map/ppermute | solution.py:312
  26.7 30.1 %all-to-all-start.1 = ((f32[32,1,128]{2,1,0:T(1,128)}), f32[32,1,128]{2,1,0:T(1,128)S(1)}, u32[]{:S(2)}, u32[]{:S(2)}) async-start(f32[32,1,128]{2,1,0:T(1,128)} %get-tuple-element.32), calls=%async_computation.1 | async-start | bytes 32768 | tf_op jit(solution)/shard_map/all_to_all | solution.py:314
  58.1 11.5 %all-to-all-start.2 = ((f32[16,16,128]{2,1,0:T(8,128)}), f32[16,16,128]{2,1,0:T(8,128)S(1)}, u32[]{:S(2)}, u32[]{:S(2)}) async-start(f32[16,16,128]{2,1,0:T(8,128)} %get-tuple-element.35), calls=%async_computation.2 | async-start | bytes 262144 | tf_op jit(solution)/shard_map/all_to_all | solution.py:307
  70.7 11.4 %collective-permute-start.2 = (f32[5,10,128]{2,1,0:T(8,128)S(1)}, f32[5,10,128]{2,1,0:T(8,128)S(1)}, u32[]{:S(2)}, u32[]{:S(2)}) collective-permute-start(f32[5,10,128]{2,1,0:T(8,128)S(1)} %get-tuple-element.36.right), channel_id=1, source_target_pairs={{0,16},{16,32},{32,48},{48,64},{64,80},{80,96},{96,112},{112,128},... | collective-permute-start | bytes 76808 | tf_op jit(solution)/shard_map/ppermute | solution.py:311
  73.9 8.3 %collective-permute-start.3 = (f32[5,10,128]{2,1,0:T(8,128)S(1)}, f32[5,10,128]{2,1,0:T(8,128)S(1)}, u32[]{:S(2)}, u32[]{:S(2)}) collective-permute-start(f32[5,10,128]{2,1,0:T(8,128)S(1)} %get-tuple-element.37.left), channel_id=1, source_target_pairs={{16,0},{32,16},{48,32},{64,48},{80,64},{96,80},{112,96},{128,112},... | collective-permute-start | bytes 76808 | tf_op jit(solution)/shard_map/ppermute | solution.py:312
  76.6 17.6 %all-to-all-start.3 = ((f32[32,1,128]{2,1,0:T(1,128)}), f32[32,1,128]{2,1,0:T(1,128)S(1)}, u32[]{:S(2)}, u32[]{:S(2)}) async-start(f32[32,1,128]{2,1,0:T(1,128)} %get-tuple-element.38), calls=%async_computation.3 | async-start | bytes 32768 | tf_op jit(solution)/shard_map/all_to_all | solution.py:314
  95.6 11.5 %all-to-all-start.4 = ((f32[16,16,128]{2,1,0:T(8,128)}), f32[16,16,128]{2,1,0:T(8,128)S(1)}, u32[]{:S(2)}, u32[]{:S(2)}) async-start(f32[16,16,128]{2,1,0:T(8,128)} %get-tuple-element.41), calls=%async_computation.4 | async-start | bytes 262144 | tf_op jit(solution)/shard_map/all_to_all | solution.py:307
  108.2 11.4 %collective-permute-start.4 = (f32[5,10,128]{2,1,0:T(8,128)S(1)}, f32[5,10,128]{2,1,0:T(8,128)S(1)}, u32[]{:S(2)}, u32[]{:S(2)}) collective-permute-start(f32[5,10,128]{2,1,0:T(8,128)S(1)} %get-tuple-element.42.right), channel_id=1, source_target_pairs={{0,16},{16,32},{32,48},{48,64},{64,80},{80,96},{96,112},{112,128},... | collective-permute-start | bytes 76808 | tf_op jit(solution)/shard_map/ppermute | solution.py:311
  111.4 8.3 %collective-permute-start.5 = (f32[5,10,128]{2,1,0:T(8,128)S(1)}, f32[5,10,128]{2,1,0:T(8,128)S(1)}, u32[]{:S(2)}, u32[]{:S(2)}) collective-permute-start(f32[5,10,128]{2,1,0:T(8,128)S(1)} %get-tuple-element.43.left), channel_id=1, source_target_pairs={{16,0},{32,16},{48,32},{64,48},{80,64},{96,80},{112,96},{128,112},... | collective-permute-start | bytes 76808 | tf_op jit(solution)/shard_map/ppermute | solution.py:312
  114.1 17.6 %all-to-all-start.5 = ((f32[32,1,128]{2,1,0:T(1,128)}), f32[32,1,128]{2,1,0:T(1,128)S(1)}, u32[]{:S(2)}, u32[]{:S(2)}) async-start(f32[32,1,128]{2,1,0:T(1,128)} %get-tuple-element.44), calls=%async_computation.5 | async-start | bytes 32768 | tf_op jit(solution)/shard_map/all_to_all | solution.py:314
  143.5 8.3 %collective-permute-start.6 = (f32[5,10,128]{2,1,0:T(8,128)S(1)}, f32[5,10,128]{2,1,0:T(8,128)S(1)}, u32[]{:S(2)}, u32[]{:S(2)}) collective-permute-start(f32[5,10,128]{2,1,0:T(8,128)S(1)} %get-tuple-element.48.right), channel_id=1, source_target_pairs={{0,16},{16,32},{32,48},{48,64},{64,80},{80,96},{96,112},{112,128},... | collective-permute-start | bytes 76808 | tf_op jit(solution)/shard_map/ppermute | solution.py:311
  146.7 6.8 %collective-permute-start.7 = (f32[5,10,128]{2,1,0:T(8,128)S(1)}, f32[5,10,128]{2,1,0:T(8,128)S(1)}, u32[]{:S(2)}, u32[]{:S(2)}) collective-permute-start(f32[5,10,128]{2,1,0:T(8,128)S(1)} %get-tuple-element.49.left), channel_id=1, source_target_pairs={{16,0},{32,16},{48,32},{64,48},{80,64},{96,80},{112,96},{128,112},... | collective-permute-start | bytes 76808 | tf_op jit(solution)/shard_map/ppermute | solution.py:312

commit v4 on v3

--- a/solution.py
+++ b/solution.py
@@ -16,7 +16,7 @@
 
 FAR = 1.0e6
 
-COST = 20_000_000_000
+COST = 100_000_000
 
 F32 = jnp.float32
 BF16 = jnp.bfloat16
@@ -68,7 +68,8 @@
     depth, ndepth = place[1], sent.shape[0]
     cols, rows = marks.shape[1:3]
     sent[...] = jnp.zeros(sent.shape, F32)
-    sent[:, 5 * cols : 5 * cols + 1, :] = jnp.broadcast_to(force[None], (ndepth, 1, force.shape[1]))
+    if force is not None:
+        sent[:, 5 * cols : 5 * cols + 1, :] = jnp.broadcast_to(force[None], (ndepth, 1, force.shape[1]))
     seen = [visible(new[c], marks[0, c]) for c in range(cols)]
 
     @pl.when(depth > 0)
@@ -89,7 +90,7 @@
     return first + 0.5 * cols, (place[1] * rows).astype(F32) + 0.5 * rows, first
 
 
-def start_kernel(place, counts, contact, first_tool, positions, velocity, density, own, marks, tool, sent):
+def start_kernel(place, counts, contact, first_tool, positions, velocity, density, own, marks, tool, sent, force):
     cols, rows, slots = density.shape
     row = lax.broadcasted_iota(jnp.int32, (rows, slots), 0)
     slot = lax.broadcasted_iota(jnp.int32, (rows, slots), 1)
@@ -108,11 +109,12 @@
     offset = jnp.zeros((1, slots), F32) + first_tool[0]
     tool[0:1] = offset
     tool[1:2] = jnp.zeros((1, slots), F32) + first_tool[1]
-    fill_depth(place, new, marks, own_force(new, marks, offset, origin(place, cols, rows)[2]), sent)
-
-
-def extend_kernel(place, own, marks, got, *refs):
-    left, right, force = refs[-3:]
+    part = own_force(new, marks, offset, origin(place, cols, rows)[2])
+    force[...] = jnp.broadcast_to(part[None], force.shape)
+    fill_depth(place, new, marks, None, sent)
+
+
+def extend(place, own, marks, got, left, right):
     depth, ndepth = place[1], got.shape[0]
     cols, rows = own.shape[1:3]
     above = got[jnp.maximum(depth - 1, 0)]
@@ -125,8 +127,22 @@
             column[f, 0:1] = jnp.where(depth > 0, above[k : k + 1], blank[f])
             column[f, 1 : rows + 1] = seen[f]
             column[f, rows + 1 : rows + 2] = jnp.where(depth < ndepth - 1, below[k : k + 1], blank[f])
-    total = jnp.sum(got[:, 5 * cols : 5 * cols + 1, :], axis=0)
-    force[...] = jnp.broadcast_to(total[None], force.shape)
+
+
+def first_extend_kernel(place, own, marks, got, inner, left, right):
+    extend(place, own, marks, got, left, right)
+
+
+def extend_kernel(scale, place, own, marks, got, inner, tool, left, right, new_tool, force):
+    cols, rows = own.shape[1:3]
+    row = 5 * cols
+    offset, speed = tool_step(tool, jnp.sum(got[:, row : row + 1, :], axis=0), scale)
+    new_tool[0:1] = offset
+    new_tool[1:2] = speed
+    state = [[own[f, c] for f in range(5)] for c in range(cols)]
+    part = own_force(state, marks, offset, origin(place, cols, rows)[2])
+    force[...] = jnp.broadcast_to(part[None], force.shape)
+    extend(place, own, marks, got, left, right)
 
 
 def pair_sums(columns, center, pairs, out, feat, acc2, acc3, earlier=None):
@@ -228,24 +244,20 @@
     return tool[0:1] + DT * speed, speed
 
 
-def update_kernel(scale, place, own, found, marks, total, tool, new_own, new_tool, sent):
-    first = origin(place, *own.shape[1:3])[2]
-    new = moved_state(own, found, marks, tool[0:1], first)
+def update_kernel(place, own, found, marks, tool, total, new_own, sent):
+    new = moved_state(own, found, marks, tool[0:1], origin(place, *own.shape[1:3])[2])
     for c, fields in enumerate(new):
         for f in range(5):
             new_own[f, c] = fields[f]
-    offset, speed = tool_step(tool, jnp.sum(total[...], axis=0), scale)
-    new_tool[0:1] = offset
-    new_tool[1:2] = speed
-    fill_depth(place, new, marks, own_force(new, marks, offset, first), sent)
-
-
-def last_kernel(near, place, own, found, marks, tool, force, sent):
+    fill_depth(place, new, marks, jnp.sum(total[...], axis=0), sent)
+
+
+def last_kernel(near, place, own, found, marks, tool, total, sent):
     cols, rows, slots = own.shape[1:]
     size = 5 * cols * rows
     new = moved_state(own, found, marks, tool[0:1], origin(place, cols, rows)[2])
     sent[...] = jnp.zeros(sent.shape, F32)
-    sent[:, size:, :] = jnp.broadcast_to(force[0:1], (near, sent.shape[1] - size, slots))
+    sent[:, size:, :] = jnp.broadcast_to(jnp.sum(total[...], axis=0, keepdims=True), (near, sent.shape[1] - size, slots))
     digit = lax.rem(place[3 + place[0]], near)
     for f in range(5):
         for c in range(cols):
@@ -301,23 +313,26 @@
     forth = [(i, i + 1) for i in range(ncut - 1)]
     back = [(i + 1, i) for i in range(ncut - 1)]
 
-    outs = [state, shape(2, cols, rows, slots), vector, message]
-    own, marks, tool, sent = call(start_kernel, outs, (place, counts, contact_mask, tool), (positions, velocity, density))
+    whole = [place]
+    outs = [state, shape(2, cols, rows, slots), vector, message, shape(ncut, 1, slots)]
+    own, marks, tool, sent, force = call(start_kernel, outs, (place, counts, contact_mask, tool), (positions, velocity, density))
     for step in range(STEPS):
         got = lax.all_to_all(sent, "depth", 0, 0, tiled=True)
-        inner = call(inner_kernel, block, (place,), (own, marks), inner_scratch, COST)
-        first = (inner,) if step < STEPS - 1 else ()
-        left, right, force = call(extend_kernel, [column, column, shape(ncut, 1, slots)], (place,), (own, marks, got) + first)
+        inner = call(inner_kernel, block, whole, (own, marks), inner_scratch, COST)
+        if step == 0:
+            left, right = call(first_extend_kernel, [column, column], whole, (own, marks, got, inner))
+        else:
+            kernel = functools.partial(extend_kernel, scale)
+            outs = [column, column, vector, shape(ncut if step < STEPS - 1 else ndepth, 1, slots)]
+            left, right, tool, force = call(kernel, outs, whole, (own, marks, got, inner, tool))
         before = lax.ppermute(right, "cut", forth)
         after = lax.ppermute(left, "cut", back)
+        total = lax.all_to_all(force, "cut" if step < STEPS - 1 else "depth", 0, 0, tiled=True)
+        found = call(outer_kernel, block, whole, (before, left, right, after, inner), outer_scratch, COST)
         if step < STEPS - 1:
-            total = lax.all_to_all(force, "cut", 0, 0, tiled=True)
-        found = call(outer_kernel, block, (place,), (before, left, right, after, inner), outer_scratch, COST)
-        if step < STEPS - 1:
-            kernel = functools.partial(update_kernel, scale)
-            own, tool, sent = call(kernel, [state, vector, message], (place,), (own, found, marks, total, tool))
+            own, sent = call(update_kernel, [state, message], whole, (own, found, marks, tool, total))
     kernel = functools.partial(last_kernel, near)
-    sent = call(kernel, shape(near, size + 8, slots), (place,), (own, found, marks, tool, force[:, 0]))
+    sent = call(kernel, shape(near, size + 8, slots), whole, (own, found, marks, tool, total))
     close = [[g * near + k for k in range(near)] for g in range(far)]
     apart = [[g * near + k for g in range(far)] for k in range(near)]
     got = lax.all_to_all(sent, "cut", 0, 0, tiled=True, axis_index_groups=close)

time: 195 us -> 207 us (1.062)
  starting transfers between devices: 66.4 us -> 81 us
  waiting for transfers between devices: 47.8 us -> 34.5 us
  blocking collectives: 46.2 us -> 56.8 us
    all_to_all x3 -> x4, waiting for transfers between devices: 29.8 us -> 4.92 us  [body(): lax.all_to_all(force, 'cut' if step < STEPS - 1 else 'depth', 0, 0, tiled...]
    all_to_all x3 -> x4, starting transfers between devices: 29.2 us -> 47 us  [body(): lax.all_to_all(force, 'cut' if step < STEPS - 1 else 'depth', 0, 0, tiled...]
    ppermute x4, waiting for transfers between devices: 1.61 us -> 13.1 us  [body(): after = lax.ppermute(left, 'cut', back)]
    all_to_all x1, blocking collectives: 13.6 us -> 18.6 us  [body(): got = lax.all_to_all(sent, 'cut', 0, 0, tiled=True, axis_index_groups=close)]
    all_to_all x1, blocking collectives: 10.6 us -> 13.9 us  [body(): got = lax.all_to_all(sent, 'depth', 0, 0, tiled=True)]
    all_to_all x3, starting transfers between devices: 13.2 us -> 10.5 us  [body(): got = lax.all_to_all(sent, 'depth', 0, 0, tiled=True)]
    all_to_all x1, blocking collectives: 21.9 us -> 24.2 us  [body(): got = lax.all_to_all(sent, 'cut', 0, 0, tiled=True, axis_index_groups=apart)]
  transfers between devices with their start and end apart: 14 -> 15, of which waited for: 7 -> 10; matrix products, arithmetic and copies ran while one was open for 0% -> 0% of each run, Pallas kernels for 8% -> 9%
where the time goes in v4:
time: 207 us; the launch traced here: 206 us
  starting transfers between devices  81 us (39%)
  blocking collectives  56.8 us (27%)
  waiting for transfers between devices  34.5 us (17%)
  Pallas kernels  30 us (14%)
  local copies, waits for them, and re-layouts  2.1 us (1%)
    all_to_all x4, starting transfers between devices, body(): lax.all_to_all(force, 'cut' if step < STEPS - 1 else 'depth', 0, 0, tiled...  47 us
    pallas_call x18, Pallas kernels, call(): pl.pallas_call(kernel, out_shape=outs, in_specs=[SMEM] * len(scalars) + [...  28.8 us
    all_to_all x1, blocking collectives, body(): got = lax.all_to_all(sent, 'cut', 0, 0, tiled=True, axis_index_groups=apart)  24.2 us
    all_to_all x1, blocking collectives, body(): got = lax.all_to_all(sent, 'cut', 0, 0, tiled=True, axis_index_groups=close)  18.6 us
    all_to_all x3, waiting for transfers between devices, body(): got = lax.all_to_all(sent, 'depth', 0, 0, tiled=True)  16.4 us
    all_to_all x1, blocking collectives, body(): got = lax.all_to_all(sent, 'depth', 0, 0, tiled=True)  13.9 us
    ppermute x4, waiting for transfers between devices, body(): after = lax.ppermute(left, 'cut', back)  13.1 us
    ppermute x4, starting transfers between devices, body(): before = lax.ppermute(right, 'cut', forth)  13.1 us
  transfers between devices with their start and end apart: 15, of which 10 were waited for; matrix products, arithmetic and copies ran while one was open for 0% of the time, Pallas kernels for 9%

profile of v4, /device:TPU:8, one launch (start us, length us, event | category | flops | bytes accessed | tf_op | source)
XLA Modules:
  0.0 206.2 jit_solution(335525811651290962)
XLA Ops:
  0.7 0.7 pad_add_fusion.place
  1.4 0.7 copy-done.1
  2.1 0.7 copy-done.2
  2.8 0.7 copy-done.4
  3.5 1.3 shard_map.86
  4.8 13.9 %all_to_all.50.got = f32[16,16,128]{2,1,0:T(8,128)S(1)} all-to-all(f32[16,16,128]{2,1,0:T(8,128)S(1)} %get-tuple-element.29), channel_id=1, replica_groups=mesh['cut'=32,'depth'=16] {'depth'}, dimensions={0} | all-to-all | bytes 262144 | tf_op jit(solution)/shard_map/all_to_all | solution.py:320
  18.7 16.7 %all-to-all-start.1 = ((f32[32,1,128]{2,1,0:T(1,128)}), f32[32,1,128]{2,1,0:T(1,128)S(1)}, u32[]{:S(2)}, u32[]{:S(2)}) async-start(f32[32,1,128]{2,1,0:T(1,128)} %get-tuple-element.33), calls=%async_computation.1 | async-start | bytes 32768 | tf_op jit(solution)/shard_map/all_to_all | solution.py:330
  35.4 2.5 %shard_map.87.inner.earlier = f32[3,2,8,128]{3,2,1,0:T(8,128)S(1)} custom-call(s32[35]{0:T(128)S(1)} %pad_add_fusion.place, f32[5,2,8,128]{3,2,1,0:T(8,128)S(1)} %get-tuple-element.27.own, f32[2,2,8,128]{3,2,1,0:T(8,128)S(1)} %get-tuple-element.28.marks), custom_call_target="tpu_custom_call" | custom-call | flops 100000000 | bytes 1048576 | tf_op jit(solution)/shard_map/pallas_call | solution.py:33
  37.9 0.6 shard_map.88
  38.5 3.4 %collective-permute-start = (f32[5,10,128]{2,1,0:T(8,128)S(1)}, f32[5,10,128]{2,1,0:T(8,128)S(1)}, u32[]{:S(2)}, u32[]{:S(2)}) collective-permute-start(f32[5,10,128]{2,1,0:T(8,128)S(1)} %get-tuple-element.30.right), channel_id=1, source_target_pairs={{0,16},{16,32},{32,48},{48,64},{64,80},{80,96},{96,112},{112,128},... | collective-permute-start | bytes 76808 | tf_op jit(solution)/shard_map/ppermute | solution.py:328
  41.8 2.5 %collective-permute-start.1 = (f32[5,10,128]{2,1,0:T(8,128)S(1)}, f32[5,10,128]{2,1,0:T(8,128)S(1)}, u32[]{:S(2)}, u32[]{:S(2)}) collective-permute-start(f32[5,10,128]{2,1,0:T(8,128)S(1)} %get-tuple-element.31.left), channel_id=1, source_target_pairs={{16,0},{32,16},{48,32},{64,48},{80,64},{96,80},{112,96},{128,112},... | collective-permute-start | bytes 76808 | tf_op jit(solution)/shard_map/ppermute | solution.py:329
  44.4 4.3 %collective-permute-done.1.after = f32[5,10,128]{2,1,0:T(8,128)S(1)} collective-permute-done((f32[5,10,128]{2,1,0:T(8,128)S(1)}, f32[5,10,128]{2,1,0:T(8,128)S(1)}, u32[]{:S(2)}, u32[]{:S(2)}) %collective-permute-start.1) | collective-permute-done | bytes 25632 | tf_op jit(solution)/shard_map/ppermute | solution.py:329
  48.6 2.1 %shard_map.89.found = f32[3,2,8,128]{3,2,1,0:T(8,128)S(1)} custom-call(s32[35]{0:T(128)S(1)} %pad_add_fusion.place, f32[5,10,128]{2,1,0:T(8,128)S(1)} %collective-permute-done.before, f32[5,10,128]{2,1,0:T(8,128)S(1)} %get-tuple-element.31.left, f32[5,10,128]{2,1,0:T(8,128)S(1)} %get-tuple-element.30.right, f32[5,10,128]{2,1,0:T(8,128)S(1)} %collective-permute-done.1.after, ...), custom_call_target="tpu_custom_call" | custom-call | flops 100000000 | bytes 1048576 | tf_op jit(solution)/shard_map/pallas_call | solution.py:33
  50.8 1.2 shard_map.90
  52.0 3.5 %all-to-all-start.2 = ((f32[16,16,128]{2,1,0:T(8,128)}), f32[16,16,128]{2,1,0:T(8,128)S(1)}, u32[]{:S(2)}, u32[]{:S(2)}) async-start(f32[16,16,128]{2,1,0:T(8,128)} %get-tuple-element.35), calls=%async_computation.2 | async-start | bytes 262144 | tf_op jit(solution)/shard_map/all_to_all | solution.py:320
  55.5 2.5 %shard_map.91.inner.earlier = f32[3,2,8,128]{3,2,1,0:T(8,128)S(1)} custom-call(s32[35]{0:T(128)S(1)} %pad_add_fusion.place, f32[5,2,8,128]{3,2,1,0:T(8,128)S(1)} %get-tuple-element.34.own, f32[2,2,8,128]{3,2,1,0:T(8,128)S(1)} %get-tuple-element.28.marks), custom_call_target="tpu_custom_call" | custom-call | flops 100000000 | bytes 1048576 | tf_op jit(solution)/shard_map/pallas_call | solution.py:33
  58.0 5.5 %all-to-all-done.2.got = f32[16,16,128]{2,1,0:T(8,128)S(1)} async-done(((f32[16,16,128]{2,1,0:T(8,128)}), f32[16,16,128]{2,1,0:T(8,128)S(1)}, u32[]{:S(2)}, u32[]{:S(2)}) %all-to-all-start.2) | async-done | bytes 131104 | tf_op jit(solution)/shard_map/all_to_all | solution.py:320
  63.5 1.3 shard_map.92
  64.7 13.4 %all-to-all-start.3 = ((f32[32,1,128]{2,1,0:T(1,128)}), f32[32,1,128]{2,1,0:T(1,128)S(1)}, u32[]{:S(2)}, u32[]{:S(2)}) async-start(f32[32,1,128]{2,1,0:T(1,128)} %get-tuple-element.39), calls=%async_computation.3 | async-start | bytes 32768 | tf_op jit(solution)/shard_map/all_to_all | solution.py:330
  78.1 3.4 %collective-permute-start.2 = (f32[5,10,128]{2,1,0:T(8,128)S(1)}, f32[5,10,128]{2,1,0:T(8,128)S(1)}, u32[]{:S(2)}, u32[]{:S(2)}) collective-permute-start(f32[5,10,128]{2,1,0:T(8,128)S(1)} %get-tuple-element.36.right), channel_id=1, source_target_pairs={{0,16},{16,32},{32,48},{48,64},{64,80},{80,96},{96,112},{112,128},... | collective-permute-start | bytes 76808 | tf_op jit(solution)/shard_map/ppermute | solution.py:328
  81.5 2.5 %collective-permute-start.3 = (f32[5,10,128]{2,1,0:T(8,128)S(1)}, f32[5,10,128]{2,1,0:T(8,128)S(1)}, u32[]{:S(2)}, u32[]{:S(2)}) collective-permute-start(f32[5,10,128]{2,1,0:T(8,128)S(1)} %get-tuple-element.37.left), channel_id=1, source_target_pairs={{16,0},{32,16},{48,32},{64,48},{80,64},{96,80},{112,96},{128,112},... | collective-permute-start | bytes 76808 | tf_op jit(solution)/shard_map/ppermute | solution.py:329
  84.0 4.3 %collective-permute-done.3.after = f32[5,10,128]{2,1,0:T(8,128)S(1)} collective-permute-done((f32[5,10,128]{2,1,0:T(8,128)S(1)}, f32[5,10,128]{2,1,0:T(8,128)S(1)}, u32[]{:S(2)}, u32[]{:S(2)}) %collective-permute-start.3) | collective-permute-done | bytes 25632 | tf_op jit(solution)/shard_map/ppermute | solution.py:329
  88.3 2.1 %shard_map.93.found = f32[3,2,8,128]{3,2,1,0:T(8,128)S(1)} custom-call(s32[35]{0:T(128)S(1)} %pad_add_fusion.place, f32[5,10,128]{2,1,0:T(8,128)S(1)} %collective-permute-done.2.before, f32[5,10,128]{2,1,0:T(8,128)S(1)} %get-tuple-element.37.left, f32[5,10,128]{2,1,0:T(8,128)S(1)} %get-tuple-element.36.right, ...), custom_call_target="tpu_custom_call" | custom-call | flops 100000000 | bytes 1048576 | tf_op jit(solution)/shard_map/pallas_call | solution.py:33
  90.4 1.2 shard_map.94
  91.6 3.5 %all-to-all-start.4 = ((f32[16,16,128]{2,1,0:T(8,128)}), f32[16,16,128]{2,1,0:T(8,128)S(1)}, u32[]{:S(2)}, u32[]{:S(2)}) async-start(f32[16,16,128]{2,1,0:T(8,128)} %get-tuple-element.41), calls=%async_computation.4 | async-start | bytes 262144 | tf_op jit(solution)/shard_map/all_to_all | solution.py:320
  95.2 2.5 %shard_map.95.inner.earlier = f32[3,2,8,128]{3,2,1,0:T(8,128)S(1)} custom-call(s32[35]{0:T(128)S(1)} %pad_add_fusion.place, f32[5,2,8,128]{3,2,1,0:T(8,128)S(1)} %get-tuple-element.40.own, f32[2,2,8,128]{3,2,1,0:T(8,128)S(1)} %get-tuple-element.28.marks), custom_call_target="tpu_custom_call" | custom-call | flops 100000000 | bytes 1048576 | tf_op jit(solution)/shard_map/pallas_call | solution.py:33
  97.6 5.5 %all-to-all-done.4.got = f32[16,16,128]{2,1,0:T(8,128)S(1)} async-done(((f32[16,16,128]{2,1,0:T(8,128)}), f32[16,16,128]{2,1,0:T(8,128)S(1)}, u32[]{:S(2)}, u32[]{:S(2)}) %all-to-all-start.4) | async-done | bytes 131104 | tf_op jit(solution)/shard_map/all_to_all | solution.py:320
  103.1 1.3 shard_map.96
  104.4 13.4 %all-to-all-start.5 = ((f32[32,1,128]{2,1,0:T(1,128)}), f32[32,1,128]{2,1,0:T(1,128)S(1)}, u32[]{:S(2)}, u32[]{:S(2)}) async-start(f32[32,1,128]{2,1,0:T(1,128)} %get-tuple-element.45), calls=%async_computation.5 | async-start | bytes 32768 | tf_op jit(solution)/shard_map/all_to_all | solution.py:330
  117.8 3.4 %collective-permute-start.4 = (f32[5,10,128]{2,1,0:T(8,128)S(1)}, f32[5,10,128]{2,1,0:T(8,128)S(1)}, u32[]{:S(2)}, u32[]{:S(2)}) collective-permute-start(f32[5,10,128]{2,1,0:T(8,128)S(1)} %get-tuple-element.42.right), channel_id=1, source_target_pairs={{0,16},{16,32},{32,48},{48,64},{64,80},{80,96},{96,112},{112,128},... | collective-permute-start | bytes 76808 | tf_op jit(solution)/shard_map/ppermute | solution.py:328
  121.1 2.6 %collective-permute-start.5 = (f32[5,10,128]{2,1,0:T(8,128)S(1)}, f32[5,10,128]{2,1,0:T(8,128)S(1)}, u32[]{:S(2)}, u32[]{:S(2)}) collective-permute-start(f32[5,10,128]{2,1,0:T(8,128)S(1)} %get-tuple-element.43.left), channel_id=1, source_target_pairs={{16,0},{32,16},{48,32},{64,48},{80,64},{96,80},{112,96},{128,112},... | collective-permute-start | bytes 76808 | tf_op jit(solution)/shard_map/ppermute | solution.py:329
  123.8 4.1 %collective-permute-done.5.after = f32[5,10,128]{2,1,0:T(8,128)S(1)} collective-permute-done((f32[5,10,128]{2,1,0:T(8,128)S(1)}, f32[5,10,128]{2,1,0:T(8,128)S(1)}, u32[]{:S(2)}, u32[]{:S(2)}) %collective-permute-start.5) | collective-permute-done | bytes 25632 | tf_op jit(solution)/shard_map/ppermute | solution.py:329
  127.9 2.1 %shard_map.97.found = f32[3,2,8,128]{3,2,1,0:T(8,128)S(1)} custom-call(s32[35]{0:T(128)S(1)} %pad_add_fusion.place, f32[5,10,128]{2,1,0:T(8,128)S(1)} %collective-permute-done.4.before, f32[5,10,128]{2,1,0:T(8,128)S(1)} %get-tuple-element.43.left, f32[5,10,128]{2,1,0:T(8,128)S(1)} %get-tuple-element.42.right, ...), custom_call_target="tpu_custom_call" | custom-call | flops 100000000 | bytes 1048576 | tf_op jit(solution)/shard_map/pallas_call | solution.py:33
  130.1 1.2 shard_map.98
  131.3 3.5 %all-to-all-start.6 = ((f32[16,16,128]{2,1,0:T(8,128)}), f32[16,16,128]{2,1,0:T(8,128)S(1)}, u32[]{:S(2)}, u32[]{:S(2)}) async-start(f32[16,16,128]{2,1,0:T(8,128)} %get-tuple-element.47), calls=%async_computation.6 | async-start | bytes 262144 | tf_op jit(solution)/shard_map/all_to_all | solution.py:320
  134.8 2.5 %shard_map.99.inner.earlier = f32[3,2,8,128]{3,2,1,0:T(8,128)S(1)} custom-call(s32[35]{0:T(128)S(1)} %pad_add_fusion.place, f32[5,2,8,128]{3,2,1,0:T(8,128)S(1)} %get-tuple-element.46.own, f32[2,2,8,128]{3,2,1,0:T(8,128)S(1)} %get-tuple-element.28.marks), custom_call_target="tpu_custom_call" | custom-call | flops 100000000 | bytes 1048576 | tf_op jit(solution)/shard_map/pallas_call | solution.py:33
  137.3 5.5 %all-to-all-done.6.got = f32[16,16,128]{2,1,0:T(8,128)S(1)} async-done(((f32[16,16,128]{2,1,0:T(8,128)}), f32[16,16,128]{2,1,0:T(8,128)S(1)}, u32[]{:S(2)}, u32[]{:S(2)}) %all-to-all-start.6) | async-done | bytes 131104 | tf_op jit(solution)/shard_map/all_to_all | solution.py:320
  142.8 1.3 shard_map.100
  144.0 2.9 %collective-permute-start.6 = (f32[5,10,128]{2,1,0:T(8,128)S(1)}, f32[5,10,128]{2,1,0:T(8,128)S(1)}, u32[]{:S(2)}, u32[]{:S(2)}) collective-permute-start(f32[5,10,128]{2,1,0:T(8,128)S(1)} %get-tuple-element.48.right), channel_id=1, source_target_pairs={{0,16},{16,32},{32,48},{48,64},{64,80},{80,96},{96,112},{112,128},... | collective-permute-start | bytes 76808 | tf_op jit(solution)/shard_map/ppermute | solution.py:328
  147.0 2.9 %collective-permute-start.7 = (f32[5,10,128]{2,1,0:T(8,128)S(1)}, f32[5,10,128]{2,1,0:T(8,128)S(1)}, u32[]{:S(2)}, u32[]{:S(2)}) collective-permute-start(f32[5,10,128]{2,1,0:T(8,128)S(1)} %get-tuple-element.49.left), channel_id=1, source_target_pairs={{16,0},{32,16},{48,32},{64,48},{80,64},{96,80},{112,96},{128,112},... | collective-permute-start | bytes 76808 | tf_op jit(solution)/shard_map/ppermute | solution.py:329
  149.9 3.5 %all-to-all-start.7 = ((f32[16,1,128]{2,1,0:T(1,128)}), f32[16,1,128]{2,1,0:T(1,128)S(1)}, u32[]{:S(2)}, u32[]{:S(2)}) async-start(f32[16,1,128]{2,1,0:T(1,128)} %get-tuple-element.51), calls=%async_computation.7 | async-start | bytes 16384 | tf_op jit(solution)/shard_map/all_to_all | solution.py:330
  153.7 2.1 %shard_map.101.found = f32[3,2,8,128]{3,2,1,0:T(8,128)S(1)} custom-call(s32[35]{0:T(128)S(1)} %pad_add_fusion.place, f32[5,10,128]{2,1,0:T(8,128)S(1)} %collective-permute-done.6.before, f32[5,10,128]{2,1,0:T(8,128)S(1)} %get-tuple-element.49.left, f32[5,10,128]{2,1,0:T(8,128)S(1)} %get-tuple-element.48.right, ...), custom_call_target="tpu_custom_call" | custom-call | flops 100000000 | bytes 1048576 | tf_op jit(solution)/shard_map/pallas_call | solution.py:33
  155.9 4.9 %all-to-all-done.7.total = f32[16,1,128]{2,1,0:T(1,128)S(1)} async-done(((f32[16,1,128]{2,1,0:T(1,128)}), f32[16,1,128]{2,1,0:T(1,128)S(1)}, u32[]{:S(2)}, u32[]{:S(2)}) %all-to-all-start.7) | async-done | bytes 8224 | tf_op jit(solution)/shard_map/all_to_all | solution.py:330
  160.8 0.6 shard_map.102
  161.3 18.6 %all_to_all.51.got = f32[8,88,128]{2,1,0:T(8,128)S(1)} all-to-all(f32[8,88,128]{2,1,0:T(8,128)S(1)} %shard_map.102), channel_id=1, replica_groups={{0,16,32,48,64,80,96,112},{128,144,160,176,192,208,224,240},{256,272,28..., dimensions={0} | all-to-all | bytes 720896 | tf_op jit(solution)/shard_map/all_to_all | solution.py:338
  180.0 0.6 shard_map.103
  180.6 24.2 %all_to_all.52.got = f32[4,88,128]{2,1,0:T(8,128)S(1)} all-to-all(f32[4,88,128]{2,1,0:T(8,128)S(1)} %shard_map.103), channel_id=1, replica_groups={{0,128,256,384},{16,144,272,400},{32,160,288,416},{48,176,304,432},{64,..., dimensions={0} | all-to-all | bytes 360448 | tf_op jit(solution)/shard_map/all_to_all | solution.py:340
  204.9 1.2 shard_map.104
  (17 shorter events, 0.5 us)
Async XLA Ops:
  0.6 0.8 copy-start
  0.6 0.8 copy-start.3
  0.7 0.8 copy-start.5
  1.4 0.7 copy-start.1
  2.1 0.7 copy-start.2
  2.8 0.7 copy-start.4
  18.7 32.0 %all-to-all-start.1 = ((f32[32,1,128]{2,1,0:T(1,128)}), f32[32,1,128]{2,1,0:T(1,128)S(1)}, u32[]{:S(2)}, u32[]{:S(2)}) async-start(f32[32,1,128]{2,1,0:T(1,128)} %get-tuple-element.33), calls=%async_computation.1 | async-start | bytes 32768 | tf_op jit(solution)/shard_map/all_to_all | solution.py:330
  38.5 5.9 %collective-permute-start = (f32[5,10,128]{2,1,0:T(8,128)S(1)}, f32[5,10,128]{2,1,0:T(8,128)S(1)}, u32[]{:S(2)}, u32[]{:S(2)}) collective-permute-start(f32[5,10,128]{2,1,0:T(8,128)S(1)} %get-tuple-element.30.right), channel_id=1, source_target_pairs={{0,16},{16,32},{32,48},{48,64},{64,80},{80,96},{96,112},{112,128},... | collective-permute-start | bytes 76808 | tf_op jit(solution)/shard_map/ppermute | solution.py:328
  41.8 6.8 %collective-permute-start.1 = (f32[5,10,128]{2,1,0:T(8,128)S(1)}, f32[5,10,128]{2,1,0:T(8,128)S(1)}, u32[]{:S(2)}, u32[]{:S(2)}) collective-permute-start(f32[5,10,128]{2,1,0:T(8,128)S(1)} %get-tuple-element.31.left), channel_id=1, source_target_pairs={{16,0},{32,16},{48,32},{64,48},{80,64},{96,80},{112,96},{128,112},... | collective-permute-start | bytes 76808 | tf_op jit(solution)/shard_map/ppermute | solution.py:329
  52.0 11.5 %all-to-all-start.2 = ((f32[16,16,128]{2,1,0:T(8,128)}), f32[16,16,128]{2,1,0:T(8,128)S(1)}, u32[]{:S(2)}, u32[]{:S(2)}) async-start(f32[16,16,128]{2,1,0:T(8,128)} %get-tuple-element.35), calls=%async_computation.2 | async-start | bytes 262144 | tf_op jit(solution)/shard_map/all_to_all | solution.py:320
  64.7 25.7 %all-to-all-start.3 = ((f32[32,1,128]{2,1,0:T(1,128)}), f32[32,1,128]{2,1,0:T(1,128)S(1)}, u32[]{:S(2)}, u32[]{:S(2)}) async-start(f32[32,1,128]{2,1,0:T(1,128)} %get-tuple-element.39), calls=%async_computation.3 | async-start | bytes 32768 | tf_op jit(solution)/shard_map/all_to_all | solution.py:330
  78.1 5.9 %collective-permute-start.2 = (f32[5,10,128]{2,1,0:T(8,128)S(1)}, f32[5,10,128]{2,1,0:T(8,128)S(1)}, u32[]{:S(2)}, u32[]{:S(2)}) collective-permute-start(f32[5,10,128]{2,1,0:T(8,128)S(1)} %get-tuple-element.36.right), channel_id=1, source_target_pairs={{0,16},{16,32},{32,48},{48,64},{64,80},{80,96},{96,112},{112,128},... | collective-permute-start | bytes 76808 | tf_op jit(solution)/shard_map/ppermute | solution.py:328
  81.5 6.8 %collective-permute-start.3 = (f32[5,10,128]{2,1,0:T(8,128)S(1)}, f32[5,10,128]{2,1,0:T(8,128)S(1)}, u32[]{:S(2)}, u32[]{:S(2)}) collective-permute-start(f32[5,10,128]{2,1,0:T(8,128)S(1)} %get-tuple-element.37.left), channel_id=1, source_target_pairs={{16,0},{32,16},{48,32},{64,48},{80,64},{96,80},{112,96},{128,112},... | collective-permute-start | bytes 76808 | tf_op jit(solution)/shard_map/ppermute | solution.py:329
  91.6 11.5 %all-to-all-start.4 = ((f32[16,16,128]{2,1,0:T(8,128)}), f32[16,16,128]{2,1,0:T(8,128)S(1)}, u32[]{:S(2)}, u32[]{:S(2)}) async-start(f32[16,16,128]{2,1,0:T(8,128)} %get-tuple-element.41), calls=%async_computation.4 | async-start | bytes 262144 | tf_op jit(solution)/shard_map/all_to_all | solution.py:320
  104.4 25.7 %all-to-all-start.5 = ((f32[32,1,128]{2,1,0:T(1,128)}), f32[32,1,128]{2,1,0:T(1,128)S(1)}, u32[]{:S(2)}, u32[]{:S(2)}) async-start(f32[32,1,128]{2,1,0:T(1,128)} %get-tuple-element.45), calls=%async_computation.5 | async-start | bytes 32768 | tf_op jit(solution)/shard_map/all_to_all | solution.py:330
  117.8 6.0 %collective-permute-start.4 = (f32[5,10,128]{2,1,0:T(8,128)S(1)}, f32[5,10,128]{2,1,0:T(8,128)S(1)}, u32[]{:S(2)}, u32[]{:S(2)}) collective-permute-start(f32[5,10,128]{2,1,0:T(8,128)S(1)} %get-tuple-element.42.right), channel_id=1, source_target_pairs={{0,16},{16,32},{32,48},{48,64},{64,80},{80,96},{96,112},{112,128},... | collective-permute-start | bytes 76808 | tf_op jit(solution)/shard_map/ppermute | solution.py:328
  121.1 6.8 %collective-permute-start.5 = (f32[5,10,128]{2,1,0:T(8,128)S(1)}, f32[5,10,128]{2,1,0:T(8,128)S(1)}, u32[]{:S(2)}, u32[]{:S(2)}) collective-permute-start(f32[5,10,128]{2,1,0:T(8,128)S(1)} %get-tuple-element.43.left), channel_id=1, source_target_pairs={{16,0},{32,16},{48,32},{64,48},{80,64},{96,80},{112,96},{128,112},... | collective-permute-start | bytes 76808 | tf_op jit(solution)/shard_map/ppermute | solution.py:329
  131.3 11.5 %all-to-all-start.6 = ((f32[16,16,128]{2,1,0:T(8,128)}), f32[16,16,128]{2,1,0:T(8,128)S(1)}, u32[]{:S(2)}, u32[]{:S(2)}) async-start(f32[16,16,128]{2,1,0:T(8,128)} %get-tuple-element.47), calls=%async_computation.6 | async-start | bytes 262144 | tf_op jit(solution)/shard_map/all_to_all | solution.py:320
  144.0 9.3 %collective-permute-start.6 = (f32[5,10,128]{2,1,0:T(8,128)S(1)}, f32[5,10,128]{2,1,0:T(8,128)S(1)}, u32[]{:S(2)}, u32[]{:S(2)}) collective-permute-start(f32[5,10,128]{2,1,0:T(8,128)S(1)} %get-tuple-element.48.right), channel_id=1, source_target_pairs={{0,16},{16,32},{32,48},{48,64},{64,80},{80,96},{96,112},{112,128},... | collective-permute-start | bytes 76808 | tf_op jit(solution)/shard_map/ppermute | solution.py:328
  147.0 6.8 %collective-permute-start.7 = (f32[5,10,128]{2,1,0:T(8,128)S(1)}, f32[5,10,128]{2,1,0:T(8,128)S(1)}, u32[]{:S(2)}, u32[]{:S(2)}) collective-permute-start(f32[5,10,128]{2,1,0:T(8,128)S(1)} %get-tuple-element.49.left), channel_id=1, source_target_pairs={{16,0},{32,16},{48,32},{64,48},{80,64},{96,80},{112,96},{128,112},... | collective-permute-start | bytes 76808 | tf_op jit(solution)/shard_map/ppermute | solution.py:329
  149.9 10.9 %all-to-all-start.7 = ((f32[16,1,128]{2,1,0:T(1,128)}), f32[16,1,128]{2,1,0:T(1,128)S(1)}, u32[]{:S(2)}, u32[]{:S(2)}) async-start(f32[16,1,128]{2,1,0:T(1,128)} %get-tuple-element.51), calls=%async_computation.7 | async-start | bytes 16384 | tf_op jit(solution)/shard_map/all_to_all | solution.py:330

commit v5 on v3

v5 whole, which is shorter than its diff:
```python
import functools

import jax
import jax.numpy as jnp
from jax import lax
from jax.experimental import pallas as pl
from jax.experimental.pallas import tpu as pltpu
from jax.sharding import PartitionSpec as P

HALO = 2
MASS = 0.02
SOUND = 20.0
VISCOSITY = 2.0
STIFF = 50.0
DT = 0.05

FAR = 1.0e6

COST = 20_000_000_000

F32 = jnp.float32
BF16 = jnp.bfloat16
PARAMS = pltpu.CompilerParams(vmem_limit_bytes=40 * 1024 * 1024)
VMEM = pl.BlockSpec(memory_space=pltpu.VMEM)
SMEM = pl.BlockSpec(memory_space=pltpu.SMEM)


def shape(*dims):
    return jax.ShapeDtypeStruct(dims, F32)


def call(kernel, outs, scalars, arrays, scratch=(), estimate=0):
    return pl.pallas_call(
        kernel,
        out_shape=outs,
        in_specs=[SMEM] * len(scalars) + [VMEM] * len(arrays),
        out_specs=[VMEM] * len(outs) if isinstance(outs, list) else VMEM,
        scratch_shapes=scratch,
        compiler_params=PARAMS,
        cost_estimate=pl.CostEstimate(flops=estimate, bytes_accessed=1 << 20, transcendentals=0) if estimate else None,
    )(*scalars, *arrays)


def pressure(s):
    inv = 1.0 / s
    return SOUND * (s - 1.0) * inv * inv, inv


def penalties(x, touch, live, offset, column):
    return touch * live * jnp.maximum(0.0, x - column + offset - 0.5)


def own_force(new, marks, offset, first):
    total = 0.0
    for c, fields in enumerate(new):
        total = total + STIFF * penalties(fields[0], marks[1, c], marks[0, c], offset, first + c)
    total = jnp.sum(total, axis=0, keepdims=True)
    return jnp.broadcast_to(jnp.sum(total, axis=1, keepdims=True), total.shape)


def visible(fields, live, touch):
    alive = live > 0
    x, y, u, v, rho = fields
    return [jnp.where(alive, x, FAR), y, u, v, jnp.where(alive, rho, 1.0), live * touch]


def fill_depth(place, state, marks, force, sent):
    depth, ndepth = place[1], sent.shape[0]
    cols, rows = marks.shape[1:3]
    row = 6 * cols * HALO
    sent[...] = jnp.zeros(sent.shape, F32)
    sent[:, row : row + 1, :] = jnp.broadcast_to(force[None], (ndepth, 1, force.shape[1]))
    seen = [visible(state[c], marks[0, c], marks[1, c]) for c in range(cols)]

    def put(target, rim):
        for c in range(cols):
            for f in range(6):
                at = (f * cols + c) * HALO
                sent[target, at : at + HALO] = seen[c][f][rim : rim + HALO]

    @pl.when(depth > 0)
    def _():
        put(depth - 1, 0)

    @pl.when(depth < ndepth - 1)
    def _():
        put(depth + 1, rows - HALO)


def origin(place, cols, rows):
    first = (place[0] * cols).astype(F32)
    return first + 0.5 * cols, (place[1] * rows).astype(F32) + 0.5 * rows, first


def start_kernel(place, counts, contact, first_tool, positions, velocity, density, own, marks, tool, sent):
    cols, rows, slots = density.shape
    row = lax.broadcasted_iota(jnp.int32, (rows, slots), 0)
    slot = lax.broadcasted_iota(jnp.int32, (rows, slots), 1)
    new = []
    for c in range(cols):
        filled = jnp.zeros((rows, slots), jnp.int32)
        touch = jnp.zeros((rows, slots), jnp.int32)
        for r in range(rows):
            filled = jnp.where(row == r, counts[c, r], filled)
            touch = jnp.where(row == r, contact[c, r], touch)
        marks[0, c] = jnp.where(slot < filled, 1.0, 0.0)
        marks[1, c] = touch.astype(F32)
        new.append([positions[0, c], positions[1, c], velocity[0, c], velocity[1, c], density[c]])
        for f in range(5):
            own[f, c] = new[c][f]
    offset = jnp.zeros((1, slots), F32) + first_tool[0]
    tool[0:1] = offset
    tool[1:2] = jnp.zeros((1, slots), F32) + first_tool[1]
    fill_depth(place, new, marks, own_force(new, marks, offset, origin(place, cols, rows)[2]), sent)


def extend_kernel(place, own, marks, got, wide, force):
    depth, ndepth = place[1], got.shape[0]
    cols, rows = own.shape[1:3]
    above = got[jnp.maximum(depth - 1, 0)]
    below = got[jnp.minimum(depth + 1, ndepth - 1)]
    blank = [FAR, 0.0, 0.0, 0.0, 1.0, 0.0]
    for c in range(cols):
        seen = visible([own[f, c] for f in range(5)], marks[0, c], marks[1, c])
        for f in range(6):
            at = (f * cols + c) * HALO
            wide[f, c, 0:HALO] = jnp.where(depth > 0, above[at : at + HALO], blank[f])
            wide[f, c, HALO : rows + HALO] = seen[f]
            wide[f, c, rows + HALO :] = jnp.where(depth < ndepth - 1, below[at : at + HALO], blank[f])
    row = 6 * cols * HALO
    total = jnp.sum(got[:, row : row + 1, :], axis=0)
    force[...] = jnp.broadcast_to(total[None], force.shape)


def spread_kernel(got, force):
    force[...] = jnp.broadcast_to(jnp.sum(got[...], axis=0, keepdims=True), force.shape)


def pair_sums(columns, center, out, feat, acc2, acc3):
    x0, y0, _ = center
    tall, slots = columns[0][0].shape
    rows = tall - 2
    for c, (x, y, u, v, s) in enumerate(columns):
        lx, ly = x - x0, y - y0
        press, inv = pressure(s)
        parts = [jnp.ones_like(x), lx, ly, press, press * lx, press * ly, u, v, u * lx + v * ly, inv, inv * u, inv * v]
        for k in range(16):
            high = parts[k].astype(BF16).astype(F32) if k < 12 else jnp.zeros_like(x)
            feat[pl.ds(c * tall * 32 + k, tall, stride=32), :] = high
            feat[pl.ds(c * tall * 32 + 16 + k, tall, stride=32), :] = parts[k] - high if k < 12 else high
    for i, (c, r) in enumerate([(c, r) for c in range(1, len(columns) - 1) for r in range(1, tall - 1)]):
        xi, yi = [jnp.broadcast_to(f[r : r + 1], (slots, slots)).T for f in columns[c][:2]]
        around = [(c + a, r + b) for a in (-1, 0, 1) for b in (-1, 0, 1)]

        def weights(a, b):
            dx = (xi - columns[a][0][b : b + 1]).astype(BF16)
            dy = (yi - columns[a][1][b : b + 1]).astype(BF16)
            q = jnp.maximum(BF16(0.0), BF16(1.0) - dx * dx - dy * dy)
            q2 = q * q
            return jnp.concatenate([q2, q2 * q], axis=0)

        total = None
        for n in range(0, 9, 2):
            pair = around[n : n + 2]
            w = jnp.concatenate([weights(a, b) for a, b in pair], axis=1)
            f = jnp.concatenate([feat[pl.ds((a * tall + b) * 32, 32), :] for a, b in pair], axis=1).astype(BF16)
            found = lax.dot_general(f, w, (((1,), (1,)), ((), ())), preferred_element_type=F32)
            total = found if total is None else total + found
        acc2[i * 32 : (i + 1) * 32] = total[:, :slots]
        acc3[i * 32 : (i + 1) * 32] = total[:, slots:]

    for n in range(len(columns) - 2):

        def summed(k):
            acc = acc2 if k < 9 else acc3
            return sum(acc[pl.ds(n * rows * 32 + k + low, rows, stride=32), :] for low in (0, 16))

        x, y, u, v, s = [f[1 : rows + 1] for f in columns[n + 1]]
        x, y = x - x0, y - y0
        press, _ = pressure(s)
        a0, ax, ay, ap, apx, apy, au, av, aw, b0, bu, bv = [summed(k) for k in range(12)]
        sx, sy = x * a0 - ax, y * a0 - ay
        out[0, n] = (6.0 * MASS) * (press * sx + x * ap - apx) - (VISCOSITY * MASS) * (u * b0 - bu)
        out[1, n] = (6.0 * MASS) * (press * sy + y * ap - apy) - (VISCOSITY * MASS) * (v * b0 - bv)
        out[2, n] = (-6.0 * MASS) * (u * sx + v * sy - x * au - y * av + aw)


def wide_columns(place, wide, swapped, other):
    even = lax.rem(place[0], 2) == 0
    cols = wide.shape[1]
    blank = [FAR, 0.0, 0.0, 0.0, 1.0, 0.0]
    columns = []
    for side in range(3):
        outside = place[0] == (0 if side == 0 else place[2] - 1)
        for c in range(cols):
            if side == 1:
                fields = [wide[f, c] for f in range(6)]
            else:
                first, second = (other, swapped) if side == 0 else (swapped, other)
                fields = [jnp.where(outside, blank[f], jnp.where(even, first[f, c], second[f, c])) for f in range(6)]
            columns.append(fields)
    return columns


def wide_rates_kernel(place, size, wide, swapped, other, out, feat, acc2, acc3):
    columns = [fields[:5] for fields in wide_columns(place, wide, swapped, other)]
    pair_sums(columns, origin(place, *size), out, feat, acc2, acc3)


def rates_kernel(place, size, ring, out, feat, acc2, acc3):
    columns = [[ring[f, c] for f in range(5)] for c in range(ring.shape[1])]
    pair_sums(columns, origin(place, *size), out, feat, acc2, acc3)


def moved_ring(place, columns, found, offset, first, ring):
    for n in range(ring.shape[1]):
        x, y, u, v, s, touch = [f[1:-1] for f in columns[n + 1]]
        live = jnp.where(x < 0.5 * FAR, 1.0, 0.0)
        pen = touch * jnp.maximum(0.0, x - (first + (n - 1)) + offset - 0.5)
        u = u + DT * live * (found[0, n] - STIFF * pen)
        v = v + DT * live * found[1, n]
        ring[0, n] = x + DT * live * u
        ring[1, n] = y + DT * live * v
        ring[2, n] = u
        ring[3, n] = v
        ring[4, n] = s + DT * live * found[2, n]


def moved_state(own, found, marks, offset, first):
    cols, rows = own.shape[1:3]
    side, rim = (found.shape[1] - cols) // 2, (found.shape[2] - rows) // 2
    new = []
    for c in range(cols):
        live = marks[0, c]
        ax, ay, drho = [found[f, c + side][rim : rim + rows] for f in range(3)]
        pen = penalties(own[0, c], marks[1, c], live, offset, first + c)
        u = own[2, c] + DT * live * (ax - STIFF * pen)
        v = own[3, c] + DT * live * ay
        x = own[0, c] + DT * live * u
        y = own[1, c] + DT * live * v
        rho = own[4, c] + DT * live * drho
        new.append([x, y, u, v, rho])
    return new


def keep(new, own):
    for c, fields in enumerate(new):
        for f in range(5):
            own[f, c] = fields[f]


def tool_step(tool, force, scale):
    speed = tool[1:2] + DT * (1.0 - force * scale)
    return tool[0:1] + DT * speed, speed


def first_update_kernel(scale, place, own, found, marks, wide, swapped, other, tool, total, new_own, ring, new_tool):
    first = origin(place, *own.shape[1:3])[2]
    keep(moved_state(own, found, marks, tool[0:1], first), new_own)
    moved_ring(place, wide_columns(place, wide, swapped, other), found, tool[0:1], first, ring)
    offset, speed = tool_step(tool, jnp.sum(total[...], axis=0), scale)
    new_tool[0:1] = offset
    new_tool[1:2] = speed


def second_update_kernel(place, own, found, marks, tool, new_own, sent):
    first = origin(place, *own.shape[1:3])[2]
    state = [[own[f, c] for f in range(5)] for c in range(own.shape[1])]
    new = moved_state(own, found, marks, tool[0:1], first)
    keep(new, new_own)
    fill_depth(place, new, marks, own_force(state, marks, tool[0:1], first), sent)


def third_update_kernel(scale, place, own, found, marks, wide, swapped, other, tool, total, new_own, ring, new_tool, force):
    first = origin(place, *own.shape[1:3])[2]
    offset, speed = tool_step(tool, jnp.sum(total[...], axis=0), scale)
    new_tool[0:1] = offset
    new_tool[1:2] = speed
    state = [[own[f, c] for f in range(5)] for c in range(own.shape[1])]
    force[...] = jnp.broadcast_to(own_force(state, marks, offset, first)[None], force.shape)
    keep(moved_state(own, found, marks, offset, first), new_own)
    moved_ring(place, wide_columns(place, wide, swapped, other), found, offset, first, ring)


def last_force_kernel(scale, place, own, marks, tool, total, new_tool, force):
    offset, speed = tool_step(tool, jnp.sum(total[...], axis=0), scale)
    new_tool[0:1] = offset
    new_tool[1:2] = speed
    state = [[own[f, c] for f in range(5)] for c in range(own.shape[1])]
    part = own_force(state, marks, offset, origin(place, *own.shape[1:3])[2])
    force[...] = jnp.broadcast_to(part[None], force.shape)


def last_kernel(near, place, own, found, marks, tool, total, sent):
    cols, rows, slots = own.shape[1:]
    size = 5 * cols * rows
    new = moved_state(own, found, marks, tool[0:1], origin(place, cols, rows)[2])
    sent[...] = jnp.zeros(sent.shape, F32)
    sent[:, size:, :] = jnp.broadcast_to(jnp.sum(total[...], axis=0, keepdims=True), (near, sent.shape[1] - size, slots))
    digit = lax.rem(place[3 + place[0]], near)
    for f in range(5):
        for c in range(cols):
            at = (f * cols + c) * rows
            sent[digit, at : at + rows] = new[c][f]


def sort_kernel(near, size, place, got, sent):
    far, most, slots = sent.shape
    group, digit = lax.div(place[0], near), lax.rem(place[0], near)
    sent[...] = jnp.zeros(sent.shape, F32)
    total = jnp.sum(got[:, size : size + 1, :], axis=0, keepdims=True)
    sent[:, size:, :] = jnp.broadcast_to(total, (far, most - size, slots))
    for k in range(near):
        target = place[3 + group * near + k]

        @pl.when(lax.rem(target, near) == digit)
        def _():
            sent[lax.div(target, near), 0:size] = got[k, 0:size]


def take_kernel(near, scale, place, got, tool, out, new_tool):
    cols, rows, slots = out.shape[1:]
    size = 5 * cols * rows
    source = 0
    for k in range(got.shape[0] * near):
        source = jnp.where(place[3 + k] == place[0], k // near, source)
    for f in range(5):
        for c in range(cols):
            at = (f * cols + c) * rows
            out[f, c] = got[source, at : at + rows]
    offset, speed = tool_step(tool, jnp.sum(got[:, size : size + 1, :], axis=0), scale)
    new_tool[0] = offset[0, 0]
    new_tool[1] = speed[0, 0]


def body(positions, velocity, density, counts, contact_mask, destination, tool):
    cols, rows, slots = density.shape
    ncut, ndepth = lax.axis_size("cut"), lax.axis_size("depth")
    here, depth = lax.axis_index("cut"), lax.axis_index("depth")
    scale = 1.0 / (ncut * cols * ndepth * rows * slots)
    place = jnp.concatenate([jnp.stack([here, depth, jnp.int32(ncut)]).astype(jnp.int32), destination])
    near = 8 if ncut % 8 == 0 else 1
    far = ncut // near
    size = 5 * cols * rows
    state, marking = shape(5, cols, rows, slots), shape(2, cols, rows, slots)
    message, vector = shape(ndepth, 32, slots), shape(2, slots)
    along_cut, along_depth = shape(ncut, 1, slots), shape(ndepth, 1, slots)
    ring, ring_rates = shape(5, cols + 2, rows + 2, slots), shape(3, cols + 2, rows + 2, slots)
    swap = [(i, i ^ 1) for i in range(ncut)]
    cross = [(i, i + 1 if i % 2 else i - 1) for i in range(1, ncut - 1)]

    def scratch(wide, tall):
        return [pltpu.VMEM((n * 32, slots), F32) for n in (wide * tall, (wide - 2) * (tall - 2), (wide - 2) * (tall - 2))]

    def rates_of(kernel, out, arrays, wide, tall):
        return call(lambda place, *refs: kernel(place, (cols, rows), *refs), out, (place,), arrays, scratch(wide, tall), COST)

    def exchange(own, marks, sent):
        got = lax.all_to_all(sent, "depth", 0, 0, tiled=True)
        wide, force = call(extend_kernel, [shape(6, cols, rows + 2 * HALO, slots), along_cut], (place,), (own, marks, got))
        swapped, other = lax.ppermute(wide, "cut", swap), lax.ppermute(wide, "cut", cross)
        total = lax.all_to_all(force, "cut", 0, 0, tiled=True)
        found = rates_of(wide_rates_kernel, ring_rates, (wide, swapped, other), 3 * cols, rows + 4)
        return found, (wide, swapped, other), total

    own, marks, tool, sent = call(
        start_kernel, [state, marking, vector, message], (place, counts, contact_mask, tool), (positions, velocity, density)
    )
    found, around, total = exchange(own, marks, sent)
    kernel = functools.partial(first_update_kernel, scale)
    own, ringed, tool = call(kernel, [state, ring, vector], (place,), (own, found, marks, *around, tool, total))

    found = rates_of(rates_kernel, shape(3, cols, rows, slots), (ringed,), cols + 2, rows + 2)
    own, sent = call(second_update_kernel, [state, message], (place,), (own, found, marks, tool))

    found, around, total = exchange(own, marks, sent)
    kernel = functools.partial(third_update_kernel, scale)
    outs = [state, ring, vector, along_depth]
    new_own, ringed, tool, force = call(kernel, outs, (place,), (own, found, marks, *around, tool, total))
    own = new_own

    got = lax.all_to_all(force, "depth", 0, 0, tiled=True)
    force = call(spread_kernel, along_cut, (), (got,))
    total = lax.all_to_all(force, "cut", 0, 0, tiled=True)
    found = rates_of(rates_kernel, shape(3, cols, rows, slots), (ringed,), cols + 2, rows + 2)
    kernel = functools.partial(last_force_kernel, scale)
    tool, force = call(kernel, [vector, along_depth], (place,), (own, marks, tool, total))
    total = lax.all_to_all(force, "depth", 0, 0, tiled=True)
    kernel = functools.partial(last_kernel, near)
    sent = call(kernel, shape(near, size + 8, slots), (place,), (own, found, marks, tool, total))
    close = [[g * near + k for k in range(near)] for g in range(far)]
    apart = [[g * near + k for g in range(far)] for k in range(near)]
    got = lax.all_to_all(sent, "cut", 0, 0, tiled=True, axis_index_groups=close)
    sent = call(functools.partial(sort_kernel, near, size), shape(far, size + 8, slots), (place,), (got,))
    got = lax.all_to_all(sent, "cut", 0, 0, tiled=True, axis_index_groups=apart)
    return pl.pallas_call(
        functools.partial(take_kernel, near, scale),
        out_shape=[state, shape(2)],
        in_specs=[SMEM, VMEM, VMEM],
        out_specs=[VMEM, SMEM],
        compiler_params=PARAMS,
    )(place, got, tool)


def solution(mesh):
    return jax.shard_map(
        body,
        mesh=mesh,
        in_specs=(
            P(None, "cut", "depth", None),
            P(None, "cut", "depth", None),
            P("cut", "depth", None),
            P("cut", "depth"),
            P("cut", "depth"),
            P(),
            P(),
        ),
        out_specs=(P(None, "cut", "depth", None), P()),
        check_vma=False,
    )
```

time: 195 us -> 183 us (0.938)
  the two profiles are of different devices: /device:TPU:8 before, /device:TPU:64 now
where the time goes in v5:
time: 183 us; the launch traced here: 182 us
  blocking collectives  95.3 us (52%)
  starting transfers between devices  41.2 us (23%)
  Pallas kernels  33.4 us (18%)
  waiting for transfers between devices  8.12 us (4%)
  local copies, waits for them, and re-layouts  2.1 us (1%)
    pallas_call x14, Pallas kernels, call(): pl.pallas_call(kernel, out_shape=outs, in_specs=[SMEM] * len(scalars) + [...  32.2 us
    all_to_all x2, blocking collectives, exchange(): got = lax.all_to_all(sent, 'depth', 0, 0, tiled=True)  28.1 us
    all_to_all x2, starting transfers between devices, exchange(): total = lax.all_to_all(force, 'cut', 0, 0, tiled=True)  24.6 us
    all_to_all x1, blocking collectives, body(): total = lax.all_to_all(force, 'cut', 0, 0, tiled=True)  21.1 us
    all_to_all x1, blocking collectives, body(): got = lax.all_to_all(sent, 'cut', 0, 0, tiled=True, axis_index_groups=apart)  20.9 us
    all_to_all x1, blocking collectives, body(): got = lax.all_to_all(sent, 'cut', 0, 0, tiled=True, axis_index_groups=close)  14.5 us
    all_to_all x1, blocking collectives, body(): got = lax.all_to_all(force, 'depth', 0, 0, tiled=True)  10.7 us
    ppermute x2, starting transfers between devices, exchange(): lax.ppermute(wide, 'cut', swap)  7.74 us
  transfers between devices with their start and end apart: 7, of which 3 were waited for; matrix products, arithmetic and copies ran while one was open for 0% of the time, Pallas kernels for 12%

profile of v5, /device:TPU:64, one launch (start us, length us, event | category | flops | bytes accessed | tf_op | source)
XLA Modules:
  0.0 181.8 jit_solution(11717421199465836128)
XLA Ops:
  0.6 0.0 copy-start
  0.6 0.0 copy-start.3
  0.7 0.0 copy-start.5
  0.7 0.7 pad_add_fusion.place
  1.4 0.0 copy-done
  1.4 0.0 copy-done.3
  1.4 0.0 copy-done.5
  1.4 0.0 copy-start.1
  1.4 0.7 copy-done.1
  2.1 0.0 copy-start.2
  2.1 0.7 copy-done.2
  2.8 0.0 copy-start.4
  2.8 0.7 copy-done.4
  3.5 0.7 shard_map.86
  4.2 16.0 %all_to_all.45.got = f32[16,32,128]{2,1,0:T(8,128)S(1)} all-to-all(f32[16,32,128]{2,1,0:T(8,128)S(1)} %get-tuple-element.23), channel_id=1, replica_groups=mesh['cut'=32,'depth'=16] {'depth'}, dimensions={0} | all-to-all | bytes 524288 | tf_op jit(solution)/shard_map/all_to_all | solution.py:359
  20.3 1.2 shard_map.87
  21.4 2.1 %collective-permute-start.1 = (f32[6,2,12,128]{3,2,1,0:T(8,128)S(1)}, f32[6,2,12,128]{3,2,1,0:T(8,128)S(1)}, u32[]{:S(2)}, u32[]{:S(2)}) collective-permute-start(f32[6,2,12,128]{3,2,1,0:T(8,128)S(1)} %get-tuple-element.24.refs_0_.wide), channel_id=1, source_target_pairs={{16,32},{32,16},{48,64},{64,48},{80,96},{96,80},{112,128},{128,112... | collective-permute-start | bytes 221192 | tf_op jit(solution)/shard_map/ppermute | solution.py:361
  23.6 5.1 %collective-permute-start = (f32[6,2,12,128]{3,2,1,0:T(8,128)S(1)}, f32[6,2,12,128]{3,2,1,0:T(8,128)S(1)}, u32[]{:S(2)}, u32[]{:S(2)}) collective-permute-start(f32[6,2,12,128]{3,2,1,0:T(8,128)S(1)} %get-tuple-element.24.refs_0_.wide), channel_id=1, source_target_pairs={{0,16},{16,0},{32,48},{48,32},{64,80},{80,64},{96,112},{112,96},{1... | collective-permute-start | bytes 221192 | tf_op jit(solution)/shard_map/ppermute | solution.py:361
  28.6 14.0 %all-to-all-start.1 = ((f32[32,1,128]{2,1,0:T(1,128)}), f32[32,1,128]{2,1,0:T(1,128)S(1)}, u32[]{:S(2)}, u32[]{:S(2)}) async-start(f32[32,1,128]{2,1,0:T(1,128)} %get-tuple-element.26), calls=%async_computation.1 | async-start | bytes 32768 | tf_op jit(solution)/shard_map/all_to_all | solution.py:362
  42.7 0.0 collective-permute-done.1.refs_2_.other
  42.7 0.0 collective-permute-done.refs_1_.swapped
  42.7 8.7 %shard_map.88.found = f32[3,4,10,128]{3,2,1,0:T(8,128)S(1)} custom-call(s32[35]{0:T(128)S(1)} %pad_add_fusion.place, f32[6,2,12,128]{3,2,1,0:T(8,128)S(1)} %get-tuple-element.24.refs_0_.wide, f32[6,2,12,128]{3,2,1,0:T(8,128)S(1)} %collective-permute-done.refs_1_.swapped, f32[6,2,12,128]{3,2,1,0:T(8,128)S(1)} %collective-permute-done.1.refs_2_.other), custom_call_target="tpu_custom_call" | custom-call | flops 20000000000 | bytes 1048576 | tf_op jit(solution)/shard_map/pallas_call | solution.py:33
  51.4 2.2 %all-to-all-done.1.total = f32[32,1,128]{2,1,0:T(1,128)S(1)} async-done(((f32[32,1,128]{2,1,0:T(1,128)}), f32[32,1,128]{2,1,0:T(1,128)S(1)}, u32[]{:S(2)}, u32[]{:S(2)}) %all-to-all-start.1) | async-done | bytes 16416 | tf_op jit(solution)/shard_map/all_to_all | solution.py:362
  53.6 0.6 shard_map.89
  54.2 3.7 %shard_map.90.found = f32[3,2,8,128]{3,2,1,0:T(8,128)S(1)} custom-call(s32[35]{0:T(128)S(1)} %pad_add_fusion.place, f32[5,4,10,128]{3,2,1,0:T(8,128)S(1)} %get-tuple-element.28.refs_0_), custom_call_target="tpu_custom_call" | custom-call | flops 20000000000 | bytes 1048576 | tf_op jit(solution)/shard_map/pallas_call | solution.py:33
  57.9 0.6 shard_map.91
  58.5 12.0 %all_to_all.46.got = f32[16,32,128]{2,1,0:T(8,128)S(1)} all-to-all(f32[16,32,128]{2,1,0:T(8,128)S(1)} %get-tuple-element.31), channel_id=1, replica_groups=mesh['cut'=32,'depth'=16] {'depth'}, dimensions={0} | all-to-all | bytes 524288 | tf_op jit(solution)/shard_map/all_to_all | solution.py:359
  70.6 1.2 shard_map.92
  71.7 3.3 %collective-permute-start.3 = (f32[6,2,12,128]{3,2,1,0:T(8,128)S(1)}, f32[6,2,12,128]{3,2,1,0:T(8,128)S(1)}, u32[]{:S(2)}, u32[]{:S(2)}) collective-permute-start(f32[6,2,12,128]{3,2,1,0:T(8,128)S(1)} %get-tuple-element.32.refs_0_.wide), channel_id=1, source_target_pairs={{16,32},{32,16},{48,64},{64,48},{80,96},{96,80},{112,128},{128,112... | collective-permute-start | bytes 221192 | tf_op jit(solution)/shard_map/ppermute | solution.py:361
  75.0 2.7 %collective-permute-start.2 = (f32[6,2,12,128]{3,2,1,0:T(8,128)S(1)}, f32[6,2,12,128]{3,2,1,0:T(8,128)S(1)}, u32[]{:S(2)}, u32[]{:S(2)}) collective-permute-start(f32[6,2,12,128]{3,2,1,0:T(8,128)S(1)} %get-tuple-element.32.refs_0_.wide), channel_id=1, source_target_pairs={{0,16},{16,0},{32,48},{48,32},{64,80},{80,64},{96,112},{112,96},{1... | collective-permute-start | bytes 221192 | tf_op jit(solution)/shard_map/ppermute | solution.py:361
  77.7 10.6 %all-to-all-start.3 = ((f32[32,1,128]{2,1,0:T(1,128)}), f32[32,1,128]{2,1,0:T(1,128)S(1)}, u32[]{:S(2)}, u32[]{:S(2)}) async-start(f32[32,1,128]{2,1,0:T(1,128)} %get-tuple-element.33), calls=%async_computation.3 | async-start | bytes 32768 | tf_op jit(solution)/shard_map/all_to_all | solution.py:362
  88.3 0.0 collective-permute-done.3.refs_2_.other
  88.3 0.0 collective-permute-done.2.refs_1_.swapped
  88.3 8.7 %shard_map.93.found = f32[3,4,10,128]{3,2,1,0:T(8,128)S(1)} custom-call(s32[35]{0:T(128)S(1)} %pad_add_fusion.place, f32[6,2,12,128]{3,2,1,0:T(8,128)S(1)} %get-tuple-element.32.refs_0_.wide, f32[6,2,12,128]{3,2,1,0:T(8,128)S(1)} %collective-permute-done.2.refs_1_.swapped, f32[6,2,12,128]{3,2,1,0:T(8,128)S(1)} %collective-permute-done.3.refs_2_.other), custom_call_target="tpu_custom_call" | custom-call | flops 20000000000 | bytes 1048576 | tf_op jit(solution)/shard_map/pallas_call | solution.py:33
  97.0 2.2 %all-to-all-done.3.total = f32[32,1,128]{2,1,0:T(1,128)S(1)} async-done(((f32[32,1,128]{2,1,0:T(1,128)}), f32[32,1,128]{2,1,0:T(1,128)S(1)}, u32[]{:S(2)}, u32[]{:S(2)}) %all-to-all-start.3) | async-done | bytes 16416 | tf_op jit(solution)/shard_map/all_to_all | solution.py:362
  99.2 0.7 shard_map.94
  99.9 10.7 %all_to_all.47.got = f32[16,1,128]{2,1,0:T(1,128)S(1)} all-to-all(f32[16,1,128]{2,1,0:T(1,128)S(1)} %get-tuple-element.37), channel_id=1, replica_groups=mesh['cut'=32,'depth'=16] {'depth'}, dimensions={0} | all-to-all | bytes 16384 | tf_op jit(solution)/shard_map/all_to_all | solution.py:382
  110.6 21.1 %all_to_all.48.total = f32[32,1,128]{2,1,0:T(1,128)S(1)} all-to-all(f32[32,1,128]{2,1,0:T(1,128)S(1)} %shard_map.96), channel_id=1, replica_groups=mesh['cut'=32,'depth'=16] {'cut'}, dimensions={0} | all-to-all | bytes 32768 | tf_op jit(solution)/shard_map/all_to_all | solution.py:384
  131.7 1.3 shard_map.97
  132.9 3.5 %all-to-all-start.6 = ((f32[16,1,128]{2,1,0:T(1,128)}), f32[16,1,128]{2,1,0:T(1,128)S(1)}, u32[]{:S(2)}, u32[]{:S(2)}) async-start(f32[16,1,128]{2,1,0:T(1,128)} %get-tuple-element.39), calls=%async_computation.6 | async-start | bytes 16384 | tf_op jit(solution)/shard_map/all_to_all | solution.py:388
  136.4 3.7 %shard_map.95.found = f32[3,2,8,128]{3,2,1,0:T(8,128)S(1)} custom-call(s32[35]{0:T(128)S(1)} %pad_add_fusion.place, f32[5,4,10,128]{3,2,1,0:T(8,128)S(1)} %get-tuple-element.35.refs_0_), custom_call_target="tpu_custom_call" | custom-call | flops 20000000000 | bytes 1048576 | tf_op jit(solution)/shard_map/pallas_call | solution.py:33
  140.1 3.7 %all-to-all-done.6.total = f32[16,1,128]{2,1,0:T(1,128)S(1)} async-done(((f32[16,1,128]{2,1,0:T(1,128)}), f32[16,1,128]{2,1,0:T(1,128)S(1)}, u32[]{:S(2)}, u32[]{:S(2)}) %all-to-all-start.6) | async-done | bytes 8224 | tf_op jit(solution)/shard_map/all_to_all | solution.py:388
  143.8 0.6 shard_map.98
  144.4 14.5 %all_to_all.49.got = f32[8,88,128]{2,1,0:T(8,128)S(1)} all-to-all(f32[8,88,128]{2,1,0:T(8,128)S(1)} %shard_map.98), channel_id=1, replica_groups={{0,16,32,48,64,80,96,112},{128,144,160,176,192,208,224,240},{256,272,28..., dimensions={0} | all-to-all | bytes 720896 | tf_op jit(solution)/shard_map/all_to_all | solution.py:393
  158.9 0.6 shard_map.99
  159.5 20.9 %all_to_all.50.got = f32[4,88,128]{2,1,0:T(8,128)S(1)} all-to-all(f32[4,88,128]{2,1,0:T(8,128)S(1)} %shard_map.99), channel_id=1, replica_groups={{0,128,256,384},{16,144,272,400},{32,160,288,416},{48,176,304,432},{64,..., dimensions={0} | all-to-all | bytes 360448 | tf_op jit(solution)/shard_map/all_to_all | solution.py:395
  180.5 1.2 shard_map.100
  (1 shorter events, 0.0 us)
Async XLA Ops:
  0.6 0.8 copy-start
  0.6 0.8 copy-start.3
  0.7 0.8 copy-start.5
  1.4 0.7 copy-start.1
  2.1 0.7 copy-start.2
  2.8 0.7 copy-start.4
  21.4 21.2 %collective-permute-start.1 = (f32[6,2,12,128]{3,2,1,0:T(8,128)S(1)}, f32[6,2,12,128]{3,2,1,0:T(8,128)S(1)}, u32[]{:S(2)}, u32[]{:S(2)}) collective-permute-start(f32[6,2,12,128]{3,2,1,0:T(8,128)S(1)} %get-tuple-element.24.refs_0_.wide), channel_id=1, source_target_pairs={{16,32},{32,16},{48,64},{64,48},{80,96},{96,80},{112,128},{128,112... | collective-permute-start | bytes 221192 | tf_op jit(solution)/shard_map/ppermute | solution.py:361
  23.6 19.1 %collective-permute-start = (f32[6,2,12,128]{3,2,1,0:T(8,128)S(1)}, f32[6,2,12,128]{3,2,1,0:T(8,128)S(1)}, u32[]{:S(2)}, u32[]{:S(2)}) collective-permute-start(f32[6,2,12,128]{3,2,1,0:T(8,128)S(1)} %get-tuple-element.24.refs_0_.wide), channel_id=1, source_target_pairs={{0,16},{16,0},{32,48},{48,32},{64,80},{80,64},{96,112},{112,96},{1... | collective-permute-start | bytes 221192 | tf_op jit(solution)/shard_map/ppermute | solution.py:361
  28.6 24.9 %all-to-all-start.1 = ((f32[32,1,128]{2,1,0:T(1,128)}), f32[32,1,128]{2,1,0:T(1,128)S(1)}, u32[]{:S(2)}, u32[]{:S(2)}) async-start(f32[32,1,128]{2,1,0:T(1,128)} %get-tuple-element.26), calls=%async_computation.1 | async-start | bytes 32768 | tf_op jit(solution)/shard_map/all_to_all | solution.py:362
  71.7 16.5 %collective-permute-start.3 = (f32[6,2,12,128]{3,2,1,0:T(8,128)S(1)}, f32[6,2,12,128]{3,2,1,0:T(8,128)S(1)}, u32[]{:S(2)}, u32[]{:S(2)}) collective-permute-start(f32[6,2,12,128]{3,2,1,0:T(8,128)S(1)} %get-tuple-element.32.refs_0_.wide), channel_id=1, source_target_pairs={{16,32},{32,16},{48,64},{64,48},{80,96},{96,80},{112,128},{128,112... | collective-permute-start | bytes 221192 | tf_op jit(solution)/shard_map/ppermute | solution.py:361
  75.0 13.3 %collective-permute-start.2 = (f32[6,2,12,128]{3,2,1,0:T(8,128)S(1)}, f32[6,2,12,128]{3,2,1,0:T(8,128)S(1)}, u32[]{:S(2)}, u32[]{:S(2)}) collective-permute-start(f32[6,2,12,128]{3,2,1,0:T(8,128)S(1)} %get-tuple-element.32.refs_0_.wide), channel_id=1, source_target_pairs={{0,16},{16,0},{32,48},{48,32},{64,80},{80,64},{96,112},{112,96},{1... | collective-permute-start | bytes 221192 | tf_op jit(solution)/shard_map/ppermute | solution.py:361
  77.7 21.5 %all-to-all-start.3 = ((f32[32,1,128]{2,1,0:T(1,128)}), f32[32,1,128]{2,1,0:T(1,128)S(1)}, u32[]{:S(2)}, u32[]{:S(2)}) async-start(f32[32,1,128]{2,1,0:T(1,128)} %get-tuple-element.33), calls=%async_computation.3 | async-start | bytes 32768 | tf_op jit(solution)/shard_map/all_to_all | solution.py:362
  132.9 10.9 %all-to-all-start.6 = ((f32[16,1,128]{2,1,0:T(1,128)}), f32[16,1,128]{2,1,0:T(1,128)S(1)}, u32[]{:S(2)}, u32[]{:S(2)}) async-start(f32[16,1,128]{2,1,0:T(1,128)} %get-tuple-element.39), calls=%async_computation.6 | async-start | bytes 16384 | tf_op jit(solution)/shard_map/all_to_all | solution.py:388

commit v6 on v5

--- a/solution.py
+++ b/solution.py
@@ -114,7 +114,7 @@
     fill_depth(place, new, marks, own_force(new, marks, offset, origin(place, cols, rows)[2]), sent)
 
 
-def extend_kernel(place, own, marks, got, wide, force):
+def extend_kernel(place, own, marks, got, wide):
     depth, ndepth = place[1], got.shape[0]
     cols, rows = own.shape[1:3]
     above = got[jnp.maximum(depth - 1, 0)]
@@ -124,12 +124,16 @@
         seen = visible([own[f, c] for f in range(5)], marks[0, c], marks[1, c])
         for f in range(6):
             at = (f * cols + c) * HALO
-            wide[f, c, 0:HALO] = jnp.where(depth > 0, above[at : at + HALO], blank[f])
-            wide[f, c, HALO : rows + HALO] = seen[f]
-            wide[f, c, rows + HALO :] = jnp.where(depth < ndepth - 1, below[at : at + HALO], blank[f])
+            wide[f * cols + c, 0:HALO] = jnp.where(depth > 0, above[at : at + HALO], blank[f])
+            wide[f * cols + c, HALO : rows + HALO] = seen[f]
+            wide[f * cols + c, rows + HALO :] = jnp.where(depth < ndepth - 1, below[at : at + HALO], blank[f])
     row = 6 * cols * HALO
-    total = jnp.sum(got[:, row : row + 1, :], axis=0)
-    force[...] = jnp.broadcast_to(total[None], force.shape)
+    wide[6 * cols] = jnp.broadcast_to(jnp.sum(got[:, row : row + 1, :], axis=0), wide.shape[1:])
+
+
+def pair_force_kernel(wide, swapped, force):
+    last = wide.shape[0] - 1
+    force[...] = jnp.broadcast_to((wide[last, 0:1] + swapped[last, 0:1])[None], force.shape)
 
 
 def spread_kernel(got, force):
@@ -185,25 +189,24 @@
         out[2, n] = (-6.0 * MASS) * (u * sx + v * sy - x * au - y * av + aw)
 
 
-def wide_columns(place, wide, swapped, other):
+def wide_columns(place, cols, wide, swapped, other):
     even = lax.rem(place[0], 2) == 0
-    cols = wide.shape[1]
     blank = [FAR, 0.0, 0.0, 0.0, 1.0, 0.0]
     columns = []
     for side in range(3):
         outside = place[0] == (0 if side == 0 else place[2] - 1)
         for c in range(cols):
             if side == 1:
-                fields = [wide[f, c] for f in range(6)]
+                fields = [wide[f * cols + c] for f in range(6)]
             else:
                 first, second = (other, swapped) if side == 0 else (swapped, other)
-                fields = [jnp.where(outside, blank[f], jnp.where(even, first[f, c], second[f, c])) for f in range(6)]
+                fields = [jnp.where(outside, blank[f], jnp.where(even, first[f * cols + c], second[f * cols + c])) for f in range(6)]
             columns.append(fields)
     return columns
 
 
 def wide_rates_kernel(place, size, wide, swapped, other, out, feat, acc2, acc3):
-    columns = [fields[:5] for fields in wide_columns(place, wide, swapped, other)]
+    columns = [fields[:5] for fields in wide_columns(place, size[0], wide, swapped, other)]
     pair_sums(columns, origin(place, *size), out, feat, acc2, acc3)
 
 
@@ -254,21 +257,21 @@
     return tool[0:1] + DT * speed, speed
 
 
-def first_update_kernel(scale, place, own, found, marks, wide, swapped, other, tool, total, new_own, ring, new_tool):
+def first_update_kernel(place, own, found, marks, wide, swapped, other, tool, new_own, ring):
     first = origin(place, *own.shape[1:3])[2]
     keep(moved_state(own, found, marks, tool[0:1], first), new_own)
-    moved_ring(place, wide_columns(place, wide, swapped, other), found, tool[0:1], first, ring)
+    moved_ring(place, wide_columns(place, own.shape[1], wide, swapped, other), found, tool[0:1], first, ring)
+
+
+def second_update_kernel(scale, place, own, found, marks, tool, total, new_own, new_tool, sent):
+    first = origin(place, *own.shape[1:3])[2]
     offset, speed = tool_step(tool, jnp.sum(total[...], axis=0), scale)
     new_tool[0:1] = offset
     new_tool[1:2] = speed
-
-
-def second_update_kernel(place, own, found, marks, tool, new_own, sent):
-    first = origin(place, *own.shape[1:3])[2]
     state = [[own[f, c] for f in range(5)] for c in range(own.shape[1])]
-    new = moved_state(own, found, marks, tool[0:1], first)
+    new = moved_state(own, found, marks, offset, first)
     keep(new, new_own)
-    fill_depth(place, new, marks, own_force(state, marks, tool[0:1], first), sent)
+    fill_depth(place, new, marks, own_force(state, marks, offset, first), sent)
 
 
 def third_update_kernel(scale, place, own, found, marks, wide, swapped, other, tool, total, new_own, ring, new_tool, force):
@@ -279,7 +282,7 @@
     state = [[own[f, c] for f in range(5)] for c in range(own.shape[1])]
     force[...] = jnp.broadcast_to(own_force(state, marks, offset, first)[None], force.shape)
     keep(moved_state(own, found, marks, offset, first), new_own)
-    moved_ring(place, wide_columns(place, wide, swapped, other), found, offset, first, ring)
+    moved_ring(place, wide_columns(place, own.shape[1], wide, swapped, other), found, offset, first, ring)
 
 
 def last_force_kernel(scale, place, own, marks, tool, total, new_tool, force):
@@ -344,7 +347,11 @@
     size = 5 * cols * rows
     state, marking = shape(5, cols, rows, slots), shape(2, cols, rows, slots)
     message, vector = shape(ndepth, 32, slots), shape(2, slots)
-    along_cut, along_depth = shape(ncut, 1, slots), shape(ndepth, 1, slots)
+    along_depth, along_plane, along_line = [shape(n, 1, slots) for n in (ndepth, 2 * ndepth, ncut // 2)]
+    both = ("cut", "depth")
+    pairs = range(0, ncut, 2)
+    planes = [[(c + k) * ndepth + d for k in range(2) for d in range(ndepth)] for c in pairs]
+    lines = [[(c + k) * ndepth + d for c in pairs] for k in range(2) for d in range(ndepth)]
     ring, ring_rates = shape(5, cols + 2, rows + 2, slots), shape(3, cols + 2, rows + 2, slots)
     swap = [(i, i ^ 1) for i in range(ncut)]
     cross = [(i, i + 1 if i % 2 else i - 1) for i in range(1, ncut - 1)]
@@ -357,9 +364,10 @@
 
     def exchange(own, marks, sent):
         got = lax.all_to_all(sent, "depth", 0, 0, tiled=True)
-        wide, force = call(extend_kernel, [shape(6, cols, rows + 2 * HALO, slots), along_cut], (place,), (own, marks, got))
+        wide = call(extend_kernel, shape(6 * cols + 1, rows + 2 * HALO, slots), (place,), (own, marks, got))
         swapped, other = lax.ppermute(wide, "cut", swap), lax.ppermute(wide, "cut", cross)
-        total = lax.all_to_all(force, "cut", 0, 0, tiled=True)
+        force = call(pair_force_kernel, along_line, (), (wide, swapped))
+        total = lax.all_to_all(force, both, 0, 0, tiled=True, axis_index_groups=lines)
         found = rates_of(wide_rates_kernel, ring_rates, (wide, swapped, other), 3 * cols, rows + 4)
         return found, (wide, swapped, other), total
 
@@ -367,21 +375,21 @@
         start_kernel, [state, marking, vector, message], (place, counts, contact_mask, tool), (positions, velocity, density)
     )
     found, around, total = exchange(own, marks, sent)
-    kernel = functools.partial(first_update_kernel, scale)
-    own, ringed, tool = call(kernel, [state, ring, vector], (place,), (own, found, marks, *around, tool, total))
+    own, ringed = call(first_update_kernel, [state, ring], (place,), (own, found, marks, *around, tool))
 
     found = rates_of(rates_kernel, shape(3, cols, rows, slots), (ringed,), cols + 2, rows + 2)
-    own, sent = call(second_update_kernel, [state, message], (place,), (own, found, marks, tool))
+    kernel = functools.partial(second_update_kernel, scale)
+    own, tool, sent = call(kernel, [state, vector, message], (place,), (own, found, marks, tool, total))
 
     found, around, total = exchange(own, marks, sent)
     kernel = functools.partial(third_update_kernel, scale)
-    outs = [state, ring, vector, along_depth]
+    outs = [state, ring, vector, along_plane]
     new_own, ringed, tool, force = call(kernel, outs, (place,), (own, found, marks, *around, tool, total))
     own = new_own
 
-    got = lax.all_to_all(force, "depth", 0, 0, tiled=True)
-    force = call(spread_kernel, along_cut, (), (got,))
-    total = lax.all_to_all(force, "cut", 0, 0, tiled=True)
+    got = lax.all_to_all(force, both, 0, 0, tiled=True, axis_index_groups=planes)
+    force = call(spread_kernel, along_line, (), (got,))
+    total = lax.all_to_all(force, both, 0, 0, tiled=True, axis_index_groups=lines)
     found = rates_of(rates_kernel, shape(3, cols, rows, slots), (ringed,), cols + 2, rows + 2)
     kernel = functools.partial(last_force_kernel, scale)
     tool, force = call(kernel, [vector, along_depth], (place,), (own, marks, tool, total))

time: 183 us -> 181 us (0.989)
    all_to_all x2, waiting for transfers between devices: 4.38 us -> 1.38 us  [exchange(): lax.all_to_all(force, both, 0, 0, tiled=True, axis_index_groups=lines)]
    ppermute x2, starting transfers between devices: 7.74 us -> 5.17 us  [exchange(): lax.ppermute(wide, 'cut', swap)]
    ppermute x2, waiting for transfers between devices: 0.01 us -> 2.51 us  [exchange(): lax.ppermute(wide, 'cut', swap)]
    all_to_all x2, starting transfers between devices: 24.6 us -> 26.8 us  [exchange(): lax.all_to_all(force, both, 0, 0, tiled=True, axis_index_groups=lines)]
    pallas_call x14 -> x16, Pallas kernels: 32.2 us -> 32.2 us  [call(): pl.pallas_call(kernel, out_shape=outs, in_specs=[SMEM] * len(scalars) + [...]
  transfers between devices with their start and end apart: 7 -> 7, of which waited for: 3 -> 4; matrix products, arithmetic and copies ran while one was open for 0% -> 0% of each run, Pallas kernels for 12% -> 15%
where the time goes in v6:
time: 181 us
  blocking collectives  94.3 us (52%)
  starting transfers between devices  41.5 us (23%)
  Pallas kernels  33.4 us (18%)
  waiting for transfers between devices  7.62 us (4%)
  local copies, waits for them, and re-layouts  2.1 us (1%)
    pallas_call x16, Pallas kernels, call(): pl.pallas_call(kernel, out_shape=outs, in_specs=[SMEM] * len(scalars) + [...  32.2 us
    all_to_all x2, blocking collectives, exchange(): got = lax.all_to_all(sent, 'depth', 0, 0, tiled=True)  28 us
    all_to_all x2, starting transfers between devices, exchange(): lax.all_to_all(force, both, 0, 0, tiled=True, axis_index_groups=lines)  26.8 us
    all_to_all x1, blocking collectives, body(): got = lax.all_to_all(sent, 'cut', 0, 0, tiled=True, axis_index_groups=apart)  21 us
    all_to_all x1, blocking collectives, body(): lax.all_to_all(force, both, 0, 0, tiled=True, axis_index_groups=lines)  20.6 us
    all_to_all x1, blocking collectives, body(): got = lax.all_to_all(sent, 'cut', 0, 0, tiled=True, axis_index_groups=close)  14.4 us
    all_to_all x1, blocking collectives, body(): lax.all_to_all(force, both, 0, 0, tiled=True, axis_index_groups=planes)  10.3 us
    ppermute x2, starting transfers between devices, exchange(): lax.ppermute(wide, 'cut', cross)  6.05 us
  transfers between devices with their start and end apart: 7, of which 4 were waited for; matrix products, arithmetic and copies ran while one was open for 0% of the time, Pallas kernels for 15%

profile of v6, /device:TPU:64, one launch (start us, length us, event | category | flops | bytes accessed | tf_op | source)
XLA Modules:
  0.0 180.6 jit_solution(1423199161245081567)
XLA Ops:
  0.6 0.0 copy-start
  0.6 0.0 copy-start.3
  0.7 0.0 copy-start.5
  0.7 0.7 pad_add_fusion.place
  1.4 0.0 copy-done
  1.4 0.0 copy-done.3
  1.4 0.0 copy-done.5
  1.4 0.0 copy-start.1
  1.4 0.7 copy-done.1
  2.1 0.0 copy-start.2
  2.1 0.7 copy-done.2
  2.8 0.7 copy-done.4
  3.5 0.7 shard_map.86
  4.2 16.0 %all_to_all.45.got = f32[16,32,128]{2,1,0:T(8,128)S(1)} all-to-all(f32[16,32,128]{2,1,0:T(8,128)S(1)} %get-tuple-element.19), channel_id=1, replica_groups=mesh['cut'=32,'depth'=16] {'depth'}, dimensions={0} | all-to-all | bytes 524288 | tf_op jit(solution)/shard_map/all_to_all | solution.py:366
  20.3 0.6 shard_map.87.refs_0_.wide
  20.8 2.6 %collective-permute-start = (f32[13,12,128]{2,1,0:T(8,128)S(1)}, f32[13,12,128]{2,1,0:T(8,128)S(1)}, u32[]{:S(2)}, u32[]{:S(2)}) collective-permute-start(f32[13,12,128]{2,1,0:T(8,128)S(1)} %shard_map.87.refs_0_.wide), channel_id=1, source_target_pairs={{0,16},{16,0},{32,48},{48,32},{64,80},{80,64},{96,112},{112,96},{1... | collective-permute-start | bytes 239624 | tf_op jit(solution)/shard_map/ppermute | solution.py:368
  23.4 2.8 %collective-permute-start.1 = (f32[13,12,128]{2,1,0:T(8,128)S(1)}, f32[13,12,128]{2,1,0:T(8,128)S(1)}, u32[]{:S(2)}, u32[]{:S(2)}) collective-permute-start(f32[13,12,128]{2,1,0:T(8,128)S(1)} %shard_map.87.refs_0_.wide), channel_id=1, source_target_pairs={{16,32},{32,16},{48,64},{64,48},{80,96},{96,80},{112,128},{128,112... | collective-permute-start | bytes 239624 | tf_op jit(solution)/shard_map/ppermute | solution.py:368
  26.2 1.5 collective-permute-done.refs_1_.swapped
  27.7 0.6 shard_map.91
  28.3 14.8 %all-to-all-start.1 = ((f32[16,1,128]{2,1,0:T(1,128)}), f32[16,1,128]{2,1,0:T(1,128)S(1)}, u32[]{:S(2)}, u32[]{:S(2)}) async-start(f32[16,1,128]{2,1,0:T(1,128)} %shard_map.91), calls=%async_computation.1 | async-start | bytes 16384 | tf_op jit(solution)/shard_map/all_to_all | solution.py:370
  43.1 0.0 collective-permute-done.1.refs_2_.other
  43.1 8.7 %shard_map.88.found = f32[3,4,10,128]{3,2,1,0:T(8,128)S(1)} custom-call(s32[35]{0:T(128)S(1)} %pad_add_fusion.place, f32[13,12,128]{2,1,0:T(8,128)S(1)} %shard_map.87.refs_0_.wide, f32[13,12,128]{2,1,0:T(8,128)S(1)} %collective-permute-done.refs_1_.swapped, f32[13,12,128]{2,1,0:T(8,128)S(1)} %collective-permute-done.1.refs_2_.other), custom_call_target="tpu_custom_call" | custom-call | flops 20000000000 | bytes 1048576 | tf_op jit(solution)/shard_map/pallas_call | solution.py:33
  51.8 0.6 shard_map.89
  52.4 3.7 %shard_map.90.found = f32[3,2,8,128]{3,2,1,0:T(8,128)S(1)} custom-call(s32[35]{0:T(128)S(1)} %pad_add_fusion.place, f32[5,4,10,128]{3,2,1,0:T(8,128)S(1)} %get-tuple-element.22.refs_0_), custom_call_target="tpu_custom_call" | custom-call | flops 20000000000 | bytes 1048576 | tf_op jit(solution)/shard_map/pallas_call | solution.py:33
  56.0 0.0 all-to-all-done.1.total
  56.1 0.7 shard_map.92
  56.7 11.9 %all_to_all.46.got = f32[16,32,128]{2,1,0:T(8,128)S(1)} all-to-all(f32[16,32,128]{2,1,0:T(8,128)S(1)} %get-tuple-element.24), channel_id=1, replica_groups=mesh['cut'=32,'depth'=16] {'depth'}, dimensions={0} | all-to-all | bytes 524288 | tf_op jit(solution)/shard_map/all_to_all | solution.py:366
  68.6 0.6 shard_map.93.refs_0_.wide
  69.2 2.6 %collective-permute-start.2 = (f32[13,12,128]{2,1,0:T(8,128)S(1)}, f32[13,12,128]{2,1,0:T(8,128)S(1)}, u32[]{:S(2)}, u32[]{:S(2)}) collective-permute-start(f32[13,12,128]{2,1,0:T(8,128)S(1)} %shard_map.93.refs_0_.wide), channel_id=1, source_target_pairs={{0,16},{16,0},{32,48},{48,32},{64,80},{80,64},{96,112},{112,96},{1... | collective-permute-start | bytes 239624 | tf_op jit(solution)/shard_map/ppermute | solution.py:368
  71.8 3.3 %collective-permute-start.3 = (f32[13,12,128]{2,1,0:T(8,128)S(1)}, f32[13,12,128]{2,1,0:T(8,128)S(1)}, u32[]{:S(2)}, u32[]{:S(2)}) collective-permute-start(f32[13,12,128]{2,1,0:T(8,128)S(1)} %shard_map.93.refs_0_.wide), channel_id=1, source_target_pairs={{16,32},{32,16},{48,64},{64,48},{80,96},{96,80},{112,128},{128,112... | collective-permute-start | bytes 239624 | tf_op jit(solution)/shard_map/ppermute | solution.py:368
  75.1 1.0 collective-permute-done.2.refs_1_.swapped
  76.1 0.6 shard_map.95
  76.7 12.0 %all-to-all-start.3 = ((f32[16,1,128]{2,1,0:T(1,128)}), f32[16,1,128]{2,1,0:T(1,128)S(1)}, u32[]{:S(2)}, u32[]{:S(2)}) async-start(f32[16,1,128]{2,1,0:T(1,128)} %shard_map.95), calls=%async_computation.3 | async-start | bytes 16384 | tf_op jit(solution)/shard_map/all_to_all | solution.py:370
  88.7 0.0 collective-permute-done.3.refs_2_.other
  88.7 8.7 %shard_map.94.found = f32[3,4,10,128]{3,2,1,0:T(8,128)S(1)} custom-call(s32[35]{0:T(128)S(1)} %pad_add_fusion.place, f32[13,12,128]{2,1,0:T(8,128)S(1)} %shard_map.93.refs_0_.wide, f32[13,12,128]{2,1,0:T(8,128)S(1)} %collective-permute-done.2.refs_1_.swapped, f32[13,12,128]{2,1,0:T(8,128)S(1)} %collective-permute-done.3.refs_2_.other), custom_call_target="tpu_custom_call" | custom-call | flops 20000000000 | bytes 1048576 | tf_op jit(solution)/shard_map/pallas_call | solution.py:33
  97.4 1.4 all-to-all-done.3.total
  98.8 0.7 shard_map.96
  99.5 10.3 %all_to_all.47.got = f32[32,1,128]{2,1,0:T(1,128)S(1)} all-to-all(f32[32,1,128]{2,1,0:T(1,128)S(1)} %get-tuple-element.29), channel_id=1, replica_groups={{0,1,2,3,4,5,6,7,8,9,10,11,12,13,14,15,16,17,18,19,20,21,22,23,24,25,26..., dimensions={0} | all-to-all | bytes 32768 | tf_op jit(solution)/shard_map/all_to_all | solution.py:390
  109.8 20.6 %all_to_all.48.total = f32[16,1,128]{2,1,0:T(1,128)S(1)} all-to-all(f32[16,1,128]{2,1,0:T(1,128)S(1)} %shard_map.98), channel_id=1, replica_groups={{0,32,64,96,128,160,192,224,256,288,320,352,384,416,448,480},{1,33,65,9..., dimensions={0} | all-to-all | bytes 16384 | tf_op jit(solution)/shard_map/all_to_all | solution.py:392
  130.4 1.3 shard_map.99
  131.7 3.5 %all-to-all-start.6 = ((f32[16,1,128]{2,1,0:T(1,128)}), f32[16,1,128]{2,1,0:T(1,128)S(1)}, u32[]{:S(2)}, u32[]{:S(2)}) async-start(f32[16,1,128]{2,1,0:T(1,128)} %get-tuple-element.31), calls=%async_computation.6 | async-start | bytes 16384 | tf_op jit(solution)/shard_map/all_to_all | solution.py:396
  135.2 3.7 %shard_map.97.found = f32[3,2,8,128]{3,2,1,0:T(8,128)S(1)} custom-call(s32[35]{0:T(128)S(1)} %pad_add_fusion.place, f32[5,4,10,128]{3,2,1,0:T(8,128)S(1)} %get-tuple-element.27.refs_0_), custom_call_target="tpu_custom_call" | custom-call | flops 20000000000 | bytes 1048576 | tf_op jit(solution)/shard_map/pallas_call | solution.py:33
  138.9 3.7 %all-to-all-done.6.total = f32[16,1,128]{2,1,0:T(1,128)S(1)} async-done(((f32[16,1,128]{2,1,0:T(1,128)}), f32[16,1,128]{2,1,0:T(1,128)S(1)}, u32[]{:S(2)}, u32[]{:S(2)}) %all-to-all-start.6) | async-done | bytes 8224 | tf_op jit(solution)/shard_map/all_to_all | solution.py:396
  142.6 0.6 shard_map.100
  143.2 14.4 %all_to_all.49.got = f32[8,88,128]{2,1,0:T(8,128)S(1)} all-to-all(f32[8,88,128]{2,1,0:T(8,128)S(1)} %shard_map.100), channel_id=1, replica_groups={{0,16,32,48,64,80,96,112},{128,144,160,176,192,208,224,240},{256,272,28..., dimensions={0} | all-to-all | bytes 720896 | tf_op jit(solution)/shard_map/all_to_all | solution.py:401
  157.6 0.6 shard_map.101
  158.2 21.0 %all_to_all.50.got = f32[4,88,128]{2,1,0:T(8,128)S(1)} all-to-all(f32[4,88,128]{2,1,0:T(8,128)S(1)} %shard_map.101), channel_id=1, replica_groups={{0,128,256,384},{16,144,272,400},{32,160,288,416},{48,176,304,432},{64,..., dimensions={0} | all-to-all | bytes 360448 | tf_op jit(solution)/shard_map/all_to_all | solution.py:403
  179.2 1.2 shard_map.102
  (2 shorter events, 0.0 us)
Async XLA Ops:
  0.6 0.8 copy-start
  0.6 0.8 copy-start.3
  0.7 0.8 copy-start.5
  1.4 0.7 copy-start.1
  2.1 0.7 copy-start.2
  2.8 0.7 copy-start.4
  20.8 6.9 %collective-permute-start = (f32[13,12,128]{2,1,0:T(8,128)S(1)}, f32[13,12,128]{2,1,0:T(8,128)S(1)}, u32[]{:S(2)}, u32[]{:S(2)}) collective-permute-start(f32[13,12,128]{2,1,0:T(8,128)S(1)} %shard_map.87.refs_0_.wide), channel_id=1, source_target_pairs={{0,16},{16,0},{32,48},{48,32},{64,80},{80,64},{96,112},{112,96},{1... | collective-permute-start | bytes 239624 | tf_op jit(solution)/shard_map/ppermute | solution.py:368
  23.4 19.7 %collective-permute-start.1 = (f32[13,12,128]{2,1,0:T(8,128)S(1)}, f32[13,12,128]{2,1,0:T(8,128)S(1)}, u32[]{:S(2)}, u32[]{:S(2)}) collective-permute-start(f32[13,12,128]{2,1,0:T(8,128)S(1)} %shard_map.87.refs_0_.wide), channel_id=1, source_target_pairs={{16,32},{32,16},{48,64},{64,48},{80,96},{96,80},{112,128},{128,112... | collective-permute-start | bytes 239624 | tf_op jit(solution)/shard_map/ppermute | solution.py:368
  28.3 27.7 %all-to-all-start.1 = ((f32[16,1,128]{2,1,0:T(1,128)}), f32[16,1,128]{2,1,0:T(1,128)S(1)}, u32[]{:S(2)}, u32[]{:S(2)}) async-start(f32[16,1,128]{2,1,0:T(1,128)} %shard_map.91), calls=%async_computation.1 | async-start | bytes 16384 | tf_op jit(solution)/shard_map/all_to_all | solution.py:370
  69.2 6.9 %collective-permute-start.2 = (f32[13,12,128]{2,1,0:T(8,128)S(1)}, f32[13,12,128]{2,1,0:T(8,128)S(1)}, u32[]{:S(2)}, u32[]{:S(2)}) collective-permute-start(f32[13,12,128]{2,1,0:T(8,128)S(1)} %shard_map.93.refs_0_.wide), channel_id=1, source_target_pairs={{0,16},{16,0},{32,48},{48,32},{64,80},{80,64},{96,112},{112,96},{1... | collective-permute-start | bytes 239624 | tf_op jit(solution)/shard_map/ppermute | solution.py:368
  71.8 16.9 %collective-permute-start.3 = (f32[13,12,128]{2,1,0:T(8,128)S(1)}, f32[13,12,128]{2,1,0:T(8,128)S(1)}, u32[]{:S(2)}, u32[]{:S(2)}) collective-permute-start(f32[13,12,128]{2,1,0:T(8,128)S(1)} %shard_map.93.refs_0_.wide), channel_id=1, source_target_pairs={{16,32},{32,16},{48,64},{64,48},{80,96},{96,80},{112,128},{128,112... | collective-permute-start | bytes 239624 | tf_op jit(solution)/shard_map/ppermute | solution.py:368
  76.7 22.1 %all-to-all-start.3 = ((f32[16,1,128]{2,1,0:T(1,128)}), f32[16,1,128]{2,1,0:T(1,128)S(1)}, u32[]{:S(2)}, u32[]{:S(2)}) async-start(f32[16,1,128]{2,1,0:T(1,128)} %shard_map.95), calls=%async_computation.3 | async-start | bytes 16384 | tf_op jit(solution)/shard_map/all_to_all | solution.py:370
  131.7 10.9 %all-to-all-start.6 = ((f32[16,1,128]{2,1,0:T(1,128)}), f32[16,1,128]{2,1,0:T(1,128)S(1)}, u32[]{:S(2)}, u32[]{:S(2)}) async-start(f32[16,1,128]{2,1,0:T(1,128)} %get-tuple-element.31), calls=%async_computation.6 | async-start | bytes 16384 | tf_op jit(solution)/shard_map/all_to_all | solution.py:396

commit v7 on v6

--- a/solution.py
+++ b/solution.py
@@ -92,11 +92,14 @@
     return first + 0.5 * cols, (place[1] * rows).astype(F32) + 0.5 * rows, first
 
 
-def start_kernel(place, counts, contact, first_tool, positions, velocity, density, own, marks, tool, sent):
+def start_kernel(place, counts, contact, first_tool, positions, velocity, density, own, marks, tool, sent, arrived):
     cols, rows, slots = density.shape
+    parts = [(positions, own.at[0:2]), (velocity, own.at[2:4]), (density, own.at[4])]
+    copies = [pltpu.make_async_copy(part, to, arrived.at[n]) for n, (part, to) in enumerate(parts)]
+    for copy in copies:
+        copy.start()
     row = lax.broadcasted_iota(jnp.int32, (rows, slots), 0)
     slot = lax.broadcasted_iota(jnp.int32, (rows, slots), 1)
-    new = []
     for c in range(cols):
         filled = jnp.zeros((rows, slots), jnp.int32)
         touch = jnp.zeros((rows, slots), jnp.int32)
@@ -105,16 +108,16 @@
             touch = jnp.where(row == r, contact[c, r], touch)
         marks[0, c] = jnp.where(slot < filled, 1.0, 0.0)
         marks[1, c] = touch.astype(F32)
-        new.append([positions[0, c], positions[1, c], velocity[0, c], velocity[1, c], density[c]])
-        for f in range(5):
-            own[f, c] = new[c][f]
+    for copy in copies:
+        copy.wait()
+    new = [[own[f, c] for f in range(5)] for c in range(cols)]
     offset = jnp.zeros((1, slots), F32) + first_tool[0]
     tool[0:1] = offset
     tool[1:2] = jnp.zeros((1, slots), F32) + first_tool[1]
     fill_depth(place, new, marks, own_force(new, marks, offset, origin(place, cols, rows)[2]), sent)
 
 
-def extend_kernel(place, own, marks, got, wide):
+def extend_kernel(place, own, marks, got, inner, wide):
     depth, ndepth = place[1], got.shape[0]
     cols, rows = own.shape[1:3]
     above = got[jnp.maximum(depth - 1, 0)]
@@ -140,21 +143,23 @@
     force[...] = jnp.broadcast_to(jnp.sum(got[...], axis=0, keepdims=True), force.shape)
 
 
-def pair_sums(columns, center, out, feat, acc2, acc3):
+def pair_sums(columns, center, pairs, out, feat, acc2, acc3, earlier=None):
     x0, y0, _ = center
     tall, slots = columns[0][0].shape
-    rows = tall - 2
+    row0 = min(r for _, r in pairs)
+    rows = 1 + max(r for _, r in pairs) - row0
     for c, (x, y, u, v, s) in enumerate(columns):
         lx, ly = x - x0, y - y0
         press, inv = pressure(s)
-        parts = [jnp.ones_like(x), lx, ly, press, press * lx, press * ly, u, v, u * lx + v * ly, inv, inv * u, inv * v]
-        for k in range(16):
-            high = parts[k].astype(BF16).astype(F32) if k < 12 else jnp.zeros_like(x)
-            feat[pl.ds(c * tall * 32 + k, tall, stride=32), :] = high
-            feat[pl.ds(c * tall * 32 + 16 + k, tall, stride=32), :] = parts[k] - high if k < 12 else high
-    for i, (c, r) in enumerate([(c, r) for c in range(1, len(columns) - 1) for r in range(1, tall - 1)]):
+        parts = [jnp.ones_like(x), press, u, v, u * lx + v * ly]
+        for part in (lx, ly, press * lx, press * ly):
+            high = part.astype(BF16).astype(F32)
+            parts += [high, part - high]
+        parts += [inv, inv * u, inv * v]
+        for k, part in enumerate(parts):
+            feat[pl.ds(c * tall * 16 + k, tall, stride=16), :] = part
+    for i, ((c, r), around) in enumerate(pairs.items()):
         xi, yi = [jnp.broadcast_to(f[r : r + 1], (slots, slots)).T for f in columns[c][:2]]
-        around = [(c + a, r + b) for a in (-1, 0, 1) for b in (-1, 0, 1)]
 
         def weights(a, b):
             dx = (xi - columns[a][0][b : b + 1]).astype(BF16)
@@ -164,29 +169,49 @@
             return jnp.concatenate([q2, q2 * q], axis=0)
 
         total = None
-        for n in range(0, 9, 2):
+        for n in range(0, len(around), 2):
             pair = around[n : n + 2]
             w = jnp.concatenate([weights(a, b) for a, b in pair], axis=1)
-            f = jnp.concatenate([feat[pl.ds((a * tall + b) * 32, 32), :] for a, b in pair], axis=1).astype(BF16)
+            f = jnp.concatenate([feat[pl.ds((a * tall + b) * 16, 16), :] for a, b in pair], axis=1).astype(BF16)
             found = lax.dot_general(f, w, (((1,), (1,)), ((), ())), preferred_element_type=F32)
             total = found if total is None else total + found
-        acc2[i * 32 : (i + 1) * 32] = total[:, :slots]
-        acc3[i * 32 : (i + 1) * 32] = total[:, slots:]
-
-    for n in range(len(columns) - 2):
+        acc2[i * 16 : (i + 1) * 16] = total[:, :slots]
+        acc3[i * 16 : (i + 1) * 16] = total[:, slots:]
+
+    for n, c in enumerate(sorted({c for c, _ in pairs})):
 
         def summed(k):
-            acc = acc2 if k < 9 else acc3
-            return sum(acc[pl.ds(n * rows * 32 + k + low, rows, stride=32), :] for low in (0, 16))
-
-        x, y, u, v, s = [f[1 : rows + 1] for f in columns[n + 1]]
+            return (acc2 if k < 13 else acc3)[pl.ds(n * rows * 16 + k, rows, stride=16), :]
+
+        x, y, u, v, s = [f[row0 : row0 + rows] for f in columns[c]]
         x, y = x - x0, y - y0
         press, _ = pressure(s)
-        a0, ax, ay, ap, apx, apy, au, av, aw, b0, bu, bv = [summed(k) for k in range(12)]
+        a0, ap, au, av, aw = [summed(k) for k in range(5)]
+        ax, ay, apx, apy = [summed(k) + summed(k + 1) for k in range(5, 13, 2)]
+        b0, bu, bv = [summed(k) for k in range(13, 16)]
         sx, sy = x * a0 - ax, y * a0 - ay
-        out[0, n] = (6.0 * MASS) * (press * sx + x * ap - apx) - (VISCOSITY * MASS) * (u * b0 - bu)
-        out[1, n] = (6.0 * MASS) * (press * sy + y * ap - apy) - (VISCOSITY * MASS) * (v * b0 - bv)
-        out[2, n] = (-6.0 * MASS) * (u * sx + v * sy - x * au - y * av + aw)
+        rates = [
+            (6.0 * MASS) * (press * sx + x * ap - apx) - (VISCOSITY * MASS) * (u * b0 - bu),
+            (6.0 * MASS) * (press * sy + y * ap - apy) - (VISCOSITY * MASS) * (v * b0 - bv),
+            (-6.0 * MASS) * (u * sx + v * sy - x * au - y * av + aw),
+        ]
+        for f in range(3):
+            out[f, n] = rates[f]
+            if earlier is not None and 0 < n <= earlier.shape[1]:
+                inner = earlier[f, n - 1]
+                out[f, n, 1 : rows - 1] = rates[f][1 : rows - 1] + inner
+
+
+def around_cell(c, r):
+    return [(c + a, r + b) for a in (-1, 0, 1) for b in (-1, 0, 1)]
+
+
+def inner_rates_kernel(place, size, own, marks, out, feat, acc2, acc3):
+    cols, rows = size
+    columns = [visible([own[f, c] for f in range(5)], marks[0, c], marks[1, c])[:5] for c in range(cols)]
+    cells = [(c, r) for c in range(cols) for r in range(rows)]
+    pairs = {cell: [j for j in around_cell(*cell) if j in cells] for cell in cells}
+    pair_sums(columns, origin(place, *size), pairs, out, feat, acc2, acc3)
 
 
 def wide_columns(place, cols, wide, swapped, other):
@@ -205,14 +230,22 @@
     return columns
 
 
-def wide_rates_kernel(place, size, wide, swapped, other, out, feat, acc2, acc3):
-    columns = [fields[:5] for fields in wide_columns(place, size[0], wide, swapped, other)]
-    pair_sums(columns, origin(place, *size), out, feat, acc2, acc3)
+def wide_rates_kernel(place, size, wide, swapped, other, inner, out, feat, acc2, acc3):
+    cols, rows = size
+    columns = [fields[:5] for fields in wide_columns(place, cols, wide, swapped, other)]
+    block = [(c + cols, r + HALO) for c in range(cols) for r in range(rows)]
+    pairs = {}
+    for c in range(1, 3 * cols - 1):
+        for r in range(1, rows + 3):
+            pairs[c, r] = [j for j in around_cell(c, r) if (c, r) not in block or j not in block]
+    pair_sums(columns, origin(place, *size), pairs, out, feat, acc2, acc3, inner)
 
 
 def rates_kernel(place, size, ring, out, feat, acc2, acc3):
-    columns = [[ring[f, c] for f in range(5)] for c in range(ring.shape[1])]
-    pair_sums(columns, origin(place, *size), out, feat, acc2, acc3)
+    cols, rows = size
+    columns = [[ring[f, c] for f in range(5)] for c in range(cols + 2)]
+    pairs = {(c, r): around_cell(c, r) for c in range(1, cols + 1) for r in range(1, rows + 1)}
+    pair_sums(columns, origin(place, *size), pairs, out, feat, acc2, acc3)
 
 
 def moved_ring(place, columns, found, offset, first, ring):
@@ -353,31 +386,36 @@
     planes = [[(c + k) * ndepth + d for k in range(2) for d in range(ndepth)] for c in pairs]
     lines = [[(c + k) * ndepth + d for c in pairs] for k in range(2) for d in range(ndepth)]
     ring, ring_rates = shape(5, cols + 2, rows + 2, slots), shape(3, cols + 2, rows + 2, slots)
+    block_rates = shape(3, cols, rows, slots)
     swap = [(i, i ^ 1) for i in range(ncut)]
     cross = [(i, i + 1 if i % 2 else i - 1) for i in range(1, ncut - 1)]
 
-    def scratch(wide, tall):
-        return [pltpu.VMEM((n * 32, slots), F32) for n in (wide * tall, (wide - 2) * (tall - 2), (wide - 2) * (tall - 2))]
-
-    def rates_of(kernel, out, arrays, wide, tall):
-        return call(lambda place, *refs: kernel(place, (cols, rows), *refs), out, (place,), arrays, scratch(wide, tall), COST)
+    def rates_of(kernel, out, arrays, read, summed):
+        scratch = [pltpu.VMEM((n * 16, slots), F32) for n in (read, summed, summed)]
+        return call(lambda place, *refs: kernel(place, (cols, rows), *refs), out, (place,), arrays, scratch, COST)
 
     def exchange(own, marks, sent):
         got = lax.all_to_all(sent, "depth", 0, 0, tiled=True)
-        wide = call(extend_kernel, shape(6 * cols + 1, rows + 2 * HALO, slots), (place,), (own, marks, got))
+        inner = rates_of(inner_rates_kernel, block_rates, (own, marks), cols * rows, cols * rows)
+        wide = call(extend_kernel, shape(6 * cols + 1, rows + 2 * HALO, slots), (place,), (own, marks, got, inner))
         swapped, other = lax.ppermute(wide, "cut", swap), lax.ppermute(wide, "cut", cross)
         force = call(pair_force_kernel, along_line, (), (wide, swapped))
         total = lax.all_to_all(force, both, 0, 0, tiled=True, axis_index_groups=lines)
-        found = rates_of(wide_rates_kernel, ring_rates, (wide, swapped, other), 3 * cols, rows + 4)
+        found = rates_of(wide_rates_kernel, ring_rates, (wide, swapped, other, inner), 3 * cols * (rows + 4), (cols + 2) * (rows + 2))
         return found, (wide, swapped, other), total
 
-    own, marks, tool, sent = call(
-        start_kernel, [state, marking, vector, message], (place, counts, contact_mask, tool), (positions, velocity, density)
-    )
+    own, marks, tool, sent = pl.pallas_call(
+        start_kernel,
+        out_shape=[state, marking, vector, message],
+        in_specs=[SMEM] * 4 + [pl.BlockSpec(memory_space=pl.ANY)] * 3,
+        out_specs=[VMEM] * 4,
+        scratch_shapes=[pltpu.SemaphoreType.DMA((3,))],
+        compiler_params=pltpu.CompilerParams(vmem_limit_bytes=60 * 1024 * 1024),
+    )(place, counts, contact_mask, tool, positions, velocity, density)
     found, around, total = exchange(own, marks, sent)
     own, ringed = call(first_update_kernel, [state, ring], (place,), (own, found, marks, *around, tool))
 
-    found = rates_of(rates_kernel, shape(3, cols, rows, slots), (ringed,), cols + 2, rows + 2)
+    found = rates_of(rates_kernel, block_rates, (ringed,), (cols + 2) * (rows + 2), cols * rows)
     kernel = functools.partial(second_update_kernel, scale)
     own, tool, sent = call(kernel, [state, vector, message], (place,), (own, found, marks, tool, total))
 
@@ -390,7 +428,7 @@
     got = lax.all_to_all(force, both, 0, 0, tiled=True, axis_index_groups=planes)
     force = call(spread_kernel, along_line, (), (got,))
     total = lax.all_to_all(force, both, 0, 0, tiled=True, axis_index_groups=lines)
-    found = rates_of(rates_kernel, shape(3, cols, rows, slots), (ringed,), cols + 2, rows + 2)
+    found = rates_of(rates_kernel, block_rates, (ringed,), (cols + 2) * (rows + 2), cols * rows)
     kernel = functools.partial(last_force_kernel, scale)
     tool, force = call(kernel, [vector, along_depth], (place,), (own, marks, tool, total))
     total = lax.all_to_all(force, "depth", 0, 0, tiled=True)

time: 181 us -> 178 us (0.983)
  blocking collectives: 94.3 us -> 63.3 us
  waiting for transfers between devices: 7.62 us -> 23 us
  starting transfers between devices: 41.5 us -> 53.1 us
    all_to_all x2 -> x0, blocking collectives: 28 us -> none  [exchange(): got = lax.all_to_all(sent, 'depth', 0, 0, tiled=True)]
    all_to_all x0 -> x2, waiting for transfers between devices: none -> 12.8 us  [exchange(): got = lax.all_to_all(sent, 'depth', 0, 0, tiled=True)]
    all_to_all x0 -> x2, starting transfers between devices: none -> 10.9 us  [exchange(): got = lax.all_to_all(sent, 'depth', 0, 0, tiled=True)]
    all_to_all x1, blocking collectives: 20.6 us -> 17.6 us  [body(): lax.all_to_all(force, both, 0, 0, tiled=True, axis_index_groups=lines)]
    all_to_all x2, waiting for transfers between devices: 1.38 us -> 4.42 us  [exchange(): lax.all_to_all(force, both, 0, 0, tiled=True, axis_index_groups=lines)]
    pallas_call x0 -> x1, Pallas kernels: none -> 2.31 us  [body(): pl.pallas_call(start_kernel, out_shape=[state, marking, vector, message],...]
    pallas_call x16 -> x17, Pallas kernels: 32.2 us -> 30.2 us  [call(): pl.pallas_call(kernel, out_shape=outs, in_specs=[SMEM] * len(scalars) + [...]
  transfers between devices with their start and end apart: 7 -> 9, of which waited for: 4 -> 6; matrix products, arithmetic and copies ran while one was open for 0% -> 0% of each run, Pallas kernels for 15% -> 14%
where the time goes in v7:
time: 178 us; the launch traced here: 177 us
  blocking collectives  63.3 us (36%)
  starting transfers between devices  53.1 us (30%)
  Pallas kernels  33.7 us (19%)
  waiting for transfers between devices  23 us (13%)
  local copies, waits for them, and re-layouts  1.91 us (1%)
    pallas_call x17, Pallas kernels, call(): pl.pallas_call(kernel, out_shape=outs, in_specs=[SMEM] * len(scalars) + [...  30.2 us
    all_to_all x2, starting transfers between devices, exchange(): lax.all_to_all(force, both, 0, 0, tiled=True, axis_index_groups=lines)  26.8 us
    all_to_all x1, blocking collectives, body(): got = lax.all_to_all(sent, 'cut', 0, 0, tiled=True, axis_index_groups=apart)  21 us
    all_to_all x1, blocking collectives, body(): lax.all_to_all(force, both, 0, 0, tiled=True, axis_index_groups=lines)  17.6 us
    all_to_all x1, blocking collectives, body(): got = lax.all_to_all(sent, 'cut', 0, 0, tiled=True, axis_index_groups=close)  14.4 us
    all_to_all x2, waiting for transfers between devices, exchange(): got = lax.all_to_all(sent, 'depth', 0, 0, tiled=True)  12.8 us
    all_to_all x2, starting transfers between devices, exchange(): got = lax.all_to_all(sent, 'depth', 0, 0, tiled=True)  10.9 us
    all_to_all x1, blocking collectives, body(): lax.all_to_all(force, both, 0, 0, tiled=True, axis_index_groups=planes)  10.3 us
  transfers between devices with their start and end apart: 9, of which 6 were waited for; matrix products, arithmetic and copies ran while one was open for 0% of the time, Pallas kernels for 14%

profile of v7, /device:TPU:64, one launch (start us, length us, event | category | flops | bytes accessed | tf_op | source)
XLA Modules:
  0.0 176.7 jit_solution(10553184023381452124)
XLA Ops:
  0.6 0.0 copy-start.4
  0.6 0.6 copy-done.4
  1.3 0.6 pad_add_fusion.place
  1.9 2.3 %shard_map.86 = (f32[5,2,8,128]{3,2,1,0:T(8,128)}, f32[2,2,8,128]{3,2,1,0:T(8,128)}, f32[2,128]{1,0:T(2,128)}, f32[16,32,128]{2,1,0:T(8,128)}) custom-call(s32[35]{0:T(128)} %pad_add_fusion.place, s32[2,8]{1,0:T(2,128)} %counts.1, s32[2,8]{1,0:T(2,128)} %contact.1, f32[2]{0:T(128)} %first_tool.1, f32[2,2,8,128]{3,2,1,0:T(8,128)} %positions.1, ...), custom_call_target="tpu_custom_call" | custom-call | tf_op jit(solution)/shard_map/pallas_call | solution.py:407
  4.2 0.0 copy-start
  4.2 0.0 copy-start.1
  4.2 7.2 %all-to-all-start = ((f32[16,32,128]{2,1,0:T(8,128)}), f32[16,32,128]{2,1,0:T(8,128)S(1)}, u32[]{:S(2)}, u32[]{:S(2)}) async-start(f32[16,32,128]{2,1,0:T(8,128)} %get-tuple-element.19), calls=%async_computation | async-start | bytes 524288 | tf_op jit(solution)/shard_map/all_to_all | solution.py:398
  11.4 0.0 copy-start.2
  11.5 0.6 copy-done.2
  12.1 2.4 %shard_map.87.inner.refs_3_ = f32[3,2,8,128]{3,2,1,0:T(8,128)S(1)} custom-call(s32[35]{0:T(128)S(1)} %copy-done.2, f32[5,2,8,128]{3,2,1,0:T(8,128)S(1)} %copy-done.1, f32[2,2,8,128]{3,2,1,0:T(8,128)S(1)} %copy-done), custom_call_target="tpu_custom_call" | custom-call | flops 20000000000 | bytes 1048576 | tf_op jit(solution)/shard_map/pallas_call | solution.py:33
  14.5 6.2 %all-to-all-done.got = f32[16,32,128]{2,1,0:T(8,128)S(1)} async-done(((f32[16,32,128]{2,1,0:T(8,128)}), f32[16,32,128]{2,1,0:T(8,128)S(1)}, u32[]{:S(2)}, u32[]{:S(2)}) %all-to-all-start) | async-done | bytes 262176 | tf_op jit(solution)/shard_map/all_to_all | solution.py:398
  20.6 0.6 shard_map.88.refs_0_.wide
  21.2 2.6 %collective-permute-start = (f32[13,12,128]{2,1,0:T(8,128)S(1)}, f32[13,12,128]{2,1,0:T(8,128)S(1)}, u32[]{:S(2)}, u32[]{:S(2)}) collective-permute-start(f32[13,12,128]{2,1,0:T(8,128)S(1)} %shard_map.88.refs_0_.wide), channel_id=1, source_target_pairs={{0,16},{16,0},{32,48},{48,32},{64,80},{80,64},{96,112},{112,96},{1... | collective-permute-start | bytes 239624 | tf_op jit(solution)/shard_map/ppermute | solution.py:401
  23.8 2.8 %collective-permute-start.1 = (f32[13,12,128]{2,1,0:T(8,128)S(1)}, f32[13,12,128]{2,1,0:T(8,128)S(1)}, u32[]{:S(2)}, u32[]{:S(2)}) collective-permute-start(f32[13,12,128]{2,1,0:T(8,128)S(1)} %shard_map.88.refs_0_.wide), channel_id=1, source_target_pairs={{16,32},{32,16},{48,64},{64,48},{80,96},{96,80},{112,128},{128,112... | collective-permute-start | bytes 239624 | tf_op jit(solution)/shard_map/ppermute | solution.py:401
  26.6 1.5 collective-permute-done.refs_1_.swapped
  28.1 0.6 shard_map.92
  28.7 14.8 %all-to-all-start.1 = ((f32[16,1,128]{2,1,0:T(1,128)}), f32[16,1,128]{2,1,0:T(1,128)S(1)}, u32[]{:S(2)}, u32[]{:S(2)}) async-start(f32[16,1,128]{2,1,0:T(1,128)} %shard_map.92), calls=%async_computation.1 | async-start | bytes 16384 | tf_op jit(solution)/shard_map/all_to_all | solution.py:403
  43.5 0.0 collective-permute-done.1.refs_2_.other
  43.5 5.6 %shard_map.89.found = f32[3,4,10,128]{3,2,1,0:T(8,128)S(1)} custom-call(s32[35]{0:T(128)S(1)} %copy-done.2, f32[13,12,128]{2,1,0:T(8,128)S(1)} %shard_map.88.refs_0_.wide, f32[13,12,128]{2,1,0:T(8,128)S(1)} %collective-permute-done.refs_1_.swapped, f32[13,12,128]{2,1,0:T(8,128)S(1)} %collective-permute-done.1.refs_2_.other, ...), custom_call_target="tpu_custom_call" | custom-call | flops 20000000000 | bytes 1048576 | tf_op jit(solution)/shard_map/pallas_call | solution.py:33
  49.1 0.6 copy-done.3
  49.8 0.6 shard_map.90
  50.4 3.3 %shard_map.91.found = f32[3,2,8,128]{3,2,1,0:T(8,128)S(1)} custom-call(s32[35]{0:T(128)S(1)} %copy-done.2, f32[5,4,10,128]{3,2,1,0:T(8,128)S(1)} %get-tuple-element.22.refs_0_), custom_call_target="tpu_custom_call" | custom-call | flops 20000000000 | bytes 1048576 | tf_op jit(solution)/shard_map/pallas_call | solution.py:33
  53.7 0.0 all-to-all-done.1.total
  53.7 1.4 shard_map.93
  55.1 3.7 %all-to-all-start.2 = ((f32[16,32,128]{2,1,0:T(8,128)}), f32[16,32,128]{2,1,0:T(8,128)S(1)}, u32[]{:S(2)}, u32[]{:S(2)}) async-start(f32[16,32,128]{2,1,0:T(8,128)} %get-tuple-element.24), calls=%async_computation.2 | async-start | bytes 524288 | tf_op jit(solution)/shard_map/all_to_all | solution.py:398
  58.8 2.4 %shard_map.94.inner.refs_3_ = f32[3,2,8,128]{3,2,1,0:T(8,128)S(1)} custom-call(s32[35]{0:T(128)S(1)} %copy-done.2, f32[5,2,8,128]{3,2,1,0:T(8,128)S(1)} %get-tuple-element.23.refs_0_.own, f32[2,2,8,128]{3,2,1,0:T(8,128)S(1)} %copy-done), custom_call_target="tpu_custom_call" | custom-call | flops 20000000000 | bytes 1048576 | tf_op jit(solution)/shard_map/pallas_call | solution.py:33
  61.2 6.6 %all-to-all-done.2.got = f32[16,32,128]{2,1,0:T(8,128)S(1)} async-done(((f32[16,32,128]{2,1,0:T(8,128)}), f32[16,32,128]{2,1,0:T(8,128)S(1)}, u32[]{:S(2)}, u32[]{:S(2)}) %all-to-all-start.2) | async-done | bytes 262176 | tf_op jit(solution)/shard_map/all_to_all | solution.py:398
  67.8 0.6 shard_map.95.refs_0_.wide
  68.4 2.6 %collective-permute-start.2 = (f32[13,12,128]{2,1,0:T(8,128)S(1)}, f32[13,12,128]{2,1,0:T(8,128)S(1)}, u32[]{:S(2)}, u32[]{:S(2)}) collective-permute-start(f32[13,12,128]{2,1,0:T(8,128)S(1)} %shard_map.95.refs_0_.wide), channel_id=1, source_target_pairs={{0,16},{16,0},{32,48},{48,32},{64,80},{80,64},{96,112},{112,96},{1... | collective-permute-start | bytes 239624 | tf_op jit(solution)/shard_map/ppermute | solution.py:401
  71.0 4.0 %collective-permute-start.3 = (f32[13,12,128]{2,1,0:T(8,128)S(1)}, f32[13,12,128]{2,1,0:T(8,128)S(1)}, u32[]{:S(2)}, u32[]{:S(2)}) collective-permute-start(f32[13,12,128]{2,1,0:T(8,128)S(1)} %shard_map.95.refs_0_.wide), channel_id=1, source_target_pairs={{16,32},{32,16},{48,64},{64,48},{80,96},{96,80},{112,128},{128,112... | collective-permute-start | bytes 239624 | tf_op jit(solution)/shard_map/ppermute | solution.py:401
  75.0 0.2 collective-permute-done.2.refs_1_.swapped
  75.2 0.6 shard_map.97
  75.8 12.0 %all-to-all-start.3 = ((f32[16,1,128]{2,1,0:T(1,128)}), f32[16,1,128]{2,1,0:T(1,128)S(1)}, u32[]{:S(2)}, u32[]{:S(2)}) async-start(f32[16,1,128]{2,1,0:T(1,128)} %shard_map.97), calls=%async_computation.3 | async-start | bytes 16384 | tf_op jit(solution)/shard_map/all_to_all | solution.py:403
  87.9 0.0 collective-permute-done.3.refs_2_.other
  87.9 5.6 %shard_map.96.found = f32[3,4,10,128]{3,2,1,0:T(8,128)S(1)} custom-call(s32[35]{0:T(128)S(1)} %copy-done.2, f32[13,12,128]{2,1,0:T(8,128)S(1)} %shard_map.95.refs_0_.wide, f32[13,12,128]{2,1,0:T(8,128)S(1)} %collective-permute-done.2.refs_1_.swapped, f32[13,12,128]{2,1,0:T(8,128)S(1)} %collective-permute-done.3.refs_2_.other, ...), custom_call_target="tpu_custom_call" | custom-call | flops 20000000000 | bytes 1048576 | tf_op jit(solution)/shard_map/pallas_call | solution.py:33
  93.5 4.4 %all-to-all-done.3.total = f32[16,1,128]{2,1,0:T(1,128)S(1)} async-done(((f32[16,1,128]{2,1,0:T(1,128)}), f32[16,1,128]{2,1,0:T(1,128)S(1)}, u32[]{:S(2)}, u32[]{:S(2)}) %all-to-all-start.3) | async-done | bytes 8224 | tf_op jit(solution)/shard_map/all_to_all | solution.py:403
  97.9 0.7 shard_map.98
  98.6 10.3 %all_to_all.45.got = f32[32,1,128]{2,1,0:T(1,128)S(1)} all-to-all(f32[32,1,128]{2,1,0:T(1,128)S(1)} %get-tuple-element.29), channel_id=1, replica_groups={{0,1,2,3,4,5,6,7,8,9,10,11,12,13,14,15,16,17,18,19,20,21,22,23,24,25,26..., dimensions={0} | all-to-all | bytes 32768 | tf_op jit(solution)/shard_map/all_to_all | solution.py:428
  109.0 17.6 %all_to_all.46.total = f32[16,1,128]{2,1,0:T(1,128)S(1)} all-to-all(f32[16,1,128]{2,1,0:T(1,128)S(1)} %shard_map.100), channel_id=1, replica_groups={{0,32,64,96,128,160,192,224,256,288,320,352,384,416,448,480},{1,33,65,9..., dimensions={0} | all-to-all | bytes 16384 | tf_op jit(solution)/shard_map/all_to_all | solution.py:430
  126.5 1.3 shard_map.101
  127.8 3.5 %all-to-all-start.6 = ((f32[16,1,128]{2,1,0:T(1,128)}), f32[16,1,128]{2,1,0:T(1,128)S(1)}, u32[]{:S(2)}, u32[]{:S(2)}) async-start(f32[16,1,128]{2,1,0:T(1,128)} %get-tuple-element.31), calls=%async_computation.6 | async-start | bytes 16384 | tf_op jit(solution)/shard_map/all_to_all | solution.py:434
  131.3 3.3 %shard_map.99.found = f32[3,2,8,128]{3,2,1,0:T(8,128)S(1)} custom-call(s32[35]{0:T(128)S(1)} %copy-done.2, f32[5,4,10,128]{3,2,1,0:T(8,128)S(1)} %get-tuple-element.27.refs_0_), custom_call_target="tpu_custom_call" | custom-call | flops 20000000000 | bytes 1048576 | tf_op jit(solution)/shard_map/pallas_call | solution.py:33
  134.6 4.1 %all-to-all-done.6.total = f32[16,1,128]{2,1,0:T(1,128)S(1)} async-done(((f32[16,1,128]{2,1,0:T(1,128)}), f32[16,1,128]{2,1,0:T(1,128)S(1)}, u32[]{:S(2)}, u32[]{:S(2)}) %all-to-all-start.6) | async-done | bytes 8224 | tf_op jit(solution)/shard_map/all_to_all | solution.py:434
  138.7 0.6 shard_map.102
  139.3 14.4 %all_to_all.47.got = f32[8,88,128]{2,1,0:T(8,128)S(1)} all-to-all(f32[8,88,128]{2,1,0:T(8,128)S(1)} %shard_map.102), channel_id=1, replica_groups={{0,16,32,48,64,80,96,112},{128,144,160,176,192,208,224,240},{256,272,28..., dimensions={0} | all-to-all | bytes 720896 | tf_op jit(solution)/shard_map/all_to_all | solution.py:439
  153.7 0.6 shard_map.103
  154.4 21.0 %all_to_all.48.got = f32[4,88,128]{2,1,0:T(8,128)S(1)} all-to-all(f32[4,88,128]{2,1,0:T(8,128)S(1)} %shard_map.103), channel_id=1, replica_groups={{0,128,256,384},{16,144,272,400},{32,160,288,416},{48,176,304,432},{64,..., dimensions={0} | all-to-all | bytes 360448 | tf_op jit(solution)/shard_map/all_to_all | solution.py:441
  175.4 1.2 shard_map.104
  (4 shorter events, 0.0 us)
Async XLA Ops:
  0.6 0.7 copy-start.4
  4.2 7.2 %copy-start = (f32[2,2,8,128]{3,2,1,0:T(8,128)S(1)}, f32[2,2,8,128]{3,2,1,0:T(8,128)}, u32[]{:S(2)}) copy-start(f32[2,2,8,128]{3,2,1,0:T(8,128)} %get-tuple-element.18.refs_1_.marks) | copy-start | bytes 49156
  4.2 7.2 %copy-start.1 = (f32[5,2,8,128]{3,2,1,0:T(8,128)S(1)}, f32[5,2,8,128]{3,2,1,0:T(8,128)}, u32[]{:S(2)}) copy-start(f32[5,2,8,128]{3,2,1,0:T(8,128)} %get-tuple-element.17.refs_0_.own) | copy-start | bytes 122884
  4.2 16.4 %all-to-all-start = ((f32[16,32,128]{2,1,0:T(8,128)}), f32[16,32,128]{2,1,0:T(8,128)S(1)}, u32[]{:S(2)}, u32[]{:S(2)}) async-start(f32[16,32,128]{2,1,0:T(8,128)} %get-tuple-element.19), calls=%async_computation | async-start | bytes 524288 | tf_op jit(solution)/shard_map/all_to_all | solution.py:398
  11.4 0.6 copy-start.2
  21.2 6.9 %collective-permute-start = (f32[13,12,128]{2,1,0:T(8,128)S(1)}, f32[13,12,128]{2,1,0:T(8,128)S(1)}, u32[]{:S(2)}, u32[]{:S(2)}) collective-permute-start(f32[13,12,128]{2,1,0:T(8,128)S(1)} %shard_map.88.refs_0_.wide), channel_id=1, source_target_pairs={{0,16},{16,0},{32,48},{48,32},{64,80},{80,64},{96,112},{112,96},{1... | collective-permute-start | bytes 239624 | tf_op jit(solution)/shard_map/ppermute | solution.py:401
  23.8 19.7 %collective-permute-start.1 = (f32[13,12,128]{2,1,0:T(8,128)S(1)}, f32[13,12,128]{2,1,0:T(8,128)S(1)}, u32[]{:S(2)}, u32[]{:S(2)}) collective-permute-start(f32[13,12,128]{2,1,0:T(8,128)S(1)} %shard_map.88.refs_0_.wide), channel_id=1, source_target_pairs={{16,32},{32,16},{48,64},{64,48},{80,96},{96,80},{112,128},{128,112... | collective-permute-start | bytes 239624 | tf_op jit(solution)/shard_map/ppermute | solution.py:401
  28.7 25.0 %all-to-all-start.1 = ((f32[16,1,128]{2,1,0:T(1,128)}), f32[16,1,128]{2,1,0:T(1,128)S(1)}, u32[]{:S(2)}, u32[]{:S(2)}) async-start(f32[16,1,128]{2,1,0:T(1,128)} %shard_map.92), calls=%async_computation.1 | async-start | bytes 16384 | tf_op jit(solution)/shard_map/all_to_all | solution.py:403
  49.1 0.7 copy-start.3
  55.1 12.7 %all-to-all-start.2 = ((f32[16,32,128]{2,1,0:T(8,128)}), f32[16,32,128]{2,1,0:T(8,128)S(1)}, u32[]{:S(2)}, u32[]{:S(2)}) async-start(f32[16,32,128]{2,1,0:T(8,128)} %get-tuple-element.24), calls=%async_computation.2 | async-start | bytes 524288 | tf_op jit(solution)/shard_map/all_to_all | solution.py:398
  68.4 6.9 %collective-permute-start.2 = (f32[13,12,128]{2,1,0:T(8,128)S(1)}, f32[13,12,128]{2,1,0:T(8,128)S(1)}, u32[]{:S(2)}, u32[]{:S(2)}) collective-permute-start(f32[13,12,128]{2,1,0:T(8,128)S(1)} %shard_map.95.refs_0_.wide), channel_id=1, source_target_pairs={{0,16},{16,0},{32,48},{48,32},{64,80},{80,64},{96,112},{112,96},{1... | collective-permute-start | bytes 239624 | tf_op jit(solution)/shard_map/ppermute | solution.py:401
  71.0 16.9 %collective-permute-start.3 = (f32[13,12,128]{2,1,0:T(8,128)S(1)}, f32[13,12,128]{2,1,0:T(8,128)S(1)}, u32[]{:S(2)}, u32[]{:S(2)}) collective-permute-start(f32[13,12,128]{2,1,0:T(8,128)S(1)} %shard_map.95.refs_0_.wide), channel_id=1, source_target_pairs={{16,32},{32,16},{48,64},{64,48},{80,96},{96,80},{112,128},{128,112... | collective-permute-start | bytes 239624 | tf_op jit(solution)/shard_map/ppermute | solution.py:401
  75.8 22.1 %all-to-all-start.3 = ((f32[16,1,128]{2,1,0:T(1,128)}), f32[16,1,128]{2,1,0:T(1,128)S(1)}, u32[]{:S(2)}, u32[]{:S(2)}) async-start(f32[16,1,128]{2,1,0:T(1,128)} %shard_map.97), calls=%async_computation.3 | async-start | bytes 16384 | tf_op jit(solution)/shard_map/all_to_all | solution.py:403
  127.8 10.9 %all-to-all-start.6 = ((f32[16,1,128]{2,1,0:T(1,128)}), f32[16,1,128]{2,1,0:T(1,128)S(1)}, u32[]{:S(2)}, u32[]{:S(2)}) async-start(f32[16,1,128]{2,1,0:T(1,128)} %get-tuple-element.31), calls=%async_computation.6 | async-start | bytes 16384 | tf_op jit(solution)/shard_map/all_to_all | solution.py:434

commit v8 on v7

--- a/solution.py
+++ b/solution.py
@@ -23,6 +23,14 @@
 PARAMS = pltpu.CompilerParams(vmem_limit_bytes=40 * 1024 * 1024)
 VMEM = pl.BlockSpec(memory_space=pltpu.VMEM)
 SMEM = pl.BlockSpec(memory_space=pltpu.SMEM)
+
+
+def here():
+    return lax.axis_index("cut")
+
+
+def row_block():
+    return lax.axis_index("depth")
 
 
 def shape(*dims):
@@ -64,8 +72,8 @@
     return [jnp.where(alive, x, FAR), y, u, v, jnp.where(alive, rho, 1.0), live * touch]
 
 
-def fill_depth(place, state, marks, force, sent):
-    depth, ndepth = place[1], sent.shape[0]
+def fill_depth(state, marks, force, sent):
+    depth, ndepth = row_block(), sent.shape[0]
     cols, rows = marks.shape[1:3]
     row = 6 * cols * HALO
     sent[...] = jnp.zeros(sent.shape, F32)
@@ -87,12 +95,12 @@
         put(depth + 1, rows - HALO)
 
 
-def origin(place, cols, rows):
-    first = (place[0] * cols).astype(F32)
-    return first + 0.5 * cols, (place[1] * rows).astype(F32) + 0.5 * rows, first
-
-
-def start_kernel(place, counts, contact, first_tool, positions, velocity, density, own, marks, tool, sent, arrived):
+def origin(cols, rows):
+    first = (here() * cols).astype(F32)
+    return first + 0.5 * cols, (row_block() * rows).astype(F32) + 0.5 * rows, first
+
+
+def start_kernel(counts, contact, first_tool, positions, velocity, density, own, marks, tool, sent, arrived):
     cols, rows, slots = density.shape
     parts = [(positions, own.at[0:2]), (velocity, own.at[2:4]), (density, own.at[4])]
     copies = [pltpu.make_async_copy(part, to, arrived.at[n]) for n, (part, to) in enumerate(parts)]
@@ -114,11 +122,11 @@
     offset = jnp.zeros((1, slots), F32) + first_tool[0]
     tool[0:1] = offset
     tool[1:2] = jnp.zeros((1, slots), F32) + first_tool[1]
-    fill_depth(place, new, marks, own_force(new, marks, offset, origin(place, cols, rows)[2]), sent)
-
-
-def extend_kernel(place, own, marks, got, inner, wide):
-    depth, ndepth = place[1], got.shape[0]
+    fill_depth(new, marks, own_force(new, marks, offset, origin(cols, rows)[2]), sent)
+
+
+def extend_kernel(own, marks, got, inner, wide):
+    depth, ndepth = row_block(), got.shape[0]
     cols, rows = own.shape[1:3]
     above = got[jnp.maximum(depth - 1, 0)]
     below = got[jnp.minimum(depth + 1, ndepth - 1)]
@@ -206,20 +214,20 @@
     return [(c + a, r + b) for a in (-1, 0, 1) for b in (-1, 0, 1)]
 
 
-def inner_rates_kernel(place, size, own, marks, out, feat, acc2, acc3):
+def inner_rates_kernel(size, own, marks, out, feat, acc2, acc3):
     cols, rows = size
     columns = [visible([own[f, c] for f in range(5)], marks[0, c], marks[1, c])[:5] for c in range(cols)]
     cells = [(c, r) for c in range(cols) for r in range(rows)]
     pairs = {cell: [j for j in around_cell(*cell) if j in cells] for cell in cells}
-    pair_sums(columns, origin(place, *size), pairs, out, feat, acc2, acc3)
-
-
-def wide_columns(place, cols, wide, swapped, other):
-    even = lax.rem(place[0], 2) == 0
+    pair_sums(columns, origin(*size), pairs, out, feat, acc2, acc3)
+
+
+def wide_columns(cols, wide, swapped, other):
+    even = lax.rem(here(), 2) == 0
     blank = [FAR, 0.0, 0.0, 0.0, 1.0, 0.0]
     columns = []
     for side in range(3):
-        outside = place[0] == (0 if side == 0 else place[2] - 1)
+        outside = here() == (0 if side == 0 else lax.axis_size("cut") - 1)
         for c in range(cols):
             if side == 1:
                 fields = [wide[f * cols + c] for f in range(6)]
@@ -230,25 +238,25 @@
     return columns
 
 
-def wide_rates_kernel(place, size, wide, swapped, other, inner, out, feat, acc2, acc3):
+def wide_rates_kernel(size, wide, swapped, other, inner, out, feat, acc2, acc3):
     cols, rows = size
-    columns = [fields[:5] for fields in wide_columns(place, cols, wide, swapped, other)]
+    columns = [fields[:5] for fields in wide_columns(cols, wide, swapped, other)]
     block = [(c + cols, r + HALO) for c in range(cols) for r in range(rows)]
     pairs = {}
     for c in range(1, 3 * cols - 1):
         for r in range(1, rows + 3):
             pairs[c, r] = [j for j in around_cell(c, r) if (c, r) not in block or j not in block]
-    pair_sums(columns, origin(place, *size), pairs, out, feat, acc2, acc3, inner)
-
-
-def rates_kernel(place, size, ring, out, feat, acc2, acc3):
+    pair_sums(columns, origin(*size), pairs, out, feat, acc2, acc3, inner)
+
+
+def rates_kernel(size, ring, out, feat, acc2, acc3):
     cols, rows = size
     columns = [[ring[f, c] for f in range(5)] for c in range(cols + 2)]
     pairs = {(c, r): around_cell(c, r) for c in range(1, cols + 1) for r in range(1, rows + 1)}
-    pair_sums(columns, origin(place, *size), pairs, out, feat, acc2, acc3)
-
-
-def moved_ring(place, columns, found, offset, first, ring):
+    pair_sums(columns, origin(*size), pairs, out, feat, acc2, acc3)
+
+
+def moved_ring(columns, found, offset, first, ring):
     for n in range(ring.shape[1]):
         x, y, u, v, s, touch = [f[1:-1] for f in columns[n + 1]]
         live = jnp.where(x < 0.5 * FAR, 1.0, 0.0)
@@ -290,76 +298,77 @@
     return tool[0:1] + DT * speed, speed
 
 
-def first_update_kernel(place, own, found, marks, wide, swapped, other, tool, new_own, ring):
-    first = origin(place, *own.shape[1:3])[2]
+def first_update_kernel(size, own, found, marks, wide, swapped, other, tool, new_own, out, feat, acc2, acc3, ring):
+    first = origin(*size)[2]
     keep(moved_state(own, found, marks, tool[0:1], first), new_own)
-    moved_ring(place, wide_columns(place, own.shape[1], wide, swapped, other), found, tool[0:1], first, ring)
-
-
-def second_update_kernel(scale, place, own, found, marks, tool, total, new_own, new_tool, sent):
-    first = origin(place, *own.shape[1:3])[2]
+    moved_ring(wide_columns(size[0], wide, swapped, other), found, tool[0:1], first, ring)
+    rates_kernel(size, ring, out, feat, acc2, acc3)
+
+
+def second_update_kernel(scale, own, found, marks, tool, total, new_own, new_tool, sent):
+    first = origin(*own.shape[1:3])[2]
     offset, speed = tool_step(tool, jnp.sum(total[...], axis=0), scale)
     new_tool[0:1] = offset
     new_tool[1:2] = speed
     state = [[own[f, c] for f in range(5)] for c in range(own.shape[1])]
     new = moved_state(own, found, marks, offset, first)
     keep(new, new_own)
-    fill_depth(place, new, marks, own_force(state, marks, offset, first), sent)
-
-
-def third_update_kernel(scale, place, own, found, marks, wide, swapped, other, tool, total, new_own, ring, new_tool, force):
-    first = origin(place, *own.shape[1:3])[2]
+    fill_depth(new, marks, own_force(state, marks, offset, first), sent)
+
+
+def third_update_kernel(scale, own, found, marks, wide, swapped, other, tool, total, new_own, ring, new_tool, force):
+    first = origin(*own.shape[1:3])[2]
     offset, speed = tool_step(tool, jnp.sum(total[...], axis=0), scale)
     new_tool[0:1] = offset
     new_tool[1:2] = speed
     state = [[own[f, c] for f in range(5)] for c in range(own.shape[1])]
     force[...] = jnp.broadcast_to(own_force(state, marks, offset, first)[None], force.shape)
     keep(moved_state(own, found, marks, offset, first), new_own)
-    moved_ring(place, wide_columns(place, own.shape[1], wide, swapped, other), found, offset, first, ring)
-
-
-def last_force_kernel(scale, place, own, marks, tool, total, new_tool, force):
+    moved_ring(wide_columns(own.shape[1], wide, swapped, other), found, offset, first, ring)
+
+
+def last_force_kernel(scale, own, marks, tool, total, new_tool, force):
     offset, speed = tool_step(tool, jnp.sum(total[...], axis=0), scale)
     new_tool[0:1] = offset
     new_tool[1:2] = speed
     state = [[own[f, c] for f in range(5)] for c in range(own.shape[1])]
-    part = own_force(state, marks, offset, origin(place, *own.shape[1:3])[2])
+    part = own_force(state, marks, offset, origin(*own.shape[1:3])[2])
     force[...] = jnp.broadcast_to(part[None], force.shape)
 
 
-def last_kernel(near, place, own, found, marks, tool, total, sent):
+def last_kernel(near, destination, own, found, marks, tool, total, sent):
     cols, rows, slots = own.shape[1:]
     size = 5 * cols * rows
-    new = moved_state(own, found, marks, tool[0:1], origin(place, cols, rows)[2])
+    new = moved_state(own, found, marks, tool[0:1], origin(cols, rows)[2])
     sent[...] = jnp.zeros(sent.shape, F32)
     sent[:, size:, :] = jnp.broadcast_to(jnp.sum(total[...], axis=0, keepdims=True), (near, sent.shape[1] - size, slots))
-    digit = lax.rem(place[3 + place[0]], near)
+    digit = lax.rem(destination[here()], near)
     for f in range(5):
         for c in range(cols):
             at = (f * cols + c) * rows
             sent[digit, at : at + rows] = new[c][f]
 
 
-def sort_kernel(near, size, place, got, sent):
+def sort_kernel(near, size, destination, got, sent):
     far, most, slots = sent.shape
-    group, digit = lax.div(place[0], near), lax.rem(place[0], near)
+    group, digit = lax.div(here(), near), lax.rem(here(), near)
     sent[...] = jnp.zeros(sent.shape, F32)
     total = jnp.sum(got[:, size : size + 1, :], axis=0, keepdims=True)
     sent[:, size:, :] = jnp.broadcast_to(total, (far, most - size, slots))
     for k in range(near):
-        target = place[3 + group * near + k]
+        target = destination[group * near + k]
 
         @pl.when(lax.rem(target, near) == digit)
         def _():
             sent[lax.div(target, near), 0:size] = got[k, 0:size]
 
 
-def take_kernel(near, scale, place, got, tool, out, new_tool):
+def take_kernel(near, scale, destination, got, tool, out, new_tool):
     cols, rows, slots = out.shape[1:]
     size = 5 * cols * rows
     source = 0
     for k in range(got.shape[0] * near):
-        source = jnp.where(place[3 + k] == place[0], k // near, source)
+        source = jnp.where(destination[k] == here(), k // near, source)
     for f in range(5):
         for c in range(cols):
             at = (f * cols + c) * rows
@@ -372,9 +381,7 @@
 def body(positions, velocity, density, counts, contact_mask, destination, tool):
     cols, rows, slots = density.shape
     ncut, ndepth = lax.axis_size("cut"), lax.axis_size("depth")
-    here, depth = lax.axis_index("cut"), lax.axis_index("depth")
     scale = 1.0 / (ncut * cols * ndepth * rows * slots)
-    place = jnp.concatenate([jnp.stack([here, depth, jnp.int32(ncut)]).astype(jnp.int32), destination])
     near = 8 if ncut % 8 == 0 else 1
     far = ncut // near
     size = 5 * cols * rows
@@ -390,14 +397,14 @@
     swap = [(i, i ^ 1) for i in range(ncut)]
     cross = [(i, i + 1 if i % 2 else i - 1) for i in range(1, ncut - 1)]
 
-    def rates_of(kernel, out, arrays, read, summed):
-        scratch = [pltpu.VMEM((n * 16, slots), F32) for n in (read, summed, summed)]
-        return call(lambda place, *refs: kernel(place, (cols, rows), *refs), out, (place,), arrays, scratch, COST)
+    def rates_of(kernel, out, arrays, read, summed, rest=()):
+        scratch = [pltpu.VMEM((n * 16, slots), F32) for n in (read, summed, summed)] + list(rest)
+        return call(lambda *refs: kernel((cols, rows), *refs), out, (), arrays, scratch, COST)
 
     def exchange(own, marks, sent):
         got = lax.all_to_all(sent, "depth", 0, 0, tiled=True)
         inner = rates_of(inner_rates_kernel, block_rates, (own, marks), cols * rows, cols * rows)
-        wide = call(extend_kernel, shape(6 * cols + 1, rows + 2 * HALO, slots), (place,), (own, marks, got, inner))
+        wide = call(extend_kernel, shape(6 * cols + 1, rows + 2 * HALO, slots), (), (own, marks, got, inner))
         swapped, other = lax.ppermute(wide, "cut", swap), lax.ppermute(wide, "cut", cross)
         force = call(pair_force_kernel, along_line, (), (wide, swapped))
         total = lax.all_to_all(force, both, 0, 0, tiled=True, axis_index_groups=lines)
@@ -407,22 +414,23 @@
     own, marks, tool, sent = pl.pallas_call(
         start_kernel,
         out_shape=[state, marking, vector, message],
-        in_specs=[SMEM] * 4 + [pl.BlockSpec(memory_space=pl.ANY)] * 3,
+        in_specs=[SMEM] * 3 + [pl.BlockSpec(memory_space=pl.ANY)] * 3,
         out_specs=[VMEM] * 4,
         scratch_shapes=[pltpu.SemaphoreType.DMA((3,))],
         compiler_params=pltpu.CompilerParams(vmem_limit_bytes=60 * 1024 * 1024),
-    )(place, counts, contact_mask, tool, positions, velocity, density)
+    )(counts, contact_mask, tool, positions, velocity, density)
     found, around, total = exchange(own, marks, sent)
-    own, ringed = call(first_update_kernel, [state, ring], (place,), (own, found, marks, *around, tool))
-
-    found = rates_of(rates_kernel, block_rates, (ringed,), (cols + 2) * (rows + 2), cols * rows)
+    rest = (pltpu.VMEM(ring.shape, F32),)
+    read, summed = (cols + 2) * (rows + 2), cols * rows
+    own, found = rates_of(first_update_kernel, [state, block_rates], (own, found, marks, *around, tool), read, summed, rest)
+
     kernel = functools.partial(second_update_kernel, scale)
-    own, tool, sent = call(kernel, [state, vector, message], (place,), (own, found, marks, tool, total))
+    own, tool, sent = call(kernel, [state, vector, message], (), (own, found, marks, tool, total))
 
     found, around, total = exchange(own, marks, sent)
     kernel = functools.partial(third_update_kernel, scale)
     outs = [state, ring, vector, along_plane]
-    new_own, ringed, tool, force = call(kernel, outs, (place,), (own, found, marks, *around, tool, total))
+    new_own, ringed, tool, force = call(kernel, outs, (), (own, found, marks, *around, tool, total))
     own = new_own
 
     got = lax.all_to_all(force, both, 0, 0, tiled=True, axis_index_groups=planes)
@@ -430,14 +438,14 @@
     total = lax.all_to_all(force, both, 0, 0, tiled=True, axis_index_groups=lines)
     found = rates_of(rates_kernel, block_rates, (ringed,), (cols + 2) * (rows + 2), cols * rows)
     kernel = functools.partial(last_force_kernel, scale)
-    tool, force = call(kernel, [vector, along_depth], (place,), (own, marks, tool, total))
+    tool, force = call(kernel, [vector, along_depth], (), (own, marks, tool, total))
     total = lax.all_to_all(force, "depth", 0, 0, tiled=True)
     kernel = functools.partial(last_kernel, near)
-    sent = call(kernel, shape(near, size + 8, slots), (place,), (own, found, marks, tool, total))
+    sent = call(kernel, shape(near, size + 8, slots), (destination,), (own, found, marks, tool, total))
     close = [[g * near + k for k in range(near)] for g in range(far)]
     apart = [[g * near + k for g in range(far)] for k in range(near)]
     got = lax.all_to_all(sent, "cut", 0, 0, tiled=True, axis_index_groups=close)
-    sent = call(functools.partial(sort_kernel, near, size), shape(far, size + 8, slots), (place,), (got,))
+    sent = call(functools.partial(sort_kernel, near, size), shape(far, size + 8, slots), (destination,), (got,))
     got = lax.all_to_all(sent, "cut", 0, 0, tiled=True, axis_index_groups=apart)
     return pl.pallas_call(
         functools.partial(take_kernel, near, scale),
@@ -445,7 +453,7 @@
         in_specs=[SMEM, VMEM, VMEM],
         out_specs=[VMEM, SMEM],
         compiler_params=PARAMS,
-    )(place, got, tool)
+    )(destination, got, tool)
 
 
 def solution(mesh):

time: 178 us -> 172 us (0.966)
  Pallas kernels: 33.7 us -> 27.4 us
  waiting for transfers between devices: 23 us -> 26.9 us
    pallas_call x17 -> x16, Pallas kernels: 30.2 us -> 23.8 us  [call(): pl.pallas_call(kernel, out_shape=outs, in_specs=[SMEM] * len(scalars) + [...]
    all_to_all x2, waiting for transfers between devices: 4.42 us -> 6.32 us  [exchange(): lax.all_to_all(force, both, 0, 0, tiled=True, axis_index_groups=lines)]
  transfers between devices with their start and end apart: 9 -> 9, of which waited for: 6 -> 6; matrix products, arithmetic and copies ran while one was open for 0% -> 0% of each run, Pallas kernels for 14% -> 12%
where the time goes in v8:
time: 172 us; the launch traced here: 171 us
  blocking collectives  62.8 us (37%)
  starting transfers between devices  52 us (30%)
  Pallas kernels  27.4 us (16%)
  waiting for transfers between devices  26.9 us (16%)
    all_to_all x2, starting transfers between devices, exchange(): lax.all_to_all(force, both, 0, 0, tiled=True, axis_index_groups=lines)  25.4 us
    pallas_call x16, Pallas kernels, call(): pl.pallas_call(kernel, out_shape=outs, in_specs=[SMEM] * len(scalars) + [...  23.8 us
    all_to_all x1, blocking collectives, body(): got = lax.all_to_all(sent, 'cut', 0, 0, tiled=True, axis_index_groups=apart)  21 us
    all_to_all x1, blocking collectives, body(): lax.all_to_all(force, both, 0, 0, tiled=True, axis_index_groups=lines)  17 us
    all_to_all x2, waiting for transfers between devices, exchange(): got = lax.all_to_all(sent, 'depth', 0, 0, tiled=True)  14.5 us
    all_to_all x1, blocking collectives, body(): got = lax.all_to_all(sent, 'cut', 0, 0, tiled=True, axis_index_groups=close)  14.4 us
    all_to_all x2, starting transfers between devices, exchange(): got = lax.all_to_all(sent, 'depth', 0, 0, tiled=True)  10.9 us
    all_to_all x1, blocking collectives, body(): lax.all_to_all(force, both, 0, 0, tiled=True, axis_index_groups=planes)  10.3 us
  transfers between devices with their start and end apart: 9, of which 6 were waited for; matrix products, arithmetic and copies ran while one was open for 0% of the time, Pallas kernels for 12%

profile of v8, /device:TPU:64, one launch (start us, length us, event | category | flops | bytes accessed | tf_op | source)
XLA Modules:
  0.0 170.7 jit_solution(9107333243814513408)
XLA Ops:
  0.6 2.3 %shard_map.86 = (f32[5,2,8,128]{3,2,1,0:T(8,128)}, f32[2,2,8,128]{3,2,1,0:T(8,128)}, f32[2,128]{1,0:T(2,128)}, f32[16,32,128]{2,1,0:T(8,128)}) custom-call(s32[2,8]{1,0:T(2,128)} %counts.1, s32[2,8]{1,0:T(2,128)} %contact.1, f32[2]{0:T(128)} %first_tool.1, f32[2,2,8,128]{3,2,1,0:T(8,128)} %positions.1, f32[2,2,8,128]{3,2,1,0:T(8,128)} %velocity.1, ...), custom_call_target="tpu_custom_call" | custom-call | tf_op jit(solution)/shard_map/pallas_call | solution.py:414
  2.9 0.0 copy-start
  3.0 0.0 copy-start.1
  3.0 7.2 %all-to-all-start = ((f32[16,32,128]{2,1,0:T(8,128)}), f32[16,32,128]{2,1,0:T(8,128)S(1)}, u32[]{:S(2)}, u32[]{:S(2)}) async-start(f32[16,32,128]{2,1,0:T(8,128)} %get-tuple-element.19), calls=%async_computation | async-start | bytes 524288 | tf_op jit(solution)/shard_map/all_to_all | solution.py:405
  10.2 0.0 copy-done
  10.2 0.0 copy-done.1
  10.2 1.8 %shard_map.87.inner.refs_3_ = f32[3,2,8,128]{3,2,1,0:T(8,128)S(1)} custom-call(f32[5,2,8,128]{3,2,1,0:T(8,128)S(1)} %copy-done.1, f32[2,2,8,128]{3,2,1,0:T(8,128)S(1)} %copy-done), custom_call_target="tpu_custom_call" | custom-call | flops 20000000000 | bytes 1048576 | tf_op jit(solution)/shard_map/pallas_call | solution.py:41
  12.0 7.3 %all-to-all-done.got = f32[16,32,128]{2,1,0:T(8,128)S(1)} async-done(((f32[16,32,128]{2,1,0:T(8,128)}), f32[16,32,128]{2,1,0:T(8,128)S(1)}, u32[]{:S(2)}, u32[]{:S(2)}) %all-to-all-start) | async-done | bytes 262176 | tf_op jit(solution)/shard_map/all_to_all | solution.py:405
  19.4 2.6 %collective-permute-start = (f32[13,12,128]{2,1,0:T(8,128)S(1)}, f32[13,12,128]{2,1,0:T(8,128)S(1)}, u32[]{:S(2)}, u32[]{:S(2)}) collective-permute-start(f32[13,12,128]{2,1,0:T(8,128)S(1)} %shard_map.88.refs_0_.refs_3_.wide), channel_id=1, source_target_pairs={{0,16},{16,0},{32,48},{48,32},{64,80},{80,64},{96,112},{112,96},{1... | collective-permute-start | bytes 239624 | tf_op jit(solution)/shard_map/ppermute | solution.py:408
  22.0 2.8 %collective-permute-start.1 = (f32[13,12,128]{2,1,0:T(8,128)S(1)}, f32[13,12,128]{2,1,0:T(8,128)S(1)}, u32[]{:S(2)}, u32[]{:S(2)}) collective-permute-start(f32[13,12,128]{2,1,0:T(8,128)S(1)} %shard_map.88.refs_0_.refs_3_.wide), channel_id=1, source_target_pairs={{16,32},{32,16},{48,64},{64,48},{80,96},{96,80},{112,128},{128,112... | collective-permute-start | bytes 239624 | tf_op jit(solution)/shard_map/ppermute | solution.py:408
  24.8 1.5 collective-permute-done.refs_1_.refs_4_.swapped
  26.3 0.6 shard_map.91
  26.9 14.8 %all-to-all-start.1 = ((f32[16,1,128]{2,1,0:T(1,128)}), f32[16,1,128]{2,1,0:T(1,128)S(1)}, u32[]{:S(2)}, u32[]{:S(2)}) async-start(f32[16,1,128]{2,1,0:T(1,128)} %shard_map.91), calls=%async_computation.1 | async-start | bytes 16384 | tf_op jit(solution)/shard_map/all_to_all | solution.py:410
  41.6 0.0 collective-permute-done.1.refs_2_.refs_5_
  41.6 5.1 %shard_map.89.refs_1_ = f32[3,4,10,128]{3,2,1,0:T(8,128)S(1)} custom-call(f32[13,12,128]{2,1,0:T(8,128)S(1)} %shard_map.88.refs_0_.refs_3_.wide, f32[13,12,128]{2,1,0:T(8,128)S(1)} %collective-permute-done.refs_1_.refs_4_.swapped, f32[13,12,128]{2,1,0:T(8,128)S(1)} %collective-permute-done.1.refs_2_.refs_5_, f32[3,2,8,128]{3,2,1,0:T(8,128)S(1)} %shard_map.87.inner.refs_3_), custom_call_target="tpu_custom_call" | custom-call | flops 20000000000 | bytes 1048576 | tf_op jit(solution)/shard_map/pallas_call | solution.py:41
  46.7 0.0 copy-start.3
  46.8 0.6 copy-done.3
  47.4 3.0 %shard_map.90 = (f32[5,2,8,128]{3,2,1,0:T(8,128)S(1)}, f32[3,2,8,128]{3,2,1,0:T(8,128)S(1)}) custom-call(f32[5,2,8,128]{3,2,1,0:T(8,128)S(1)} %copy-done.1, f32[3,4,10,128]{3,2,1,0:T(8,128)S(1)} %shard_map.89.refs_1_, f32[2,2,8,128]{3,2,1,0:T(8,128)S(1)} %copy-done, f32[13,12,128]{2,1,0:T(8,128)S(1)} %shard_map.88.refs_0_.refs_3_.wide, ...), custom_call_target="tpu_custom_call" | custom-call | flops 20000000000 | bytes 1048576 | tf_op jit(solution)/shard_map/pallas_call | solution.py:41
  50.3 1.4 all-to-all-done.1.total
  51.7 0.8 shard_map.92
  52.5 3.7 %all-to-all-start.2 = ((f32[16,32,128]{2,1,0:T(8,128)}), f32[16,32,128]{2,1,0:T(8,128)S(1)}, u32[]{:S(2)}, u32[]{:S(2)}) async-start(f32[16,32,128]{2,1,0:T(8,128)} %get-tuple-element.24), calls=%async_computation.2 | async-start | bytes 524288 | tf_op jit(solution)/shard_map/all_to_all | solution.py:405
  56.2 1.8 %shard_map.93.inner.refs_3_ = f32[3,2,8,128]{3,2,1,0:T(8,128)S(1)} custom-call(f32[5,2,8,128]{3,2,1,0:T(8,128)S(1)} %get-tuple-element.23.refs_0_.own, f32[2,2,8,128]{3,2,1,0:T(8,128)S(1)} %copy-done), custom_call_target="tpu_custom_call" | custom-call | flops 20000000000 | bytes 1048576 | tf_op jit(solution)/shard_map/pallas_call | solution.py:41
  58.1 7.1 %all-to-all-done.2.got = f32[16,32,128]{2,1,0:T(8,128)S(1)} async-done(((f32[16,32,128]{2,1,0:T(8,128)}), f32[16,32,128]{2,1,0:T(8,128)S(1)}, u32[]{:S(2)}, u32[]{:S(2)}) %all-to-all-start.2) | async-done | bytes 262176 | tf_op jit(solution)/shard_map/all_to_all | solution.py:405
  65.3 2.6 %collective-permute-start.2 = (f32[13,12,128]{2,1,0:T(8,128)S(1)}, f32[13,12,128]{2,1,0:T(8,128)S(1)}, u32[]{:S(2)}, u32[]{:S(2)}) collective-permute-start(f32[13,12,128]{2,1,0:T(8,128)S(1)} %shard_map.94.refs_0_.wide), channel_id=1, source_target_pairs={{0,16},{16,0},{32,48},{48,32},{64,80},{80,64},{96,112},{112,96},{1... | collective-permute-start | bytes 239624 | tf_op jit(solution)/shard_map/ppermute | solution.py:408
  67.8 4.2 %collective-permute-start.3 = (f32[13,12,128]{2,1,0:T(8,128)S(1)}, f32[13,12,128]{2,1,0:T(8,128)S(1)}, u32[]{:S(2)}, u32[]{:S(2)}) collective-permute-start(f32[13,12,128]{2,1,0:T(8,128)S(1)} %shard_map.94.refs_0_.wide), channel_id=1, source_target_pairs={{16,32},{32,16},{48,64},{64,48},{80,96},{96,80},{112,128},{128,112... | collective-permute-start | bytes 239624 | tf_op jit(solution)/shard_map/ppermute | solution.py:408
  72.1 0.0 collective-permute-done.2.refs_1_.swapped
  72.1 0.6 shard_map.96
  72.7 10.7 %all-to-all-start.3 = ((f32[16,1,128]{2,1,0:T(1,128)}), f32[16,1,128]{2,1,0:T(1,128)S(1)}, u32[]{:S(2)}, u32[]{:S(2)}) async-start(f32[16,1,128]{2,1,0:T(1,128)} %shard_map.96), calls=%async_computation.3 | async-start | bytes 16384 | tf_op jit(solution)/shard_map/all_to_all | solution.py:410
  83.4 0.0 collective-permute-done.3.refs_2_.other
  83.4 5.1 %shard_map.95.found = f32[3,4,10,128]{3,2,1,0:T(8,128)S(1)} custom-call(f32[13,12,128]{2,1,0:T(8,128)S(1)} %shard_map.94.refs_0_.wide, f32[13,12,128]{2,1,0:T(8,128)S(1)} %collective-permute-done.2.refs_1_.swapped, f32[13,12,128]{2,1,0:T(8,128)S(1)} %collective-permute-done.3.refs_2_.other, f32[3,2,8,128]{3,2,1,0:T(8,128)S(1)} %shard_map.93.inner.refs_3_), custom_call_target="tpu_custom_call" | custom-call | flops 20000000000 | bytes 1048576 | tf_op jit(solution)/shard_map/pallas_call | solution.py:41
  88.5 5.0 %all-to-all-done.3.total = f32[16,1,128]{2,1,0:T(1,128)S(1)} async-done(((f32[16,1,128]{2,1,0:T(1,128)}), f32[16,1,128]{2,1,0:T(1,128)S(1)}, u32[]{:S(2)}, u32[]{:S(2)}) %all-to-all-start.3) | async-done | bytes 8224 | tf_op jit(solution)/shard_map/all_to_all | solution.py:410
  93.5 0.1 shard_map.97
  93.6 10.3 %all_to_all.45.got = f32[32,1,128]{2,1,0:T(1,128)S(1)} all-to-all(f32[32,1,128]{2,1,0:T(1,128)S(1)} %get-tuple-element.29), channel_id=1, replica_groups={{0,1,2,3,4,5,6,7,8,9,10,11,12,13,14,15,16,17,18,19,20,21,22,23,24,25,26..., dimensions={0} | all-to-all | bytes 32768 | tf_op jit(solution)/shard_map/all_to_all | solution.py:436
  104.0 17.0 %all_to_all.46.total = f32[16,1,128]{2,1,0:T(1,128)S(1)} all-to-all(f32[16,1,128]{2,1,0:T(1,128)S(1)} %shard_map.99), channel_id=1, replica_groups={{0,32,64,96,128,160,192,224,256,288,320,352,384,416,448,480},{1,33,65,9..., dimensions={0} | all-to-all | bytes 16384 | tf_op jit(solution)/shard_map/all_to_all | solution.py:438
  121.0 0.7 shard_map.100
  121.7 3.5 %all-to-all-start.6 = ((f32[16,1,128]{2,1,0:T(1,128)}), f32[16,1,128]{2,1,0:T(1,128)S(1)}, u32[]{:S(2)}, u32[]{:S(2)}) async-start(f32[16,1,128]{2,1,0:T(1,128)} %get-tuple-element.31), calls=%async_computation.6 | async-start | bytes 16384 | tf_op jit(solution)/shard_map/all_to_all | solution.py:442
  125.2 2.8 %shard_map.98.found = f32[3,2,8,128]{3,2,1,0:T(8,128)S(1)} custom-call(f32[5,4,10,128]{3,2,1,0:T(8,128)S(1)} %get-tuple-element.27.refs_0_), custom_call_target="tpu_custom_call" | custom-call | flops 20000000000 | bytes 1048576 | tf_op jit(solution)/shard_map/pallas_call | solution.py:41
  128.0 0.0 copy-start.2
  128.0 4.6 %all-to-all-done.6.total = f32[16,1,128]{2,1,0:T(1,128)S(1)} async-done(((f32[16,1,128]{2,1,0:T(1,128)}), f32[16,1,128]{2,1,0:T(1,128)S(1)}, u32[]{:S(2)}, u32[]{:S(2)}) %all-to-all-start.6) | async-done | bytes 8224 | tf_op jit(solution)/shard_map/all_to_all | solution.py:442
  132.6 0.0 copy-done.2
  132.6 0.6 shard_map.101
  133.2 14.4 %all_to_all.47.got = f32[8,88,128]{2,1,0:T(8,128)S(1)} all-to-all(f32[8,88,128]{2,1,0:T(8,128)S(1)} %shard_map.101), channel_id=1, replica_groups={{0,16,32,48,64,80,96,112},{128,144,160,176,192,208,224,240},{256,272,28..., dimensions={0} | all-to-all | bytes 720896 | tf_op jit(solution)/shard_map/all_to_all | solution.py:447
  147.6 0.7 shard_map.102
  148.3 21.0 %all_to_all.48.got = f32[4,88,128]{2,1,0:T(8,128)S(1)} all-to-all(f32[4,88,128]{2,1,0:T(8,128)S(1)} %shard_map.102), channel_id=1, replica_groups={{0,128,256,384},{16,144,272,400},{32,160,288,416},{48,176,304,432},{64,..., dimensions={0} | all-to-all | bytes 360448 | tf_op jit(solution)/shard_map/all_to_all | solution.py:449
  169.3 1.2 shard_map.103
  (3 shorter events, 0.1 us)
Async XLA Ops:
  2.9 7.2 %copy-start = (f32[2,2,8,128]{3,2,1,0:T(8,128)S(1)}, f32[2,2,8,128]{3,2,1,0:T(8,128)}, u32[]{:S(2)}) copy-start(f32[2,2,8,128]{3,2,1,0:T(8,128)} %get-tuple-element.18.refs_1_.marks.refs_2_) | copy-start | bytes 49156
  3.0 7.2 %copy-start.1 = (f32[5,2,8,128]{3,2,1,0:T(8,128)S(1)}, f32[5,2,8,128]{3,2,1,0:T(8,128)}, u32[]{:S(2)}) copy-start(f32[5,2,8,128]{3,2,1,0:T(8,128)} %get-tuple-element.17.refs_0_.own) | copy-start | bytes 122884
  3.0 16.4 %all-to-all-start = ((f32[16,32,128]{2,1,0:T(8,128)}), f32[16,32,128]{2,1,0:T(8,128)S(1)}, u32[]{:S(2)}, u32[]{:S(2)}) async-start(f32[16,32,128]{2,1,0:T(8,128)} %get-tuple-element.19), calls=%async_computation | async-start | bytes 524288 | tf_op jit(solution)/shard_map/all_to_all | solution.py:405
  19.4 6.9 %collective-permute-start = (f32[13,12,128]{2,1,0:T(8,128)S(1)}, f32[13,12,128]{2,1,0:T(8,128)S(1)}, u32[]{:S(2)}, u32[]{:S(2)}) collective-permute-start(f32[13,12,128]{2,1,0:T(8,128)S(1)} %shard_map.88.refs_0_.refs_3_.wide), channel_id=1, source_target_pairs={{0,16},{16,0},{32,48},{48,32},{64,80},{80,64},{96,112},{112,96},{1... | collective-permute-start | bytes 239624 | tf_op jit(solution)/shard_map/ppermute | solution.py:408
  22.0 19.7 %collective-permute-start.1 = (f32[13,12,128]{2,1,0:T(8,128)S(1)}, f32[13,12,128]{2,1,0:T(8,128)S(1)}, u32[]{:S(2)}, u32[]{:S(2)}) collective-permute-start(f32[13,12,128]{2,1,0:T(8,128)S(1)} %shard_map.88.refs_0_.refs_3_.wide), channel_id=1, source_target_pairs={{16,32},{32,16},{48,64},{64,48},{80,96},{96,80},{112,128},{128,112... | collective-permute-start | bytes 239624 | tf_op jit(solution)/shard_map/ppermute | solution.py:408
  26.9 24.8 %all-to-all-start.1 = ((f32[16,1,128]{2,1,0:T(1,128)}), f32[16,1,128]{2,1,0:T(1,128)S(1)}, u32[]{:S(2)}, u32[]{:S(2)}) async-start(f32[16,1,128]{2,1,0:T(1,128)} %shard_map.91), calls=%async_computation.1 | async-start | bytes 16384 | tf_op jit(solution)/shard_map/all_to_all | solution.py:410
  46.7 0.6 copy-start.3
  52.5 12.7 %all-to-all-start.2 = ((f32[16,32,128]{2,1,0:T(8,128)}), f32[16,32,128]{2,1,0:T(8,128)S(1)}, u32[]{:S(2)}, u32[]{:S(2)}) async-start(f32[16,32,128]{2,1,0:T(8,128)} %get-tuple-element.24), calls=%async_computation.2 | async-start | bytes 524288 | tf_op jit(solution)/shard_map/all_to_all | solution.py:405
  65.3 6.9 %collective-permute-start.2 = (f32[13,12,128]{2,1,0:T(8,128)S(1)}, f32[13,12,128]{2,1,0:T(8,128)S(1)}, u32[]{:S(2)}, u32[]{:S(2)}) collective-permute-start(f32[13,12,128]{2,1,0:T(8,128)S(1)} %shard_map.94.refs_0_.wide), channel_id=1, source_target_pairs={{0,16},{16,0},{32,48},{48,32},{64,80},{80,64},{96,112},{112,96},{1... | collective-permute-start | bytes 239624 | tf_op jit(solution)/shard_map/ppermute | solution.py:408
  67.8 15.6 %collective-permute-start.3 = (f32[13,12,128]{2,1,0:T(8,128)S(1)}, f32[13,12,128]{2,1,0:T(8,128)S(1)}, u32[]{:S(2)}, u32[]{:S(2)}) collective-permute-start(f32[13,12,128]{2,1,0:T(8,128)S(1)} %shard_map.94.refs_0_.wide), channel_id=1, source_target_pairs={{16,32},{32,16},{48,64},{64,48},{80,96},{96,80},{112,128},{128,112... | collective-permute-start | bytes 239624 | tf_op jit(solution)/shard_map/ppermute | solution.py:408
  72.7 20.8 %all-to-all-start.3 = ((f32[16,1,128]{2,1,0:T(1,128)}), f32[16,1,128]{2,1,0:T(1,128)S(1)}, u32[]{:S(2)}, u32[]{:S(2)}) async-start(f32[16,1,128]{2,1,0:T(1,128)} %shard_map.96), calls=%async_computation.3 | async-start | bytes 16384 | tf_op jit(solution)/shard_map/all_to_all | solution.py:410
  121.7 10.9 %all-to-all-start.6 = ((f32[16,1,128]{2,1,0:T(1,128)}), f32[16,1,128]{2,1,0:T(1,128)S(1)}, u32[]{:S(2)}, u32[]{:S(2)}) async-start(f32[16,1,128]{2,1,0:T(1,128)} %get-tuple-element.31), calls=%async_computation.6 | async-start | bytes 16384 | tf_op jit(solution)/shard_map/all_to_all | solution.py:442
  128.0 4.6 %copy-start.2 = (s32[32]{0:T(128)S(1)}, s32[32]{0:T(128)}, u32[]{:S(2)}) copy-start(s32[32]{0:T(128)} %destination.5) | copy-start | bytes 388

commit v9 on v8

--- a/solution.py
+++ b/solution.py
@@ -100,29 +100,43 @@
     return first + 0.5 * cols, (row_block() * rows).astype(F32) + 0.5 * rows, first
 
 
-def start_kernel(counts, contact, first_tool, positions, velocity, density, own, marks, tool, sent, arrived):
-    cols, rows, slots = density.shape
-    parts = [(positions, own.at[0:2]), (velocity, own.at[2:4]), (density, own.at[4])]
-    copies = [pltpu.make_async_copy(part, to, arrived.at[n]) for n, (part, to) in enumerate(parts)]
+def start_kernel(near, *refs):
+    inputs, (own, marks, route, sent), (counts, contact, target, first_tool, arrived) = refs[:7], refs[7:11], refs[11:]
+    homes = [own.at[0:2], own.at[2:4], own.at[4], counts, contact, target, first_tool]
+    copies = [pltpu.make_async_copy(part, to, arrived.at[n]) for n, (part, to) in enumerate(zip(inputs, homes))]
     for copy in copies:
         copy.start()
+    for copy in copies:
+        copy.wait()
+    cols, rows, slots = own.shape[1:]
     row = lax.broadcasted_iota(jnp.int32, (rows, slots), 0)
     slot = lax.broadcasted_iota(jnp.int32, (rows, slots), 1)
     for c in range(cols):
         filled = jnp.zeros((rows, slots), jnp.int32)
         touch = jnp.zeros((rows, slots), jnp.int32)
         for r in range(rows):
-            filled = jnp.where(row == r, counts[c, r], filled)
-            touch = jnp.where(row == r, contact[c, r], touch)
+            filled = jnp.where(row == r, counts[c : c + 1, r : r + 1], filled)
+            touch = jnp.where(row == r, contact[c : c + 1, r : r + 1], touch)
         marks[0, c] = jnp.where(slot < filled, 1.0, 0.0)
         marks[1, c] = touch.astype(F32)
-    for copy in copies:
-        copy.wait()
     new = [[own[f, c] for f in range(5)] for c in range(cols)]
-    offset = jnp.zeros((1, slots), F32) + first_tool[0]
-    tool[0:1] = offset
-    tool[1:2] = jnp.zeros((1, slots), F32) + first_tool[1]
+    offset = jnp.broadcast_to(first_tool[0:1, 0:1], (1, slots))
+    marks[2, 0] = jnp.broadcast_to(offset, (rows, slots))
+    marks[2, 1] = jnp.broadcast_to(first_tool[0:1, 1:2], (rows, slots))
     fill_depth(new, marks, own_force(new, marks, offset, origin(cols, rows)[2]), sent)
+
+    block = lax.broadcasted_iota(jnp.int32, target.shape, 1)
+
+    def entry(at):
+        return jnp.sum(jnp.where(block == at, target[...], 0), axis=1, keepdims=True)
+
+    route[...] = jnp.zeros(route.shape, jnp.int32)
+    route[0:1] = jnp.broadcast_to(entry(here()), (1, slots))
+    source = jnp.sum(jnp.where(target[...] == here(), block, 0), axis=1, keepdims=True)
+    route[1:2] = jnp.broadcast_to(source, (1, slots))
+    group = lax.div(here(), near)
+    for k in range(near):
+        route[2 + k : 3 + k] = jnp.broadcast_to(entry(group * near + k), (1, slots))
 
 
 def extend_kernel(own, marks, got, inner, wide):
@@ -293,21 +307,22 @@
             own[f, c] = fields[f]
 
 
-def tool_step(tool, force, scale):
-    speed = tool[1:2] + DT * (1.0 - force * scale)
-    return tool[0:1] + DT * speed, speed
-
-
-def first_update_kernel(size, own, found, marks, wide, swapped, other, tool, new_own, out, feat, acc2, acc3, ring):
+def tool_step(offset, speed, force, scale):
+    speed = speed + DT * (1.0 - force * scale)
+    return offset + DT * speed, speed
+
+
+def first_update_kernel(size, own, found, marks, wide, swapped, other, new_own, out, feat, acc2, acc3, ring):
     first = origin(*size)[2]
-    keep(moved_state(own, found, marks, tool[0:1], first), new_own)
-    moved_ring(wide_columns(size[0], wide, swapped, other), found, tool[0:1], first, ring)
+    offset = marks[2, 0, 0:1]
+    keep(moved_state(own, found, marks, offset, first), new_own)
+    moved_ring(wide_columns(size[0], wide, swapped, other), found, offset, first, ring)
     rates_kernel(size, ring, out, feat, acc2, acc3)
 
 
-def second_update_kernel(scale, own, found, marks, tool, total, new_own, new_tool, sent):
+def second_update_kernel(scale, own, found, marks, total, new_own, new_tool, sent):
     first = origin(*own.shape[1:3])[2]
-    offset, speed = tool_step(tool, jnp.sum(total[...], axis=0), scale)
+    offset, speed = tool_step(marks[2, 0, 0:1], marks[2, 1, 0:1], jnp.sum(total[...], axis=0), scale)
     new_tool[0:1] = offset
     new_tool[1:2] = speed
     state = [[own[f, c] for f in range(5)] for c in range(own.shape[1])]
@@ -318,7 +333,7 @@
 
 def third_update_kernel(scale, own, found, marks, wide, swapped, other, tool, total, new_own, ring, new_tool, force):
     first = origin(*own.shape[1:3])[2]
-    offset, speed = tool_step(tool, jnp.sum(total[...], axis=0), scale)
+    offset, speed = tool_step(tool[0:1], tool[1:2], jnp.sum(total[...], axis=0), scale)
     new_tool[0:1] = offset
     new_tool[1:2] = speed
     state = [[own[f, c] for f in range(5)] for c in range(own.shape[1])]
@@ -328,7 +343,7 @@
 
 
 def last_force_kernel(scale, own, marks, tool, total, new_tool, force):
-    offset, speed = tool_step(tool, jnp.sum(total[...], axis=0), scale)
+    offset, speed = tool_step(tool[0:1], tool[1:2], jnp.sum(total[...], axis=0), scale)
     new_tool[0:1] = offset
     new_tool[1:2] = speed
     state = [[own[f, c] for f in range(5)] for c in range(own.shape[1])]
@@ -336,46 +351,46 @@
     force[...] = jnp.broadcast_to(part[None], force.shape)
 
 
-def last_kernel(near, destination, own, found, marks, tool, total, sent):
+def last_kernel(near, route, own, found, marks, tool, total, sent):
     cols, rows, slots = own.shape[1:]
     size = 5 * cols * rows
     new = moved_state(own, found, marks, tool[0:1], origin(cols, rows)[2])
-    sent[...] = jnp.zeros(sent.shape, F32)
     sent[:, size:, :] = jnp.broadcast_to(jnp.sum(total[...], axis=0, keepdims=True), (near, sent.shape[1] - size, slots))
-    digit = lax.rem(destination[here()], near)
+    target = route[0:1]
+    for k in range(near):
+        chosen = jnp.bitwise_and(target, near - 1) == k
+        for f in range(5):
+            for c in range(cols):
+                at = (f * cols + c) * rows
+                sent[k, at : at + rows] = jnp.where(chosen, new[c][f], 0.0)
+
+
+def sort_kernel(near, size, route, got, sent):
+    far, most, slots = sent.shape
+    digit = lax.rem(here(), near)
+    total = jnp.sum(got[:, size : size + 1, :], axis=0, keepdims=True)
+    sent[:, size:, :] = jnp.broadcast_to(total, (far, most - size, slots))
+    for g in range(far):
+        block = jnp.zeros((size, slots), F32)
+        for k in range(near):
+            block = jnp.where(route[2 + k : 3 + k] == g * near + digit, got[k, 0:size], block)
+        sent[g, 0:size] = block
+
+
+def take_kernel(near, scale, route, got, tool, out, new_tool):
+    cols, rows, slots = out.shape[1:]
+    size = 5 * cols * rows
+    source = route[1:2]
     for f in range(5):
         for c in range(cols):
             at = (f * cols + c) * rows
-            sent[digit, at : at + rows] = new[c][f]
-
-
-def sort_kernel(near, size, destination, got, sent):
-    far, most, slots = sent.shape
-    group, digit = lax.div(here(), near), lax.rem(here(), near)
-    sent[...] = jnp.zeros(sent.shape, F32)
-    total = jnp.sum(got[:, size : size + 1, :], axis=0, keepdims=True)
-    sent[:, size:, :] = jnp.broadcast_to(total, (far, most - size, slots))
-    for k in range(near):
-        target = destination[group * near + k]
-
-        @pl.when(lax.rem(target, near) == digit)
-        def _():
-            sent[lax.div(target, near), 0:size] = got[k, 0:size]
-
-
-def take_kernel(near, scale, destination, got, tool, out, new_tool):
-    cols, rows, slots = out.shape[1:]
-    size = 5 * cols * rows
-    source = 0
-    for k in range(got.shape[0] * near):
-        source = jnp.where(destination[k] == here(), k // near, source)
-    for f in range(5):
-        for c in range(cols):
-            at = (f * cols + c) * rows
-            out[f, c] = got[source, at : at + rows]
-    offset, speed = tool_step(tool, jnp.sum(got[:, size : size + 1, :], axis=0), scale)
-    new_tool[0] = offset[0, 0]
-    new_tool[1] = speed[0, 0]
+            field = got[0, at : at + rows]
+            for g in range(1, got.shape[0]):
+                field = jnp.where(source >= g * near, got[g, at : at + rows], field)
+            out[f, c] = field
+    offset, speed = tool_step(tool[0:1], tool[1:2], jnp.sum(got[:, size : size + 1, :], axis=0), scale)
+    slot = lax.broadcasted_iota(jnp.int32, (1, slots), 1)
+    new_tool[...] = jnp.where(slot == 0, offset, speed)[:, 0:2]
 
 
 def body(positions, velocity, density, counts, contact_mask, destination, tool):
@@ -385,7 +400,7 @@
     near = 8 if ncut % 8 == 0 else 1
     far = ncut // near
     size = 5 * cols * rows
-    state, marking = shape(5, cols, rows, slots), shape(2, cols, rows, slots)
+    state, marking = shape(5, cols, rows, slots), shape(3, cols, rows, slots)
     message, vector = shape(ndepth, 32, slots), shape(2, slots)
     along_depth, along_plane, along_line = [shape(n, 1, slots) for n in (ndepth, 2 * ndepth, ncut // 2)]
     both = ("cut", "depth")
@@ -411,21 +426,22 @@
         found = rates_of(wide_rates_kernel, ring_rates, (wide, swapped, other, inner), 3 * cols * (rows + 4), (cols + 2) * (rows + 2))
         return found, (wide, swapped, other), total
 
-    own, marks, tool, sent = pl.pallas_call(
-        start_kernel,
-        out_shape=[state, marking, vector, message],
-        in_specs=[SMEM] * 3 + [pl.BlockSpec(memory_space=pl.ANY)] * 3,
+    inputs = (positions, velocity, density, counts, contact_mask, destination[None], tool[None])
+    own, marks, route, sent = pl.pallas_call(
+        functools.partial(start_kernel, near),
+        out_shape=[state, marking, jax.ShapeDtypeStruct((16, slots), jnp.int32), message],
+        in_specs=[pl.BlockSpec(memory_space=pl.ANY)] * 7,
         out_specs=[VMEM] * 4,
-        scratch_shapes=[pltpu.SemaphoreType.DMA((3,))],
+        scratch_shapes=[pltpu.VMEM(part.shape, part.dtype) for part in inputs[3:]] + [pltpu.SemaphoreType.DMA((7,))],
         compiler_params=pltpu.CompilerParams(vmem_limit_bytes=60 * 1024 * 1024),
-    )(counts, contact_mask, tool, positions, velocity, density)
+    )(*inputs)
     found, around, total = exchange(own, marks, sent)
     rest = (pltpu.VMEM(ring.shape, F32),)
     read, summed = (cols + 2) * (rows + 2), cols * rows
-    own, found = rates_of(first_update_kernel, [state, block_rates], (own, found, marks, *around, tool), read, summed, rest)
+    own, found = rates_of(first_update_kernel, [state, block_rates], (own, found, marks, *around), read, summed, rest)
 
     kernel = functools.partial(second_update_kernel, scale)
-    own, tool, sent = call(kernel, [state, vector, message], (), (own, found, marks, tool, total))
+    own, tool, sent = call(kernel, [state, vector, message], (), (own, found, marks, total))
 
     found, around, total = exchange(own, marks, sent)
     kernel = functools.partial(third_update_kernel, scale)
@@ -441,19 +457,14 @@
     tool, force = call(kernel, [vector, along_depth], (), (own, marks, tool, total))
     total = lax.all_to_all(force, "depth", 0, 0, tiled=True)
     kernel = functools.partial(last_kernel, near)
-    sent = call(kernel, shape(near, size + 8, slots), (destination,), (own, found, marks, tool, total))
+    sent = call(kernel, shape(near, size + 8, slots), (), (route, own, found, marks, tool, total))
     close = [[g * near + k for k in range(near)] for g in range(far)]
     apart = [[g * near + k for g in range(far)] for k in range(near)]
     got = lax.all_to_all(sent, "cut", 0, 0, tiled=True, axis_index_groups=close)
-    sent = call(functools.partial(sort_kernel, near, size), shape(far, size + 8, slots), (destination,), (got,))
+    sent = call(functools.partial(sort_kernel, near, size), shape(far, size + 8, slots), (), (route, got))
     got = lax.all_to_all(sent, "cut", 0, 0, tiled=True, axis_index_groups=apart)
-    return pl.pallas_call(
-        functools.partial(take_kernel, near, scale),
-        out_shape=[state, shape(2)],
-        in_specs=[SMEM, VMEM, VMEM],
-        out_specs=[VMEM, SMEM],
-        compiler_params=PARAMS,
-    )(destination, got, tool)
+    moved, tool = call(functools.partial(take_kernel, near, scale), [state, shape(1, 2)], (), (route, got, tool))
+    return moved, tool[0]
 
 
 def solution(mesh):

time: 172 us -> 169 us (0.983)
  Pallas kernels: 27.4 us -> 25.2 us
    pallas_call x2 -> x1, Pallas kernels: 3.52 us -> 1.77 us  [body(): pl.pallas_call(functools.partial(start_kernel, near), out_shape=[state, m...]
    pallas_call x16 -> x17, Pallas kernels: 23.8 us -> 23.4 us  [call(): pl.pallas_call(kernel, out_shape=outs, in_specs=[SMEM] * len(scalars) + [...]
where the time goes in v9:
time: 169 us; the launch traced here: 168 us
  blocking collectives  62.8 us (37%)
  starting transfers between devices  51.4 us (30%)
  waiting for transfers between devices  27.5 us (16%)
  Pallas kernels  25.2 us (15%)
    all_to_all x2, starting transfers between devices, exchange(): lax.all_to_all(force, both, 0, 0, tiled=True, axis_index_groups=lines)  24.8 us
    pallas_call x17, Pallas kernels, call(): pl.pallas_call(kernel, out_shape=outs, in_specs=[SMEM] * len(scalars) + [...  23.4 us
    all_to_all x1, blocking collectives, body(): got = lax.all_to_all(sent, 'cut', 0, 0, tiled=True, axis_index_groups=apart)  21 us
    all_to_all x1, blocking collectives, body(): lax.all_to_all(force, both, 0, 0, tiled=True, axis_index_groups=lines)  17 us
    all_to_all x2, waiting for transfers between devices, exchange(): got = lax.all_to_all(sent, 'depth', 0, 0, tiled=True)  14.5 us
    all_to_all x1, blocking collectives, body(): got = lax.all_to_all(sent, 'cut', 0, 0, tiled=True, axis_index_groups=close)  14.4 us
    all_to_all x2, starting transfers between devices, exchange(): got = lax.all_to_all(sent, 'depth', 0, 0, tiled=True)  10.9 us
    all_to_all x1, blocking collectives, body(): lax.all_to_all(force, both, 0, 0, tiled=True, axis_index_groups=planes)  10.3 us
  transfers between devices with their start and end apart: 9, of which 6 were waited for; matrix products, arithmetic and copies ran while one was open for 0% of the time, Pallas kernels for 12%

profile of v9, /device:TPU:64, one launch (start us, length us, event | category | flops | bytes accessed | tf_op | source)
XLA Modules:
  0.0 167.7 jit_solution(7795349264859621908)
XLA Ops:
  0.6 1.8 %shard_map.86 = (f32[5,2,8,128]{3,2,1,0:T(8,128)}, f32[3,2,8,128]{3,2,1,0:T(8,128)}, s32[16,128]{1,0:T(8,128)}, f32[16,32,128]{2,1,0:T(8,128)}) custom-call(f32[2,2,8,128]{3,2,1,0:T(8,128)} %refs_0_.1, f32[2,2,8,128]{3,2,1,0:T(8,128)} %refs_1_.1, f32[2,8,128]{2,1,0:T(8,128)} %refs_2_.1, s32[2,8]{1,0:T(2,128)} %refs_3_.1, s32[2,8]{1,0:T(2,128)} %refs_4_.1, ...), custom_call_target="tpu_custom_call" | custom-call | tf_op jit(solution)/shard_map/pallas_call | solution.py:430
  2.4 0.0 copy-start
  2.4 0.0 copy-start.2
  2.4 7.2 %all-to-all-start = ((f32[16,32,128]{2,1,0:T(8,128)}), f32[16,32,128]{2,1,0:T(8,128)S(1)}, u32[]{:S(2)}, u32[]{:S(2)}) async-start(f32[16,32,128]{2,1,0:T(8,128)} %get-tuple-element.22), calls=%async_computation | async-start | bytes 524288 | tf_op jit(solution)/shard_map/all_to_all | solution.py:420
  9.6 0.0 copy-done
  9.6 0.0 copy-done.2
  9.6 1.9 %shard_map.87.inner.refs_3_ = f32[3,2,8,128]{3,2,1,0:T(8,128)S(1)} custom-call(f32[5,2,8,128]{3,2,1,0:T(8,128)S(1)} %copy-done.2, f32[3,2,8,128]{3,2,1,0:T(8,128)S(1)} %copy-done), custom_call_target="tpu_custom_call" | custom-call | flops 20000000000 | bytes 1048576 | tf_op jit(solution)/shard_map/pallas_call | solution.py:41
  11.5 7.3 %all-to-all-done.got = f32[16,32,128]{2,1,0:T(8,128)S(1)} async-done(((f32[16,32,128]{2,1,0:T(8,128)}), f32[16,32,128]{2,1,0:T(8,128)S(1)}, u32[]{:S(2)}, u32[]{:S(2)}) %all-to-all-start) | async-done | bytes 262176 | tf_op jit(solution)/shard_map/all_to_all | solution.py:420
  18.9 2.6 %collective-permute-start = (f32[13,12,128]{2,1,0:T(8,128)S(1)}, f32[13,12,128]{2,1,0:T(8,128)S(1)}, u32[]{:S(2)}, u32[]{:S(2)}) collective-permute-start(f32[13,12,128]{2,1,0:T(8,128)S(1)} %shard_map.88.refs_0_.refs_3_.wide), channel_id=1, source_target_pairs={{0,16},{16,0},{32,48},{48,32},{64,80},{80,64},{96,112},{112,96},{1... | collective-permute-start | bytes 239624 | tf_op jit(solution)/shard_map/ppermute | solution.py:423
  21.4 2.8 %collective-permute-start.1 = (f32[13,12,128]{2,1,0:T(8,128)S(1)}, f32[13,12,128]{2,1,0:T(8,128)S(1)}, u32[]{:S(2)}, u32[]{:S(2)}) collective-permute-start(f32[13,12,128]{2,1,0:T(8,128)S(1)} %shard_map.88.refs_0_.refs_3_.wide), channel_id=1, source_target_pairs={{16,32},{32,16},{48,64},{64,48},{80,96},{96,80},{112,128},{128,112... | collective-permute-start | bytes 239624 | tf_op jit(solution)/shard_map/ppermute | solution.py:423
  24.3 1.5 collective-permute-done.refs_1_.refs_4_.swapped
  25.7 0.6 shard_map.91
  26.3 14.8 %all-to-all-start.1 = ((f32[16,1,128]{2,1,0:T(1,128)}), f32[16,1,128]{2,1,0:T(1,128)S(1)}, u32[]{:S(2)}, u32[]{:S(2)}) async-start(f32[16,1,128]{2,1,0:T(1,128)} %shard_map.91), calls=%async_computation.1 | async-start | bytes 16384 | tf_op jit(solution)/shard_map/all_to_all | solution.py:425
  41.1 0.0 collective-permute-done.1.refs_2_.refs_5_
  41.1 5.1 %shard_map.89.refs_1_ = f32[3,4,10,128]{3,2,1,0:T(8,128)S(1)} custom-call(f32[13,12,128]{2,1,0:T(8,128)S(1)} %shard_map.88.refs_0_.refs_3_.wide, f32[13,12,128]{2,1,0:T(8,128)S(1)} %collective-permute-done.refs_1_.refs_4_.swapped, f32[13,12,128]{2,1,0:T(8,128)S(1)} %collective-permute-done.1.refs_2_.refs_5_, f32[3,2,8,128]{3,2,1,0:T(8,128)S(1)} %shard_map.87.inner.refs_3_), custom_call_target="tpu_custom_call" | custom-call | flops 20000000000 | bytes 1048576 | tf_op jit(solution)/shard_map/pallas_call | solution.py:41
  46.2 3.0 %shard_map.90 = (f32[5,2,8,128]{3,2,1,0:T(8,128)S(1)}, f32[3,2,8,128]{3,2,1,0:T(8,128)S(1)}) custom-call(f32[5,2,8,128]{3,2,1,0:T(8,128)S(1)} %copy-done.2, f32[3,4,10,128]{3,2,1,0:T(8,128)S(1)} %shard_map.89.refs_1_, f32[3,2,8,128]{3,2,1,0:T(8,128)S(1)} %copy-done, f32[13,12,128]{2,1,0:T(8,128)S(1)} %shard_map.88.refs_0_.refs_3_.wide, ...), custom_call_target="tpu_custom_call" | custom-call | flops 20000000000 | bytes 1048576 | tf_op jit(solution)/shard_map/pallas_call | solution.py:41
  49.2 2.0 %all-to-all-done.1.total = f32[16,1,128]{2,1,0:T(1,128)S(1)} async-done(((f32[16,1,128]{2,1,0:T(1,128)}), f32[16,1,128]{2,1,0:T(1,128)S(1)}, u32[]{:S(2)}, u32[]{:S(2)}) %all-to-all-start.1) | async-done | bytes 8224 | tf_op jit(solution)/shard_map/all_to_all | solution.py:425
  51.2 0.8 shard_map.92
  52.0 3.7 %all-to-all-start.2 = ((f32[16,32,128]{2,1,0:T(8,128)}), f32[16,32,128]{2,1,0:T(8,128)S(1)}, u32[]{:S(2)}, u32[]{:S(2)}) async-start(f32[16,32,128]{2,1,0:T(8,128)} %get-tuple-element.26), calls=%async_computation.2 | async-start | bytes 524288 | tf_op jit(solution)/shard_map/all_to_all | solution.py:420
  55.7 1.9 %shard_map.93.inner.refs_3_ = f32[3,2,8,128]{3,2,1,0:T(8,128)S(1)} custom-call(f32[5,2,8,128]{3,2,1,0:T(8,128)S(1)} %get-tuple-element.25.refs_0_.own, f32[3,2,8,128]{3,2,1,0:T(8,128)S(1)} %copy-done), custom_call_target="tpu_custom_call" | custom-call | flops 20000000000 | bytes 1048576 | tf_op jit(solution)/shard_map/pallas_call | solution.py:41
  57.6 7.1 %all-to-all-done.2.got = f32[16,32,128]{2,1,0:T(8,128)S(1)} async-done(((f32[16,32,128]{2,1,0:T(8,128)}), f32[16,32,128]{2,1,0:T(8,128)S(1)}, u32[]{:S(2)}, u32[]{:S(2)}) %all-to-all-start.2) | async-done | bytes 262176 | tf_op jit(solution)/shard_map/all_to_all | solution.py:420
  64.7 2.6 %collective-permute-start.2 = (f32[13,12,128]{2,1,0:T(8,128)S(1)}, f32[13,12,128]{2,1,0:T(8,128)S(1)}, u32[]{:S(2)}, u32[]{:S(2)}) collective-permute-start(f32[13,12,128]{2,1,0:T(8,128)S(1)} %shard_map.94.refs_0_.wide), channel_id=1, source_target_pairs={{0,16},{16,0},{32,48},{48,32},{64,80},{80,64},{96,112},{112,96},{1... | collective-permute-start | bytes 239624 | tf_op jit(solution)/shard_map/ppermute | solution.py:423
  67.3 4.2 %collective-permute-start.3 = (f32[13,12,128]{2,1,0:T(8,128)S(1)}, f32[13,12,128]{2,1,0:T(8,128)S(1)}, u32[]{:S(2)}, u32[]{:S(2)}) collective-permute-start(f32[13,12,128]{2,1,0:T(8,128)S(1)} %shard_map.94.refs_0_.wide), channel_id=1, source_target_pairs={{16,32},{32,16},{48,64},{64,48},{80,96},{96,80},{112,128},{128,112... | collective-permute-start | bytes 239624 | tf_op jit(solution)/shard_map/ppermute | solution.py:423
  71.6 0.0 collective-permute-done.2.refs_1_.swapped
  71.6 0.6 shard_map.96
  72.2 10.1 %all-to-all-start.3 = ((f32[16,1,128]{2,1,0:T(1,128)}), f32[16,1,128]{2,1,0:T(1,128)S(1)}, u32[]{:S(2)}, u32[]{:S(2)}) async-start(f32[16,1,128]{2,1,0:T(1,128)} %shard_map.96), calls=%async_computation.3 | async-start | bytes 16384 | tf_op jit(solution)/shard_map/all_to_all | solution.py:425
  82.3 0.0 collective-permute-done.3.refs_2_.other
  82.3 5.1 %shard_map.95.found = f32[3,4,10,128]{3,2,1,0:T(8,128)S(1)} custom-call(f32[13,12,128]{2,1,0:T(8,128)S(1)} %shard_map.94.refs_0_.wide, f32[13,12,128]{2,1,0:T(8,128)S(1)} %collective-permute-done.2.refs_1_.swapped, f32[13,12,128]{2,1,0:T(8,128)S(1)} %collective-permute-done.3.refs_2_.other, f32[3,2,8,128]{3,2,1,0:T(8,128)S(1)} %shard_map.93.inner.refs_3_), custom_call_target="tpu_custom_call" | custom-call | flops 20000000000 | bytes 1048576 | tf_op jit(solution)/shard_map/pallas_call | solution.py:41
  87.4 5.0 %all-to-all-done.3.total = f32[16,1,128]{2,1,0:T(1,128)S(1)} async-done(((f32[16,1,128]{2,1,0:T(1,128)}), f32[16,1,128]{2,1,0:T(1,128)S(1)}, u32[]{:S(2)}, u32[]{:S(2)}) %all-to-all-start.3) | async-done | bytes 8224 | tf_op jit(solution)/shard_map/all_to_all | solution.py:425
  92.3 0.1 shard_map.97
  92.5 10.3 %all_to_all.45.got = f32[32,1,128]{2,1,0:T(1,128)S(1)} all-to-all(f32[32,1,128]{2,1,0:T(1,128)S(1)} %get-tuple-element.31), channel_id=1, replica_groups={{0,1,2,3,4,5,6,7,8,9,10,11,12,13,14,15,16,17,18,19,20,21,22,23,24,25,26..., dimensions={0} | all-to-all | bytes 32768 | tf_op jit(solution)/shard_map/all_to_all | solution.py:452
  102.8 17.0 %all_to_all.46.total = f32[16,1,128]{2,1,0:T(1,128)S(1)} all-to-all(f32[16,1,128]{2,1,0:T(1,128)S(1)} %shard_map.99), channel_id=1, replica_groups={{0,32,64,96,128,160,192,224,256,288,320,352,384,416,448,480},{1,33,65,9..., dimensions={0} | all-to-all | bytes 16384 | tf_op jit(solution)/shard_map/all_to_all | solution.py:454
  119.9 0.7 shard_map.100
  120.6 3.5 %all-to-all-start.6 = ((f32[16,1,128]{2,1,0:T(1,128)}), f32[16,1,128]{2,1,0:T(1,128)S(1)}, u32[]{:S(2)}, u32[]{:S(2)}) async-start(f32[16,1,128]{2,1,0:T(1,128)} %get-tuple-element.33), calls=%async_computation.6 | async-start | bytes 16384 | tf_op jit(solution)/shard_map/all_to_all | solution.py:458
  124.1 0.0 copy-start.1
  124.1 2.8 %shard_map.98.found = f32[3,2,8,128]{3,2,1,0:T(8,128)S(1)} custom-call(f32[5,4,10,128]{3,2,1,0:T(8,128)S(1)} %get-tuple-element.29.refs_0_), custom_call_target="tpu_custom_call" | custom-call | flops 20000000000 | bytes 1048576 | tf_op jit(solution)/shard_map/pallas_call | solution.py:41
  126.9 4.6 %all-to-all-done.6.total = f32[16,1,128]{2,1,0:T(1,128)S(1)} async-done(((f32[16,1,128]{2,1,0:T(1,128)}), f32[16,1,128]{2,1,0:T(1,128)S(1)}, u32[]{:S(2)}, u32[]{:S(2)}) %all-to-all-start.6) | async-done | bytes 8224 | tf_op jit(solution)/shard_map/all_to_all | solution.py:458
  131.5 0.0 copy-done.1
  131.5 14.4 %all_to_all.47.got = f32[8,88,128]{2,1,0:T(8,128)S(1)} all-to-all(f32[8,88,128]{2,1,0:T(8,128)S(1)} %shard_map.101), channel_id=1, replica_groups={{0,16,32,48,64,80,96,112},{128,144,160,176,192,208,224,240},{256,272,28..., dimensions={0} | all-to-all | bytes 720896 | tf_op jit(solution)/shard_map/all_to_all | solution.py:463
  146.0 0.1 shard_map.102
  146.0 21.0 %all_to_all.48.got = f32[4,88,128]{2,1,0:T(8,128)S(1)} all-to-all(f32[4,88,128]{2,1,0:T(8,128)S(1)} %shard_map.102), channel_id=1, replica_groups={{0,128,256,384},{16,144,272,400},{32,160,288,416},{48,176,304,432},{64,..., dimensions={0} | all-to-all | bytes 360448 | tf_op jit(solution)/shard_map/all_to_all | solution.py:465
  167.0 0.6 shard_map.103
  (4 shorter events, 0.1 us)
Async XLA Ops:
  2.4 7.2 %copy-start = (f32[3,2,8,128]{3,2,1,0:T(8,128)S(1)}, f32[3,2,8,128]{3,2,1,0:T(8,128)}, u32[]{:S(2)}) copy-start(f32[3,2,8,128]{3,2,1,0:T(8,128)} %get-tuple-element.21.refs_1_.marks.refs_2_) | copy-start | bytes 73732
  2.4 7.2 %copy-start.2 = (f32[5,2,8,128]{3,2,1,0:T(8,128)S(1)}, f32[5,2,8,128]{3,2,1,0:T(8,128)}, u32[]{:S(2)}) copy-start(f32[5,2,8,128]{3,2,1,0:T(8,128)} %get-tuple-element.20.refs_0_.own) | copy-start | bytes 122884
  2.4 16.4 %all-to-all-start = ((f32[16,32,128]{2,1,0:T(8,128)}), f32[16,32,128]{2,1,0:T(8,128)S(1)}, u32[]{:S(2)}, u32[]{:S(2)}) async-start(f32[16,32,128]{2,1,0:T(8,128)} %get-tuple-element.22), calls=%async_computation | async-start | bytes 524288 | tf_op jit(solution)/shard_map/all_to_all | solution.py:420
  18.9 6.9 %collective-permute-start = (f32[13,12,128]{2,1,0:T(8,128)S(1)}, f32[13,12,128]{2,1,0:T(8,128)S(1)}, u32[]{:S(2)}, u32[]{:S(2)}) collective-permute-start(f32[13,12,128]{2,1,0:T(8,128)S(1)} %shard_map.88.refs_0_.refs_3_.wide), channel_id=1, source_target_pairs={{0,16},{16,0},{32,48},{48,32},{64,80},{80,64},{96,112},{112,96},{1... | collective-permute-start | bytes 239624 | tf_op jit(solution)/shard_map/ppermute | solution.py:423
  21.4 19.7 %collective-permute-start.1 = (f32[13,12,128]{2,1,0:T(8,128)S(1)}, f32[13,12,128]{2,1,0:T(8,128)S(1)}, u32[]{:S(2)}, u32[]{:S(2)}) collective-permute-start(f32[13,12,128]{2,1,0:T(8,128)S(1)} %shard_map.88.refs_0_.refs_3_.wide), channel_id=1, source_target_pairs={{16,32},{32,16},{48,64},{64,48},{80,96},{96,80},{112,128},{128,112... | collective-permute-start | bytes 239624 | tf_op jit(solution)/shard_map/ppermute | solution.py:423
  26.3 24.8 %all-to-all-start.1 = ((f32[16,1,128]{2,1,0:T(1,128)}), f32[16,1,128]{2,1,0:T(1,128)S(1)}, u32[]{:S(2)}, u32[]{:S(2)}) async-start(f32[16,1,128]{2,1,0:T(1,128)} %shard_map.91), calls=%async_computation.1 | async-start | bytes 16384 | tf_op jit(solution)/shard_map/all_to_all | solution.py:425
  52.0 12.7 %all-to-all-start.2 = ((f32[16,32,128]{2,1,0:T(8,128)}), f32[16,32,128]{2,1,0:T(8,128)S(1)}, u32[]{:S(2)}, u32[]{:S(2)}) async-start(f32[16,32,128]{2,1,0:T(8,128)} %get-tuple-element.26), calls=%async_computation.2 | async-start | bytes 524288 | tf_op jit(solution)/shard_map/all_to_all | solution.py:420
  64.7 6.9 %collective-permute-start.2 = (f32[13,12,128]{2,1,0:T(8,128)S(1)}, f32[13,12,128]{2,1,0:T(8,128)S(1)}, u32[]{:S(2)}, u32[]{:S(2)}) collective-permute-start(f32[13,12,128]{2,1,0:T(8,128)S(1)} %shard_map.94.refs_0_.wide), channel_id=1, source_target_pairs={{0,16},{16,0},{32,48},{48,32},{64,80},{80,64},{96,112},{112,96},{1... | collective-permute-start | bytes 239624 | tf_op jit(solution)/shard_map/ppermute | solution.py:423
  67.3 14.9 %collective-permute-start.3 = (f32[13,12,128]{2,1,0:T(8,128)S(1)}, f32[13,12,128]{2,1,0:T(8,128)S(1)}, u32[]{:S(2)}, u32[]{:S(2)}) collective-permute-start(f32[13,12,128]{2,1,0:T(8,128)S(1)} %shard_map.94.refs_0_.wide), channel_id=1, source_target_pairs={{16,32},{32,16},{48,64},{64,48},{80,96},{96,80},{112,128},{128,112... | collective-permute-start | bytes 239624 | tf_op jit(solution)/shard_map/ppermute | solution.py:423
  72.2 20.1 %all-to-all-start.3 = ((f32[16,1,128]{2,1,0:T(1,128)}), f32[16,1,128]{2,1,0:T(1,128)S(1)}, u32[]{:S(2)}, u32[]{:S(2)}) async-start(f32[16,1,128]{2,1,0:T(1,128)} %shard_map.96), calls=%async_computation.3 | async-start | bytes 16384 | tf_op jit(solution)/shard_map/all_to_all | solution.py:425
  120.6 10.9 %all-to-all-start.6 = ((f32[16,1,128]{2,1,0:T(1,128)}), f32[16,1,128]{2,1,0:T(1,128)S(1)}, u32[]{:S(2)}, u32[]{:S(2)}) async-start(f32[16,1,128]{2,1,0:T(1,128)} %get-tuple-element.33), calls=%async_computation.6 | async-start | bytes 16384 | tf_op jit(solution)/shard_map/all_to_all | solution.py:458
  124.1 7.4 %copy-start.1 = (s32[16,128]{1,0:T(8,128)S(1)}, s32[16,128]{1,0:T(8,128)}, u32[]{:S(2)}) copy-start(s32[16,128]{1,0:T(8,128)} %get-tuple-element.19.route) | copy-start | bytes 24580

commit v10 on v9

--- a/solution.py
+++ b/solution.py
@@ -161,11 +161,11 @@
     force[...] = jnp.broadcast_to((wide[last, 0:1] + swapped[last, 0:1])[None], force.shape)
 
 
-def spread_kernel(got, force):
+def spread_kernel(got, before, force):
     force[...] = jnp.broadcast_to(jnp.sum(got[...], axis=0, keepdims=True), force.shape)
 
 
-def pair_sums(columns, center, pairs, out, feat, acc2, acc3, earlier=None):
+def pair_sums(columns, center, pairs, out, feat, acc2, acc3, earlier={}):
     x0, y0, _ = center
     tall, slots = columns[0][0].shape
     row0 = min(r for _, r in pairs)
@@ -219,9 +219,8 @@
         ]
         for f in range(3):
             out[f, n] = rates[f]
-            if earlier is not None and 0 < n <= earlier.shape[1]:
-                inner = earlier[f, n - 1]
-                out[f, n, 1 : rows - 1] = rates[f][1 : rows - 1] + inner
+            if c in earlier:
+                out[f, n, 1 : rows - 1] = rates[f][1 : rows - 1] + earlier[c][f]
 
 
 def around_cell(c, r):
@@ -252,15 +251,18 @@
     return columns
 
 
-def wide_rates_kernel(size, wide, swapped, other, inner, out, feat, acc2, acc3):
+def wide_rates_kernel(wanted, size, wide, swapped, other, inner, out, feat, acc2, acc3):
     cols, rows = size
-    columns = [fields[:5] for fields in wide_columns(cols, wide, swapped, other)]
+    start, stop = wanted[0] - 1, wanted[-1] + 2
+    columns = [fields[:5] for fields in wide_columns(cols, wide, swapped, other)[start:stop]]
     block = [(c + cols, r + HALO) for c in range(cols) for r in range(rows)]
     pairs = {}
-    for c in range(1, 3 * cols - 1):
+    for c in wanted:
         for r in range(1, rows + 3):
-            pairs[c, r] = [j for j in around_cell(c, r) if (c, r) not in block or j not in block]
-    pair_sums(columns, origin(*size), pairs, out, feat, acc2, acc3, inner)
+            around = [j for j in around_cell(c, r) if (c, r) not in block or j not in block]
+            pairs[c - start, r] = [(a - start, b) for a, b in around]
+    earlier = {c + cols - start: [inner[f, c] for f in range(3)] for c in range(cols)}
+    pair_sums(columns, origin(*size), pairs, out, feat, acc2, acc3, earlier)
 
 
 def rates_kernel(size, ring, out, feat, acc2, acc3):
@@ -270,27 +272,31 @@
     pair_sums(columns, origin(*size), pairs, out, feat, acc2, acc3)
 
 
+def by_column(*found):
+    return [[part[f, n] for f in range(3)] for part in found for n in range(part.shape[1])]
+
+
 def moved_ring(columns, found, offset, first, ring):
     for n in range(ring.shape[1]):
         x, y, u, v, s, touch = [f[1:-1] for f in columns[n + 1]]
         live = jnp.where(x < 0.5 * FAR, 1.0, 0.0)
         pen = touch * jnp.maximum(0.0, x - (first + (n - 1)) + offset - 0.5)
-        u = u + DT * live * (found[0, n] - STIFF * pen)
-        v = v + DT * live * found[1, n]
+        u = u + DT * live * (found[n][0] - STIFF * pen)
+        v = v + DT * live * found[n][1]
         ring[0, n] = x + DT * live * u
         ring[1, n] = y + DT * live * v
         ring[2, n] = u
         ring[3, n] = v
-        ring[4, n] = s + DT * live * found[2, n]
+        ring[4, n] = s + DT * live * found[n][2]
 
 
 def moved_state(own, found, marks, offset, first):
     cols, rows = own.shape[1:3]
-    side, rim = (found.shape[1] - cols) // 2, (found.shape[2] - rows) // 2
+    side, rim = (len(found) - cols) // 2, (found[0][0].shape[0] - rows) // 2
     new = []
     for c in range(cols):
         live = marks[0, c]
-        ax, ay, drho = [found[f, c + side][rim : rim + rows] for f in range(3)]
+        ax, ay, drho = [part[rim : rim + rows] for part in found[c + side]]
         pen = penalties(own[0, c], marks[1, c], live, offset, first + c)
         u = own[2, c] + DT * live * (ax - STIFF * pen)
         v = own[3, c] + DT * live * ay
@@ -315,6 +321,7 @@
 def first_update_kernel(size, own, found, marks, wide, swapped, other, new_own, out, feat, acc2, acc3, ring):
     first = origin(*size)[2]
     offset = marks[2, 0, 0:1]
+    found = by_column(found)
     keep(moved_state(own, found, marks, offset, first), new_own)
     moved_ring(wide_columns(size[0], wide, swapped, other), found, offset, first, ring)
     rates_kernel(size, ring, out, feat, acc2, acc3)
@@ -326,23 +333,19 @@
     new_tool[0:1] = offset
     new_tool[1:2] = speed
     state = [[own[f, c] for f in range(5)] for c in range(own.shape[1])]
-    new = moved_state(own, found, marks, offset, first)
+    new = moved_state(own, by_column(found), marks, offset, first)
     keep(new, new_own)
     fill_depth(new, marks, own_force(state, marks, offset, first), sent)
 
 
-def third_update_kernel(scale, own, found, marks, wide, swapped, other, tool, total, new_own, ring, new_tool, force):
+def third_update_kernel(own, first_found, last_found, marks, wide, swapped, other, tool, new_own, ring):
     first = origin(*own.shape[1:3])[2]
-    offset, speed = tool_step(tool[0:1], tool[1:2], jnp.sum(total[...], axis=0), scale)
-    new_tool[0:1] = offset
-    new_tool[1:2] = speed
-    state = [[own[f, c] for f in range(5)] for c in range(own.shape[1])]
-    force[...] = jnp.broadcast_to(own_force(state, marks, offset, first)[None], force.shape)
-    keep(moved_state(own, found, marks, offset, first), new_own)
-    moved_ring(wide_columns(own.shape[1], wide, swapped, other), found, offset, first, ring)
-
-
-def last_force_kernel(scale, own, marks, tool, total, new_tool, force):
+    found = by_column(first_found, last_found)
+    keep(moved_state(own, found, marks, tool[0:1], first), new_own)
+    moved_ring(wide_columns(own.shape[1], wide, swapped, other), found, tool[0:1], first, ring)
+
+
+def next_force_kernel(scale, own, marks, tool, total, new_tool, force):
     offset, speed = tool_step(tool[0:1], tool[1:2], jnp.sum(total[...], axis=0), scale)
     new_tool[0:1] = offset
     new_tool[1:2] = speed
@@ -354,7 +357,7 @@
 def last_kernel(near, route, own, found, marks, tool, total, sent):
     cols, rows, slots = own.shape[1:]
     size = 5 * cols * rows
-    new = moved_state(own, found, marks, tool[0:1], origin(cols, rows)[2])
+    new = moved_state(own, by_column(found), marks, tool[0:1], origin(cols, rows)[2])
     sent[:, size:, :] = jnp.broadcast_to(jnp.sum(total[...], axis=0, keepdims=True), (near, sent.shape[1] - size, slots))
     target = route[0:1]
     for k in range(near):
@@ -407,7 +410,7 @@
     pairs = range(0, ncut, 2)
     planes = [[(c + k) * ndepth + d for k in range(2) for d in range(ndepth)] for c in pairs]
     lines = [[(c + k) * ndepth + d for c in pairs] for k in range(2) for d in range(ndepth)]
-    ring, ring_rates = shape(5, cols + 2, rows + 2, slots), shape(3, cols + 2, rows + 2, slots)
+    ring = shape(5, cols + 2, rows + 2, slots)
     block_rates = shape(3, cols, rows, slots)
     swap = [(i, i ^ 1) for i in range(ncut)]
     cross = [(i, i + 1 if i % 2 else i - 1) for i in range(1, ncut - 1)]
@@ -423,8 +426,12 @@
         swapped, other = lax.ppermute(wide, "cut", swap), lax.ppermute(wide, "cut", cross)
         force = call(pair_force_kernel, along_line, (), (wide, swapped))
         total = lax.all_to_all(force, both, 0, 0, tiled=True, axis_index_groups=lines)
-        found = rates_of(wide_rates_kernel, ring_rates, (wide, swapped, other, inner), 3 * cols * (rows + 4), (cols + 2) * (rows + 2))
-        return found, (wide, swapped, other), total
+        return (wide, swapped, other), inner, total
+
+    def wide_rates(around, inner, first, last):
+        out = shape(3, last - first, rows + 2, slots)
+        read, summed = (last - first + 2) * (rows + 4), (last - first) * (rows + 2)
+        return rates_of(functools.partial(wide_rates_kernel, range(first, last)), out, (*around, inner), read, summed)
 
     inputs = (positions, velocity, density, counts, contact_mask, destination[None], tool[None])
     own, marks, route, sent = pl.pallas_call(
@@ -435,7 +442,8 @@
         scratch_shapes=[pltpu.VMEM(part.shape, part.dtype) for part in inputs[3:]] + [pltpu.SemaphoreType.DMA((7,))],
         compiler_params=pltpu.CompilerParams(vmem_limit_bytes=60 * 1024 * 1024),
     )(*inputs)
-    found, around, total = exchange(own, marks, sent)
+    around, inner, total = exchange(own, marks, sent)
+    found = wide_rates(around, inner, 1, 3 * cols - 1)
     rest = (pltpu.VMEM(ring.shape, F32),)
     read, summed = (cols + 2) * (rows + 2), cols * rows
     own, found = rates_of(first_update_kernel, [state, block_rates], (own, found, marks, *around), read, summed, rest)
@@ -443,17 +451,18 @@
     kernel = functools.partial(second_update_kernel, scale)
     own, tool, sent = call(kernel, [state, vector, message], (), (own, found, marks, total))
 
-    found, around, total = exchange(own, marks, sent)
-    kernel = functools.partial(third_update_kernel, scale)
-    outs = [state, ring, vector, along_plane]
-    new_own, ringed, tool, force = call(kernel, outs, (), (own, found, marks, *around, tool, total))
-    own = new_own
-
+    around, inner, total = exchange(own, marks, sent)
+    kernel = functools.partial(next_force_kernel, scale)
+    tool, force = call(kernel, [vector, along_plane], (), (own, marks, tool, total))
     got = lax.all_to_all(force, both, 0, 0, tiled=True, axis_index_groups=planes)
-    force = call(spread_kernel, along_line, (), (got,))
+    middle = 3 * cols // 2
+    first_found = wide_rates(around, inner, 1, middle)
+    force = call(spread_kernel, along_line, (), (got, first_found))
     total = lax.all_to_all(force, both, 0, 0, tiled=True, axis_index_groups=lines)
+    last_found = wide_rates(around, inner, middle, 3 * cols - 1)
+    own, ringed = call(third_update_kernel, [state, ring], (), (own, first_found, last_found, marks, *around, tool))
     found = rates_of(rates_kernel, block_rates, (ringed,), (cols + 2) * (rows + 2), cols * rows)
-    kernel = functools.partial(last_force_kernel, scale)
+    kernel = functools.partial(next_force_kernel, scale)
     tool, force = call(kernel, [vector, along_depth], (), (own, marks, tool, total))
     total = lax.all_to_all(force, "depth", 0, 0, tiled=True)
     kernel = functools.partial(last_kernel, near)

time: 169 us -> 168 us (level)
  blocking collectives: 62.8 us -> 55.5 us
  waiting for transfers between devices: 27.5 us -> 34.4 us
    all_to_all x0 -> x2, waiting for transfers between devices: none -> 11.9 us  [the longest x1 7.37 us: body(): lax.all_to_all(force, both, 0, 0, tiled=True, axis_index_groups=lines)]
    all_to_all x2 -> x1, starting transfers between devices: 24.8 us -> 14.8 us  [exchange(): lax.all_to_all(force, both, 0, 0, tiled=True, axis_index_groups=lines)]
    all_to_all x0 -> x2, starting transfers between devices: none -> 9.5 us  [the longest x1 5.67 us: body(): lax.all_to_all(force, both, 0, 0, tiled=True, axis_index_groups=lines)]
    all_to_all x2 -> x1, blocking collectives: 27.4 us -> 20 us  [exchange(): lax.all_to_all(force, both, 0, 0, tiled=True, axis_index_groups=lines)]
    all_to_all x2 -> x1, waiting for transfers between devices: 6.93 us -> 1.97 us  [exchange(): lax.all_to_all(force, both, 0, 0, tiled=True, axis_index_groups=lines)]
    pallas_call x17 -> x19, Pallas kernels: 23.4 us -> 24.3 us  [call(): pl.pallas_call(kernel, out_shape=outs, in_specs=[SMEM] * len(scalars) + [...]
  transfers between devices with their start and end apart: 9 -> 10, of which waited for: 6 -> 7; matrix products, arithmetic and copies ran while one was open for 0% -> 0% of each run, Pallas kernels for 12% -> 13%
where the time goes in v10:
time: 168 us
  blocking collectives  55.5 us (33%)
  starting transfers between devices  50.8 us (30%)
  waiting for transfers between devices  34.4 us (20%)
  Pallas kernels  26.1 us (16%)
    pallas_call x19, Pallas kernels, call(): pl.pallas_call(kernel, out_shape=outs, in_specs=[SMEM] * len(scalars) + [...  24.3 us
    all_to_all x1, blocking collectives, body(): got = lax.all_to_all(sent, 'cut', 0, 0, tiled=True, axis_index_groups=apart)  21.1 us
    all_to_all x1, blocking collectives, exchange(): lax.all_to_all(force, both, 0, 0, tiled=True, axis_index_groups=lines)  20 us
    all_to_all x1, starting transfers between devices, exchange(): lax.all_to_all(force, both, 0, 0, tiled=True, axis_index_groups=lines)  14.8 us
    all_to_all x2, waiting for transfers between devices, exchange(): got = lax.all_to_all(sent, 'depth', 0, 0, tiled=True)  14.5 us
    all_to_all x1, blocking collectives, body(): got = lax.all_to_all(sent, 'cut', 0, 0, tiled=True, axis_index_groups=close)  14.4 us
    all_to_all x2, starting transfers between devices, exchange(): got = lax.all_to_all(sent, 'depth', 0, 0, tiled=True)  10.9 us
    all_to_all x1, waiting for transfers between devices, body(): lax.all_to_all(force, both, 0, 0, tiled=True, axis_index_groups=lines)  7.37 us
  transfers between devices with their start and end apart: 10, of which 7 were waited for; matrix products, arithmetic and copies ran while one was open for 0% of the time, Pallas kernels for 13%

profile of v10, /device:TPU:64, one launch (start us, length us, event | category | flops | bytes accessed | tf_op | source)
XLA Modules:
  0.0 167.7 jit_solution(5324813267072784880)
XLA Ops:
  0.6 1.8 %shard_map.86 = (f32[5,2,8,128]{3,2,1,0:T(8,128)}, f32[3,2,8,128]{3,2,1,0:T(8,128)}, s32[16,128]{1,0:T(8,128)}, f32[16,32,128]{2,1,0:T(8,128)}) custom-call(f32[2,2,8,128]{3,2,1,0:T(8,128)} %refs_0_.1, f32[2,2,8,128]{3,2,1,0:T(8,128)} %refs_1_.1, f32[2,8,128]{2,1,0:T(8,128)} %refs_2_.1, s32[2,8]{1,0:T(2,128)} %refs_3_.1, s32[2,8]{1,0:T(2,128)} %refs_4_.1, ...), custom_call_target="tpu_custom_call" | custom-call | tf_op jit(solution)/shard_map/pallas_call | solution.py:437
  2.4 0.0 copy-start
  2.4 0.0 copy-start.2
  2.4 7.2 %all-to-all-start = ((f32[16,32,128]{2,1,0:T(8,128)}), f32[16,32,128]{2,1,0:T(8,128)S(1)}, u32[]{:S(2)}, u32[]{:S(2)}) async-start(f32[16,32,128]{2,1,0:T(8,128)} %get-tuple-element.22), calls=%async_computation | async-start | bytes 524288 | tf_op jit(solution)/shard_map/all_to_all | solution.py:423
  9.6 0.0 copy-done
  9.6 0.0 copy-done.2
  9.6 1.9 %shard_map.87.inner.refs_3_ = f32[3,2,8,128]{3,2,1,0:T(8,128)S(1)} custom-call(f32[5,2,8,128]{3,2,1,0:T(8,128)S(1)} %copy-done.2, f32[3,2,8,128]{3,2,1,0:T(8,128)S(1)} %copy-done), custom_call_target="tpu_custom_call" | custom-call | flops 20000000000 | bytes 1048576 | tf_op jit(solution)/shard_map/pallas_call | solution.py:41
  11.5 7.3 %all-to-all-done.got = f32[16,32,128]{2,1,0:T(8,128)S(1)} async-done(((f32[16,32,128]{2,1,0:T(8,128)}), f32[16,32,128]{2,1,0:T(8,128)S(1)}, u32[]{:S(2)}, u32[]{:S(2)}) %all-to-all-start) | async-done | bytes 262176 | tf_op jit(solution)/shard_map/all_to_all | solution.py:423
  18.9 2.6 %collective-permute-start = (f32[13,12,128]{2,1,0:T(8,128)S(1)}, f32[13,12,128]{2,1,0:T(8,128)S(1)}, u32[]{:S(2)}, u32[]{:S(2)}) collective-permute-start(f32[13,12,128]{2,1,0:T(8,128)S(1)} %shard_map.88.refs_0_.refs_3_.wide), channel_id=1, source_target_pairs={{0,16},{16,0},{32,48},{48,32},{64,80},{80,64},{96,112},{112,96},{1... | collective-permute-start | bytes 239624 | tf_op jit(solution)/shard_map/ppermute | solution.py:426
  21.5 2.8 %collective-permute-start.1 = (f32[13,12,128]{2,1,0:T(8,128)S(1)}, f32[13,12,128]{2,1,0:T(8,128)S(1)}, u32[]{:S(2)}, u32[]{:S(2)}) collective-permute-start(f32[13,12,128]{2,1,0:T(8,128)S(1)} %shard_map.88.refs_0_.refs_3_.wide), channel_id=1, source_target_pairs={{16,32},{32,16},{48,64},{64,48},{80,96},{96,80},{112,128},{128,112... | collective-permute-start | bytes 239624 | tf_op jit(solution)/shard_map/ppermute | solution.py:426
  24.3 1.5 collective-permute-done.refs_1_.refs_4_.swapped
  25.7 0.6 shard_map.91
  26.3 14.8 %all-to-all-start.1 = ((f32[16,1,128]{2,1,0:T(1,128)}), f32[16,1,128]{2,1,0:T(1,128)S(1)}, u32[]{:S(2)}, u32[]{:S(2)}) async-start(f32[16,1,128]{2,1,0:T(1,128)} %shard_map.91), calls=%async_computation.1 | async-start | bytes 16384 | tf_op jit(solution)/shard_map/all_to_all | solution.py:428
  41.1 0.0 collective-permute-done.1.refs_2_.refs_5_
  41.1 5.1 %shard_map.89.refs_1_ = f32[3,4,10,128]{3,2,1,0:T(8,128)S(1)} custom-call(f32[13,12,128]{2,1,0:T(8,128)S(1)} %shard_map.88.refs_0_.refs_3_.wide, f32[13,12,128]{2,1,0:T(8,128)S(1)} %collective-permute-done.refs_1_.refs_4_.swapped, f32[13,12,128]{2,1,0:T(8,128)S(1)} %collective-permute-done.1.refs_2_.refs_5_, f32[3,2,8,128]{3,2,1,0:T(8,128)S(1)} %shard_map.87.inner.refs_3_), custom_call_target="tpu_custom_call" | custom-call | flops 20000000000 | bytes 1048576 | tf_op jit(solution)/shard_map/pallas_call | solution.py:41
  46.2 3.0 %shard_map.90 = (f32[5,2,8,128]{3,2,1,0:T(8,128)S(1)}, f32[3,2,8,128]{3,2,1,0:T(8,128)S(1)}) custom-call(f32[5,2,8,128]{3,2,1,0:T(8,128)S(1)} %copy-done.2, f32[3,4,10,128]{3,2,1,0:T(8,128)S(1)} %shard_map.89.refs_1_, f32[3,2,8,128]{3,2,1,0:T(8,128)S(1)} %copy-done, f32[13,12,128]{2,1,0:T(8,128)S(1)} %shard_map.88.refs_0_.refs_3_.wide, ...), custom_call_target="tpu_custom_call" | custom-call | flops 20000000000 | bytes 1048576 | tf_op jit(solution)/shard_map/pallas_call | solution.py:41
  49.2 2.0 %all-to-all-done.1.total = f32[16,1,128]{2,1,0:T(1,128)S(1)} async-done(((f32[16,1,128]{2,1,0:T(1,128)}), f32[16,1,128]{2,1,0:T(1,128)S(1)}, u32[]{:S(2)}, u32[]{:S(2)}) %all-to-all-start.1) | async-done | bytes 8224 | tf_op jit(solution)/shard_map/all_to_all | solution.py:428
  51.2 0.8 shard_map.92
  52.0 3.7 %all-to-all-start.2 = ((f32[16,32,128]{2,1,0:T(8,128)}), f32[16,32,128]{2,1,0:T(8,128)S(1)}, u32[]{:S(2)}, u32[]{:S(2)}) async-start(f32[16,32,128]{2,1,0:T(8,128)} %get-tuple-element.26), calls=%async_computation.2 | async-start | bytes 524288 | tf_op jit(solution)/shard_map/all_to_all | solution.py:423
  55.7 1.9 %shard_map.93.inner.refs_3_ = f32[3,2,8,128]{3,2,1,0:T(8,128)S(1)} custom-call(f32[5,2,8,128]{3,2,1,0:T(8,128)S(1)} %get-tuple-element.25.refs_0_.own, f32[3,2,8,128]{3,2,1,0:T(8,128)S(1)} %copy-done), custom_call_target="tpu_custom_call" | custom-call | flops 20000000000 | bytes 1048576 | tf_op jit(solution)/shard_map/pallas_call | solution.py:41
  57.6 7.1 %all-to-all-done.2.got = f32[16,32,128]{2,1,0:T(8,128)S(1)} async-done(((f32[16,32,128]{2,1,0:T(8,128)}), f32[16,32,128]{2,1,0:T(8,128)S(1)}, u32[]{:S(2)}, u32[]{:S(2)}) %all-to-all-start.2) | async-done | bytes 262176 | tf_op jit(solution)/shard_map/all_to_all | solution.py:423
  64.7 2.6 %collective-permute-start.2 = (f32[13,12,128]{2,1,0:T(8,128)S(1)}, f32[13,12,128]{2,1,0:T(8,128)S(1)}, u32[]{:S(2)}, u32[]{:S(2)}) collective-permute-start(f32[13,12,128]{2,1,0:T(8,128)S(1)} %shard_map.94.refs_0_.wide), channel_id=1, source_target_pairs={{0,16},{16,0},{32,48},{48,32},{64,80},{80,64},{96,112},{112,96},{1... | collective-permute-start | bytes 239624 | tf_op jit(solution)/shard_map/ppermute | solution.py:426
  67.3 4.2 %collective-permute-start.3 = (f32[13,12,128]{2,1,0:T(8,128)S(1)}, f32[13,12,128]{2,1,0:T(8,128)S(1)}, u32[]{:S(2)}, u32[]{:S(2)}) collective-permute-start(f32[13,12,128]{2,1,0:T(8,128)S(1)} %shard_map.94.refs_0_.wide), channel_id=1, source_target_pairs={{16,32},{32,16},{48,64},{64,48},{80,96},{96,80},{112,128},{128,112... | collective-permute-start | bytes 239624 | tf_op jit(solution)/shard_map/ppermute | solution.py:426
  71.6 0.0 collective-permute-done.2.refs_1_.swapped
  71.6 20.0 %all_to_all.45.total = f32[16,1,128]{2,1,0:T(1,128)S(1)} all-to-all(f32[16,1,128]{2,1,0:T(1,128)S(1)} %shard_map.97), channel_id=1, replica_groups={{0,32,64,96,128,160,192,224,256,288,320,352,384,416,448,480},{1,33,65,9..., dimensions={0} | all-to-all | bytes 16384 | tf_op jit(solution)/shard_map/all_to_all | solution.py:428
  91.6 0.7 shard_map.98
  92.3 3.8 %all-to-all-start.4 = ((f32[32,1,128]{2,1,0:T(1,128)}), f32[32,1,128]{2,1,0:T(1,128)S(1)}, u32[]{:S(2)}, u32[]{:S(2)}) async-start(f32[32,1,128]{2,1,0:T(1,128)} %get-tuple-element.31), calls=%async_computation.4 | async-start | bytes 32768 | tf_op jit(solution)/shard_map/all_to_all | solution.py:457
  96.2 0.0 collective-permute-done.3.refs_2_.other
  96.2 2.7 %shard_map.95.first_found.before = f32[3,2,10,128]{3,2,1,0:T(8,128)S(1)} custom-call(f32[13,12,128]{2,1,0:T(8,128)S(1)} %shard_map.94.refs_0_.wide, f32[13,12,128]{2,1,0:T(8,128)S(1)} %collective-permute-done.2.refs_1_.swapped, f32[13,12,128]{2,1,0:T(8,128)S(1)} %collective-permute-done.3.refs_2_.other, f32[3,2,8,128]{3,2,1,0:T(8,128)S(1)} %shard_map.93.inner.refs_3_), custom_call_target="tpu_custom_call" | custom-call | flops 20000000000 | bytes 1048576 | tf_op jit(solution)/shard_map/pallas_call | solution.py:41
  98.9 4.5 %all-to-all-done.4.got = f32[32,1,128]{2,1,0:T(1,128)S(1)} async-done(((f32[32,1,128]{2,1,0:T(1,128)}), f32[32,1,128]{2,1,0:T(1,128)S(1)}, u32[]{:S(2)}, u32[]{:S(2)}) %all-to-all-start.4) | async-done | bytes 16416 | tf_op jit(solution)/shard_map/all_to_all | solution.py:457
  103.4 0.6 shard_map.101
  104.0 5.7 %all-to-all-start.5 = ((f32[16,1,128]{2,1,0:T(1,128)}), f32[16,1,128]{2,1,0:T(1,128)S(1)}, u32[]{:S(2)}, u32[]{:S(2)}) async-start(f32[16,1,128]{2,1,0:T(1,128)} %shard_map.101), calls=%async_computation.5 | async-start | bytes 16384 | tf_op jit(solution)/shard_map/all_to_all | solution.py:461
  109.7 2.7 %shard_map.96.last_found = f32[3,2,10,128]{3,2,1,0:T(8,128)S(1)} custom-call(f32[13,12,128]{2,1,0:T(8,128)S(1)} %shard_map.94.refs_0_.wide, f32[13,12,128]{2,1,0:T(8,128)S(1)} %collective-permute-done.2.refs_1_.swapped, f32[13,12,128]{2,1,0:T(8,128)S(1)} %collective-permute-done.3.refs_2_.other, f32[3,2,8,128]{3,2,1,0:T(8,128)S(1)} %shard_map.93.inner.refs_3_), custom_call_target="tpu_custom_call" | custom-call | flops 20000000000 | bytes 1048576 | tf_op jit(solution)/shard_map/pallas_call | solution.py:41
  112.3 0.1 shard_map.99
  112.4 7.4 %all-to-all-done.5.total = f32[16,1,128]{2,1,0:T(1,128)S(1)} async-done(((f32[16,1,128]{2,1,0:T(1,128)}), f32[16,1,128]{2,1,0:T(1,128)S(1)}, u32[]{:S(2)}, u32[]{:S(2)}) %all-to-all-start.5) | async-done | bytes 8224 | tf_op jit(solution)/shard_map/all_to_all | solution.py:461
  119.8 0.7 shard_map.102
  120.5 3.5 %all-to-all-start.6 = ((f32[16,1,128]{2,1,0:T(1,128)}), f32[16,1,128]{2,1,0:T(1,128)S(1)}, u32[]{:S(2)}, u32[]{:S(2)}) async-start(f32[16,1,128]{2,1,0:T(1,128)} %get-tuple-element.33), calls=%async_computation.6 | async-start | bytes 16384 | tf_op jit(solution)/shard_map/all_to_all | solution.py:467
  124.0 0.0 copy-start.1
  124.0 2.8 %shard_map.100.found = f32[3,2,8,128]{3,2,1,0:T(8,128)S(1)} custom-call(f32[5,4,10,128]{3,2,1,0:T(8,128)S(1)} %get-tuple-element.30.refs_0_), custom_call_target="tpu_custom_call" | custom-call | flops 20000000000 | bytes 1048576 | tf_op jit(solution)/shard_map/pallas_call | solution.py:41
  126.8 4.6 %all-to-all-done.6.total = f32[16,1,128]{2,1,0:T(1,128)S(1)} async-done(((f32[16,1,128]{2,1,0:T(1,128)}), f32[16,1,128]{2,1,0:T(1,128)S(1)}, u32[]{:S(2)}, u32[]{:S(2)}) %all-to-all-start.6) | async-done | bytes 8224 | tf_op jit(solution)/shard_map/all_to_all | solution.py:467
  131.4 0.0 copy-done.1
  131.4 14.4 %all_to_all.46.got = f32[8,88,128]{2,1,0:T(8,128)S(1)} all-to-all(f32[8,88,128]{2,1,0:T(8,128)S(1)} %shard_map.103), channel_id=1, replica_groups={{0,16,32,48,64,80,96,112},{128,144,160,176,192,208,224,240},{256,272,28..., dimensions={0} | all-to-all | bytes 720896 | tf_op jit(solution)/shard_map/all_to_all | solution.py:472
  145.9 0.1 shard_map.104
  146.0 21.1 %all_to_all.47.got = f32[4,88,128]{2,1,0:T(8,128)S(1)} all-to-all(f32[4,88,128]{2,1,0:T(8,128)S(1)} %shard_map.104), channel_id=1, replica_groups={{0,128,256,384},{16,144,272,400},{32,160,288,416},{48,176,304,432},{64,..., dimensions={0} | all-to-all | bytes 360448 | tf_op jit(solution)/shard_map/all_to_all | solution.py:474
  167.0 0.6 shard_map.105
  (4 shorter events, 0.1 us)
Async XLA Ops:
  2.4 7.2 %copy-start = (f32[3,2,8,128]{3,2,1,0:T(8,128)S(1)}, f32[3,2,8,128]{3,2,1,0:T(8,128)}, u32[]{:S(2)}) copy-start(f32[3,2,8,128]{3,2,1,0:T(8,128)} %get-tuple-element.21.refs_1_.marks.refs_2_) | copy-start | bytes 73732
  2.4 7.2 %copy-start.2 = (f32[5,2,8,128]{3,2,1,0:T(8,128)S(1)}, f32[5,2,8,128]{3,2,1,0:T(8,128)}, u32[]{:S(2)}) copy-start(f32[5,2,8,128]{3,2,1,0:T(8,128)} %get-tuple-element.20.refs_0_.own) | copy-start | bytes 122884
  2.4 16.4 %all-to-all-start = ((f32[16,32,128]{2,1,0:T(8,128)}), f32[16,32,128]{2,1,0:T(8,128)S(1)}, u32[]{:S(2)}, u32[]{:S(2)}) async-start(f32[16,32,128]{2,1,0:T(8,128)} %get-tuple-element.22), calls=%async_computation | async-start | bytes 524288 | tf_op jit(solution)/shard_map/all_to_all | solution.py:423
  18.9 6.9 %collective-permute-start = (f32[13,12,128]{2,1,0:T(8,128)S(1)}, f32[13,12,128]{2,1,0:T(8,128)S(1)}, u32[]{:S(2)}, u32[]{:S(2)}) collective-permute-start(f32[13,12,128]{2,1,0:T(8,128)S(1)} %shard_map.88.refs_0_.refs_3_.wide), channel_id=1, source_target_pairs={{0,16},{16,0},{32,48},{48,32},{64,80},{80,64},{96,112},{112,96},{1... | collective-permute-start | bytes 239624 | tf_op jit(solution)/shard_map/ppermute | solution.py:426
  21.5 19.7 %collective-permute-start.1 = (f32[13,12,128]{2,1,0:T(8,128)S(1)}, f32[13,12,128]{2,1,0:T(8,128)S(1)}, u32[]{:S(2)}, u32[]{:S(2)}) collective-permute-start(f32[13,12,128]{2,1,0:T(8,128)S(1)} %shard_map.88.refs_0_.refs_3_.wide), channel_id=1, source_target_pairs={{16,32},{32,16},{48,64},{64,48},{80,96},{96,80},{112,128},{128,112... | collective-permute-start | bytes 239624 | tf_op jit(solution)/shard_map/ppermute | solution.py:426
  26.3 24.8 %all-to-all-start.1 = ((f32[16,1,128]{2,1,0:T(1,128)}), f32[16,1,128]{2,1,0:T(1,128)S(1)}, u32[]{:S(2)}, u32[]{:S(2)}) async-start(f32[16,1,128]{2,1,0:T(1,128)} %shard_map.91), calls=%async_computation.1 | async-start | bytes 16384 | tf_op jit(solution)/shard_map/all_to_all | solution.py:428
  52.0 12.7 %all-to-all-start.2 = ((f32[16,32,128]{2,1,0:T(8,128)}), f32[16,32,128]{2,1,0:T(8,128)S(1)}, u32[]{:S(2)}, u32[]{:S(2)}) async-start(f32[16,32,128]{2,1,0:T(8,128)} %get-tuple-element.26), calls=%async_computation.2 | async-start | bytes 524288 | tf_op jit(solution)/shard_map/all_to_all | solution.py:423
  64.7 6.9 %collective-permute-start.2 = (f32[13,12,128]{2,1,0:T(8,128)S(1)}, f32[13,12,128]{2,1,0:T(8,128)S(1)}, u32[]{:S(2)}, u32[]{:S(2)}) collective-permute-start(f32[13,12,128]{2,1,0:T(8,128)S(1)} %shard_map.94.refs_0_.wide), channel_id=1, source_target_pairs={{0,16},{16,0},{32,48},{48,32},{64,80},{80,64},{96,112},{112,96},{1... | collective-permute-start | bytes 239624 | tf_op jit(solution)/shard_map/ppermute | solution.py:426
  67.3 28.8 %collective-permute-start.3 = (f32[13,12,128]{2,1,0:T(8,128)S(1)}, f32[13,12,128]{2,1,0:T(8,128)S(1)}, u32[]{:S(2)}, u32[]{:S(2)}) collective-permute-start(f32[13,12,128]{2,1,0:T(8,128)S(1)} %shard_map.94.refs_0_.wide), channel_id=1, source_target_pairs={{16,32},{32,16},{48,64},{64,48},{80,96},{96,80},{112,128},{128,112... | collective-permute-start | bytes 239624 | tf_op jit(solution)/shard_map/ppermute | solution.py:426
  92.3 11.0 %all-to-all-start.4 = ((f32[32,1,128]{2,1,0:T(1,128)}), f32[32,1,128]{2,1,0:T(1,128)S(1)}, u32[]{:S(2)}, u32[]{:S(2)}) async-start(f32[32,1,128]{2,1,0:T(1,128)} %get-tuple-element.31), calls=%async_computation.4 | async-start | bytes 32768 | tf_op jit(solution)/shard_map/all_to_all | solution.py:457
  104.0 15.8 %all-to-all-start.5 = ((f32[16,1,128]{2,1,0:T(1,128)}), f32[16,1,128]{2,1,0:T(1,128)S(1)}, u32[]{:S(2)}, u32[]{:S(2)}) async-start(f32[16,1,128]{2,1,0:T(1,128)} %shard_map.101), calls=%async_computation.5 | async-start | bytes 16384 | tf_op jit(solution)/shard_map/all_to_all | solution.py:461
  120.5 10.9 %all-to-all-start.6 = ((f32[16,1,128]{2,1,0:T(1,128)}), f32[16,1,128]{2,1,0:T(1,128)S(1)}, u32[]{:S(2)}, u32[]{:S(2)}) async-start(f32[16,1,128]{2,1,0:T(1,128)} %get-tuple-element.33), calls=%async_computation.6 | async-start | bytes 16384 | tf_op jit(solution)/shard_map/all_to_all | solution.py:467
  124.0 7.4 %copy-start.1 = (s32[16,128]{1,0:T(8,128)S(1)}, s32[16,128]{1,0:T(8,128)}, u32[]{:S(2)}) copy-start(s32[16,128]{1,0:T(8,128)} %get-tuple-element.19.route) | copy-start | bytes 24580

commit v11 on v10

--- a/solution.py
+++ b/solution.py
@@ -15,6 +15,8 @@
 DT = 0.05
 
 FAR = 1.0e6
+
+ROWS = 32
 
 COST = 20_000_000_000
 
@@ -173,20 +175,18 @@
     for c, (x, y, u, v, s) in enumerate(columns):
         lx, ly = x - x0, y - y0
         press, inv = pressure(s)
-        parts = [jnp.ones_like(x), press, u, v, u * lx + v * ly]
-        for part in (lx, ly, press * lx, press * ly):
-            high = part.astype(BF16).astype(F32)
-            parts += [high, part - high]
-        parts += [inv, inv * u, inv * v]
-        for k, part in enumerate(parts):
-            feat[pl.ds(c * tall * 16 + k, tall, stride=16), :] = part
+        parts = [jnp.ones_like(x), lx, ly, press, press * lx, press * ly, u, v, u * lx + v * ly, inv, inv * u, inv * v]
+        highs = [part.astype(BF16).astype(F32) for part in parts]
+        lows = [part - high for part, high in zip(parts, highs)]
+        for k, part in enumerate(highs + lows + [jnp.zeros_like(x)] * (ROWS - 24)):
+            feat[pl.ds(c * tall * ROWS + k, tall, stride=ROWS), :] = part
     for i, ((c, r), around) in enumerate(pairs.items()):
         xi, yi = [jnp.broadcast_to(f[r : r + 1], (slots, slots)).T for f in columns[c][:2]]
 
         def weights(a, b):
-            dx = (xi - columns[a][0][b : b + 1]).astype(BF16)
-            dy = (yi - columns[a][1][b : b + 1]).astype(BF16)
-            q = jnp.maximum(BF16(0.0), BF16(1.0) - dx * dx - dy * dy)
+            dx = xi - columns[a][0][b : b + 1]
+            dy = yi - columns[a][1][b : b + 1]
+            q = jnp.maximum(0.0, 1.0 - dx * dx - dy * dy).astype(BF16)
             q2 = q * q
             return jnp.concatenate([q2, q2 * q], axis=0)
 
@@ -194,23 +194,22 @@
         for n in range(0, len(around), 2):
             pair = around[n : n + 2]
             w = jnp.concatenate([weights(a, b) for a, b in pair], axis=1)
-            f = jnp.concatenate([feat[pl.ds((a * tall + b) * 16, 16), :] for a, b in pair], axis=1).astype(BF16)
+            f = jnp.concatenate([feat[pl.ds((a * tall + b) * ROWS, ROWS), :] for a, b in pair], axis=1).astype(BF16)
             found = lax.dot_general(f, w, (((1,), (1,)), ((), ())), preferred_element_type=F32)
             total = found if total is None else total + found
-        acc2[i * 16 : (i + 1) * 16] = total[:, :slots]
-        acc3[i * 16 : (i + 1) * 16] = total[:, slots:]
+        acc2[i * ROWS : (i + 1) * ROWS] = total[:, :slots]
+        acc3[i * ROWS : (i + 1) * ROWS] = total[:, slots:]
 
     for n, c in enumerate(sorted({c for c, _ in pairs})):
 
         def summed(k):
-            return (acc2 if k < 13 else acc3)[pl.ds(n * rows * 16 + k, rows, stride=16), :]
+            acc = acc2 if k < 9 else acc3
+            return sum(acc[pl.ds(n * rows * ROWS + k + low, rows, stride=ROWS), :] for low in (0, 12))
 
         x, y, u, v, s = [f[row0 : row0 + rows] for f in columns[c]]
         x, y = x - x0, y - y0
         press, _ = pressure(s)
-        a0, ap, au, av, aw = [summed(k) for k in range(5)]
-        ax, ay, apx, apy = [summed(k) + summed(k + 1) for k in range(5, 13, 2)]
-        b0, bu, bv = [summed(k) for k in range(13, 16)]
+        a0, ax, ay, ap, apx, apy, au, av, aw, b0, bu, bv = [summed(k) for k in range(12)]
         sx, sy = x * a0 - ax, y * a0 - ay
         rates = [
             (6.0 * MASS) * (press * sx + x * ap - apx) - (VISCOSITY * MASS) * (u * b0 - bu),
@@ -416,7 +415,7 @@
     cross = [(i, i + 1 if i % 2 else i - 1) for i in range(1, ncut - 1)]
 
     def rates_of(kernel, out, arrays, read, summed, rest=()):
-        scratch = [pltpu.VMEM((n * 16, slots), F32) for n in (read, summed, summed)] + list(rest)
+        scratch = [pltpu.VMEM((n * ROWS, slots), F32) for n in (read, summed, summed)] + list(rest)
         return call(lambda *refs: kernel((cols, rows), *refs), out, (), arrays, scratch, COST)
 
     def exchange(own, marks, sent):

time: 168 us -> 171 us (1.018)
  Pallas kernels: 26.1 us -> 31 us
  waiting for transfers between devices: 34.4 us -> 29.6 us
  blocking collectives: 55.5 us -> 57.5 us
    pallas_call x19, Pallas kernels: 24.3 us -> 29.2 us  [call(): pl.pallas_call(kernel, out_shape=outs, in_specs=[SMEM] * len(scalars) + [...]
    all_to_all x1, waiting for transfers between devices: 1.97 us -> 0.01 us  [exchange(): lax.all_to_all(force, both, 0, 0, tiled=True, axis_index_groups=lines)]
    all_to_all x1, blocking collectives: 20 us -> 22 us  [exchange(): lax.all_to_all(force, both, 0, 0, tiled=True, axis_index_groups=lines)]
  transfers between devices with their start and end apart: 10 -> 10, of which waited for: 7 -> 7; matrix products, arithmetic and copies ran while one was open for 0% -> 0% of each run, Pallas kernels for 13% -> 15%
where the time goes in v11:
time: 171 us; the launch traced here: 170 us
  blocking collectives  57.5 us (34%)
  starting transfers between devices  50.9 us (30%)
  Pallas kernels  31 us (18%)
  waiting for transfers between devices  29.6 us (17%)
    pallas_call x19, Pallas kernels, call(): pl.pallas_call(kernel, out_shape=outs, in_specs=[SMEM] * len(scalars) + [...  29.2 us
    all_to_all x1, blocking collectives, exchange(): lax.all_to_all(force, both, 0, 0, tiled=True, axis_index_groups=lines)  22 us
    all_to_all x1, blocking collectives, body(): got = lax.all_to_all(sent, 'cut', 0, 0, tiled=True, axis_index_groups=apart)  21.1 us
    all_to_all x1, starting transfers between devices, exchange(): lax.all_to_all(force, both, 0, 0, tiled=True, axis_index_groups=lines)  14.8 us
    all_to_all x1, blocking collectives, body(): got = lax.all_to_all(sent, 'cut', 0, 0, tiled=True, axis_index_groups=close)  14.4 us
    all_to_all x2, waiting for transfers between devices, exchange(): got = lax.all_to_all(sent, 'depth', 0, 0, tiled=True)  13.8 us
    all_to_all x2, starting transfers between devices, exchange(): got = lax.all_to_all(sent, 'depth', 0, 0, tiled=True)  10.9 us
    ppermute x2, starting transfers between devices, exchange(): lax.ppermute(wide, 'cut', cross)  6.84 us
  transfers between devices with their start and end apart: 10, of which 7 were waited for; matrix products, arithmetic and copies ran while one was open for 0% of the time, Pallas kernels for 15%

profile of v11, /device:TPU:64, one launch (start us, length us, event | category | flops | bytes accessed | tf_op | source)
XLA Modules:
  0.0 169.8 jit_solution(3333980422833141641)
XLA Ops:
  0.6 1.8 %shard_map.86 = (f32[5,2,8,128]{3,2,1,0:T(8,128)}, f32[3,2,8,128]{3,2,1,0:T(8,128)}, s32[16,128]{1,0:T(8,128)}, f32[16,32,128]{2,1,0:T(8,128)}) custom-call(f32[2,2,8,128]{3,2,1,0:T(8,128)} %refs_0_.1, f32[2,2,8,128]{3,2,1,0:T(8,128)} %refs_1_.1, f32[2,8,128]{2,1,0:T(8,128)} %refs_2_.1, s32[2,8]{1,0:T(2,128)} %refs_3_.1, s32[2,8]{1,0:T(2,128)} %refs_4_.1, ...), custom_call_target="tpu_custom_call" | custom-call | tf_op jit(solution)/shard_map/pallas_call | solution.py:436
  2.4 0.0 copy-start
  2.4 0.0 copy-start.2
  2.4 7.2 %all-to-all-start = ((f32[16,32,128]{2,1,0:T(8,128)}), f32[16,32,128]{2,1,0:T(8,128)S(1)}, u32[]{:S(2)}, u32[]{:S(2)}) async-start(f32[16,32,128]{2,1,0:T(8,128)} %get-tuple-element.22), calls=%async_computation | async-start | bytes 524288 | tf_op jit(solution)/shard_map/all_to_all | solution.py:422
  9.6 0.0 copy-done
  9.6 0.0 copy-done.2
  9.6 2.1 %shard_map.87.inner.refs_3_ = f32[3,2,8,128]{3,2,1,0:T(8,128)S(1)} custom-call(f32[5,2,8,128]{3,2,1,0:T(8,128)S(1)} %copy-done.2, f32[3,2,8,128]{3,2,1,0:T(8,128)S(1)} %copy-done), custom_call_target="tpu_custom_call" | custom-call | flops 20000000000 | bytes 1048576 | tf_op jit(solution)/shard_map/pallas_call | solution.py:43
  11.8 7.0 %all-to-all-done.got = f32[16,32,128]{2,1,0:T(8,128)S(1)} async-done(((f32[16,32,128]{2,1,0:T(8,128)}), f32[16,32,128]{2,1,0:T(8,128)S(1)}, u32[]{:S(2)}, u32[]{:S(2)}) %all-to-all-start) | async-done | bytes 262176 | tf_op jit(solution)/shard_map/all_to_all | solution.py:422
  18.9 2.6 %collective-permute-start = (f32[13,12,128]{2,1,0:T(8,128)S(1)}, f32[13,12,128]{2,1,0:T(8,128)S(1)}, u32[]{:S(2)}, u32[]{:S(2)}) collective-permute-start(f32[13,12,128]{2,1,0:T(8,128)S(1)} %shard_map.88.refs_0_.refs_3_.wide), channel_id=1, source_target_pairs={{0,16},{16,0},{32,48},{48,32},{64,80},{80,64},{96,112},{112,96},{1... | collective-permute-start | bytes 239624 | tf_op jit(solution)/shard_map/ppermute | solution.py:425
  21.5 2.8 %collective-permute-start.1 = (f32[13,12,128]{2,1,0:T(8,128)S(1)}, f32[13,12,128]{2,1,0:T(8,128)S(1)}, u32[]{:S(2)}, u32[]{:S(2)}) collective-permute-start(f32[13,12,128]{2,1,0:T(8,128)S(1)} %shard_map.88.refs_0_.refs_3_.wide), channel_id=1, source_target_pairs={{16,32},{32,16},{48,64},{64,48},{80,96},{96,80},{112,128},{128,112... | collective-permute-start | bytes 239624 | tf_op jit(solution)/shard_map/ppermute | solution.py:425
  24.3 1.5 collective-permute-done.refs_1_.refs_4_.swapped
  25.7 0.6 shard_map.91
  26.3 14.8 %all-to-all-start.1 = ((f32[16,1,128]{2,1,0:T(1,128)}), f32[16,1,128]{2,1,0:T(1,128)S(1)}, u32[]{:S(2)}, u32[]{:S(2)}) async-start(f32[16,1,128]{2,1,0:T(1,128)} %shard_map.91), calls=%async_computation.1 | async-start | bytes 16384 | tf_op jit(solution)/shard_map/all_to_all | solution.py:427
  41.1 0.0 collective-permute-done.1.refs_2_.refs_5_
  41.1 6.6 %shard_map.89.refs_1_ = f32[3,4,10,128]{3,2,1,0:T(8,128)S(1)} custom-call(f32[13,12,128]{2,1,0:T(8,128)S(1)} %shard_map.88.refs_0_.refs_3_.wide, f32[13,12,128]{2,1,0:T(8,128)S(1)} %collective-permute-done.refs_1_.refs_4_.swapped, f32[13,12,128]{2,1,0:T(8,128)S(1)} %collective-permute-done.1.refs_2_.refs_5_, f32[3,2,8,128]{3,2,1,0:T(8,128)S(1)} %shard_map.87.inner.refs_3_), custom_call_target="tpu_custom_call" | custom-call | flops 20000000000 | bytes 1048576 | tf_op jit(solution)/shard_map/pallas_call | solution.py:43
  47.7 3.6 %shard_map.90 = (f32[5,2,8,128]{3,2,1,0:T(8,128)S(1)}, f32[3,2,8,128]{3,2,1,0:T(8,128)S(1)}) custom-call(f32[5,2,8,128]{3,2,1,0:T(8,128)S(1)} %copy-done.2, f32[3,4,10,128]{3,2,1,0:T(8,128)S(1)} %shard_map.89.refs_1_, f32[3,2,8,128]{3,2,1,0:T(8,128)S(1)} %copy-done, f32[13,12,128]{2,1,0:T(8,128)S(1)} %shard_map.88.refs_0_.refs_3_.wide, ...), custom_call_target="tpu_custom_call" | custom-call | flops 20000000000 | bytes 1048576 | tf_op jit(solution)/shard_map/pallas_call | solution.py:43
  51.4 0.0 all-to-all-done.1.total
  51.4 0.8 shard_map.92
  52.2 3.8 %all-to-all-start.2 = ((f32[16,32,128]{2,1,0:T(8,128)}), f32[16,32,128]{2,1,0:T(8,128)S(1)}, u32[]{:S(2)}, u32[]{:S(2)}) async-start(f32[16,32,128]{2,1,0:T(8,128)} %get-tuple-element.26), calls=%async_computation.2 | async-start | bytes 524288 | tf_op jit(solution)/shard_map/all_to_all | solution.py:422
  56.0 2.1 %shard_map.93.inner.refs_3_ = f32[3,2,8,128]{3,2,1,0:T(8,128)S(1)} custom-call(f32[5,2,8,128]{3,2,1,0:T(8,128)S(1)} %get-tuple-element.25.refs_0_.own, f32[3,2,8,128]{3,2,1,0:T(8,128)S(1)} %copy-done), custom_call_target="tpu_custom_call" | custom-call | flops 20000000000 | bytes 1048576 | tf_op jit(solution)/shard_map/pallas_call | solution.py:43
  58.1 6.8 %all-to-all-done.2.got = f32[16,32,128]{2,1,0:T(8,128)S(1)} async-done(((f32[16,32,128]{2,1,0:T(8,128)}), f32[16,32,128]{2,1,0:T(8,128)S(1)}, u32[]{:S(2)}, u32[]{:S(2)}) %all-to-all-start.2) | async-done | bytes 262176 | tf_op jit(solution)/shard_map/all_to_all | solution.py:422
  64.9 2.6 %collective-permute-start.2 = (f32[13,12,128]{2,1,0:T(8,128)S(1)}, f32[13,12,128]{2,1,0:T(8,128)S(1)}, u32[]{:S(2)}, u32[]{:S(2)}) collective-permute-start(f32[13,12,128]{2,1,0:T(8,128)S(1)} %shard_map.94.refs_0_.wide), channel_id=1, source_target_pairs={{0,16},{16,0},{32,48},{48,32},{64,80},{80,64},{96,112},{112,96},{1... | collective-permute-start | bytes 239624 | tf_op jit(solution)/shard_map/ppermute | solution.py:425
  67.5 4.0 %collective-permute-start.3 = (f32[13,12,128]{2,1,0:T(8,128)S(1)}, f32[13,12,128]{2,1,0:T(8,128)S(1)}, u32[]{:S(2)}, u32[]{:S(2)}) collective-permute-start(f32[13,12,128]{2,1,0:T(8,128)S(1)} %shard_map.94.refs_0_.wide), channel_id=1, source_target_pairs={{16,32},{32,16},{48,64},{64,48},{80,96},{96,80},{112,128},{128,112... | collective-permute-start | bytes 239624 | tf_op jit(solution)/shard_map/ppermute | solution.py:425
  71.6 0.2 collective-permute-done.2.refs_1_.swapped
  71.8 22.0 %all_to_all.45.total = f32[16,1,128]{2,1,0:T(1,128)S(1)} all-to-all(f32[16,1,128]{2,1,0:T(1,128)S(1)} %shard_map.97), channel_id=1, replica_groups={{0,32,64,96,128,160,192,224,256,288,320,352,384,416,448,480},{1,33,65,9..., dimensions={0} | all-to-all | bytes 16384 | tf_op jit(solution)/shard_map/all_to_all | solution.py:427
  93.7 0.7 shard_map.98
  94.5 3.8 %all-to-all-start.4 = ((f32[32,1,128]{2,1,0:T(1,128)}), f32[32,1,128]{2,1,0:T(1,128)S(1)}, u32[]{:S(2)}, u32[]{:S(2)}) async-start(f32[32,1,128]{2,1,0:T(1,128)} %get-tuple-element.31), calls=%async_computation.4 | async-start | bytes 32768 | tf_op jit(solution)/shard_map/all_to_all | solution.py:456
  98.3 0.0 collective-permute-done.3.refs_2_.other
  98.3 3.4 %shard_map.95.first_found.before = f32[3,2,10,128]{3,2,1,0:T(8,128)S(1)} custom-call(f32[13,12,128]{2,1,0:T(8,128)S(1)} %shard_map.94.refs_0_.wide, f32[13,12,128]{2,1,0:T(8,128)S(1)} %collective-permute-done.2.refs_1_.swapped, f32[13,12,128]{2,1,0:T(8,128)S(1)} %collective-permute-done.3.refs_2_.other, f32[3,2,8,128]{3,2,1,0:T(8,128)S(1)} %shard_map.93.inner.refs_3_), custom_call_target="tpu_custom_call" | custom-call | flops 20000000000 | bytes 1048576 | tf_op jit(solution)/shard_map/pallas_call | solution.py:43
  101.7 3.8 %all-to-all-done.4.got = f32[32,1,128]{2,1,0:T(1,128)S(1)} async-done(((f32[32,1,128]{2,1,0:T(1,128)}), f32[32,1,128]{2,1,0:T(1,128)S(1)}, u32[]{:S(2)}, u32[]{:S(2)}) %all-to-all-start.4) | async-done | bytes 16416 | tf_op jit(solution)/shard_map/all_to_all | solution.py:456
  105.5 0.6 shard_map.101
  106.2 5.7 %all-to-all-start.5 = ((f32[16,1,128]{2,1,0:T(1,128)}), f32[16,1,128]{2,1,0:T(1,128)S(1)}, u32[]{:S(2)}, u32[]{:S(2)}) async-start(f32[16,1,128]{2,1,0:T(1,128)} %shard_map.101), calls=%async_computation.5 | async-start | bytes 16384 | tf_op jit(solution)/shard_map/all_to_all | solution.py:460
  111.8 3.5 %shard_map.96.last_found = f32[3,2,10,128]{3,2,1,0:T(8,128)S(1)} custom-call(f32[13,12,128]{2,1,0:T(8,128)S(1)} %shard_map.94.refs_0_.wide, f32[13,12,128]{2,1,0:T(8,128)S(1)} %collective-permute-done.2.refs_1_.swapped, f32[13,12,128]{2,1,0:T(8,128)S(1)} %collective-permute-done.3.refs_2_.other, f32[3,2,8,128]{3,2,1,0:T(8,128)S(1)} %shard_map.93.inner.refs_3_), custom_call_target="tpu_custom_call" | custom-call | flops 20000000000 | bytes 1048576 | tf_op jit(solution)/shard_map/pallas_call | solution.py:43
  115.3 0.1 shard_map.99
  115.4 6.5 %all-to-all-done.5.total = f32[16,1,128]{2,1,0:T(1,128)S(1)} async-done(((f32[16,1,128]{2,1,0:T(1,128)}), f32[16,1,128]{2,1,0:T(1,128)S(1)}, u32[]{:S(2)}, u32[]{:S(2)}) %all-to-all-start.5) | async-done | bytes 8224 | tf_op jit(solution)/shard_map/all_to_all | solution.py:460
  121.9 0.7 shard_map.102
  122.6 3.7 %all-to-all-start.6 = ((f32[16,1,128]{2,1,0:T(1,128)}), f32[16,1,128]{2,1,0:T(1,128)S(1)}, u32[]{:S(2)}, u32[]{:S(2)}) async-start(f32[16,1,128]{2,1,0:T(1,128)} %get-tuple-element.33), calls=%async_computation.6 | async-start | bytes 16384 | tf_op jit(solution)/shard_map/all_to_all | solution.py:466
  126.4 0.0 copy-start.1
  126.4 3.4 %shard_map.100.found = f32[3,2,8,128]{3,2,1,0:T(8,128)S(1)} custom-call(f32[5,4,10,128]{3,2,1,0:T(8,128)S(1)} %get-tuple-element.30.refs_0_), custom_call_target="tpu_custom_call" | custom-call | flops 20000000000 | bytes 1048576 | tf_op jit(solution)/shard_map/pallas_call | solution.py:43
  129.8 3.7 %all-to-all-done.6.total = f32[16,1,128]{2,1,0:T(1,128)S(1)} async-done(((f32[16,1,128]{2,1,0:T(1,128)}), f32[16,1,128]{2,1,0:T(1,128)S(1)}, u32[]{:S(2)}, u32[]{:S(2)}) %all-to-all-start.6) | async-done | bytes 8224 | tf_op jit(solution)/shard_map/all_to_all | solution.py:466
  133.5 0.0 copy-done.1
  133.6 14.4 %all_to_all.46.got = f32[8,88,128]{2,1,0:T(8,128)S(1)} all-to-all(f32[8,88,128]{2,1,0:T(8,128)S(1)} %shard_map.103), channel_id=1, replica_groups={{0,16,32,48,64,80,96,112},{128,144,160,176,192,208,224,240},{256,272,28..., dimensions={0} | all-to-all | bytes 720896 | tf_op jit(solution)/shard_map/all_to_all | solution.py:471
  148.0 0.1 shard_map.104
  148.1 21.1 %all_to_all.47.got = f32[4,88,128]{2,1,0:T(8,128)S(1)} all-to-all(f32[4,88,128]{2,1,0:T(8,128)S(1)} %shard_map.104), channel_id=1, replica_groups={{0,128,256,384},{16,144,272,400},{32,160,288,416},{48,176,304,432},{64,..., dimensions={0} | all-to-all | bytes 360448 | tf_op jit(solution)/shard_map/all_to_all | solution.py:473
  169.2 0.6 shard_map.105
  (4 shorter events, 0.1 us)
Async XLA Ops:
  2.4 7.2 %copy-start = (f32[3,2,8,128]{3,2,1,0:T(8,128)S(1)}, f32[3,2,8,128]{3,2,1,0:T(8,128)}, u32[]{:S(2)}) copy-start(f32[3,2,8,128]{3,2,1,0:T(8,128)} %get-tuple-element.21.refs_1_.marks.refs_2_) | copy-start | bytes 73732
  2.4 7.2 %copy-start.2 = (f32[5,2,8,128]{3,2,1,0:T(8,128)S(1)}, f32[5,2,8,128]{3,2,1,0:T(8,128)}, u32[]{:S(2)}) copy-start(f32[5,2,8,128]{3,2,1,0:T(8,128)} %get-tuple-element.20.refs_0_.own) | copy-start | bytes 122884
  2.4 16.4 %all-to-all-start = ((f32[16,32,128]{2,1,0:T(8,128)}), f32[16,32,128]{2,1,0:T(8,128)S(1)}, u32[]{:S(2)}, u32[]{:S(2)}) async-start(f32[16,32,128]{2,1,0:T(8,128)} %get-tuple-element.22), calls=%async_computation | async-start | bytes 524288 | tf_op jit(solution)/shard_map/all_to_all | solution.py:422
  18.9 6.9 %collective-permute-start = (f32[13,12,128]{2,1,0:T(8,128)S(1)}, f32[13,12,128]{2,1,0:T(8,128)S(1)}, u32[]{:S(2)}, u32[]{:S(2)}) collective-permute-start(f32[13,12,128]{2,1,0:T(8,128)S(1)} %shard_map.88.refs_0_.refs_3_.wide), channel_id=1, source_target_pairs={{0,16},{16,0},{32,48},{48,32},{64,80},{80,64},{96,112},{112,96},{1... | collective-permute-start | bytes 239624 | tf_op jit(solution)/shard_map/ppermute | solution.py:425
  21.5 19.7 %collective-permute-start.1 = (f32[13,12,128]{2,1,0:T(8,128)S(1)}, f32[13,12,128]{2,1,0:T(8,128)S(1)}, u32[]{:S(2)}, u32[]{:S(2)}) collective-permute-start(f32[13,12,128]{2,1,0:T(8,128)S(1)} %shard_map.88.refs_0_.refs_3_.wide), channel_id=1, source_target_pairs={{16,32},{32,16},{48,64},{64,48},{80,96},{96,80},{112,128},{128,112... | collective-permute-start | bytes 239624 | tf_op jit(solution)/shard_map/ppermute | solution.py:425
  26.3 25.0 %all-to-all-start.1 = ((f32[16,1,128]{2,1,0:T(1,128)}), f32[16,1,128]{2,1,0:T(1,128)S(1)}, u32[]{:S(2)}, u32[]{:S(2)}) async-start(f32[16,1,128]{2,1,0:T(1,128)} %shard_map.91), calls=%async_computation.1 | async-start | bytes 16384 | tf_op jit(solution)/shard_map/all_to_all | solution.py:427
  52.2 12.7 %all-to-all-start.2 = ((f32[16,32,128]{2,1,0:T(8,128)}), f32[16,32,128]{2,1,0:T(8,128)S(1)}, u32[]{:S(2)}, u32[]{:S(2)}) async-start(f32[16,32,128]{2,1,0:T(8,128)} %get-tuple-element.26), calls=%async_computation.2 | async-start | bytes 524288 | tf_op jit(solution)/shard_map/all_to_all | solution.py:422
  64.9 6.9 %collective-permute-start.2 = (f32[13,12,128]{2,1,0:T(8,128)S(1)}, f32[13,12,128]{2,1,0:T(8,128)S(1)}, u32[]{:S(2)}, u32[]{:S(2)}) collective-permute-start(f32[13,12,128]{2,1,0:T(8,128)S(1)} %shard_map.94.refs_0_.wide), channel_id=1, source_target_pairs={{0,16},{16,0},{32,48},{48,32},{64,80},{80,64},{96,112},{112,96},{1... | collective-permute-start | bytes 239624 | tf_op jit(solution)/shard_map/ppermute | solution.py:425
  67.5 30.8 %collective-permute-start.3 = (f32[13,12,128]{2,1,0:T(8,128)S(1)}, f32[13,12,128]{2,1,0:T(8,128)S(1)}, u32[]{:S(2)}, u32[]{:S(2)}) collective-permute-start(f32[13,12,128]{2,1,0:T(8,128)S(1)} %shard_map.94.refs_0_.wide), channel_id=1, source_target_pairs={{16,32},{32,16},{48,64},{64,48},{80,96},{96,80},{112,128},{128,112... | collective-permute-start | bytes 239624 | tf_op jit(solution)/shard_map/ppermute | solution.py:425
  94.5 11.0 %all-to-all-start.4 = ((f32[32,1,128]{2,1,0:T(1,128)}), f32[32,1,128]{2,1,0:T(1,128)S(1)}, u32[]{:S(2)}, u32[]{:S(2)}) async-start(f32[32,1,128]{2,1,0:T(1,128)} %get-tuple-element.31), calls=%async_computation.4 | async-start | bytes 32768 | tf_op jit(solution)/shard_map/all_to_all | solution.py:456
  106.2 15.8 %all-to-all-start.5 = ((f32[16,1,128]{2,1,0:T(1,128)}), f32[16,1,128]{2,1,0:T(1,128)S(1)}, u32[]{:S(2)}, u32[]{:S(2)}) async-start(f32[16,1,128]{2,1,0:T(1,128)} %shard_map.101), calls=%async_computation.5 | async-start | bytes 16384 | tf_op jit(solution)/shard_map/all_to_all | solution.py:460
  122.6 10.9 %all-to-all-start.6 = ((f32[16,1,128]{2,1,0:T(1,128)}), f32[16,1,128]{2,1,0:T(1,128)S(1)}, u32[]{:S(2)}, u32[]{:S(2)}) async-start(f32[16,1,128]{2,1,0:T(1,128)} %get-tuple-element.33), calls=%async_computation.6 | async-start | bytes 16384 | tf_op jit(solution)/shard_map/all_to_all | solution.py:466
  126.4 7.2 %copy-start.1 = (s32[16,128]{1,0:T(8,128)S(1)}, s32[16,128]{1,0:T(8,128)}, u32[]{:S(2)}) copy-start(s32[16,128]{1,0:T(8,128)} %get-tuple-element.19.route) | copy-start | bytes 24580

commit v12 on v11

--- a/solution.py
+++ b/solution.py
@@ -399,7 +399,7 @@
     cols, rows, slots = density.shape
     ncut, ndepth = lax.axis_size("cut"), lax.axis_size("depth")
     scale = 1.0 / (ncut * cols * ndepth * rows * slots)
-    near = 8 if ncut % 8 == 0 else 1
+    near = 4 if ncut % 4 == 0 else 1
     far = ncut // near
     size = 5 * cols * rows
     state, marking = shape(5, cols, rows, slots), shape(3, cols, rows, slots)

time: 171 us -> 172 us (level)
  the two profiles are of different devices: /device:TPU:64 before, /device:TPU:8 now
where the time goes in v12:
time: 172 us; the launch traced here: 171 us
  blocking collectives  57.4 us (33%)
  starting transfers between devices  49 us (28%)
  waiting for transfers between devices  33.2 us (19%)
  Pallas kernels  31 us (18%)
    pallas_call x19, Pallas kernels, call(): pl.pallas_call(kernel, out_shape=outs, in_specs=[SMEM] * len(scalars) + [...  29.2 us
    all_to_all x1, blocking collectives, body(): got = lax.all_to_all(sent, 'cut', 0, 0, tiled=True, axis_index_groups=apart)  27.4 us
    all_to_all x1, blocking collectives, exchange(): lax.all_to_all(force, both, 0, 0, tiled=True, axis_index_groups=lines)  22.2 us
    all_to_all x2, waiting for transfers between devices, exchange(): got = lax.all_to_all(sent, 'depth', 0, 0, tiled=True)  13.8 us
    all_to_all x1, starting transfers between devices, exchange(): lax.all_to_all(force, both, 0, 0, tiled=True, axis_index_groups=lines)  13.8 us
    all_to_all x2, starting transfers between devices, exchange(): got = lax.all_to_all(sent, 'depth', 0, 0, tiled=True)  10 us
    all_to_all x1, waiting for transfers between devices, body(): lax.all_to_all(force, both, 0, 0, tiled=True, axis_index_groups=lines)  8.7 us
    ppermute x2, starting transfers between devices, exchange(): lax.ppermute(wide, 'cut', swap)  8.34 us
  transfers between devices with their start and end apart: 10, of which 8 were waited for; matrix products, arithmetic and copies ran while one was open for 0% of the time, Pallas kernels for 15%

profile of v12, /device:TPU:8, one launch (start us, length us, event | category | flops | bytes accessed | tf_op | source)
XLA Modules:
  0.0 171.4 jit_solution(243231991412321226)
XLA Ops:
  0.6 1.8 %shard_map.86 = (f32[5,2,8,128]{3,2,1,0:T(8,128)}, f32[3,2,8,128]{3,2,1,0:T(8,128)}, s32[16,128]{1,0:T(8,128)}, f32[16,32,128]{2,1,0:T(8,128)}) custom-call(f32[2,2,8,128]{3,2,1,0:T(8,128)} %refs_0_.1, f32[2,2,8,128]{3,2,1,0:T(8,128)} %refs_1_.1, f32[2,8,128]{2,1,0:T(8,128)} %refs_2_.1, s32[2,8]{1,0:T(2,128)} %refs_3_.1, s32[2,8]{1,0:T(2,128)} %refs_4_.1, ...), custom_call_target="tpu_custom_call" | custom-call | tf_op jit(solution)/shard_map/pallas_call | solution.py:436
  2.4 0.0 copy-start
  2.4 0.0 copy-start.2
  2.4 6.3 %all-to-all-start = ((f32[16,32,128]{2,1,0:T(8,128)}), f32[16,32,128]{2,1,0:T(8,128)S(1)}, u32[]{:S(2)}, u32[]{:S(2)}) async-start(f32[16,32,128]{2,1,0:T(8,128)} %get-tuple-element.22), calls=%async_computation | async-start | bytes 524288 | tf_op jit(solution)/shard_map/all_to_all | solution.py:422
  8.7 0.0 copy-done
  8.7 0.0 copy-done.2
  8.8 2.1 %shard_map.87.inner.refs_3_ = f32[3,2,8,128]{3,2,1,0:T(8,128)S(1)} custom-call(f32[5,2,8,128]{3,2,1,0:T(8,128)S(1)} %copy-done.2, f32[3,2,8,128]{3,2,1,0:T(8,128)S(1)} %copy-done), custom_call_target="tpu_custom_call" | custom-call | flops 20000000000 | bytes 1048576 | tf_op jit(solution)/shard_map/pallas_call | solution.py:43
  10.9 7.0 %all-to-all-done.got = f32[16,32,128]{2,1,0:T(8,128)S(1)} async-done(((f32[16,32,128]{2,1,0:T(8,128)}), f32[16,32,128]{2,1,0:T(8,128)S(1)}, u32[]{:S(2)}, u32[]{:S(2)}) %all-to-all-start) | async-done | bytes 262176 | tf_op jit(solution)/shard_map/all_to_all | solution.py:422
  18.0 5.1 %collective-permute-start = (f32[13,12,128]{2,1,0:T(8,128)S(1)}, f32[13,12,128]{2,1,0:T(8,128)S(1)}, u32[]{:S(2)}, u32[]{:S(2)}) collective-permute-start(f32[13,12,128]{2,1,0:T(8,128)S(1)} %shard_map.88.refs_0_.refs_3_.wide), channel_id=1, source_target_pairs={{0,16},{16,0},{32,48},{48,32},{64,80},{80,64},{96,112},{112,96},{1... | collective-permute-start | bytes 239624 | tf_op jit(solution)/shard_map/ppermute | solution.py:425
  23.1 2.1 %collective-permute-start.1 = (f32[13,12,128]{2,1,0:T(8,128)S(1)}, f32[13,12,128]{2,1,0:T(8,128)S(1)}, u32[]{:S(2)}, u32[]{:S(2)}) collective-permute-start(f32[13,12,128]{2,1,0:T(8,128)S(1)} %shard_map.88.refs_0_.refs_3_.wide), channel_id=1, source_target_pairs={{16,32},{32,16},{48,64},{64,48},{80,96},{96,80},{112,128},{128,112... | collective-permute-start | bytes 239624 | tf_op jit(solution)/shard_map/ppermute | solution.py:425
  25.2 1.1 collective-permute-done.refs_1_.refs_4_.swapped
  26.3 0.6 shard_map.91
  26.9 13.8 %all-to-all-start.1 = ((f32[16,1,128]{2,1,0:T(1,128)}), f32[16,1,128]{2,1,0:T(1,128)S(1)}, u32[]{:S(2)}, u32[]{:S(2)}) async-start(f32[16,1,128]{2,1,0:T(1,128)} %shard_map.91), calls=%async_computation.1 | async-start | bytes 16384 | tf_op jit(solution)/shard_map/all_to_all | solution.py:427
  40.7 0.0 collective-permute-done.1.refs_2_.refs_5_
  40.7 6.6 %shard_map.89.refs_1_ = f32[3,4,10,128]{3,2,1,0:T(8,128)S(1)} custom-call(f32[13,12,128]{2,1,0:T(8,128)S(1)} %shard_map.88.refs_0_.refs_3_.wide, f32[13,12,128]{2,1,0:T(8,128)S(1)} %collective-permute-done.refs_1_.refs_4_.swapped, f32[13,12,128]{2,1,0:T(8,128)S(1)} %collective-permute-done.1.refs_2_.refs_5_, f32[3,2,8,128]{3,2,1,0:T(8,128)S(1)} %shard_map.87.inner.refs_3_), custom_call_target="tpu_custom_call" | custom-call | flops 20000000000 | bytes 1048576 | tf_op jit(solution)/shard_map/pallas_call | solution.py:43
  47.3 3.6 %shard_map.90 = (f32[5,2,8,128]{3,2,1,0:T(8,128)S(1)}, f32[3,2,8,128]{3,2,1,0:T(8,128)S(1)}) custom-call(f32[5,2,8,128]{3,2,1,0:T(8,128)S(1)} %copy-done.2, f32[3,4,10,128]{3,2,1,0:T(8,128)S(1)} %shard_map.89.refs_1_, f32[3,2,8,128]{3,2,1,0:T(8,128)S(1)} %copy-done, f32[13,12,128]{2,1,0:T(8,128)S(1)} %shard_map.88.refs_0_.refs_3_.wide, ...), custom_call_target="tpu_custom_call" | custom-call | flops 20000000000 | bytes 1048576 | tf_op jit(solution)/shard_map/pallas_call | solution.py:43
  50.9 2.1 %all-to-all-done.1.total = f32[16,1,128]{2,1,0:T(1,128)S(1)} async-done(((f32[16,1,128]{2,1,0:T(1,128)}), f32[16,1,128]{2,1,0:T(1,128)S(1)}, u32[]{:S(2)}, u32[]{:S(2)}) %all-to-all-start.1) | async-done | bytes 8224 | tf_op jit(solution)/shard_map/all_to_all | solution.py:427
  53.0 0.8 shard_map.92
  53.9 3.8 %all-to-all-start.2 = ((f32[16,32,128]{2,1,0:T(8,128)}), f32[16,32,128]{2,1,0:T(8,128)S(1)}, u32[]{:S(2)}, u32[]{:S(2)}) async-start(f32[16,32,128]{2,1,0:T(8,128)} %get-tuple-element.26), calls=%async_computation.2 | async-start | bytes 524288 | tf_op jit(solution)/shard_map/all_to_all | solution.py:422
  57.6 2.1 %shard_map.93.inner.refs_3_ = f32[3,2,8,128]{3,2,1,0:T(8,128)S(1)} custom-call(f32[5,2,8,128]{3,2,1,0:T(8,128)S(1)} %get-tuple-element.25.refs_0_.own, f32[3,2,8,128]{3,2,1,0:T(8,128)S(1)} %copy-done), custom_call_target="tpu_custom_call" | custom-call | flops 20000000000 | bytes 1048576 | tf_op jit(solution)/shard_map/pallas_call | solution.py:43
  59.8 6.8 %all-to-all-done.2.got = f32[16,32,128]{2,1,0:T(8,128)S(1)} async-done(((f32[16,32,128]{2,1,0:T(8,128)}), f32[16,32,128]{2,1,0:T(8,128)S(1)}, u32[]{:S(2)}, u32[]{:S(2)}) %all-to-all-start.2) | async-done | bytes 262176 | tf_op jit(solution)/shard_map/all_to_all | solution.py:422
  66.6 3.3 %collective-permute-start.2 = (f32[13,12,128]{2,1,0:T(8,128)S(1)}, f32[13,12,128]{2,1,0:T(8,128)S(1)}, u32[]{:S(2)}, u32[]{:S(2)}) collective-permute-start(f32[13,12,128]{2,1,0:T(8,128)S(1)} %shard_map.94.refs_0_.wide), channel_id=1, source_target_pairs={{0,16},{16,0},{32,48},{48,32},{64,80},{80,64},{96,112},{112,96},{1... | collective-permute-start | bytes 239624 | tf_op jit(solution)/shard_map/ppermute | solution.py:425
  69.8 2.6 %collective-permute-start.3 = (f32[13,12,128]{2,1,0:T(8,128)S(1)}, f32[13,12,128]{2,1,0:T(8,128)S(1)}, u32[]{:S(2)}, u32[]{:S(2)}) collective-permute-start(f32[13,12,128]{2,1,0:T(8,128)S(1)} %shard_map.94.refs_0_.wide), channel_id=1, source_target_pairs={{16,32},{32,16},{48,64},{64,48},{80,96},{96,80},{112,128},{128,112... | collective-permute-start | bytes 239624 | tf_op jit(solution)/shard_map/ppermute | solution.py:425
  72.5 1.0 collective-permute-done.2.refs_1_.swapped
  73.4 22.2 %all_to_all.45.total = f32[16,1,128]{2,1,0:T(1,128)S(1)} all-to-all(f32[16,1,128]{2,1,0:T(1,128)S(1)} %shard_map.97), channel_id=1, replica_groups={{0,32,64,96,128,160,192,224,256,288,320,352,384,416,448,480},{1,33,65,9..., dimensions={0} | all-to-all | bytes 16384 | tf_op jit(solution)/shard_map/all_to_all | solution.py:427
  95.6 0.7 shard_map.98
  96.3 4.9 %all-to-all-start.4 = ((f32[32,1,128]{2,1,0:T(1,128)}), f32[32,1,128]{2,1,0:T(1,128)S(1)}, u32[]{:S(2)}, u32[]{:S(2)}) async-start(f32[32,1,128]{2,1,0:T(1,128)} %get-tuple-element.31), calls=%async_computation.4 | async-start | bytes 32768 | tf_op jit(solution)/shard_map/all_to_all | solution.py:456
  101.3 0.0 collective-permute-done.3.refs_2_.other
  101.3 3.4 %shard_map.95.first_found.before = f32[3,2,10,128]{3,2,1,0:T(8,128)S(1)} custom-call(f32[13,12,128]{2,1,0:T(8,128)S(1)} %shard_map.94.refs_0_.wide, f32[13,12,128]{2,1,0:T(8,128)S(1)} %collective-permute-done.2.refs_1_.swapped, f32[13,12,128]{2,1,0:T(8,128)S(1)} %collective-permute-done.3.refs_2_.other, f32[3,2,8,128]{3,2,1,0:T(8,128)S(1)} %shard_map.93.inner.refs_3_), custom_call_target="tpu_custom_call" | custom-call | flops 20000000000 | bytes 1048576 | tf_op jit(solution)/shard_map/pallas_call | solution.py:43
  104.7 2.7 %all-to-all-done.4.got = f32[32,1,128]{2,1,0:T(1,128)S(1)} async-done(((f32[32,1,128]{2,1,0:T(1,128)}), f32[32,1,128]{2,1,0:T(1,128)S(1)}, u32[]{:S(2)}, u32[]{:S(2)}) %all-to-all-start.4) | async-done | bytes 16416 | tf_op jit(solution)/shard_map/all_to_all | solution.py:456
  107.4 0.6 shard_map.101
  108.0 3.5 %all-to-all-start.5 = ((f32[16,1,128]{2,1,0:T(1,128)}), f32[16,1,128]{2,1,0:T(1,128)S(1)}, u32[]{:S(2)}, u32[]{:S(2)}) async-start(f32[16,1,128]{2,1,0:T(1,128)} %shard_map.101), calls=%async_computation.5 | async-start | bytes 16384 | tf_op jit(solution)/shard_map/all_to_all | solution.py:460
  111.5 3.5 %shard_map.96.last_found = f32[3,2,10,128]{3,2,1,0:T(8,128)S(1)} custom-call(f32[13,12,128]{2,1,0:T(8,128)S(1)} %shard_map.94.refs_0_.wide, f32[13,12,128]{2,1,0:T(8,128)S(1)} %collective-permute-done.2.refs_1_.swapped, f32[13,12,128]{2,1,0:T(8,128)S(1)} %collective-permute-done.3.refs_2_.other, f32[3,2,8,128]{3,2,1,0:T(8,128)S(1)} %shard_map.93.inner.refs_3_), custom_call_target="tpu_custom_call" | custom-call | flops 20000000000 | bytes 1048576 | tf_op jit(solution)/shard_map/pallas_call | solution.py:43
  115.0 0.1 shard_map.99
  115.1 8.7 %all-to-all-done.5.total = f32[16,1,128]{2,1,0:T(1,128)S(1)} async-done(((f32[16,1,128]{2,1,0:T(1,128)}), f32[16,1,128]{2,1,0:T(1,128)S(1)}, u32[]{:S(2)}, u32[]{:S(2)}) %all-to-all-start.5) | async-done | bytes 8224 | tf_op jit(solution)/shard_map/all_to_all | solution.py:460
  123.8 0.7 shard_map.102
  124.5 3.7 %all-to-all-start.6 = ((f32[16,1,128]{2,1,0:T(1,128)}), f32[16,1,128]{2,1,0:T(1,128)S(1)}, u32[]{:S(2)}, u32[]{:S(2)}) async-start(f32[16,1,128]{2,1,0:T(1,128)} %get-tuple-element.33), calls=%async_computation.6 | async-start | bytes 16384 | tf_op jit(solution)/shard_map/all_to_all | solution.py:466
  128.2 0.0 copy-start.1
  128.2 3.4 %shard_map.100.found = f32[3,2,8,128]{3,2,1,0:T(8,128)S(1)} custom-call(f32[5,4,10,128]{3,2,1,0:T(8,128)S(1)} %get-tuple-element.30.refs_0_), custom_call_target="tpu_custom_call" | custom-call | flops 20000000000 | bytes 1048576 | tf_op jit(solution)/shard_map/pallas_call | solution.py:43
  131.7 3.8 %all-to-all-done.6.total = f32[16,1,128]{2,1,0:T(1,128)S(1)} async-done(((f32[16,1,128]{2,1,0:T(1,128)}), f32[16,1,128]{2,1,0:T(1,128)S(1)}, u32[]{:S(2)}, u32[]{:S(2)}) %all-to-all-start.6) | async-done | bytes 8224 | tf_op jit(solution)/shard_map/all_to_all | solution.py:466
  135.4 0.0 copy-done.1
  135.5 7.8 %all_to_all.46.got = f32[4,88,128]{2,1,0:T(8,128)S(1)} all-to-all(f32[4,88,128]{2,1,0:T(8,128)S(1)} %shard_map.103), channel_id=1, replica_groups={{0,16,32,48},{64,80,96,112},{128,144,160,176},{192,208,224,240},{256,27..., dimensions={0} | all-to-all | bytes 360448 | tf_op jit(solution)/shard_map/all_to_all | solution.py:471
  143.3 0.1 shard_map.104
  143.4 27.4 %all_to_all.47.got = f32[8,88,128]{2,1,0:T(8,128)S(1)} all-to-all(f32[8,88,128]{2,1,0:T(8,128)S(1)} %shard_map.104), channel_id=1, replica_groups={{0,64,128,192,256,320,384,448},{16,80,144,208,272,336,400,464},{32,96,1..., dimensions={0} | all-to-all | bytes 720896 | tf_op jit(solution)/shard_map/all_to_all | solution.py:473
  170.8 0.6 shard_map.105
  (4 shorter events, 0.1 us)
Async XLA Ops:
  2.4 6.3 %copy-start = (f32[3,2,8,128]{3,2,1,0:T(8,128)S(1)}, f32[3,2,8,128]{3,2,1,0:T(8,128)}, u32[]{:S(2)}) copy-start(f32[3,2,8,128]{3,2,1,0:T(8,128)} %get-tuple-element.21.refs_1_.marks.refs_2_) | copy-start | bytes 73732
  2.4 6.3 %copy-start.2 = (f32[5,2,8,128]{3,2,1,0:T(8,128)S(1)}, f32[5,2,8,128]{3,2,1,0:T(8,128)}, u32[]{:S(2)}) copy-start(f32[5,2,8,128]{3,2,1,0:T(8,128)} %get-tuple-element.20.refs_0_.own) | copy-start | bytes 122884
  2.4 15.5 %all-to-all-start = ((f32[16,32,128]{2,1,0:T(8,128)}), f32[16,32,128]{2,1,0:T(8,128)S(1)}, u32[]{:S(2)}, u32[]{:S(2)}) async-start(f32[16,32,128]{2,1,0:T(8,128)} %get-tuple-element.22), calls=%async_computation | async-start | bytes 524288 | tf_op jit(solution)/shard_map/all_to_all | solution.py:422
  18.0 8.3 %collective-permute-start = (f32[13,12,128]{2,1,0:T(8,128)S(1)}, f32[13,12,128]{2,1,0:T(8,128)S(1)}, u32[]{:S(2)}, u32[]{:S(2)}) collective-permute-start(f32[13,12,128]{2,1,0:T(8,128)S(1)} %shard_map.88.refs_0_.refs_3_.wide), channel_id=1, source_target_pairs={{0,16},{16,0},{32,48},{48,32},{64,80},{80,64},{96,112},{112,96},{1... | collective-permute-start | bytes 239624 | tf_op jit(solution)/shard_map/ppermute | solution.py:425
  23.1 17.6 %collective-permute-start.1 = (f32[13,12,128]{2,1,0:T(8,128)S(1)}, f32[13,12,128]{2,1,0:T(8,128)S(1)}, u32[]{:S(2)}, u32[]{:S(2)}) collective-permute-start(f32[13,12,128]{2,1,0:T(8,128)S(1)} %shard_map.88.refs_0_.refs_3_.wide), channel_id=1, source_target_pairs={{16,32},{32,16},{48,64},{64,48},{80,96},{96,80},{112,128},{128,112... | collective-permute-start | bytes 239624 | tf_op jit(solution)/shard_map/ppermute | solution.py:425
  26.9 26.2 %all-to-all-start.1 = ((f32[16,1,128]{2,1,0:T(1,128)}), f32[16,1,128]{2,1,0:T(1,128)S(1)}, u32[]{:S(2)}, u32[]{:S(2)}) async-start(f32[16,1,128]{2,1,0:T(1,128)} %shard_map.91), calls=%async_computation.1 | async-start | bytes 16384 | tf_op jit(solution)/shard_map/all_to_all | solution.py:427
  53.9 12.7 %all-to-all-start.2 = ((f32[16,32,128]{2,1,0:T(8,128)}), f32[16,32,128]{2,1,0:T(8,128)S(1)}, u32[]{:S(2)}, u32[]{:S(2)}) async-start(f32[16,32,128]{2,1,0:T(8,128)} %get-tuple-element.26), calls=%async_computation.2 | async-start | bytes 524288 | tf_op jit(solution)/shard_map/all_to_all | solution.py:422
  66.6 6.9 %collective-permute-start.2 = (f32[13,12,128]{2,1,0:T(8,128)S(1)}, f32[13,12,128]{2,1,0:T(8,128)S(1)}, u32[]{:S(2)}, u32[]{:S(2)}) collective-permute-start(f32[13,12,128]{2,1,0:T(8,128)S(1)} %shard_map.94.refs_0_.wide), channel_id=1, source_target_pairs={{0,16},{16,0},{32,48},{48,32},{64,80},{80,64},{96,112},{112,96},{1... | collective-permute-start | bytes 239624 | tf_op jit(solution)/shard_map/ppermute | solution.py:425
  69.8 31.4 %collective-permute-start.3 = (f32[13,12,128]{2,1,0:T(8,128)S(1)}, f32[13,12,128]{2,1,0:T(8,128)S(1)}, u32[]{:S(2)}, u32[]{:S(2)}) collective-permute-start(f32[13,12,128]{2,1,0:T(8,128)S(1)} %shard_map.94.refs_0_.wide), channel_id=1, source_target_pairs={{16,32},{32,16},{48,64},{64,48},{80,96},{96,80},{112,128},{128,112... | collective-permute-start | bytes 239624 | tf_op jit(solution)/shard_map/ppermute | solution.py:425
  96.3 11.0 %all-to-all-start.4 = ((f32[32,1,128]{2,1,0:T(1,128)}), f32[32,1,128]{2,1,0:T(1,128)S(1)}, u32[]{:S(2)}, u32[]{:S(2)}) async-start(f32[32,1,128]{2,1,0:T(1,128)} %get-tuple-element.31), calls=%async_computation.4 | async-start | bytes 32768 | tf_op jit(solution)/shard_map/all_to_all | solution.py:456
  108.0 15.8 %all-to-all-start.5 = ((f32[16,1,128]{2,1,0:T(1,128)}), f32[16,1,128]{2,1,0:T(1,128)S(1)}, u32[]{:S(2)}, u32[]{:S(2)}) async-start(f32[16,1,128]{2,1,0:T(1,128)} %shard_map.101), calls=%async_computation.5 | async-start | bytes 16384 | tf_op jit(solution)/shard_map/all_to_all | solution.py:460
  124.5 11.0 %all-to-all-start.6 = ((f32[16,1,128]{2,1,0:T(1,128)}), f32[16,1,128]{2,1,0:T(1,128)S(1)}, u32[]{:S(2)}, u32[]{:S(2)}) async-start(f32[16,1,128]{2,1,0:T(1,128)} %get-tuple-element.33), calls=%async_computation.6 | async-start | bytes 16384 | tf_op jit(solution)/shard_map/all_to_all | solution.py:466
  128.2 7.2 %copy-start.1 = (s32[16,128]{1,0:T(8,128)S(1)}, s32[16,128]{1,0:T(8,128)}, u32[]{:S(2)}) copy-start(s32[16,128]{1,0:T(8,128)} %get-tuple-element.19.route) | copy-start | bytes 24580

commit v13 on v11

--- a/solution.py
+++ b/solution.py
@@ -186,7 +186,7 @@
         def weights(a, b):
             dx = xi - columns[a][0][b : b + 1]
             dy = yi - columns[a][1][b : b + 1]
-            q = jnp.maximum(0.0, 1.0 - dx * dx - dy * dy).astype(BF16)
+            q = jnp.maximum(BF16(0.0), (1.0 - dx * dx - dy * dy).astype(BF16))
             q2 = q * q
             return jnp.concatenate([q2, q2 * q], axis=0)
 

time: 171 us -> 170 us (level)
  no operation moved by 1% of the time
where the time goes in v13:
time: 170 us; the launch traced here: 169 us
  blocking collectives  57.2 us (34%)
  starting transfers between devices  50.6 us (30%)
  waiting for transfers between devices  30.7 us (18%)
  Pallas kernels  30 us (18%)
    pallas_call x19, Pallas kernels, call(): pl.pallas_call(kernel, out_shape=outs, in_specs=[SMEM] * len(scalars) + [...  28.2 us
    all_to_all x1, blocking collectives, exchange(): lax.all_to_all(force, both, 0, 0, tiled=True, axis_index_groups=lines)  21.7 us
    all_to_all x1, blocking collectives, body(): got = lax.all_to_all(sent, 'cut', 0, 0, tiled=True, axis_index_groups=apart)  21.1 us
    all_to_all x1, starting transfers between devices, exchange(): lax.all_to_all(force, both, 0, 0, tiled=True, axis_index_groups=lines)  14.8 us
    all_to_all x1, blocking collectives, body(): got = lax.all_to_all(sent, 'cut', 0, 0, tiled=True, axis_index_groups=close)  14.4 us
    all_to_all x2, waiting for transfers between devices, exchange(): got = lax.all_to_all(sent, 'depth', 0, 0, tiled=True)  14.3 us
    all_to_all x2, starting transfers between devices, exchange(): got = lax.all_to_all(sent, 'depth', 0, 0, tiled=True)  10.7 us
    ppermute x2, starting transfers between devices, exchange(): lax.ppermute(wide, 'cut', cross)  7.03 us
  transfers between devices with their start and end apart: 10, of which 7 were waited for; matrix products, arithmetic and copies ran while one was open for 0% of the time, Pallas kernels for 15%

profile of v13, /device:TPU:64, one launch (start us, length us, event | category | flops | bytes accessed | tf_op | source)
XLA Modules:
  0.0 169.4 jit_solution(2555640739164659638)
XLA Ops:
  0.6 1.8 %shard_map.86 = (f32[5,2,8,128]{3,2,1,0:T(8,128)}, f32[3,2,8,128]{3,2,1,0:T(8,128)}, s32[16,128]{1,0:T(8,128)}, f32[16,32,128]{2,1,0:T(8,128)}) custom-call(f32[2,2,8,128]{3,2,1,0:T(8,128)} %refs_0_.1, f32[2,2,8,128]{3,2,1,0:T(8,128)} %refs_1_.1, f32[2,8,128]{2,1,0:T(8,128)} %refs_2_.1, s32[2,8]{1,0:T(2,128)} %refs_3_.1, s32[2,8]{1,0:T(2,128)} %refs_4_.1, ...), custom_call_target="tpu_custom_call" | custom-call | tf_op jit(solution)/shard_map/pallas_call | solution.py:436
  2.4 0.0 copy-start
  2.4 0.0 copy-start.2
  2.4 7.2 %all-to-all-start = ((f32[16,32,128]{2,1,0:T(8,128)}), f32[16,32,128]{2,1,0:T(8,128)S(1)}, u32[]{:S(2)}, u32[]{:S(2)}) async-start(f32[16,32,128]{2,1,0:T(8,128)} %get-tuple-element.22), calls=%async_computation | async-start | bytes 524288 | tf_op jit(solution)/shard_map/all_to_all | solution.py:422
  9.6 0.0 copy-done
  9.6 0.0 copy-done.2
  9.6 2.0 %shard_map.87.inner.refs_3_ = f32[3,2,8,128]{3,2,1,0:T(8,128)S(1)} custom-call(f32[5,2,8,128]{3,2,1,0:T(8,128)S(1)} %copy-done.2, f32[3,2,8,128]{3,2,1,0:T(8,128)S(1)} %copy-done), custom_call_target="tpu_custom_call" | custom-call | flops 20000000000 | bytes 1048576 | tf_op jit(solution)/shard_map/pallas_call | solution.py:43
  11.7 7.1 %all-to-all-done.got = f32[16,32,128]{2,1,0:T(8,128)S(1)} async-done(((f32[16,32,128]{2,1,0:T(8,128)}), f32[16,32,128]{2,1,0:T(8,128)S(1)}, u32[]{:S(2)}, u32[]{:S(2)}) %all-to-all-start) | async-done | bytes 262176 | tf_op jit(solution)/shard_map/all_to_all | solution.py:422
  18.9 2.6 %collective-permute-start = (f32[13,12,128]{2,1,0:T(8,128)S(1)}, f32[13,12,128]{2,1,0:T(8,128)S(1)}, u32[]{:S(2)}, u32[]{:S(2)}) collective-permute-start(f32[13,12,128]{2,1,0:T(8,128)S(1)} %shard_map.88.refs_0_.refs_3_.wide), channel_id=1, source_target_pairs={{0,16},{16,0},{32,48},{48,32},{64,80},{80,64},{96,112},{112,96},{1... | collective-permute-start | bytes 239624 | tf_op jit(solution)/shard_map/ppermute | solution.py:425
  21.5 2.8 %collective-permute-start.1 = (f32[13,12,128]{2,1,0:T(8,128)S(1)}, f32[13,12,128]{2,1,0:T(8,128)S(1)}, u32[]{:S(2)}, u32[]{:S(2)}) collective-permute-start(f32[13,12,128]{2,1,0:T(8,128)S(1)} %shard_map.88.refs_0_.refs_3_.wide), channel_id=1, source_target_pairs={{16,32},{32,16},{48,64},{64,48},{80,96},{96,80},{112,128},{128,112... | collective-permute-start | bytes 239624 | tf_op jit(solution)/shard_map/ppermute | solution.py:425
  24.3 1.5 collective-permute-done.refs_1_.refs_4_.swapped
  25.7 0.6 shard_map.91
  26.3 14.8 %all-to-all-start.1 = ((f32[16,1,128]{2,1,0:T(1,128)}), f32[16,1,128]{2,1,0:T(1,128)S(1)}, u32[]{:S(2)}, u32[]{:S(2)}) async-start(f32[16,1,128]{2,1,0:T(1,128)} %shard_map.91), calls=%async_computation.1 | async-start | bytes 16384 | tf_op jit(solution)/shard_map/all_to_all | solution.py:427
  41.1 0.0 collective-permute-done.1.refs_2_.refs_5_
  41.1 6.3 %shard_map.89.refs_1_ = f32[3,4,10,128]{3,2,1,0:T(8,128)S(1)} custom-call(f32[13,12,128]{2,1,0:T(8,128)S(1)} %shard_map.88.refs_0_.refs_3_.wide, f32[13,12,128]{2,1,0:T(8,128)S(1)} %collective-permute-done.refs_1_.refs_4_.swapped, f32[13,12,128]{2,1,0:T(8,128)S(1)} %collective-permute-done.1.refs_2_.refs_5_, f32[3,2,8,128]{3,2,1,0:T(8,128)S(1)} %shard_map.87.inner.refs_3_), custom_call_target="tpu_custom_call" | custom-call | flops 20000000000 | bytes 1048576 | tf_op jit(solution)/shard_map/pallas_call | solution.py:43
  47.4 3.5 %shard_map.90 = (f32[5,2,8,128]{3,2,1,0:T(8,128)S(1)}, f32[3,2,8,128]{3,2,1,0:T(8,128)S(1)}) custom-call(f32[5,2,8,128]{3,2,1,0:T(8,128)S(1)} %copy-done.2, f32[3,4,10,128]{3,2,1,0:T(8,128)S(1)} %shard_map.89.refs_1_, f32[3,2,8,128]{3,2,1,0:T(8,128)S(1)} %copy-done, f32[13,12,128]{2,1,0:T(8,128)S(1)} %shard_map.88.refs_0_.refs_3_.wide, ...), custom_call_target="tpu_custom_call" | custom-call | flops 20000000000 | bytes 1048576 | tf_op jit(solution)/shard_map/pallas_call | solution.py:43
  51.0 0.2 all-to-all-done.1.total
  51.2 0.8 shard_map.92
  52.0 3.5 %all-to-all-start.2 = ((f32[16,32,128]{2,1,0:T(8,128)}), f32[16,32,128]{2,1,0:T(8,128)S(1)}, u32[]{:S(2)}, u32[]{:S(2)}) async-start(f32[16,32,128]{2,1,0:T(8,128)} %get-tuple-element.26), calls=%async_computation.2 | async-start | bytes 524288 | tf_op jit(solution)/shard_map/all_to_all | solution.py:422
  55.5 2.0 %shard_map.93.inner.refs_3_ = f32[3,2,8,128]{3,2,1,0:T(8,128)S(1)} custom-call(f32[5,2,8,128]{3,2,1,0:T(8,128)S(1)} %get-tuple-element.25.refs_0_.own, f32[3,2,8,128]{3,2,1,0:T(8,128)S(1)} %copy-done), custom_call_target="tpu_custom_call" | custom-call | flops 20000000000 | bytes 1048576 | tf_op jit(solution)/shard_map/pallas_call | solution.py:43
  57.6 7.1 %all-to-all-done.2.got = f32[16,32,128]{2,1,0:T(8,128)S(1)} async-done(((f32[16,32,128]{2,1,0:T(8,128)}), f32[16,32,128]{2,1,0:T(8,128)S(1)}, u32[]{:S(2)}, u32[]{:S(2)}) %all-to-all-start.2) | async-done | bytes 262176 | tf_op jit(solution)/shard_map/all_to_all | solution.py:422
  64.7 2.6 %collective-permute-start.2 = (f32[13,12,128]{2,1,0:T(8,128)S(1)}, f32[13,12,128]{2,1,0:T(8,128)S(1)}, u32[]{:S(2)}, u32[]{:S(2)}) collective-permute-start(f32[13,12,128]{2,1,0:T(8,128)S(1)} %shard_map.94.refs_0_.wide), channel_id=1, source_target_pairs={{0,16},{16,0},{32,48},{48,32},{64,80},{80,64},{96,112},{112,96},{1... | collective-permute-start | bytes 239624 | tf_op jit(solution)/shard_map/ppermute | solution.py:425
  67.3 4.2 %collective-permute-start.3 = (f32[13,12,128]{2,1,0:T(8,128)S(1)}, f32[13,12,128]{2,1,0:T(8,128)S(1)}, u32[]{:S(2)}, u32[]{:S(2)}) collective-permute-start(f32[13,12,128]{2,1,0:T(8,128)S(1)} %shard_map.94.refs_0_.wide), channel_id=1, source_target_pairs={{16,32},{32,16},{48,64},{64,48},{80,96},{96,80},{112,128},{128,112... | collective-permute-start | bytes 239624 | tf_op jit(solution)/shard_map/ppermute | solution.py:425
  71.6 0.0 collective-permute-done.2.refs_1_.swapped
  71.6 21.7 %all_to_all.45.total = f32[16,1,128]{2,1,0:T(1,128)S(1)} all-to-all(f32[16,1,128]{2,1,0:T(1,128)S(1)} %shard_map.97), channel_id=1, replica_groups={{0,32,64,96,128,160,192,224,256,288,320,352,384,416,448,480},{1,33,65,9..., dimensions={0} | all-to-all | bytes 16384 | tf_op jit(solution)/shard_map/all_to_all | solution.py:427
  93.3 0.7 shard_map.98
  94.1 3.8 %all-to-all-start.4 = ((f32[32,1,128]{2,1,0:T(1,128)}), f32[32,1,128]{2,1,0:T(1,128)S(1)}, u32[]{:S(2)}, u32[]{:S(2)}) async-start(f32[32,1,128]{2,1,0:T(1,128)} %get-tuple-element.31), calls=%async_computation.4 | async-start | bytes 32768 | tf_op jit(solution)/shard_map/all_to_all | solution.py:456
  97.9 0.0 collective-permute-done.3.refs_2_.other
  97.9 3.2 %shard_map.95.first_found.before = f32[3,2,10,128]{3,2,1,0:T(8,128)S(1)} custom-call(f32[13,12,128]{2,1,0:T(8,128)S(1)} %shard_map.94.refs_0_.wide, f32[13,12,128]{2,1,0:T(8,128)S(1)} %collective-permute-done.2.refs_1_.swapped, f32[13,12,128]{2,1,0:T(8,128)S(1)} %collective-permute-done.3.refs_2_.other, f32[3,2,8,128]{3,2,1,0:T(8,128)S(1)} %shard_map.93.inner.refs_3_), custom_call_target="tpu_custom_call" | custom-call | flops 20000000000 | bytes 1048576 | tf_op jit(solution)/shard_map/pallas_call | solution.py:43
  101.2 3.9 %all-to-all-done.4.got = f32[32,1,128]{2,1,0:T(1,128)S(1)} async-done(((f32[32,1,128]{2,1,0:T(1,128)}), f32[32,1,128]{2,1,0:T(1,128)S(1)}, u32[]{:S(2)}, u32[]{:S(2)}) %all-to-all-start.4) | async-done | bytes 16416 | tf_op jit(solution)/shard_map/all_to_all | solution.py:456
  105.1 0.6 shard_map.101
  105.7 5.7 %all-to-all-start.5 = ((f32[16,1,128]{2,1,0:T(1,128)}), f32[16,1,128]{2,1,0:T(1,128)S(1)}, u32[]{:S(2)}, u32[]{:S(2)}) async-start(f32[16,1,128]{2,1,0:T(1,128)} %shard_map.101), calls=%async_computation.5 | async-start | bytes 16384 | tf_op jit(solution)/shard_map/all_to_all | solution.py:460
  111.4 3.4 %shard_map.96.last_found = f32[3,2,10,128]{3,2,1,0:T(8,128)S(1)} custom-call(f32[13,12,128]{2,1,0:T(8,128)S(1)} %shard_map.94.refs_0_.wide, f32[13,12,128]{2,1,0:T(8,128)S(1)} %collective-permute-done.2.refs_1_.swapped, f32[13,12,128]{2,1,0:T(8,128)S(1)} %collective-permute-done.3.refs_2_.other, f32[3,2,8,128]{3,2,1,0:T(8,128)S(1)} %shard_map.93.inner.refs_3_), custom_call_target="tpu_custom_call" | custom-call | flops 20000000000 | bytes 1048576 | tf_op jit(solution)/shard_map/pallas_call | solution.py:43
  114.8 0.1 shard_map.99
  114.9 6.7 %all-to-all-done.5.total = f32[16,1,128]{2,1,0:T(1,128)S(1)} async-done(((f32[16,1,128]{2,1,0:T(1,128)}), f32[16,1,128]{2,1,0:T(1,128)S(1)}, u32[]{:S(2)}, u32[]{:S(2)}) %all-to-all-start.5) | async-done | bytes 8224 | tf_op jit(solution)/shard_map/all_to_all | solution.py:460
  121.5 0.7 shard_map.102
  122.2 3.5 %all-to-all-start.6 = ((f32[16,1,128]{2,1,0:T(1,128)}), f32[16,1,128]{2,1,0:T(1,128)S(1)}, u32[]{:S(2)}, u32[]{:S(2)}) async-start(f32[16,1,128]{2,1,0:T(1,128)} %get-tuple-element.33), calls=%async_computation.6 | async-start | bytes 16384 | tf_op jit(solution)/shard_map/all_to_all | solution.py:466
  125.7 0.0 copy-start.1
  125.7 3.3 %shard_map.100.found = f32[3,2,8,128]{3,2,1,0:T(8,128)S(1)} custom-call(f32[5,4,10,128]{3,2,1,0:T(8,128)S(1)} %get-tuple-element.30.refs_0_), custom_call_target="tpu_custom_call" | custom-call | flops 20000000000 | bytes 1048576 | tf_op jit(solution)/shard_map/pallas_call | solution.py:43
  129.0 4.1 %all-to-all-done.6.total = f32[16,1,128]{2,1,0:T(1,128)S(1)} async-done(((f32[16,1,128]{2,1,0:T(1,128)}), f32[16,1,128]{2,1,0:T(1,128)S(1)}, u32[]{:S(2)}, u32[]{:S(2)}) %all-to-all-start.6) | async-done | bytes 8224 | tf_op jit(solution)/shard_map/all_to_all | solution.py:466
  133.1 0.0 copy-done.1
  133.2 14.4 %all_to_all.46.got = f32[8,88,128]{2,1,0:T(8,128)S(1)} all-to-all(f32[8,88,128]{2,1,0:T(8,128)S(1)} %shard_map.103), channel_id=1, replica_groups={{0,16,32,48,64,80,96,112},{128,144,160,176,192,208,224,240},{256,272,28..., dimensions={0} | all-to-all | bytes 720896 | tf_op jit(solution)/shard_map/all_to_all | solution.py:471
  147.6 0.1 shard_map.104
  147.7 21.1 %all_to_all.47.got = f32[4,88,128]{2,1,0:T(8,128)S(1)} all-to-all(f32[4,88,128]{2,1,0:T(8,128)S(1)} %shard_map.104), channel_id=1, replica_groups={{0,128,256,384},{16,144,272,400},{32,160,288,416},{48,176,304,432},{64,..., dimensions={0} | all-to-all | bytes 360448 | tf_op jit(solution)/shard_map/all_to_all | solution.py:473
  168.8 0.6 shard_map.105
  (4 shorter events, 0.1 us)
Async XLA Ops:
  2.4 7.2 %copy-start = (f32[3,2,8,128]{3,2,1,0:T(8,128)S(1)}, f32[3,2,8,128]{3,2,1,0:T(8,128)}, u32[]{:S(2)}) copy-start(f32[3,2,8,128]{3,2,1,0:T(8,128)} %get-tuple-element.21.refs_1_.marks.refs_2_) | copy-start | bytes 73732
  2.4 7.2 %copy-start.2 = (f32[5,2,8,128]{3,2,1,0:T(8,128)S(1)}, f32[5,2,8,128]{3,2,1,0:T(8,128)}, u32[]{:S(2)}) copy-start(f32[5,2,8,128]{3,2,1,0:T(8,128)} %get-tuple-element.20.refs_0_.own) | copy-start | bytes 122884
  2.4 16.4 %all-to-all-start = ((f32[16,32,128]{2,1,0:T(8,128)}), f32[16,32,128]{2,1,0:T(8,128)S(1)}, u32[]{:S(2)}, u32[]{:S(2)}) async-start(f32[16,32,128]{2,1,0:T(8,128)} %get-tuple-element.22), calls=%async_computation | async-start | bytes 524288 | tf_op jit(solution)/shard_map/all_to_all | solution.py:422
  18.9 6.9 %collective-permute-start = (f32[13,12,128]{2,1,0:T(8,128)S(1)}, f32[13,12,128]{2,1,0:T(8,128)S(1)}, u32[]{:S(2)}, u32[]{:S(2)}) collective-permute-start(f32[13,12,128]{2,1,0:T(8,128)S(1)} %shard_map.88.refs_0_.refs_3_.wide), channel_id=1, source_target_pairs={{0,16},{16,0},{32,48},{48,32},{64,80},{80,64},{96,112},{112,96},{1... | collective-permute-start | bytes 239624 | tf_op jit(solution)/shard_map/ppermute | solution.py:425
  21.5 19.7 %collective-permute-start.1 = (f32[13,12,128]{2,1,0:T(8,128)S(1)}, f32[13,12,128]{2,1,0:T(8,128)S(1)}, u32[]{:S(2)}, u32[]{:S(2)}) collective-permute-start(f32[13,12,128]{2,1,0:T(8,128)S(1)} %shard_map.88.refs_0_.refs_3_.wide), channel_id=1, source_target_pairs={{16,32},{32,16},{48,64},{64,48},{80,96},{96,80},{112,128},{128,112... | collective-permute-start | bytes 239624 | tf_op jit(solution)/shard_map/ppermute | solution.py:425
  26.3 24.8 %all-to-all-start.1 = ((f32[16,1,128]{2,1,0:T(1,128)}), f32[16,1,128]{2,1,0:T(1,128)S(1)}, u32[]{:S(2)}, u32[]{:S(2)}) async-start(f32[16,1,128]{2,1,0:T(1,128)} %shard_map.91), calls=%async_computation.1 | async-start | bytes 16384 | tf_op jit(solution)/shard_map/all_to_all | solution.py:427
  52.0 12.7 %all-to-all-start.2 = ((f32[16,32,128]{2,1,0:T(8,128)}), f32[16,32,128]{2,1,0:T(8,128)S(1)}, u32[]{:S(2)}, u32[]{:S(2)}) async-start(f32[16,32,128]{2,1,0:T(8,128)} %get-tuple-element.26), calls=%async_computation.2 | async-start | bytes 524288 | tf_op jit(solution)/shard_map/all_to_all | solution.py:422
  64.7 6.9 %collective-permute-start.2 = (f32[13,12,128]{2,1,0:T(8,128)S(1)}, f32[13,12,128]{2,1,0:T(8,128)S(1)}, u32[]{:S(2)}, u32[]{:S(2)}) collective-permute-start(f32[13,12,128]{2,1,0:T(8,128)S(1)} %shard_map.94.refs_0_.wide), channel_id=1, source_target_pairs={{0,16},{16,0},{32,48},{48,32},{64,80},{80,64},{96,112},{112,96},{1... | collective-permute-start | bytes 239624 | tf_op jit(solution)/shard_map/ppermute | solution.py:425
  67.3 30.6 %collective-permute-start.3 = (f32[13,12,128]{2,1,0:T(8,128)S(1)}, f32[13,12,128]{2,1,0:T(8,128)S(1)}, u32[]{:S(2)}, u32[]{:S(2)}) collective-permute-start(f32[13,12,128]{2,1,0:T(8,128)S(1)} %shard_map.94.refs_0_.wide), channel_id=1, source_target_pairs={{16,32},{32,16},{48,64},{64,48},{80,96},{96,80},{112,128},{128,112... | collective-permute-start | bytes 239624 | tf_op jit(solution)/shard_map/ppermute | solution.py:425
  94.1 11.0 %all-to-all-start.4 = ((f32[32,1,128]{2,1,0:T(1,128)}), f32[32,1,128]{2,1,0:T(1,128)S(1)}, u32[]{:S(2)}, u32[]{:S(2)}) async-start(f32[32,1,128]{2,1,0:T(1,128)} %get-tuple-element.31), calls=%async_computation.4 | async-start | bytes 32768 | tf_op jit(solution)/shard_map/all_to_all | solution.py:456
  105.7 15.8 %all-to-all-start.5 = ((f32[16,1,128]{2,1,0:T(1,128)}), f32[16,1,128]{2,1,0:T(1,128)S(1)}, u32[]{:S(2)}, u32[]{:S(2)}) async-start(f32[16,1,128]{2,1,0:T(1,128)} %shard_map.101), calls=%async_computation.5 | async-start | bytes 16384 | tf_op jit(solution)/shard_map/all_to_all | solution.py:460
  122.2 10.9 %all-to-all-start.6 = ((f32[16,1,128]{2,1,0:T(1,128)}), f32[16,1,128]{2,1,0:T(1,128)S(1)}, u32[]{:S(2)}, u32[]{:S(2)}) async-start(f32[16,1,128]{2,1,0:T(1,128)} %get-tuple-element.33), calls=%async_computation.6 | async-start | bytes 16384 | tf_op jit(solution)/shard_map/all_to_all | solution.py:466
  125.7 7.4 %copy-start.1 = (s32[16,128]{1,0:T(8,128)S(1)}, s32[16,128]{1,0:T(8,128)}, u32[]{:S(2)}) copy-start(s32[16,128]{1,0:T(8,128)} %get-tuple-element.19.route) | copy-start | bytes 24580

commit v14 on v13

--- a/solution.py
+++ b/solution.py
@@ -77,16 +77,21 @@
 def fill_depth(state, marks, force, sent):
     depth, ndepth = row_block(), sent.shape[0]
     cols, rows = marks.shape[1:3]
-    row = 6 * cols * HALO
+    row = 5 * cols * HALO
     sent[...] = jnp.zeros(sent.shape, F32)
     sent[:, row : row + 1, :] = jnp.broadcast_to(force[None], (ndepth, 1, force.shape[1]))
     seen = [visible(state[c], marks[0, c], marks[1, c]) for c in range(cols)]
+    slot = lax.broadcasted_iota(jnp.int32, force.shape, 1)
 
     def put(target, rim):
+        last = force
         for c in range(cols):
-            for f in range(6):
+            for f in range(5):
                 at = (f * cols + c) * HALO
                 sent[target, at : at + HALO] = seen[c][f][rim : rim + HALO]
+            for k in range(HALO):
+                last = jnp.where(slot == 1 + c * HALO + k, marks[1, c][rim + k : rim + k + 1], last)
+        sent[target, row : row + 1] = last
 
     @pl.when(depth > 0)
     def _():
@@ -147,15 +152,22 @@
     above = got[jnp.maximum(depth - 1, 0)]
     below = got[jnp.minimum(depth + 1, ndepth - 1)]
     blank = [FAR, 0.0, 0.0, 0.0, 1.0, 0.0]
+    row = 5 * cols * HALO
     for c in range(cols):
         seen = visible([own[f, c] for f in range(5)], marks[0, c], marks[1, c])
         for f in range(6):
             at = (f * cols + c) * HALO
-            wide[f * cols + c, 0:HALO] = jnp.where(depth > 0, above[at : at + HALO], blank[f])
             wide[f * cols + c, HALO : rows + HALO] = seen[f]
-            wide[f * cols + c, rows + HALO :] = jnp.where(depth < ndepth - 1, below[at : at + HALO], blank[f])
-    row = 6 * cols * HALO
-    wide[6 * cols] = jnp.broadcast_to(jnp.sum(got[:, row : row + 1, :], axis=0), wide.shape[1:])
+            if f < 5:
+                wide[f * cols + c, 0:HALO] = jnp.where(depth > 0, above[at : at + HALO], blank[f])
+                wide[f * cols + c, rows + HALO :] = jnp.where(depth < ndepth - 1, below[at : at + HALO], blank[f])
+        for rim, start in ((above, 0), (below, rows + HALO)):
+            for k in range(HALO):
+                at, lane = start + k, 1 + c * HALO + k
+                live = jnp.where(wide[c, at : at + 1] < 0.5 * FAR, 1.0, 0.0)
+                wide[5 * cols + c, at : at + 1] = live * rim[row : row + 1, lane : lane + 1]
+    total = jnp.sum(got[:, row : row + 1, :], axis=0)[:, 0:1]
+    wide[6 * cols] = jnp.broadcast_to(total, wide.shape[1:])
 
 
 def pair_force_kernel(wide, swapped, force):
@@ -403,7 +415,7 @@
     far = ncut // near
     size = 5 * cols * rows
     state, marking = shape(5, cols, rows, slots), shape(3, cols, rows, slots)
-    message, vector = shape(ndepth, 32, slots), shape(2, slots)
+    message, vector = shape(ndepth, 24, slots), shape(2, slots)
     along_depth, along_plane, along_line = [shape(n, 1, slots) for n in (ndepth, 2 * ndepth, ncut // 2)]
     both = ("cut", "depth")
     pairs = range(0, ncut, 2)

time: 170 us -> 169 us (level)
  no operation moved by 1% of the time
where the time goes in v14:
time: 169 us; the launch traced here: 168 us
  blocking collectives  57 us (34%)
  starting transfers between devices  50.8 us (30%)
  Pallas kernels  30.1 us (18%)
  waiting for transfers between devices  29.5 us (17%)
    pallas_call x19, Pallas kernels, call(): pl.pallas_call(kernel, out_shape=outs, in_specs=[SMEM] * len(scalars) + [...  28.3 us
    all_to_all x1, blocking collectives, exchange(): lax.all_to_all(force, both, 0, 0, tiled=True, axis_index_groups=lines)  21.5 us
    all_to_all x1, blocking collectives, body(): got = lax.all_to_all(sent, 'cut', 0, 0, tiled=True, axis_index_groups=apart)  21.1 us
    all_to_all x1, starting transfers between devices, exchange(): lax.all_to_all(force, both, 0, 0, tiled=True, axis_index_groups=lines)  14.8 us
    all_to_all x1, blocking collectives, body(): got = lax.all_to_all(sent, 'cut', 0, 0, tiled=True, axis_index_groups=close)  14.4 us
    all_to_all x2, waiting for transfers between devices, exchange(): got = lax.all_to_all(sent, 'depth', 0, 0, tiled=True)  13 us
    all_to_all x2, starting transfers between devices, exchange(): got = lax.all_to_all(sent, 'depth', 0, 0, tiled=True)  10.7 us
    ppermute x2, starting transfers between devices, exchange(): lax.ppermute(wide, 'cut', cross)  7.25 us
  transfers between devices with their start and end apart: 10, of which 7 were waited for; matrix products, arithmetic and copies ran while one was open for 0% of the time, Pallas kernels for 15%

profile of v14, /device:TPU:64, one launch (start us, length us, event | category | flops | bytes accessed | tf_op | source)
XLA Modules:
  0.0 168.2 jit_solution(15016733396829764317)
XLA Ops:
  0.6 1.8 %shard_map.86 = (f32[5,2,8,128]{3,2,1,0:T(8,128)}, f32[3,2,8,128]{3,2,1,0:T(8,128)}, s32[16,128]{1,0:T(8,128)}, f32[16,24,128]{2,1,0:T(8,128)}) custom-call(f32[2,2,8,128]{3,2,1,0:T(8,128)} %refs_0_.1, f32[2,2,8,128]{3,2,1,0:T(8,128)} %refs_1_.1, f32[2,8,128]{2,1,0:T(8,128)} %refs_2_.1, s32[2,8]{1,0:T(2,128)} %refs_3_.1, s32[2,8]{1,0:T(2,128)} %refs_4_.1, ...), custom_call_target="tpu_custom_call" | custom-call | tf_op jit(solution)/shard_map/pallas_call | solution.py:448
  2.4 0.0 copy-start
  2.4 0.0 copy-start.2
  2.4 7.2 %all-to-all-start = ((f32[16,24,128]{2,1,0:T(8,128)}), f32[16,24,128]{2,1,0:T(8,128)S(1)}, u32[]{:S(2)}, u32[]{:S(2)}) async-start(f32[16,24,128]{2,1,0:T(8,128)} %get-tuple-element.22), calls=%async_computation | async-start | bytes 393216 | tf_op jit(solution)/shard_map/all_to_all | solution.py:434
  9.6 0.0 copy-done
  9.6 0.0 copy-done.2
  9.6 2.0 %shard_map.87.inner.refs_3_ = f32[3,2,8,128]{3,2,1,0:T(8,128)S(1)} custom-call(f32[5,2,8,128]{3,2,1,0:T(8,128)S(1)} %copy-done.2, f32[3,2,8,128]{3,2,1,0:T(8,128)S(1)} %copy-done), custom_call_target="tpu_custom_call" | custom-call | flops 20000000000 | bytes 1048576 | tf_op jit(solution)/shard_map/pallas_call | solution.py:43
  11.7 6.5 %all-to-all-done.got = f32[16,24,128]{2,1,0:T(8,128)S(1)} async-done(((f32[16,24,128]{2,1,0:T(8,128)}), f32[16,24,128]{2,1,0:T(8,128)S(1)}, u32[]{:S(2)}, u32[]{:S(2)}) %all-to-all-start) | async-done | bytes 196640 | tf_op jit(solution)/shard_map/all_to_all | solution.py:434
  18.2 0.1 shard_map.88.refs_0_.refs_3_.wide
  18.3 2.6 %collective-permute-start = (f32[13,12,128]{2,1,0:T(8,128)S(1)}, f32[13,12,128]{2,1,0:T(8,128)S(1)}, u32[]{:S(2)}, u32[]{:S(2)}) collective-permute-start(f32[13,12,128]{2,1,0:T(8,128)S(1)} %shard_map.88.refs_0_.refs_3_.wide), channel_id=1, source_target_pairs={{0,16},{16,0},{32,48},{48,32},{64,80},{80,64},{96,112},{112,96},{1... | collective-permute-start | bytes 239624 | tf_op jit(solution)/shard_map/ppermute | solution.py:437
  20.9 2.8 %collective-permute-start.1 = (f32[13,12,128]{2,1,0:T(8,128)S(1)}, f32[13,12,128]{2,1,0:T(8,128)S(1)}, u32[]{:S(2)}, u32[]{:S(2)}) collective-permute-start(f32[13,12,128]{2,1,0:T(8,128)S(1)} %shard_map.88.refs_0_.refs_3_.wide), channel_id=1, source_target_pairs={{16,32},{32,16},{48,64},{64,48},{80,96},{96,80},{112,128},{128,112... | collective-permute-start | bytes 239624 | tf_op jit(solution)/shard_map/ppermute | solution.py:437
  23.7 1.5 collective-permute-done.refs_1_.refs_4_.swapped
  25.2 0.6 shard_map.91
  25.8 14.8 %all-to-all-start.1 = ((f32[16,1,128]{2,1,0:T(1,128)}), f32[16,1,128]{2,1,0:T(1,128)S(1)}, u32[]{:S(2)}, u32[]{:S(2)}) async-start(f32[16,1,128]{2,1,0:T(1,128)} %shard_map.91), calls=%async_computation.1 | async-start | bytes 16384 | tf_op jit(solution)/shard_map/all_to_all | solution.py:439
  40.5 0.0 collective-permute-done.1.refs_2_.refs_5_
  40.5 6.3 %shard_map.89.refs_1_ = f32[3,4,10,128]{3,2,1,0:T(8,128)S(1)} custom-call(f32[13,12,128]{2,1,0:T(8,128)S(1)} %shard_map.88.refs_0_.refs_3_.wide, f32[13,12,128]{2,1,0:T(8,128)S(1)} %collective-permute-done.refs_1_.refs_4_.swapped, f32[13,12,128]{2,1,0:T(8,128)S(1)} %collective-permute-done.1.refs_2_.refs_5_, f32[3,2,8,128]{3,2,1,0:T(8,128)S(1)} %shard_map.87.inner.refs_3_), custom_call_target="tpu_custom_call" | custom-call | flops 20000000000 | bytes 1048576 | tf_op jit(solution)/shard_map/pallas_call | solution.py:43
  46.8 3.5 %shard_map.90 = (f32[5,2,8,128]{3,2,1,0:T(8,128)S(1)}, f32[3,2,8,128]{3,2,1,0:T(8,128)S(1)}) custom-call(f32[5,2,8,128]{3,2,1,0:T(8,128)S(1)} %copy-done.2, f32[3,4,10,128]{3,2,1,0:T(8,128)S(1)} %shard_map.89.refs_1_, f32[3,2,8,128]{3,2,1,0:T(8,128)S(1)} %copy-done, f32[13,12,128]{2,1,0:T(8,128)S(1)} %shard_map.88.refs_0_.refs_3_.wide, ...), custom_call_target="tpu_custom_call" | custom-call | flops 20000000000 | bytes 1048576 | tf_op jit(solution)/shard_map/pallas_call | solution.py:43
  50.4 0.2 all-to-all-done.1.total
  50.6 0.8 shard_map.92
  51.4 3.5 %all-to-all-start.2 = ((f32[16,24,128]{2,1,0:T(8,128)}), f32[16,24,128]{2,1,0:T(8,128)S(1)}, u32[]{:S(2)}, u32[]{:S(2)}) async-start(f32[16,24,128]{2,1,0:T(8,128)} %get-tuple-element.26), calls=%async_computation.2 | async-start | bytes 393216 | tf_op jit(solution)/shard_map/all_to_all | solution.py:434
  54.9 2.0 %shard_map.93.inner.refs_3_ = f32[3,2,8,128]{3,2,1,0:T(8,128)S(1)} custom-call(f32[5,2,8,128]{3,2,1,0:T(8,128)S(1)} %get-tuple-element.25.refs_0_.own, f32[3,2,8,128]{3,2,1,0:T(8,128)S(1)} %copy-done), custom_call_target="tpu_custom_call" | custom-call | flops 20000000000 | bytes 1048576 | tf_op jit(solution)/shard_map/pallas_call | solution.py:43
  57.0 6.5 %all-to-all-done.2.got = f32[16,24,128]{2,1,0:T(8,128)S(1)} async-done(((f32[16,24,128]{2,1,0:T(8,128)}), f32[16,24,128]{2,1,0:T(8,128)S(1)}, u32[]{:S(2)}, u32[]{:S(2)}) %all-to-all-start.2) | async-done | bytes 196640 | tf_op jit(solution)/shard_map/all_to_all | solution.py:434
  63.5 0.1 shard_map.94.refs_0_.wide
  63.6 2.6 %collective-permute-start.2 = (f32[13,12,128]{2,1,0:T(8,128)S(1)}, f32[13,12,128]{2,1,0:T(8,128)S(1)}, u32[]{:S(2)}, u32[]{:S(2)}) collective-permute-start(f32[13,12,128]{2,1,0:T(8,128)S(1)} %shard_map.94.refs_0_.wide), channel_id=1, source_target_pairs={{0,16},{16,0},{32,48},{48,32},{64,80},{80,64},{96,112},{112,96},{1... | collective-permute-start | bytes 239624 | tf_op jit(solution)/shard_map/ppermute | solution.py:437
  66.2 4.4 %collective-permute-start.3 = (f32[13,12,128]{2,1,0:T(8,128)S(1)}, f32[13,12,128]{2,1,0:T(8,128)S(1)}, u32[]{:S(2)}, u32[]{:S(2)}) collective-permute-start(f32[13,12,128]{2,1,0:T(8,128)S(1)} %shard_map.94.refs_0_.wide), channel_id=1, source_target_pairs={{16,32},{32,16},{48,64},{64,48},{80,96},{96,80},{112,128},{128,112... | collective-permute-start | bytes 239624 | tf_op jit(solution)/shard_map/ppermute | solution.py:437
  70.6 0.0 collective-permute-done.2.refs_1_.swapped
  70.6 21.5 %all_to_all.45.total = f32[16,1,128]{2,1,0:T(1,128)S(1)} all-to-all(f32[16,1,128]{2,1,0:T(1,128)S(1)} %shard_map.97), channel_id=1, replica_groups={{0,32,64,96,128,160,192,224,256,288,320,352,384,416,448,480},{1,33,65,9..., dimensions={0} | all-to-all | bytes 16384 | tf_op jit(solution)/shard_map/all_to_all | solution.py:439
  92.2 0.7 shard_map.98
  92.9 3.8 %all-to-all-start.4 = ((f32[32,1,128]{2,1,0:T(1,128)}), f32[32,1,128]{2,1,0:T(1,128)S(1)}, u32[]{:S(2)}, u32[]{:S(2)}) async-start(f32[32,1,128]{2,1,0:T(1,128)} %get-tuple-element.31), calls=%async_computation.4 | async-start | bytes 32768 | tf_op jit(solution)/shard_map/all_to_all | solution.py:468
  96.7 0.0 collective-permute-done.3.refs_2_.other
  96.8 3.2 %shard_map.95.first_found.before = f32[3,2,10,128]{3,2,1,0:T(8,128)S(1)} custom-call(f32[13,12,128]{2,1,0:T(8,128)S(1)} %shard_map.94.refs_0_.wide, f32[13,12,128]{2,1,0:T(8,128)S(1)} %collective-permute-done.2.refs_1_.swapped, f32[13,12,128]{2,1,0:T(8,128)S(1)} %collective-permute-done.3.refs_2_.other, f32[3,2,8,128]{3,2,1,0:T(8,128)S(1)} %shard_map.93.inner.refs_3_), custom_call_target="tpu_custom_call" | custom-call | flops 20000000000 | bytes 1048576 | tf_op jit(solution)/shard_map/pallas_call | solution.py:43
  100.0 3.9 %all-to-all-done.4.got = f32[32,1,128]{2,1,0:T(1,128)S(1)} async-done(((f32[32,1,128]{2,1,0:T(1,128)}), f32[32,1,128]{2,1,0:T(1,128)S(1)}, u32[]{:S(2)}, u32[]{:S(2)}) %all-to-all-start.4) | async-done | bytes 16416 | tf_op jit(solution)/shard_map/all_to_all | solution.py:468
  104.0 0.6 shard_map.101
  104.6 5.7 %all-to-all-start.5 = ((f32[16,1,128]{2,1,0:T(1,128)}), f32[16,1,128]{2,1,0:T(1,128)S(1)}, u32[]{:S(2)}, u32[]{:S(2)}) async-start(f32[16,1,128]{2,1,0:T(1,128)} %shard_map.101), calls=%async_computation.5 | async-start | bytes 16384 | tf_op jit(solution)/shard_map/all_to_all | solution.py:472
  110.3 3.4 %shard_map.96.last_found = f32[3,2,10,128]{3,2,1,0:T(8,128)S(1)} custom-call(f32[13,12,128]{2,1,0:T(8,128)S(1)} %shard_map.94.refs_0_.wide, f32[13,12,128]{2,1,0:T(8,128)S(1)} %collective-permute-done.2.refs_1_.swapped, f32[13,12,128]{2,1,0:T(8,128)S(1)} %collective-permute-done.3.refs_2_.other, f32[3,2,8,128]{3,2,1,0:T(8,128)S(1)} %shard_map.93.inner.refs_3_), custom_call_target="tpu_custom_call" | custom-call | flops 20000000000 | bytes 1048576 | tf_op jit(solution)/shard_map/pallas_call | solution.py:43
  113.6 0.1 shard_map.99
  113.7 6.7 %all-to-all-done.5.total = f32[16,1,128]{2,1,0:T(1,128)S(1)} async-done(((f32[16,1,128]{2,1,0:T(1,128)}), f32[16,1,128]{2,1,0:T(1,128)S(1)}, u32[]{:S(2)}, u32[]{:S(2)}) %all-to-all-start.5) | async-done | bytes 8224 | tf_op jit(solution)/shard_map/all_to_all | solution.py:472
  120.4 0.7 shard_map.102
  121.1 3.5 %all-to-all-start.6 = ((f32[16,1,128]{2,1,0:T(1,128)}), f32[16,1,128]{2,1,0:T(1,128)S(1)}, u32[]{:S(2)}, u32[]{:S(2)}) async-start(f32[16,1,128]{2,1,0:T(1,128)} %get-tuple-element.33), calls=%async_computation.6 | async-start | bytes 16384 | tf_op jit(solution)/shard_map/all_to_all | solution.py:478
  124.6 0.0 copy-start.1
  124.6 3.3 %shard_map.100.found = f32[3,2,8,128]{3,2,1,0:T(8,128)S(1)} custom-call(f32[5,4,10,128]{3,2,1,0:T(8,128)S(1)} %get-tuple-element.30.refs_0_), custom_call_target="tpu_custom_call" | custom-call | flops 20000000000 | bytes 1048576 | tf_op jit(solution)/shard_map/pallas_call | solution.py:43
  127.9 4.1 %all-to-all-done.6.total = f32[16,1,128]{2,1,0:T(1,128)S(1)} async-done(((f32[16,1,128]{2,1,0:T(1,128)}), f32[16,1,128]{2,1,0:T(1,128)S(1)}, u32[]{:S(2)}, u32[]{:S(2)}) %all-to-all-start.6) | async-done | bytes 8224 | tf_op jit(solution)/shard_map/all_to_all | solution.py:478
  132.0 0.0 copy-done.1
  132.0 14.4 %all_to_all.46.got = f32[8,88,128]{2,1,0:T(8,128)S(1)} all-to-all(f32[8,88,128]{2,1,0:T(8,128)S(1)} %shard_map.103), channel_id=1, replica_groups={{0,16,32,48,64,80,96,112},{128,144,160,176,192,208,224,240},{256,272,28..., dimensions={0} | all-to-all | bytes 720896 | tf_op jit(solution)/shard_map/all_to_all | solution.py:483
  146.5 0.1 shard_map.104
  146.5 21.1 %all_to_all.47.got = f32[4,88,128]{2,1,0:T(8,128)S(1)} all-to-all(f32[4,88,128]{2,1,0:T(8,128)S(1)} %shard_map.104), channel_id=1, replica_groups={{0,128,256,384},{16,144,272,400},{32,160,288,416},{48,176,304,432},{64,..., dimensions={0} | all-to-all | bytes 360448 | tf_op jit(solution)/shard_map/all_to_all | solution.py:485
  167.6 0.6 shard_map.105
  (2 shorter events, 0.0 us)
Async XLA Ops:
  2.4 7.2 %copy-start = (f32[3,2,8,128]{3,2,1,0:T(8,128)S(1)}, f32[3,2,8,128]{3,2,1,0:T(8,128)}, u32[]{:S(2)}) copy-start(f32[3,2,8,128]{3,2,1,0:T(8,128)} %get-tuple-element.21.refs_1_.marks.refs_2_) | copy-start | bytes 73732
  2.4 7.2 %copy-start.2 = (f32[5,2,8,128]{3,2,1,0:T(8,128)S(1)}, f32[5,2,8,128]{3,2,1,0:T(8,128)}, u32[]{:S(2)}) copy-start(f32[5,2,8,128]{3,2,1,0:T(8,128)} %get-tuple-element.20.refs_0_.own) | copy-start | bytes 122884
  2.4 15.8 %all-to-all-start = ((f32[16,24,128]{2,1,0:T(8,128)}), f32[16,24,128]{2,1,0:T(8,128)S(1)}, u32[]{:S(2)}, u32[]{:S(2)}) async-start(f32[16,24,128]{2,1,0:T(8,128)} %get-tuple-element.22), calls=%async_computation | async-start | bytes 393216 | tf_op jit(solution)/shard_map/all_to_all | solution.py:434
  18.3 6.9 %collective-permute-start = (f32[13,12,128]{2,1,0:T(8,128)S(1)}, f32[13,12,128]{2,1,0:T(8,128)S(1)}, u32[]{:S(2)}, u32[]{:S(2)}) collective-permute-start(f32[13,12,128]{2,1,0:T(8,128)S(1)} %shard_map.88.refs_0_.refs_3_.wide), channel_id=1, source_target_pairs={{0,16},{16,0},{32,48},{48,32},{64,80},{80,64},{96,112},{112,96},{1... | collective-permute-start | bytes 239624 | tf_op jit(solution)/shard_map/ppermute | solution.py:437
  20.9 19.7 %collective-permute-start.1 = (f32[13,12,128]{2,1,0:T(8,128)S(1)}, f32[13,12,128]{2,1,0:T(8,128)S(1)}, u32[]{:S(2)}, u32[]{:S(2)}) collective-permute-start(f32[13,12,128]{2,1,0:T(8,128)S(1)} %shard_map.88.refs_0_.refs_3_.wide), channel_id=1, source_target_pairs={{16,32},{32,16},{48,64},{64,48},{80,96},{96,80},{112,128},{128,112... | collective-permute-start | bytes 239624 | tf_op jit(solution)/shard_map/ppermute | solution.py:437
  25.8 24.8 %all-to-all-start.1 = ((f32[16,1,128]{2,1,0:T(1,128)}), f32[16,1,128]{2,1,0:T(1,128)S(1)}, u32[]{:S(2)}, u32[]{:S(2)}) async-start(f32[16,1,128]{2,1,0:T(1,128)} %shard_map.91), calls=%async_computation.1 | async-start | bytes 16384 | tf_op jit(solution)/shard_map/all_to_all | solution.py:439
  51.4 12.1 %all-to-all-start.2 = ((f32[16,24,128]{2,1,0:T(8,128)}), f32[16,24,128]{2,1,0:T(8,128)S(1)}, u32[]{:S(2)}, u32[]{:S(2)}) async-start(f32[16,24,128]{2,1,0:T(8,128)} %get-tuple-element.26), calls=%async_computation.2 | async-start | bytes 393216 | tf_op jit(solution)/shard_map/all_to_all | solution.py:434
  63.6 7.0 %collective-permute-start.2 = (f32[13,12,128]{2,1,0:T(8,128)S(1)}, f32[13,12,128]{2,1,0:T(8,128)S(1)}, u32[]{:S(2)}, u32[]{:S(2)}) collective-permute-start(f32[13,12,128]{2,1,0:T(8,128)S(1)} %shard_map.94.refs_0_.wide), channel_id=1, source_target_pairs={{0,16},{16,0},{32,48},{48,32},{64,80},{80,64},{96,112},{112,96},{1... | collective-permute-start | bytes 239624 | tf_op jit(solution)/shard_map/ppermute | solution.py:437
  66.2 30.6 %collective-permute-start.3 = (f32[13,12,128]{2,1,0:T(8,128)S(1)}, f32[13,12,128]{2,1,0:T(8,128)S(1)}, u32[]{:S(2)}, u32[]{:S(2)}) collective-permute-start(f32[13,12,128]{2,1,0:T(8,128)S(1)} %shard_map.94.refs_0_.wide), channel_id=1, source_target_pairs={{16,32},{32,16},{48,64},{64,48},{80,96},{96,80},{112,128},{128,112... | collective-permute-start | bytes 239624 | tf_op jit(solution)/shard_map/ppermute | solution.py:437
  92.9 11.0 %all-to-all-start.4 = ((f32[32,1,128]{2,1,0:T(1,128)}), f32[32,1,128]{2,1,0:T(1,128)S(1)}, u32[]{:S(2)}, u32[]{:S(2)}) async-start(f32[32,1,128]{2,1,0:T(1,128)} %get-tuple-element.31), calls=%async_computation.4 | async-start | bytes 32768 | tf_op jit(solution)/shard_map/all_to_all | solution.py:468
  104.6 15.8 %all-to-all-start.5 = ((f32[16,1,128]{2,1,0:T(1,128)}), f32[16,1,128]{2,1,0:T(1,128)S(1)}, u32[]{:S(2)}, u32[]{:S(2)}) async-start(f32[16,1,128]{2,1,0:T(1,128)} %shard_map.101), calls=%async_computation.5 | async-start | bytes 16384 | tf_op jit(solution)/shard_map/all_to_all | solution.py:472
  121.1 10.9 %all-to-all-start.6 = ((f32[16,1,128]{2,1,0:T(1,128)}), f32[16,1,128]{2,1,0:T(1,128)S(1)}, u32[]{:S(2)}, u32[]{:S(2)}) async-start(f32[16,1,128]{2,1,0:T(1,128)} %get-tuple-element.33), calls=%async_computation.6 | async-start | bytes 16384 | tf_op jit(solution)/shard_map/all_to_all | solution.py:478
  124.6 7.4 %copy-start.1 = (s32[16,128]{1,0:T(8,128)S(1)}, s32[16,128]{1,0:T(8,128)}, u32[]{:S(2)}) copy-start(s32[16,128]{1,0:T(8,128)} %get-tuple-element.19.route) | copy-start | bytes 24580
